TPU v7x, 32 devices: a whole 2x2x4 slice. The times are simulated.
32 devices in a mesh: pair: 16 (over z, x, core), pw: 2 (over y).
Axes of the slice: x: 2, y: 2, z: 4, core: 2. Of those that a mesh axis runs over, the one named last changes fastest.
Arguments:
- screened: bfloat16 [16, 4096, 4096], P('pair', 'pw'), may hold values from -0.09375 to 0.09375
- density: bfloat16 [16, 4096, 256], P('pair', 'pw'), may hold values from -0.75 to 0.75
- transform: bfloat16 [64, 256, 256], P('pw'), may hold values from -0.375 to 0.375
- energy: float32 [16384], P('pw'), may hold values from -1 to 1
- trial: bfloat16 [16384, 128], P('pw'), may hold values from -6 to 6
- coarse_index: int32 [64, 64, 4], P('pair', 'pw'), may hold values from 0 to 15, as said below
- interp_weight: bfloat16 [64, 64, 4], P('pair', 'pw'), may hold values from 0.1 to 1, as said below
- bands: int32 [64], replicated, may hold values from 8 to 16, as said below
Outputs:
- first_step: bfloat16 [16384, 128], P('pair')
- second_step: float32 [16384, 128], P('pw')
Inputs may be any that keep to these rules, and one draw needn't show every extreme that they name: coarse_index[k, q, j] equals coarse_index[q, k, j]. interp_weight[k, q, j] equals interp_weight[q, k, j]. Some fine k-point has all 16 conduction bands live.
All inputs are finite; a program needn't handle non-finite values.
Results may differ from a plain program's by a relative error of at most 0.01.
Values may be sent and summed in bfloat16 or wider, within the bound.
No kernel may reach another device: no remote copies, remote signals or barrier semaphores. Data moves between devices by JAX's collectives and lax.ppermute only.
A program may use at most 128 MiB of HBM per device.

v0:
```python
import math

import jax
import jax.numpy as jnp
from jax import lax
from jax.sharding import PartitionSpec as P

NCOND = 16


def spread(value, axis, source):
    kept = jnp.where(lax.axis_index(axis) == source, value, 0).astype(value.dtype)
    return lax.psum(kept, axis)


def shards(screened, density, transform, energy, trial, coarse_index, interp_weight, bands):
    pair_count = lax.axis_size("pair")
    row_index = lax.axis_index("pair")
    col_index = lax.axis_index("pw")
    local_pairs = screened.shape[0]
    transitions = density.shape[2]
    row_points = coarse_index.shape[0]
    col_points = coarse_index.shape[1]
    fine_points = bands.shape[0]
    coarse_count = local_pairs * pair_count
    applied = jnp.einsum(
        "pgh,pht->pgt",
        screened,
        lax.all_gather(density, "pw", axis=1, tiled=True),
        preferred_element_type=jnp.float32,
    ).astype(jnp.bfloat16)
    raw_sum = jnp.einsum("pgs,pgt->pst", density, applied, preferred_element_type=jnp.float32)
    symmetric = 0.5 * (raw_sum + jnp.swapaxes(raw_sum, 1, 2))
    selector = (
        coarse_index[:, :, :, None]
        == jnp.arange(coarse_count, dtype=jnp.int32)[None, None, None, :]
    ).astype(jnp.bfloat16)
    mix_coef = interp_weight[:, :, :, None] * selector
    kernel = lax.psum(symmetric, "pw").astype(jnp.bfloat16)
    mixture = jnp.einsum(
        "abjc,cst->abst",
        mix_coef,
        lax.all_gather(kernel, "pair", axis=0, tiled=True),
        preferred_element_type=jnp.float32,
    )
    mixture = mixture.astype(jnp.bfloat16)
    first_point = row_index * row_points
    root_index = first_point // col_points
    point_offset = first_point % col_points
    wanted_block = lax.dynamic_slice_in_dim(transform, point_offset, row_points, 0)
    left_turn = spread(wanted_block, "pw", root_index)
    turned = jnp.einsum(
        "abst,btu->absu", mixture, transform, preferred_element_type=jnp.float32
    ).astype(jnp.bfloat16)
    product = jnp.einsum("asv,absu->avbu", left_turn, turned, preferred_element_type=jnp.float32)
    positions = jnp.arange(transitions) % NCOND
    row_bands = lax.dynamic_slice_in_dim(bands, first_point, row_points, 0)
    col_bands = lax.dynamic_slice_in_dim(bands, col_index * col_points, col_points, 0)
    row_live = (positions[None, :] < row_bands[:, None]).astype(jnp.float32)
    col_live = (positions[None, :] < col_bands[:, None]).astype(jnp.float32)
    norm_scale = 1.0 / math.sqrt(fine_points * transitions)
    row_ids = first_point + jnp.arange(row_points)
    col_ids = col_index * col_points + jnp.arange(col_points)
    same_point = (row_ids[:, None] == col_ids[None, :]).astype(jnp.float32)
    energies = energy.reshape(col_points, transitions)
    identity = jnp.eye(transitions, dtype=jnp.float32)
    diagonal_part = identity[None, :, None, :] * (
        same_point[:, None, :, None] * energies[None, None, :, :]
    )
    local_matrix = (
        product * row_live[:, :, None, None] * col_live[None, None, :, :] * norm_scale
        + diagonal_part
    )
    local_matrix = local_matrix.astype(jnp.bfloat16).reshape(
        row_points * transitions, col_points * transitions
    )
    partial_rows = jnp.dot(local_matrix, trial, preferred_element_type=jnp.float32)
    first_step = lax.psum(partial_rows, "pw").astype(jnp.bfloat16)
    partial_cols = lax.dot_general(
        local_matrix, first_step, (((0,), (0,)), ((), ())), preferred_element_type=jnp.float32
    )
    summed = lax.psum(partial_cols, "pair")
    second_step = 2.0 * summed - trial.astype(jnp.float32)
    return (first_step, second_step)


def solution(mesh):
    in_specs = (
        P("pair", "pw", None),
        P("pair", "pw", None),
        P("pw", None, None),
        P("pw"),
        P("pw", None),
        P("pair", "pw", None),
        P("pair", "pw", None),
        P(),
    )
    out_specs = (P("pair", None), P("pw", None))
    return jax.shard_map(shards, mesh=mesh, in_specs=in_specs, out_specs=out_specs, check_vma=False)
```

profile of v0, /device:TPU:0, one launch (start us, length us, event | category | flops | bytes accessed | tf_op | source)
XLA Modules:
  0.0 355.4 jit_solution(14734177207356460512)
XLA Ops:
  7.2 0.0 all-gather.3.cloned.1.call-start
  7.2 0.7 all-gather.3.cloned.1.call-update
  7.9 0.0 copy-start.6
  7.9 0.0 copy-start.3
  7.9 0.0 copy-start.4
  7.9 0.0 copy-start.5
  7.9 0.0 all-gather.5.cloned.1.call-start
  8.0 37.4 %all-gather.3.cloned.1.call-done = bf16[1,4096,256]{2,1,0:T(8,128)(2,1)} async-done(((bf16[1,2048,256]{2,1,0:T(8,128)(2,1)}), bf16[1,4096,256]{2,1,0:T(8,128)(2,1)}) %all-gather.3.cloned.1.call-update) | async-done | bytes 2097168 | tf_op jit(solution)/shard_map/all_gather | solution.py:29
  45.4 11.7 %convolution_bitcast_fusion = f32[1,256,256]{1,2,0:T(8,128)S(1)} fusion(bf16[1,2048,256]{2,1,0:T(8,128)(2,1)} %param.9, bf16[1,2048,4096]{2,1,0:T(8,128)(2,1)} %param.8, bf16[1,4096,256]{2,1,0:T(8,128)(2,1)} %all-gather.3.cloned.1.call-done), kind=kOutput, calls=%fused_computation.15 | convolution fusion | flops 4563927040 | bytes 20185088 | tf_op jit(solution)/shard_map/pgs,pgt->pst/dot_general | solution.py:32
  57.1 0.1 copy.28
  57.3 10.5 %all-reduce.8 = bf16[1,256,256]{1,2,0:T(8,128)(2,1)S(1)} all-reduce(f32[1,256,256]{1,2,0:T(8,128)S(1)} %fusion.29), channel_id=1, replica_groups=mesh['pair'=16,'pw'=2] {'pw'}, use_global_device_ids=true, to_apply=%region_2.3 | all-reduce | flops 65536 | bytes 393216 | tf_op jit(solution)/shard_map/psum | solution.py:39
  67.8 0.8 copy.29
  68.6 0.0 all-gather.5.cloned.1.call-update
  68.6 0.0 all-reduce.5.cloned.1.call-start
  68.7 1.1 constant_dynamic-slice_fusion
  69.8 0.2 copy.35
  70.0 0.8 broadcast_select_fusion
  70.8 0.0 all-reduce.5.cloned.1.call-update
  70.9 0.2 all-reduce.7.cloned.1.call-start
  71.1 0.0 copy-done.6
  71.2 0.1 dynamic_slice.11
  71.2 0.1 dynamic_slice.10
  71.3 0.1 compare_convert_fusion.1
  71.4 0.1 compare_convert_fusion
  71.5 0.0 copy-done.3
  71.5 0.1 compare_convert_fusion.2
  71.6 0.0 copy-done.4
  71.6 0.0 copy-done.5
  71.6 0.1 broadcast_multiply_fusion
  71.7 39.5 %all-gather.5.cloned.1.call-done = bf16[16,256,256]{2,1,0:T(8,128)(2,1)} async-done(((bf16[1,256,256]{2,1,0:T(8,128)(2,1)}), bf16[16,256,256]{2,1,0:T(8,128)(2,1)}) %all-gather.5.cloned.1.call-update) | async-done | bytes 2097168 | tf_op jit(solution)/shard_map/all_gather | solution.py:43
  111.2 9.8 %convolution_convert_fusion = bf16[4,32,256,256]{3,1,2,0:T(8,128)(2,1)} fusion(bf16[16,256,256]{2,1,0:T(8,128)(2,1)} %all-gather.5.cloned.1.call-done, bf16[4,32,16]{1,2,0:T(8,128)(2,1)S(1)} %convert_reduce_fusion), kind=kOutput, calls=%fused_computation.8 | convolution fusion | flops 268435456 | bytes 18878464 | tf_op jit(solution)/shard_map/abjc,cst->abst/dot_general | solution.py:40
  121.0 20.5 %all-reduce.5.cloned.1.call-done = bf16[4,256,256]{1,2,0:T(8,128)(2,1)} async-done(((bf16[4,256,256]{1,2,0:T(8,128)(2,1)}), bf16[4,256,256]{1,2,0:T(8,128)(2,1)}) %all-reduce.5.cloned.1.call-update) | async-done | bytes 524304 | tf_op jit(solution)/shard_map/psum | solution.py:13
  141.4 19.4 %add_convert_fusion = bf16[4,256,32,256]{3,1,2,0:T(8,128)(2,1)} fusion(f32[4,32,256]{2,1,0:T(8,128)S(1)} %broadcast_multiply_fusion, f32[256,256]{1,0:T(8,128)S(1)} %fusion.30, f32[32,256]{1,0:T(8,128)S(1)} %compare_convert_fusion, f32[4,256]{1,0:T(4,128)S(1)} %compare_convert_fusion.1, bf16[4,32,256,256]{3,1,2,0:T(8,128)(2,1)} %convolution_convert_fusion, ...), kind=kOutput, calls=%fused_computation | convolution fusion | flops 8648654848 | bytes 38703104 | tf_op jit(solution)/shard_map/asv,absu->avbu/dot_general | solution.py:55
  160.8 17.9 %copy.32 = bf16[4,256,32,256]{3,2,1,0:T(8,128)(2,1)} copy(bf16[4,256,32,256]{3,1,2,0:T(8,128)(2,1)} %add_convert_fusion) | data formatting | bytes 33554432 | tf_op jit(solution)/shard_map/convert_element_type | solution.py:74
  178.7 0.0 copy-start.1
  178.7 16.2 %copy.36 = bf16[128,8,32,256]{3,1,2,0:T(8,128)(2,1)S(1)} copy(bf16[128,8,32,256]{3,2,1,0:T(8,128)(2,1)} %bitcast.54) | data formatting | bytes 33554432
  194.9 0.0 copy-start
  194.9 5.7 %copy-done = bf16[128,8,32,256]{3,1,2,0:T(8,128)(2,1)} copy-done((bf16[128,8,32,256]{3,1,2,0:T(8,128)(2,1)}, bf16[128,8,32,256]{3,1,2,0:T(8,128)(2,1)S(1)}, u32[]{:S(2)}) %copy-start) | copy-done | bytes 16777240
  200.6 0.0 copy-done.1
  200.6 4.5 %fusion.33 = f32[1024,128]{1,0:T(8,128)S(1)} fusion(bf16[1024,8192]{1,0:T(8,128)(2,1)S(1)} %bitcast.52, bf16[8192,128]{1,0:T(8,128)(2,1)S(1)} %copy-done.1), kind=kOutput, calls=%fused_computation.35 | convolution fusion | flops 2147483648 | bytes 19398656 | tf_op jit(solution)/shard_map/dot_general | solution.py:77
  205.1 16.3 %all-reduce.9 = bf16[1024,128]{1,0:T(8,128)(2,1)S(1)} all-reduce(f32[1024,128]{1,0:T(8,128)S(1)} %fusion.33), channel_id=1, replica_groups=mesh['pair'=16,'pw'=2] {'pw'}, use_global_device_ids=true, to_apply=%region_3.4 | all-reduce | flops 131072 | bytes 786432 | tf_op jit(solution)/shard_map/psum | solution.py:78
  221.4 0.0 copy-start.2
  221.4 10.3 %fusion.34 = f32[8192,128]{1,0:T(8,128)} fusion(bf16[1024,8192]{1,0:T(8,128)(2,1)} %bitcast.53, bf16[1024,128]{1,0:T(8,128)(2,1)S(1)} %all-reduce.9), kind=kOutput, calls=%fused_computation.36 | convolution fusion | flops 2147483648 | bytes 21233664 | tf_op jit(solution)/shard_map/dot_general | solution.py:79
  231.7 0.0 all-reduce.7.cloned.1.call-update
  231.7 112.6 %all-reduce.7.cloned.1.call-done = f32[8192,128]{1,0:T(8,128)} async-done(((f32[8192,128]{1,0:T(8,128)}), f32[8192,128]{1,0:T(8,128)}) %all-reduce.7.cloned.1.call-update) | async-done | bytes 4194320 | tf_op jit(solution)/shard_map/psum | solution.py:82
  344.3 4.6 %convert_subtract_fusion = f32[8192,128]{1,0:T(8,128)} fusion(bf16[8192,128]{1,0:T(8,128)(2,1)S(1)} %copy-done.1, f32[8192,128]{1,0:T(8,128)} %all-reduce.7.cloned.1.call-done), kind=kLoop, calls=%fused_computation.10 | loop fusion | flops 3145728 | bytes 10485760 | tf_op jit(solution)/shard_map/sub | solution.py:83
  348.9 0.0 copy-done.2
  (7 shorter events, 0.1 us)
Async XLA Ops:
  7.2 38.2 %all-gather.3.cloned.1.call-start = ((), (), s32[]{:S(2)}) async-start(), calls=%async_computation.1 | async-start | bytes 3145728 | tf_op jit(solution)/shard_map/all_gather | solution.py:29
  7.9 63.3 %copy-start.6 = (s32[64]{0:T(128)S(1)}, s32[64]{0:T(128)}, u32[]{:S(2)}) copy-start(s32[64]{0:T(128)} %param.15) | copy-start | bytes 772
  7.9 63.6 %copy-start.3 = (f32[8192]{0:T(1024)S(1)}, f32[8192]{0:T(1024)}, u32[]{:S(2)}) copy-start(f32[8192]{0:T(1024)} %param.11) | copy-start | bytes 98308
  7.9 63.6 %copy-start.4 = (s32[4,32,4]{1,2,0:T(4,128)S(1)}, s32[4,32,4]{1,2,0:T(4,128)}, u32[]{:S(2)}) copy-start(s32[4,32,4]{1,2,0:T(4,128)} %param.13) | copy-start | bytes 6148
  7.9 63.6 %copy-start.5 = (bf16[4,32,4]{1,2,0:T(4,128)(2,1)S(1)}, bf16[4,32,4]{1,2,0:T(4,128)(2,1)}, u32[]{:S(2)}) copy-start(bf16[4,32,4]{1,2,0:T(4,128)(2,1)} %param.14) | copy-start | bytes 3076
  7.9 103.2 %all-gather.5.cloned.1.call-start = ((), (), s32[]{:S(2)}) async-start(), calls=%async_computation.2 | async-start | bytes 2228224 | tf_op jit(solution)/shard_map/all_gather | solution.py:43
  68.6 72.8 %all-reduce.5.cloned.1.call-start = ((), (), s32[]{:S(2)}) async-start(), calls=%async_computation | async-start | bytes 1048576 | tf_op jit(solution)/shard_map/psum | solution.py:13
  70.9 273.4 %all-reduce.7.cloned.1.call-start = ((), (), s32[]{:S(2)}) async-start(), calls=%async_computation.3 | async-start | bytes 8388608 | tf_op jit(solution)/shard_map/psum | solution.py:82
  178.7 21.9 %copy-start.1 = (bf16[8192,128]{1,0:T(8,128)(2,1)S(1)}, bf16[8192,128]{1,0:T(8,128)(2,1)}, u32[]{:S(2)}) copy-start(bf16[8192,128]{1,0:T(8,128)(2,1)} %param.12) | copy-start | bytes 6291460
  194.9 5.7 %copy-start = (bf16[128,8,32,256]{3,1,2,0:T(8,128)(2,1)}, bf16[128,8,32,256]{3,1,2,0:T(8,128)(2,1)S(1)}, u32[]{:S(2)}) copy-start(bf16[128,8,32,256]{3,1,2,0:T(8,128)(2,1)S(1)} %copy.36) | copy-start | bytes 50331652
  221.4 127.5 %copy-start.2 = (bf16[1024,128]{1,0:T(8,128)(2,1)}, bf16[1024,128]{1,0:T(8,128)(2,1)S(1)}, u32[]{:S(2)}) copy-start(bf16[1024,128]{1,0:T(8,128)(2,1)S(1)} %all-reduce.9) | copy-start | bytes 786436
Sparse Core Ops, SparseCore 0:
  9.5 35.8 all-gather.2
  68.7 42.3 all-gather.4
  114.0 27.3 all-reduce.4
  231.8 112.3 all-reduce.6
where the time goes:
time: 356 us; the launch traced here: 355 us
  waiting for transfers between devices  211 us (59%)
  matrix products  55.7 us (16%)
  local copies, waits for them, and re-layouts  42.1 us (12%)
  blocking collectives  26.8 us (8%)
  between operations  14 us (4%)
  other arithmetic  5.82 us (2%)
    psum x1, waiting for transfers between devices, shards(): summed = lax.psum(partial_cols, 'pair')  113 us
    all_gather x1, waiting for transfers between devices, shards(): lax.all_gather(kernel, 'pair', axis=0, tiled=True)  39.5 us
    all_gather x1, waiting for transfers between devices, shards(): lax.all_gather(density, 'pw', axis=1, tiled=True)  37.4 us
    unnamed x16, local copies, waits for them, and re-layouts  22.1 us
    psum x1, waiting for transfers between devices, spread(): return lax.psum(kept, axis)  20.5 us
    dot_general x1, matrix products, shards(): jnp.einsum('asv,absu->avbu', left_turn, turned, preferred_element_type=jn...  19.4 us
    convert_element_type x1, local copies, waits for them, and re-layouts, shards(): local_matrix.astype(jnp.bfloat16)  17.9 us
    psum x1, blocking collectives, shards(): first_step = lax.psum(partial_rows, 'pw').astype(jnp.bfloat16)  16.3 us
  transfers between devices with their start and end apart: 4, of which 4 were waited for; matrix products, arithmetic and copies ran while one was open for 3% of the time, Pallas kernels for 0%

commit v1 on v0

v1 whole, which is shorter than its diff:
```python
import math

import jax
import jax.numpy as jnp
from jax import lax
from jax.sharding import PartitionSpec as P

NCOND = 16
F32 = jnp.float32
BF16 = jnp.bfloat16


def from_ahead(value, axis, step):
    count = lax.axis_size(axis)
    return lax.ppermute(value, axis, [((s + step) % count, s) for s in range(count)])


def flipped(value, axis, bit):
    count = lax.axis_size(axis)
    return lax.ppermute(value, axis, [(s, s ^ bit) for s in range(count)])


def plane_blocks(value):
    return [value] + [from_ahead(value, "pw", d) for d in range(1, lax.axis_size("pw"))]


def pair_blocks(value):
    count = lax.axis_size("pair")
    far = [value] + [from_ahead(value, "pair", 4 * d) for d in range(1, count // 4)]
    side = far + [flipped(block, "pair", 2) for block in far]
    return side + [flipped(block, "pair", 1) for block in side]


def pair_order():
    count = lax.axis_size("pair")
    me = lax.axis_index("pair")
    steps = jnp.arange(count // 4)
    far = (me + 4 * steps) % count
    side = jnp.concatenate([far, far ^ 2])
    return jnp.concatenate([side, side ^ 1])


def plane_sum(value):
    blocks = plane_blocks(value)
    if len(blocks) == 2:
        return blocks[0].astype(F32) + blocks[1].astype(F32)
    stacked = jnp.roll(jnp.stack(blocks), lax.axis_index("pw"), axis=0)
    return jnp.sum(stacked.astype(F32), axis=0)


def shards(screened, density, transform, energy, trial, coarse_index, interp_weight, bands):
    pair_count = lax.axis_size("pair")
    plane_count = lax.axis_size("pw")
    row_index = lax.axis_index("pair")
    col_index = lax.axis_index("pw")
    rows_here = density.shape[1]
    transitions = density.shape[2]
    row_points = coarse_index.shape[0]
    col_points = coarse_index.shape[1]
    fine_points = bands.shape[0]
    columns = trial.shape[1]
    mine = columns // pair_count
    norm_scale = 1.0 / math.sqrt(fine_points * transitions)

    table = jnp.concatenate([coarse_index.astype(BF16), interp_weight], axis=2)
    table = lax.all_gather(table.reshape(row_points, -1), "pair", axis=0, tiled=True)
    table = table.reshape(fine_points, col_points, -1)
    table = jnp.roll(table, -col_index * col_points, axis=0)
    neighbours = coarse_index.shape[2]
    order = pair_order().astype(F32)

    def coefficients(index, weight):
        hit = index.astype(F32)[..., None, :] == order[:, None]
        return jnp.sum(jnp.where(hit, weight.astype(F32)[..., None, :], 0.0), axis=-1)

    mix = coefficients(table[..., :neighbours], table[..., neighbours:])
    mix = jnp.transpose(mix, (2, 1, 0)).astype(BF16)
    widen = (
        jnp.arange(fine_points)[:, None] == jnp.arange(fine_points * mine)[None, :] // mine
    ).astype(BF16)
    wide = jnp.einsum("ckq,qm->ckm", mix, widen, preferred_element_type=F32).astype(BF16)
    same_column = jnp.arange(mine)[:, None] == (jnp.arange(fine_points * mine) % mine)[None, :]
    mixer = jnp.where(same_column[None, None], wide[:, :, None, :], 0).reshape(
        pair_count, col_points * mine, fine_points * mine
    )

    positions = jnp.arange(transitions) % NCOND
    live = (positions[None, :] < bands[:, None]).astype(F32)
    my_live = lax.dynamic_slice_in_dim(live, col_index * col_points, col_points, 0)
    energies = energy.reshape(col_points, transitions)
    trial_blocks = trial.reshape(col_points, transitions, columns)
    pick = (
        jnp.arange(columns)[None, :] == row_index * mine + jnp.arange(mine)[:, None]
    ).astype(BF16)
    my_trial = jnp.einsum("nm,qum->qnu", pick, trial_blocks, preferred_element_type=F32)

    def turn(vectors):
        return jnp.einsum("qnu,qtu->qnt", vectors, transform, preferred_element_type=F32)

    def turn_back(vectors):
        return jnp.einsum("qns,qsv->qnv", vectors, transform, preferred_element_type=F32)

    density_blocks = plane_blocks(density[0])
    start = turn((my_trial * my_live[:, None, :]).astype(BF16)).astype(BF16)
    start = jnp.concatenate(plane_blocks(start), axis=0)

    def mixed(vectors):
        return jnp.einsum(
            "crm,mt->crt", mixer, vectors.reshape(-1, transitions), preferred_element_type=F32
        ).astype(BF16)

    first_mixed = mixed(start)

    all_start = jnp.einsum(
        "qtu,qun->qnt",
        transform,
        (trial_blocks * my_live[:, :, None]).astype(BF16),
        preferred_element_type=F32,
    ).astype(BF16)
    row_mix = coefficients(coarse_index, interp_weight).astype(BF16)
    row_mixed = jnp.einsum("kqc,qnt->cknt", row_mix, all_start, preferred_element_type=F32)
    row_mixed = row_mixed.astype(BF16).reshape(pair_count, row_points * columns, transitions)
    first_point = row_index * row_points
    wanted = lax.dynamic_slice_in_dim(transform, first_point % col_points, row_points, 0)
    wanted_blocks = plane_blocks(wanted)
    root = first_point // col_points
    row_transform = wanted
    for step in range(1, plane_count):
        from_root = (col_index + step) % plane_count == root
        row_transform = jnp.where(from_root, wanted_blocks[step], row_transform)

    applied = 0.0
    for step in range(plane_count):
        at = ((col_index + step) % plane_count) * rows_here
        block = lax.dynamic_slice_in_dim(screened[0], at, rows_here, 1)
        applied = applied + jnp.dot(block, density_blocks[step], preferred_element_type=F32)
    raw_sum = lax.dot_general(
        density[0], applied.astype(BF16), (((0,), (0,)), ((), ())), preferred_element_type=F32
    )
    symmetric = (0.5 * (raw_sum + raw_sum.T)).astype(BF16)
    kernel = plane_sum(symmetric).astype(BF16)
    kernels = jnp.stack(pair_blocks(kernel))

    def through(vectors):
        return jnp.einsum("crt,cts->rs", vectors, kernels, preferred_element_type=F32)

    back = through(first_mixed).astype(BF16).reshape(col_points, mine, transitions)
    first = turn_back(back) * norm_scale * my_live[:, None, :] + energies[:, None, :] * my_trial
    first = first.astype(BF16)
    again = turn((first * my_live[:, None, :]).astype(BF16)).astype(BF16)
    again = jnp.concatenate(plane_blocks(again), axis=0)

    row_back = through(row_mixed).astype(BF16).reshape(row_points, columns, transitions)
    row_part = jnp.einsum("ksv,kns->kvn", row_transform, row_back, preferred_element_type=F32)
    row_live = lax.dynamic_slice_in_dim(live, first_point, row_points, 0)
    row_energy = lax.dynamic_slice_in_dim(energies, first_point % col_points, row_points, 0)
    row_trial = lax.dynamic_slice_in_dim(trial_blocks, first_point % col_points, row_points, 0)
    diagonal = jnp.where(root == col_index, row_energy[:, :, None] * row_trial.astype(F32), 0.0)
    row_part = row_part * norm_scale * row_live[:, :, None] + diagonal
    first_step = plane_sum(row_part.astype(BF16)).astype(BF16)
    first_step = first_step.reshape(row_points * transitions, columns)

    back = through(mixed(again)).astype(BF16).reshape(col_points, mine, transitions)
    second = turn_back(back) * norm_scale * my_live[:, None, :] + energies[:, None, :] * first
    blocks = jnp.stack(pair_blocks(second.astype(BF16)))
    place = jnp.zeros((pair_count,), jnp.int32).at[pair_order()].set(jnp.arange(pair_count))
    blocks = blocks[place]
    whole = jnp.transpose(blocks, (1, 3, 0, 2)).reshape(-1, columns).astype(F32)
    second_step = 2.0 * whole - trial.astype(F32)
    return (first_step, second_step)


def solution(mesh):
    in_specs = (
        P("pair", "pw", None),
        P("pair", "pw", None),
        P("pw", None, None),
        P("pw"),
        P("pw", None),
        P("pair", "pw", None),
        P("pair", "pw", None),
        P(),
    )
    out_specs = (P("pair", None), P("pw", None))
    return jax.shard_map(shards, mesh=mesh, in_specs=in_specs, out_specs=out_specs, check_vma=False)
```

time: 356 us -> 169 us (0.47)
  waiting for transfers between devices: 211 us -> 39 us
  starting transfers between devices: 0.34 us -> 20.4 us
  local copies, waits for them, and re-layouts: 42.1 us -> 24.7 us
  between operations: 14 us -> 1.17 us
  matrix products: 55.7 us -> 48.9 us
  other arithmetic: 5.82 us -> 12.3 us
  blocking collectives: 26.8 us -> 21.7 us
    psum x2 -> x0, waiting for transfers between devices: 133 us -> none  [the longest x1 113 us: shards(): summed = lax.psum(partial_cols, 'pair')]
    all_gather x2 -> x0, waiting for transfers between devices: 76.9 us -> none  [the longest x1 39.5 us: shards(): lax.all_gather(kernel, 'pair', axis=0, tiled=True)]
    ppermute x0 -> x36, waiting for transfers between devices: none -> 39 us  [the longest x12 22.6 us: from_ahead(): lax.ppermute(value, axis, [((s + step) % count, s) for s in range(count)])]
    psum x2 -> x0, blocking collectives: 26.8 us -> none  [the longest x1 16.3 us: shards(): first_step = lax.psum(partial_rows, 'pw').astype(jnp.bfloat16)]
    all_gather x0 -> x1, blocking collectives: none -> 21.7 us  [shards(): lax.all_gather(table.reshape(row_points, -1), 'pair', axis=0, tiled=True)]
    ppermute x0 -> x36, starting transfers between devices: none -> 20.4 us  [the longest x12 12.4 us: from_ahead(): lax.ppermute(value, axis, [((s + step) % count, s) for s in range(count)])]
    convert_element_type x2 -> x1, local copies, waits for them, and re-layouts: 18.6 us -> 6.67 us  [shards(): row_mixed.astype(BF16)]
    unnamed x16 -> x57, local copies, waits for them, and re-layouts: 22.1 us -> 11.3 us
  transfers between devices with their start and end apart: 4 -> 36, of which waited for: 4 -> 18; matrix products, arithmetic and copies ran while one was open for 3% -> 42% of each run, Pallas kernels for 0% -> 0%
where the time goes in v1:
time: 169 us; the launch traced here: 168 us
  matrix products  48.9 us (29%)
  waiting for transfers between devices  39 us (23%)
  local copies, waits for them, and re-layouts  24.7 us (15%)
  blocking collectives  21.7 us (13%)
  starting transfers between devices  20.4 us (12%)
  other arithmetic  12.3 us (7%)
    ppermute x12, waiting for transfers between devices, from_ahead(): lax.ppermute(value, axis, [((s + step) % count, s) for s in range(count)])  22.6 us
    all_gather x1, blocking collectives, shards(): lax.all_gather(table.reshape(row_points, -1), 'pair', axis=0, tiled=True)  21.7 us
    ppermute x24, waiting for transfers between devices, flipped(): return lax.ppermute(value, axis, [(s, s ^ bit) for s in range(count)])  16.5 us
    ppermute x12, starting transfers between devices, from_ahead(): lax.ppermute(value, axis, [((s + step) % count, s) for s in range(count)])  12.4 us
    unnamed x57, local copies, waits for them, and re-layouts  11.3 us
    dot_general x3, matrix products, through(): jnp.einsum('crt,cts->rs', vectors, kernels, preferred_element_type=F32)  10.8 us
    ppermute x24, starting transfers between devices, flipped(): return lax.ppermute(value, axis, [(s, s ^ bit) for s in range(count)])  8 us
    dot_general x1, matrix products, shards(): lax.dot_general(density[0], applied.astype(BF16), (((0,), (0,)), ((), ())...  7.37 us
  transfers between devices with their start and end apart: 36, of which 18 were waited for; matrix products, arithmetic and copies ran while one was open for 42% of the time, Pallas kernels for 0%

profile of v1, /device:TPU:0, one launch (start us, length us, event | category | flops | bytes accessed | tf_op | source)
XLA Modules:
  0.0 168.1 jit_solution(9156585608915145916)
XLA Ops:
  0.6 3.0 %collective-permute-start.1 = (bf16[2048,256]{1,0:T(8,128)(2,1)}, bf16[2048,256]{1,0:T(8,128)(2,1)}, u32[]{:S(2)}, u32[]{:S(2)}) collective-permute-start(bf16[2048,256]{1,0:T(8,128)(2,1)} %bitcast.201), channel_id=1, source_target_pairs={{1,0},{0,1},{3,2},{2,3},{5,4},{4,5},{7,6},{6,7},{9,8},{8,9},{11,10... | collective-permute-start | bytes 3145736 | tf_op jit(solution)/shard_map/ppermute | solution.py:15
  3.7 1.9 %constant_dynamic-slice_fusion.2 = bf16[4,256,256]{2,1,0:T(8,128)(2,1)} fusion(bf16[32,256,256]{2,1,0:T(8,128)(2,1)} %param.10, s32[]{:T(128)S(6)} %select_n.179), kind=kLoop, calls=%fused_computation.137 | loop fusion | bytes 1048580 | tf_op jit(solution)/shard_map/dynamic_slice | solution.py:124
  5.6 0.7 compare_convert_fusion
  6.4 2.4 %fusion.103 = f32[8,32,256]{2,0,1:T(8,128)S(1)} fusion(bf16[32,256,128]{2,1,0:T(8,128)(2,1)} %bitcast.194, s32[8]{0:T(128)S(1)} %iota_add_fusion), kind=kOutput, calls=%fused_computation.126 | convolution fusion | flops 16778240 | bytes 2359328 | tf_op jit(solution)/shard_map/nm,qum->qnu/dot_general | solution.py:95
  8.8 4.2 %convolution_convert_fusion.2 = bf16[32,8,256]{2,1,0:T(8,128)(2,1)} fusion(bf16[32,256,256]{2,1,0:T(8,128)(2,1)} %param.10, f32[8,32,256]{2,0,1:T(8,128)S(1)} %fusion.103, f32[32,256]{1,0:T(8,128)S(1)} %get-tuple-element.9), kind=kOutput, calls=%fused_computation.52 | convolution fusion | flops 33751040 | bytes 4620288 | tf_op jit(solution)/shard_map/qnu,qtu->qnt/dot_general | solution.py:98
  13.0 2.0 %collective-permute-start.19 = (bf16[32,8,256]{2,1,0:T(8,128)(2,1)}, bf16[32,8,256]{2,1,0:T(8,128)(2,1)}, u32[]{:S(2)}, u32[]{:S(2)}) collective-permute-start(bf16[32,8,256]{2,1,0:T(8,128)(2,1)} %convolution_convert_fusion.2), channel_id=1, source_target_pairs={{1,0},{0,1},{3,2},{2,3},{5,4},{4,5},{7,6},{6,7},{9,8},{8,9},{11,10... | collective-permute-start | bytes 393224 | tf_op jit(solution)/shard_map/ppermute | solution.py:15
  15.0 3.8 %convert_bitcast_fusion.1 = bf16[32,128,256,1]{2,1,0,3:T(8,128)(2,1)} fusion(bf16[32,256,256]{2,1,0:T(8,128)(2,1)S(1)} %copy-done, bf16[32,256,128]{2,1,0:T(8,128)(2,1)S(1)} %bitcast.195, f32[32,256]{1,0:T(8,128)S(1)} %get-tuple-element.9), kind=kOutput, calls=%fused_computation.32 | convolution fusion | flops 541065216 | bytes 8421376 | tf_op jit(solution)/shard_map/qtu,qun->qnt/dot_general | solution.py:114
  20.1 0.6 iota_compare_fusion.1
  21.0 21.7 %all-gather = bf16[16,4,256]{2,1,0:T(4,128)(2,1)S(1)} all-gather(bf16[1,4,256]{2,1,0:T(4,128)(2,1)S(1)} %reshape.333), channel_id=1, replica_groups=mesh['pair'=16,'pw'=2] {'pair'}, dimensions={0}, use_global_device_ids=true | all-gather | bytes 34816 | tf_op jit(solution)/shard_map/all_gather | solution.py:66
  42.6 0.6 reshape.311
  44.5 0.7 fusion.115
  45.3 0.6 scatter_custom_fusion
  45.9 0.7 select_reduce_fusion.1
  46.7 5.3 %convert_bitcast_fusion = bf16[16,4,128,256]{3,0,1,2:T(8,128)(2,1)} fusion(bf16[32,128,256,1]{2,1,0,3:T(8,128)(2,1)} %convert_bitcast_fusion.1, bf16[4,32,16]{1,2,0:T(8,128)(2,1)S(1)} %select_reduce_fusion.1), kind=kOutput, calls=%fused_computation.16 | convolution fusion | flops 136314880 | bytes 6295552 | tf_op jit(solution)/shard_map/kqc,qnt->cknt/dot_general | solution.py:121
  52.0 7.1 %fusion.2 = f32[2048,256]{1,0:T(8,128)} fusion(bf16[1,2048,4096]{2,1,0:T(8,128)(2,1)} %param.8, s32[]{:T(128)S(6)} %select_n.186, bf16[1,2048,256]{2,1,0:T(8,128)(2,1)S(1)} %copy-done.12), kind=kOutput, calls=%fused_computation.4 | convolution fusion | flops 2147483648 | bytes 11534340 | tf_op jit(solution)/shard_map/dot_general | solution.py:136
  59.1 7.4 %fusion.78 = f32[256,256]{1,0:T(8,128)S(1)} fusion(f32[2048,256]{1,0:T(8,128)} %fusion.2, bf16[2048,256]{1,0:T(8,128)(2,1)} %collective-permute-done.1, bf16[1,2048,4096]{2,1,0:T(8,128)(2,1)} %param.8, s32[]{:T(128)S(6)} %select_n.187, bf16[1,2048,256]{2,1,0:T(8,128)(2,1)} %param.9), kind=kOutput, calls=%fused_computation.56 | convolution fusion | flops 2416967680 | bytes 12845060 | tf_op jit(solution)/shard_map/dot_general | solution.py:137
  66.6 0.7 fusion.91
  67.8 0.8 reshape.308
  68.5 4.7 %collective-permute-done.2 = bf16[256,256]{1,0:T(8,128)(2,1)S(1)} collective-permute-done((bf16[256,256]{1,0:T(8,128)(2,1)}, bf16[256,256]{1,0:T(8,128)(2,1)S(1)}, u32[]{:S(2)}, u32[]{:S(2)}) %collective-permute-start.2) | collective-permute-done | bytes 131104 | tf_op jit(solution)/shard_map/ppermute | solution.py:15
  73.2 1.6 bitcast_dynamic-update-slice_fusion.31
  74.9 3.0 %copy.45 = bf16[8192,128]{0,1:T(8,128)(2,1)} copy(bf16[8192,128]{1,0:T(8,128)(2,1)S(1)} %copy-done.2) | data formatting | bytes 4194304 | tf_op args[4]
  77.8 6.7 %copy.38 = bf16[16,4,128,256]{3,2,1,0:T(8,128)(2,1)} copy(bf16[16,4,128,256]{3,0,1,2:T(8,128)(2,1)} %convert_bitcast_fusion) | data formatting | bytes 8388608 | tf_op jit(solution)/shard_map/convert_element_type | solution.py:122
  84.8 1.9 %collective-permute-start.5 = (bf16[256,256]{1,0:T(8,128)(2,1)}, bf16[256,256]{1,0:T(8,128)(2,1)S(1)}, u32[]{:S(2)}, u32[]{:S(2)}) collective-permute-start(bf16[256,256]{1,0:T(8,128)(2,1)} %get-tuple-element.11), channel_id=1, source_target_pairs={{24,0},{26,2},{28,4},{30,6},{0,8},{2,10},{4,12},{6,14},{8,16},{10,... | collective-permute-start | bytes 393224 | tf_op jit(solution)/shard_map/ppermute | solution.py:15
  86.6 9.6 %collective-permute-done.4 = bf16[256,256]{1,0:T(8,128)(2,1)S(1)} collective-permute-done((bf16[256,256]{1,0:T(8,128)(2,1)}, bf16[256,256]{1,0:T(8,128)(2,1)S(1)}, u32[]{:S(2)}, u32[]{:S(2)}) %collective-permute-start.4) | collective-permute-done | bytes 131104 | tf_op jit(solution)/shard_map/ppermute | solution.py:15
  96.4 2.1 %collective-permute-start.8 = (bf16[256,256]{1,0:T(8,128)(2,1)S(1)}, bf16[256,256]{1,0:T(8,128)(2,1)S(1)}, u32[]{:S(2)}, u32[]{:S(2)}) collective-permute-start(bf16[256,256]{1,0:T(8,128)(2,1)S(1)} %collective-permute-done.4), channel_id=1, source_target_pairs={{0,4},{2,6},{4,0},{6,2},{8,12},{10,14},{12,8},{14,10},{16,20},{18,... | collective-permute-start | bytes 393224 | tf_op jit(solution)/shard_map/ppermute | solution.py:20
  98.4 4.2 %collective-permute-done.7 = bf16[256,256]{1,0:T(8,128)(2,1)S(1)} collective-permute-done((bf16[256,256]{1,0:T(8,128)(2,1)S(1)}, bf16[256,256]{1,0:T(8,128)(2,1)S(1)}, u32[]{:S(2)}, u32[]{:S(2)}) %collective-permute-start.7) | collective-permute-done | bytes 131104 | tf_op jit(solution)/shard_map/ppermute | solution.py:20
  102.7 2.7 %collective-permute-done.8 = bf16[256,256]{1,0:T(8,128)(2,1)S(1)} collective-permute-done((bf16[256,256]{1,0:T(8,128)(2,1)S(1)}, bf16[256,256]{1,0:T(8,128)(2,1)S(1)}, u32[]{:S(2)}, u32[]{:S(2)}) %collective-permute-start.8) | collective-permute-done | bytes 131104 | tf_op jit(solution)/shard_map/ppermute | solution.py:20
  105.4 2.4 %collective-permute-done.9 = bf16[256,256]{1,0:T(8,128)(2,1)S(1)} collective-permute-done((bf16[256,256]{1,0:T(8,128)(2,1)S(1)}, bf16[256,256]{1,0:T(8,128)(2,1)S(1)}, u32[]{:S(2)}, u32[]{:S(2)}) %collective-permute-start.9) | collective-permute-done | bytes 131104 | tf_op jit(solution)/shard_map/ppermute | solution.py:20
  108.6 0.6 collective-permute-done.12
  111.3 1.3 copy-done.9
  112.6 3.7 %fusion.67 = bf16[32,8,256]{2,1,0:T(8,128)(2,1)S(1)} fusion(bf16[16,256,256]{2,1,0:T(8,128)(2,1)} %copy-done.9, pred[8,512]{1,0:T(8,128)(4,1)S(1)} %copy-done.11, bf16[16,32,512]{2,1,0:T(8,128)(2,1)S(1)} %convolution_convert_fusion, bf16[32,8,256]{2,1,0:T(8,128)(2,1)} %collective-permute-done.19, bf16[32,8,256]{2,1,0:T(8,128)(2,1)} %convolution_convert_fusion.2), kind=kOutput, calls=%fused_computation.53 | convolution fusion | flops 1613955072 | bytes 3018752 | tf_op jit(solution)/shard_map/crt,cts->rs/dot_general | solution.py:145
  116.3 3.0 %fusion.55 = f32[32,8,256]{2,1,0:T(8,128)S(1)} fusion(bf16[32,8,256]{2,1,0:T(8,128)(2,1)S(1)} %fusion.67, bf16[32,256,256]{2,1,0:T(8,128)(2,1)} %param.10, f32[8,32,256]{2,0,1:T(8,128)S(1)} %fusion.103, f32[32,256]{1,0:T(8,128)S(1)} %reshape.308, f32[32,256]{1,0:T(8,128)S(1)} %get-tuple-element.8), kind=kOutput, calls=%fused_computation.47 | convolution fusion | flops 33882112 | bytes 4915200 | tf_op jit(solution)/shard_map/qns,qsv->qnv/dot_general | solution.py:101
  119.7 1.2 convolution_convert_fusion.1
  122.0 2.8 %fusion.41 = bf16[512,256]{1,0:T(8,128)(2,1)S(1)} fusion(bf16[16,512,256]{2,1,0:T(8,128)(2,1)S(1)} %bitcast.198, bf16[16,256,256]{2,1,0:T(8,128)(2,1)} %copy-done.9), kind=kOutput, calls=%fused_computation.39 | convolution fusion | flops 1073872896 | bytes 6553600 | tf_op jit(solution)/shard_map/crt,cts->rs/dot_general | solution.py:145
  125.4 2.1 %collective-permute-start.18 = (bf16[4,256,128]{2,1,0:T(8,128)(2,1)S(1)}, bf16[4,256,128]{2,1,0:T(8,128)(2,1)S(1)}, u32[]{:S(2)}, u32[]{:S(2)}) collective-permute-start(bf16[4,256,128]{2,1,0:T(8,128)(2,1)S(1)} %fusion.40), channel_id=1, source_target_pairs={{1,0},{0,1},{3,2},{2,3},{5,4},{4,5},{7,6},{6,7},{9,8},{8,9},{11,10... | collective-permute-start | bytes 786440 | tf_op jit(solution)/shard_map/ppermute | solution.py:15
  127.5 4.3 %fusion.72 = bf16[32,8,256]{2,1,0:T(8,128)(2,1)} fusion(bf16[16,256,256]{2,1,0:T(8,128)(2,1)} %copy-done.9, pred[8,512]{1,0:T(8,128)(4,1)S(1)} %copy-done.11, bf16[16,32,512]{2,1,0:T(8,128)(2,1)S(1)} %convolution_convert_fusion, bf16[32,8,256]{2,1,0:T(8,128)(2,1)} %collective-permute-done.20, bf16[32,8,256]{2,1,0:T(8,128)(2,1)} %copy-done.5), kind=kOutput, calls=%fused_computation.54 | convolution fusion | flops 1613955072 | bytes 3018752 | tf_op jit(solution)/shard_map/crt,cts->rs/dot_general | solution.py:145
  131.8 2.9 %bitcast_dynamic-update-slice_fusion.15 = (bf16[16,32,8,256]{3,2,1,0:T(8,128)(2,1)S(1)}, bf16[32,8,256]{2,1,0:T(8,128)(2,1)S(1)}) fusion(f32[32,8,256]{2,1,0:T(8,128)S(1)} %fusion.55, f32[32,256]{1,0:T(8,128)S(1)} %reshape.308, f32[32,256]{1,0:T(8,128)S(1)} %get-tuple-element.8, bf16[32,8,256]{2,1,0:T(8,128)(2,1)} %fusion.72, bf16[32,256,256]{2,1,0:T(8,128)(2,1)} %param.10), kind=kOutput, calls=%fused_computation.88 | convolution fusion | flops 33816576 | bytes 4915200 | tf_op jit(solution)/shard_map/qns,qsv->qnv/dot_general | solution.py:101
  134.8 1.9 %collective-permute-start.23 = (bf16[32,8,256]{2,1,0:T(8,128)(2,1)S(1)}, bf16[32,8,256]{2,1,0:T(8,128)(2,1)S(1)}, u32[]{:S(2)}, u32[]{:S(2)}) collective-permute-start(bf16[32,8,256]{2,1,0:T(8,128)(2,1)S(1)} %get-tuple-element.17), channel_id=1, source_target_pairs={{24,0},{26,2},{28,4},{30,6},{0,8},{2,10},{4,12},{6,14},{8,16},{10,... | collective-permute-start | bytes 393224 | tf_op jit(solution)/shard_map/ppermute | solution.py:15
  137.0 0.8 add_convert_fusion
  137.8 3.7 %collective-permute-done.21 = bf16[32,8,256]{2,1,0:T(8,128)(2,1)S(1)} collective-permute-done((bf16[32,8,256]{2,1,0:T(8,128)(2,1)S(1)}, bf16[32,8,256]{2,1,0:T(8,128)(2,1)S(1)}, u32[]{:S(2)}, u32[]{:S(2)}) %collective-permute-start.21) | collective-permute-done | bytes 131104 | tf_op jit(solution)/shard_map/ppermute | solution.py:15
  141.8 4.6 %collective-permute-done.22 = bf16[32,8,256]{2,1,0:T(8,128)(2,1)S(1)} collective-permute-done((bf16[32,8,256]{2,1,0:T(8,128)(2,1)S(1)}, bf16[32,8,256]{2,1,0:T(8,128)(2,1)S(1)}, u32[]{:S(2)}, u32[]{:S(2)}) %collective-permute-start.22) | collective-permute-done | bytes 131104 | tf_op jit(solution)/shard_map/ppermute | solution.py:15
  146.6 1.8 %collective-permute-start.27 = (bf16[32,8,256]{2,1,0:T(8,128)(2,1)S(1)}, bf16[32,8,256]{2,1,0:T(8,128)(2,1)S(1)}, u32[]{:S(2)}, u32[]{:S(2)}) collective-permute-start(bf16[32,8,256]{2,1,0:T(8,128)(2,1)S(1)} %collective-permute-done.23), channel_id=1, source_target_pairs={{0,4},{2,6},{4,0},{6,2},{8,12},{10,14},{12,8},{14,10},{16,20},{18,... | collective-permute-start | bytes 393224 | tf_op jit(solution)/shard_map/ppermute | solution.py:20
  149.2 2.9 %collective-permute-done.26 = bf16[32,8,256]{2,1,0:T(8,128)(2,1)S(1)} collective-permute-done((bf16[32,8,256]{2,1,0:T(8,128)(2,1)S(1)}, bf16[32,8,256]{2,1,0:T(8,128)(2,1)S(1)}, u32[]{:S(2)}, u32[]{:S(2)}) %collective-permute-start.26) | collective-permute-done | bytes 131104 | tf_op jit(solution)/shard_map/ppermute | solution.py:20
  152.1 1.4 collective-permute-done.27
  155.8 2.0 %gather_fusion = bf16[16,32,8,256]{3,2,1,0:T(8,128)(2,1)} fusion(bf16[16,32,8,256]{3,2,1,0:T(8,128)(2,1)S(1)} %bitcast_dynamic-update-slice_fusion, s32[1024]{0:T(1024)S(1)} %pad_clamp_fusion), kind=kCustom, calls=%fused_computation | custom fusion | bytes 4194368 | tf_op jit(solution)/shard_map/gather | solution.py:167
  157.8 2.1 %convert_multiply_fusion = f32[16,32,8,256]{3,2,1,0:T(8,128)S(1)} fusion(bf16[16,32,8,256]{3,2,1,0:T(8,128)(2,1)} %gather_fusion), kind=kLoop, calls=%fused_computation.15 | loop fusion | flops 2097152 | bytes 6291456 | tf_op jit(solution)/shard_map/mul | solution.py:169
  160.0 2.5 %convert_subtract_fusion = f32[8192,128]{0,1:T(8,128)} fusion(f32[8192,128]{0,1:T(8,128)S(1)} %bitcast.197, bf16[8192,128]{0,1:T(8,128)(2,1)S(1)} %copy-done.3), kind=kLoop, calls=%fused_computation.14 | loop fusion | flops 2097152 | bytes 10485760 | tf_op jit(solution)/shard_map/sub | solution.py:169
  162.5 5.6 %copy.46 = f32[8192,128]{1,0:T(8,128)} copy(f32[8192,128]{0,1:T(8,128)} %convert_subtract_fusion) | data formatting | bytes 8388608
  (136 shorter events, 12.6 us)
Async XLA Ops:
  0.6 58.4 %collective-permute-start.1 = (bf16[2048,256]{1,0:T(8,128)(2,1)}, bf16[2048,256]{1,0:T(8,128)(2,1)}, u32[]{:S(2)}, u32[]{:S(2)}) collective-permute-start(bf16[2048,256]{1,0:T(8,128)(2,1)} %bitcast.201), channel_id=1, source_target_pairs={{1,0},{0,1},{3,2},{2,3},{5,4},{4,5},{7,6},{6,7},{9,8},{8,9},{11,10... | collective-permute-start | bytes 3145736 | tf_op jit(solution)/shard_map/ppermute | solution.py:15
  5.5 119.3 %collective-permute-start = (bf16[4,256,256]{2,1,0:T(8,128)(2,1)}, bf16[4,256,256]{2,1,0:T(8,128)(2,1)}, u32[]{:S(2)}, u32[]{:S(2)}) collective-permute-start(bf16[4,256,256]{2,1,0:T(8,128)(2,1)} %constant_dynamic-slice_fusion.2), channel_id=1, source_target_pairs={{1,0},{0,1},{3,2},{2,3},{5,4},{4,5},{7,6},{6,7},{9,8},{8,9},{11,10... | collective-permute-start | bytes 1572872 | tf_op jit(solution)/shard_map/ppermute | solution.py:15
  6.3 8.6 %copy-start.2 = (bf16[8192,128]{1,0:T(8,128)(2,1)S(1)}, bf16[8192,128]{1,0:T(8,128)(2,1)}, u32[]{:S(2)}) copy-start(bf16[8192,128]{1,0:T(8,128)(2,1)} %param.12) | copy-start | bytes 6291460
  8.8 6.2 %copy-start = (bf16[32,256,256]{2,1,0:T(8,128)(2,1)S(1)}, bf16[32,256,256]{2,1,0:T(8,128)(2,1)}, u32[]{:S(2)}) copy-start(bf16[32,256,256]{2,1,0:T(8,128)(2,1)} %param.10) | copy-start | bytes 12582916
  13.0 7.1 %copy-start.7 = (s32[4,32,4]{1,2,0:T(4,128)S(1)}, s32[4,32,4]{1,2,0:T(4,128)}, u32[]{:S(2)}) copy-start(s32[4,32,4]{1,2,0:T(4,128)} %param.13) | copy-start | bytes 6148
  13.0 7.7 %copy-start.6 = (bf16[4,32,4]{1,2,0:T(4,128)(2,1)S(1)}, bf16[4,32,4]{1,2,0:T(4,128)(2,1)}, u32[]{:S(2)}) copy-start(bf16[4,32,4]{1,2,0:T(4,128)(2,1)} %param.14) | copy-start | bytes 3076
  13.0 99.6 %collective-permute-start.19 = (bf16[32,8,256]{2,1,0:T(8,128)(2,1)}, bf16[32,8,256]{2,1,0:T(8,128)(2,1)}, u32[]{:S(2)}, u32[]{:S(2)}) collective-permute-start(bf16[32,8,256]{2,1,0:T(8,128)(2,1)} %convolution_convert_fusion.2), channel_id=1, source_target_pairs={{1,0},{0,1},{3,2},{2,3},{5,4},{4,5},{7,6},{6,7},{9,8},{8,9},{11,10... | collective-permute-start | bytes 393224 | tf_op jit(solution)/shard_map/ppermute | solution.py:15
  20.1 24.1 %copy-start.10 = (f32[16]{0:T(128)}, f32[16]{0:T(128)S(1)}, u32[]{:S(2)}) copy-start(f32[16]{0:T(128)S(1)} %add_convert_fusion.2) | copy-start | bytes 196
  46.7 5.3 %copy-start.12 = (bf16[1,2048,256]{2,1,0:T(8,128)(2,1)S(1)}, bf16[1,2048,256]{2,1,0:T(8,128)(2,1)}, u32[]{:S(2)}) copy-start(bf16[1,2048,256]{2,1,0:T(8,128)(2,1)} %param.9) | copy-start | bytes 3145732
  67.3 5.9 %collective-permute-start.2 = (bf16[256,256]{1,0:T(8,128)(2,1)}, bf16[256,256]{1,0:T(8,128)(2,1)S(1)}, u32[]{:S(2)}, u32[]{:S(2)}) collective-permute-start(bf16[256,256]{1,0:T(8,128)(2,1)} %fusion.91), channel_id=1, source_target_pairs={{1,0},{0,1},{3,2},{2,3},{5,4},{4,5},{7,6},{6,7},{9,8},{8,9},{11,10... | collective-permute-start | bytes 393224 | tf_op jit(solution)/shard_map/ppermute | solution.py:15
  74.8 11.8 %collective-permute-start.3 = (bf16[256,256]{1,0:T(8,128)(2,1)}, bf16[256,256]{1,0:T(8,128)(2,1)S(1)}, u32[]{:S(2)}, u32[]{:S(2)}) collective-permute-start(bf16[256,256]{1,0:T(8,128)(2,1)} %get-tuple-element.11), channel_id=1, source_target_pairs={{8,0},{10,2},{12,4},{14,6},{16,8},{18,10},{20,12},{22,14},{24,16},... | collective-permute-start | bytes 393224 | tf_op jit(solution)/shard_map/ppermute | solution.py:15
  77.8 8.8 %copy-start.8 = (bf16[16,256,256]{2,1,0:T(8,128)(2,1)S(1)}, bf16[16,256,256]{2,1,0:T(8,128)(2,1)}, u32[]{:S(2)}) copy-start(bf16[16,256,256]{2,1,0:T(8,128)(2,1)} %get-tuple-element.10) | copy-start | bytes 6291460
  84.5 28.1 %copy-start.11 = (pred[8,512]{1,0:T(8,128)(4,1)S(1)}, pred[8,512]{1,0:T(8,128)(4,1)}, u32[]{:S(2)}) copy-start(pred[8,512]{1,0:T(8,128)(4,1)} %iota_compare_fusion.1) | copy-start | bytes 12292
  84.5 11.7 %collective-permute-start.4 = (bf16[256,256]{1,0:T(8,128)(2,1)}, bf16[256,256]{1,0:T(8,128)(2,1)S(1)}, u32[]{:S(2)}, u32[]{:S(2)}) collective-permute-start(bf16[256,256]{1,0:T(8,128)(2,1)} %get-tuple-element.11), channel_id=1, source_target_pairs={{16,0},{18,2},{20,4},{22,6},{24,8},{26,10},{28,12},{30,14},{0,16},... | collective-permute-start | bytes 393224 | tf_op jit(solution)/shard_map/ppermute | solution.py:15
  84.8 11.5 %collective-permute-start.5 = (bf16[256,256]{1,0:T(8,128)(2,1)}, bf16[256,256]{1,0:T(8,128)(2,1)S(1)}, u32[]{:S(2)}, u32[]{:S(2)}) collective-permute-start(bf16[256,256]{1,0:T(8,128)(2,1)} %get-tuple-element.11), channel_id=1, source_target_pairs={{24,0},{26,2},{28,4},{30,6},{0,8},{2,10},{4,12},{6,14},{8,16},{10,... | collective-permute-start | bytes 393224 | tf_op jit(solution)/shard_map/ppermute | solution.py:15
  86.6 9.7 %collective-permute-start.6 = (bf16[256,256]{1,0:T(8,128)(2,1)}, bf16[256,256]{1,0:T(8,128)(2,1)S(1)}, u32[]{:S(2)}, u32[]{:S(2)}) collective-permute-start(bf16[256,256]{1,0:T(8,128)(2,1)} %get-tuple-element.11), channel_id=1, source_target_pairs={{0,4},{2,6},{4,0},{6,2},{8,12},{10,14},{12,8},{14,10},{16,20},{18,... | collective-permute-start | bytes 393224 | tf_op jit(solution)/shard_map/ppermute | solution.py:20
  96.2 11.7 %collective-permute-start.10 = (bf16[256,256]{1,0:T(8,128)(2,1)}, bf16[256,256]{1,0:T(8,128)(2,1)S(1)}, u32[]{:S(2)}, u32[]{:S(2)}) collective-permute-start(bf16[256,256]{1,0:T(8,128)(2,1)} %get-tuple-element.11), channel_id=1, source_target_pairs={{0,2},{2,0},{4,6},{6,4},{8,10},{10,8},{12,14},{14,12},{16,18},{18,... | collective-permute-start | bytes 393224 | tf_op jit(solution)/shard_map/ppermute | solution.py:20
  96.3 6.4 %collective-permute-start.7 = (bf16[256,256]{1,0:T(8,128)(2,1)S(1)}, bf16[256,256]{1,0:T(8,128)(2,1)S(1)}, u32[]{:S(2)}, u32[]{:S(2)}) collective-permute-start(bf16[256,256]{1,0:T(8,128)(2,1)S(1)} %collective-permute-done.3), channel_id=1, source_target_pairs={{0,4},{2,6},{4,0},{6,2},{8,12},{10,14},{12,8},{14,10},{16,20},{18,... | collective-permute-start | bytes 393224 | tf_op jit(solution)/shard_map/ppermute | solution.py:20
  96.4 9.1 %collective-permute-start.8 = (bf16[256,256]{1,0:T(8,128)(2,1)S(1)}, bf16[256,256]{1,0:T(8,128)(2,1)S(1)}, u32[]{:S(2)}, u32[]{:S(2)}) collective-permute-start(bf16[256,256]{1,0:T(8,128)(2,1)S(1)} %collective-permute-done.4), channel_id=1, source_target_pairs={{0,4},{2,6},{4,0},{6,2},{8,12},{10,14},{12,8},{14,10},{16,20},{18,... | collective-permute-start | bytes 393224 | tf_op jit(solution)/shard_map/ppermute | solution.py:20
  102.6 5.3 %collective-permute-start.9 = (bf16[256,256]{1,0:T(8,128)(2,1)S(1)}, bf16[256,256]{1,0:T(8,128)(2,1)S(1)}, u32[]{:S(2)}, u32[]{:S(2)}) collective-permute-start(bf16[256,256]{1,0:T(8,128)(2,1)S(1)} %collective-permute-done.5), channel_id=1, source_target_pairs={{0,4},{2,6},{4,0},{6,2},{8,12},{10,14},{12,8},{14,10},{16,20},{18,... | collective-permute-start | bytes 393224 | tf_op jit(solution)/shard_map/ppermute | solution.py:20
  105.4 3.1 %collective-permute-start.11 = (bf16[256,256]{1,0:T(8,128)(2,1)S(1)}, bf16[256,256]{1,0:T(8,128)(2,1)S(1)}, u32[]{:S(2)}, u32[]{:S(2)}) collective-permute-start(bf16[256,256]{1,0:T(8,128)(2,1)S(1)} %collective-permute-done.3), channel_id=1, source_target_pairs={{0,2},{2,0},{4,6},{6,4},{8,10},{10,8},{12,14},{14,12},{16,18},{18,... | collective-permute-start | bytes 393224 | tf_op jit(solution)/shard_map/ppermute | solution.py:20
  107.9 1.3 collective-permute-start.12
  107.9 1.6 collective-permute-start.13
  108.5 1.4 collective-permute-start.14
  109.2 1.3 collective-permute-start.15
  109.5 1.3 collective-permute-start.16
  109.9 1.3 collective-permute-start.17
  116.3 3.5 %copy-start.1 = (bf16[32,256,256]{2,1,0:T(8,128)(2,1)S(1)}, bf16[32,256,256]{2,1,0:T(8,128)(2,1)}, u32[]{:S(2)}) copy-start(bf16[32,256,256]{2,1,0:T(8,128)(2,1)} %param.10) | copy-start | bytes 12582916
  119.7 2.2 %copy-start.4 = (bf16[16,4,128,256]{3,2,1,0:T(8,128)(2,1)S(1)}, bf16[16,4,128,256]{3,2,1,0:T(8,128)(2,1)}, u32[]{:S(2)}) copy-start(bf16[16,4,128,256]{3,2,1,0:T(8,128)(2,1)} %copy.38) | copy-start | bytes 12582916
  120.9 3.9 %copy-start.5 = (bf16[32,8,256]{2,1,0:T(8,128)(2,1)}, bf16[32,8,256]{2,1,0:T(8,128)(2,1)S(1)}, u32[]{:S(2)}) copy-start(bf16[32,8,256]{2,1,0:T(8,128)(2,1)S(1)} %convolution_convert_fusion.1) | copy-start | bytes 393220
  120.9 6.6 %collective-permute-start.20 = (bf16[32,8,256]{2,1,0:T(8,128)(2,1)S(1)}, bf16[32,8,256]{2,1,0:T(8,128)(2,1)}, u32[]{:S(2)}, u32[]{:S(2)}) collective-permute-start(bf16[32,8,256]{2,1,0:T(8,128)(2,1)S(1)} %convolution_convert_fusion.1), channel_id=1, source_target_pairs={{1,0},{0,1},{3,2},{2,3},{5,4},{4,5},{7,6},{6,7},{9,8},{8,9},{11,10... | collective-permute-start | bytes 393224 | tf_op jit(solution)/shard_map/ppermute | solution.py:15
  125.4 11.7 %collective-permute-start.18 = (bf16[4,256,128]{2,1,0:T(8,128)(2,1)S(1)}, bf16[4,256,128]{2,1,0:T(8,128)(2,1)S(1)}, u32[]{:S(2)}, u32[]{:S(2)}) collective-permute-start(bf16[4,256,128]{2,1,0:T(8,128)(2,1)S(1)} %fusion.40), channel_id=1, source_target_pairs={{1,0},{0,1},{3,2},{2,3},{5,4},{4,5},{7,6},{6,7},{9,8},{8,9},{11,10... | collective-permute-start | bytes 786440 | tf_op jit(solution)/shard_map/ppermute | solution.py:15
  134.7 6.8 %collective-permute-start.21 = (bf16[32,8,256]{2,1,0:T(8,128)(2,1)S(1)}, bf16[32,8,256]{2,1,0:T(8,128)(2,1)S(1)}, u32[]{:S(2)}, u32[]{:S(2)}) collective-permute-start(bf16[32,8,256]{2,1,0:T(8,128)(2,1)S(1)} %get-tuple-element.17), channel_id=1, source_target_pairs={{8,0},{10,2},{12,4},{14,6},{16,8},{18,10},{20,12},{22,14},{24,16},... | collective-permute-start | bytes 393224 | tf_op jit(solution)/shard_map/ppermute | solution.py:15
  134.7 11.6 %collective-permute-start.22 = (bf16[32,8,256]{2,1,0:T(8,128)(2,1)S(1)}, bf16[32,8,256]{2,1,0:T(8,128)(2,1)S(1)}, u32[]{:S(2)}, u32[]{:S(2)}) collective-permute-start(bf16[32,8,256]{2,1,0:T(8,128)(2,1)S(1)} %get-tuple-element.17), channel_id=1, source_target_pairs={{16,0},{18,2},{20,4},{22,6},{24,8},{26,10},{28,12},{30,14},{0,16},... | collective-permute-start | bytes 393224 | tf_op jit(solution)/shard_map/ppermute | solution.py:15
  134.8 11.8 %collective-permute-start.23 = (bf16[32,8,256]{2,1,0:T(8,128)(2,1)S(1)}, bf16[32,8,256]{2,1,0:T(8,128)(2,1)S(1)}, u32[]{:S(2)}, u32[]{:S(2)}) collective-permute-start(bf16[32,8,256]{2,1,0:T(8,128)(2,1)S(1)} %get-tuple-element.17), channel_id=1, source_target_pairs={{24,0},{26,2},{28,4},{30,6},{0,8},{2,10},{4,12},{6,14},{8,16},{10,... | collective-permute-start | bytes 393224 | tf_op jit(solution)/shard_map/ppermute | solution.py:15
  136.8 11.7 %collective-permute-start.24 = (bf16[32,8,256]{2,1,0:T(8,128)(2,1)S(1)}, bf16[32,8,256]{2,1,0:T(8,128)(2,1)S(1)}, u32[]{:S(2)}, u32[]{:S(2)}) collective-permute-start(bf16[32,8,256]{2,1,0:T(8,128)(2,1)S(1)} %get-tuple-element.17), channel_id=1, source_target_pairs={{0,4},{2,6},{4,0},{6,2},{8,12},{10,14},{12,8},{14,10},{16,20},{18,... | collective-permute-start | bytes 393224 | tf_op jit(solution)/shard_map/ppermute | solution.py:20
  137.0 16.5 %collective-permute-start.28 = (bf16[32,8,256]{2,1,0:T(8,128)(2,1)S(1)}, bf16[32,8,256]{2,1,0:T(8,128)(2,1)S(1)}, u32[]{:S(2)}, u32[]{:S(2)}) collective-permute-start(bf16[32,8,256]{2,1,0:T(8,128)(2,1)S(1)} %get-tuple-element.17), channel_id=1, source_target_pairs={{0,2},{2,0},{4,6},{6,4},{8,10},{10,8},{12,14},{14,12},{16,18},{18,... | collective-permute-start | bytes 393224 | tf_op jit(solution)/shard_map/ppermute | solution.py:20
  141.5 7.1 %collective-permute-start.25 = (bf16[32,8,256]{2,1,0:T(8,128)(2,1)S(1)}, bf16[32,8,256]{2,1,0:T(8,128)(2,1)S(1)}, u32[]{:S(2)}, u32[]{:S(2)}) collective-permute-start(bf16[32,8,256]{2,1,0:T(8,128)(2,1)S(1)} %collective-permute-done.21), channel_id=1, source_target_pairs={{0,4},{2,6},{4,0},{6,2},{8,12},{10,14},{12,8},{14,10},{16,20},{18,... | collective-permute-start | bytes 393224 | tf_op jit(solution)/shard_map/ppermute | solution.py:20
  146.4 5.7 %collective-permute-start.26 = (bf16[32,8,256]{2,1,0:T(8,128)(2,1)S(1)}, bf16[32,8,256]{2,1,0:T(8,128)(2,1)S(1)}, u32[]{:S(2)}, u32[]{:S(2)}) collective-permute-start(bf16[32,8,256]{2,1,0:T(8,128)(2,1)S(1)} %collective-permute-done.22), channel_id=1, source_target_pairs={{0,4},{2,6},{4,0},{6,2},{8,12},{10,14},{12,8},{14,10},{16,20},{18,... | collective-permute-start | bytes 393224 | tf_op jit(solution)/shard_map/ppermute | solution.py:20
  146.6 6.8 %collective-permute-start.27 = (bf16[32,8,256]{2,1,0:T(8,128)(2,1)S(1)}, bf16[32,8,256]{2,1,0:T(8,128)(2,1)S(1)}, u32[]{:S(2)}, u32[]{:S(2)}) collective-permute-start(bf16[32,8,256]{2,1,0:T(8,128)(2,1)S(1)} %collective-permute-done.23), channel_id=1, source_target_pairs={{0,4},{2,6},{4,0},{6,2},{8,12},{10,14},{12,8},{14,10},{16,20},{18,... | collective-permute-start | bytes 393224 | tf_op jit(solution)/shard_map/ppermute | solution.py:20
  148.5 5.6 %collective-permute-start.29 = (bf16[32,8,256]{2,1,0:T(8,128)(2,1)S(1)}, bf16[32,8,256]{2,1,0:T(8,128)(2,1)S(1)}, u32[]{:S(2)}, u32[]{:S(2)}) collective-permute-start(bf16[32,8,256]{2,1,0:T(8,128)(2,1)S(1)} %collective-permute-done.21), channel_id=1, source_target_pairs={{0,2},{2,0},{4,6},{6,4},{8,10},{10,8},{12,14},{14,12},{16,18},{18,... | collective-permute-start | bytes 393224 | tf_op jit(solution)/shard_map/ppermute | solution.py:20
  148.6 5.6 %collective-permute-start.30 = (bf16[32,8,256]{2,1,0:T(8,128)(2,1)S(1)}, bf16[32,8,256]{2,1,0:T(8,128)(2,1)S(1)}, u32[]{:S(2)}, u32[]{:S(2)}) collective-permute-start(bf16[32,8,256]{2,1,0:T(8,128)(2,1)S(1)} %collective-permute-done.22), channel_id=1, source_target_pairs={{0,2},{2,0},{4,6},{6,4},{8,10},{10,8},{12,14},{14,12},{16,18},{18,... | collective-permute-start | bytes 393224 | tf_op jit(solution)/shard_map/ppermute | solution.py:20
  152.1 2.7 %collective-permute-start.31 = (bf16[32,8,256]{2,1,0:T(8,128)(2,1)S(1)}, bf16[32,8,256]{2,1,0:T(8,128)(2,1)S(1)}, u32[]{:S(2)}, u32[]{:S(2)}) collective-permute-start(bf16[32,8,256]{2,1,0:T(8,128)(2,1)S(1)} %collective-permute-done.23), channel_id=1, source_target_pairs={{0,2},{2,0},{4,6},{6,4},{8,10},{10,8},{12,14},{14,12},{16,18},{18,... | collective-permute-start | bytes 393224 | tf_op jit(solution)/shard_map/ppermute | solution.py:20
  153.5 1.3 collective-permute-start.32
  153.5 1.6 collective-permute-start.33
  154.1 1.4 collective-permute-start.34
  154.2 1.5 collective-permute-start.35
  157.8 2.2 %copy-start.3 = (bf16[8192,128]{0,1:T(8,128)(2,1)S(1)}, bf16[8192,128]{0,1:T(8,128)(2,1)}, u32[]{:S(2)}) copy-start(bf16[8192,128]{0,1:T(8,128)(2,1)} %copy.45) | copy-start | bytes 6291460
  (1 other events, 1.3 us)

commit v2 on v1

v2 whole, which is shorter than its diff:
```python
import functools
import math

import jax
import jax.numpy as jnp
from jax import lax
from jax.experimental import pallas as pl
from jax.experimental.pallas import tpu as pltpu
from jax.sharding import PartitionSpec as P

NCOND = 16
F32 = jnp.float32
BF16 = jnp.bfloat16
MIB = 1 << 20
NN = (((1,), (0,)), ((), ()))
NT = (((1,), (1,)), ((), ()))
TN = (((0,), (0,)), ((), ()))


def dot(a, b, dims=NN):
    return lax.dot_general(a, b, dims, preferred_element_type=F32)


def cost(flops, read):
    return pl.CostEstimate(flops=int(flops), bytes_accessed=int(read), transcendentals=0)


def params(mib):
    return pltpu.CompilerParams(vmem_limit_bytes=mib * MIB)


def whole(shape):
    return pl.BlockSpec(shape, lambda *_: (0,) * len(shape))


ANY = pl.BlockSpec(memory_space=pl.ANY)


def from_ahead(value, axis, step):
    count = lax.axis_size(axis)
    return lax.ppermute(value, axis, [((s + step) % count, s) for s in range(count)])


def flipped(value, axis, bit):
    count = lax.axis_size(axis)
    return lax.ppermute(value, axis, [(s, s ^ bit) for s in range(count)])


def plane_blocks(value):
    return [value] + [from_ahead(value, "pw", d) for d in range(1, lax.axis_size("pw"))]


def pair_moves():
    groups = lax.axis_size("pair") // 4
    far = sorted(range(groups), key=lambda d: min(d, groups - d))
    early = [(d, 0, 0) for d in far] + [(0, 1, 0)] + [(d, 0, 1) for d in far] + [(0, 1, 1)]
    early += [(d, 1, 0) for d in far[1:-1]]
    late = [(d, 1, 1) for d in far[1:-1]] + [(far[-1], 1, 0), (far[-1], 1, 1)]
    return early, late


def pair_blocks(value):
    early, late = pair_moves()
    held = {(0, 0, 0): value}
    for move in early + late:
        far, side, core = move
        if core:
            held[move] = flipped(held[far, side, 0], "pair", 1)
        elif side:
            held[move] = flipped(held[far, 0, 0], "pair", 2)
        elif far:
            held[move] = from_ahead(value, "pair", 4 * far)
    return [held[move] for move in early + late]


def pair_order():
    early, late = pair_moves()
    me = lax.axis_index("pair")
    count = lax.axis_size("pair")
    return jnp.stack([((me + 4 * far) % count) ^ (2 * side + core) for far, side, core in early + late])


def small_pair_blocks(value):
    count = lax.axis_size("pair")
    me = lax.axis_index("pair")
    far = jnp.stack([value] + [from_ahead(value, "pair", 4 * d) for d in range(1, count // 4)])
    side = jnp.concatenate([far, flipped(far, "pair", 2)])
    names = (me + 4 * jnp.arange(count // 4)) % count
    names = jnp.concatenate([names, names ^ 2])
    return jnp.concatenate([side, flipped(side, "pair", 1)]), jnp.concatenate([names, names ^ 1])


def plane_sum(value):
    blocks = plane_blocks(value)
    if len(blocks) == 2:
        return blocks[0].astype(F32) + blocks[1].astype(F32)
    stacked = jnp.roll(jnp.stack(blocks), lax.axis_index("pw"), axis=0)
    return jnp.sum(stacked.astype(F32), axis=0)


def iotas(rows, cols):
    return (
        lax.broadcasted_iota(jnp.int32, (rows, cols), 0),
        lax.broadcasted_iota(jnp.int32, (rows, cols), 1),
    )


def pack(symmetric, out):
    half = symmetric.shape[0] // 2
    row, col = iotas(half, half)
    upper, lower = symmetric[:half, :half], symmetric[half:, half:]
    diagonal = jnp.sum(jnp.where(row == col, upper, 0.0), axis=0, keepdims=True)
    out[:half] = symmetric[:half, half:].astype(BF16)
    out[half : 2 * half] = jnp.where(row > col, upper, lower).astype(BF16)
    out[2 * half :] = jnp.broadcast_to(diagonal, (16, half)).astype(BF16)


def unpack(packed):
    half = packed.shape[1]
    row, col = iotas(half, half)
    corner = packed[:half]
    both = packed[half : 2 * half].astype(F32)
    diagonal = packed[2 * half : 2 * half + 1].astype(F32)
    other = both.T
    upper = jnp.where(row > col, both, jnp.where(row == col, diagonal, other))
    lower = jnp.where(row <= col, both, other)
    top = jnp.concatenate([upper.astype(BF16), corner], axis=1)
    bottom = jnp.concatenate([corner.T, lower.astype(BF16)], axis=1)
    return jnp.concatenate([top, bottom], axis=0)


def left_kernel(plane, screened, density, out, total, turned):
    step = pl.program_id(0)
    size = out.shape[1]
    rows = density.shape[0]
    per_plane = max(rows // size, 1)

    @pl.when(step == 0)
    def _():
        turned[...] = density[...].T
        total[...] = jnp.zeros_like(total)

    part = dot(turned[...], screened[0]).astype(BF16)
    out[...] = part

    @pl.when(step // per_plane == plane[0])
    def _():
        at = pl.multiple_of((step % per_plane) * size, size)
        total[...] += dot(part, density[pl.ds(at, size), :])


def left_product(plane, screened, density):
    rows, width = density.shape
    depth = screened.shape[2]
    step = min(rows, 512)
    return pl.pallas_call(
        left_kernel,
        grid_spec=pltpu.PrefetchScalarGridSpec(
            num_scalar_prefetch=1,
            grid=(depth // step,),
            in_specs=[
                pl.BlockSpec((1, rows, step), lambda g, p: (0, 0, g)),
                pl.BlockSpec((rows, width), lambda g, p: (0, 0)),
            ],
            out_specs=[
                pl.BlockSpec((width, step), lambda g, p: (0, g)),
                pl.BlockSpec((width, width), lambda g, p: (0, 0)),
            ],
            scratch_shapes=[pltpu.VMEM((width, rows), BF16)],
        ),
        out_shape=[
            jax.ShapeDtypeStruct((width, depth), BF16),
            jax.ShapeDtypeStruct((width, width), F32),
        ],
        compiler_params=params(56),
        cost_estimate=cost(2 * rows * depth * width, 2 * rows * depth),
        name="left_product",
    )(plane, screened, density)


def coarse_kernel(planes, left, total, *refs):
    *blocks, out = refs
    raw = total[...]
    for step, block in enumerate(blocks):
        rows = block.shape[0]
        at = pl.multiple_of(planes[step] * rows, rows)
        raw = raw + dot(left[:, pl.ds(at, rows)], block[...])
    pack(0.5 * (raw + raw.T), out)


def coarse_block(planes, left, total, density_blocks):
    width = left.shape[0]
    vmem = pl.BlockSpec(memory_space=pltpu.VMEM)
    return pl.pallas_call(
        coarse_kernel,
        in_specs=[pl.BlockSpec(memory_space=pltpu.SMEM)] + [vmem] * (2 + len(density_blocks)),
        out_specs=vmem,
        out_shape=jax.ShapeDtypeStruct((width + 16, width // 2), BF16),
        compiler_params=params(16),
        cost_estimate=cost(2 * width * width * left.shape[1] // 2, 4 * MIB),
        name="coarse_block",
    )(planes, left, total, *density_blocks)


def spread_parts(rows, cols, each, repeat, widen, same):
    row, at = iotas(rows * each, rows)
    repeat[...] = jnp.where((row >= at * each) & (row < (at + 1) * each), 1.0, 0.0).astype(BF16)
    at, col = iotas(cols, cols * each)
    widen[...] = jnp.where((col >= at * each) & (col < (at + 1) * each), 1.0, 0.0).astype(BF16)
    row, col = iotas(rows * each, cols * each)
    same[...] = jnp.where(row % each == col % each, 1.0, 0.0)


def spread_table(table, repeat, widen, same):
    wide = dot(dot(repeat[...], table).astype(BF16), widen[...])
    return (wide * same[...]).astype(BF16)


def mix_kernel(each, mix, *refs):
    *blocks, _, mixer, mixed, repeat, widen, same = refs

    @pl.when(pl.program_id(0) == 0)
    def _():
        spread_parts(mix.shape[1], mix.shape[2], each, repeat, widen, same)

    for c in range(mix.shape[0]):
        table = spread_table(mix[c], repeat, widen, same)
        mixer[c] = table
        total, at = 0.0, 0
        for block in blocks:
            depth = block.shape[0]
            total = total + dot(table[:, at : at + depth], block[...])
            at += depth
        mixed[c] = total.astype(BF16)


def mix_all(mix, blocks, each, after):
    count, points, fine = mix.shape
    depth, width = blocks[0].shape
    group = 4
    return pl.pallas_call(
        functools.partial(mix_kernel, each),
        grid=(count // group,),
        in_specs=[pl.BlockSpec((group, points, fine), lambda c: (c, 0, 0))]
        + [pl.BlockSpec((depth, width), lambda c: (0, 0)) for _ in blocks]
        + [ANY],
        out_specs=[
            pl.BlockSpec((group, points * each, fine * each), lambda c: (c, 0, 0)),
            pl.BlockSpec((group, points * each, width), lambda c: (c, 0, 0)),
        ],
        out_shape=[
            jax.ShapeDtypeStruct((count, points * each, fine * each), BF16),
            jax.ShapeDtypeStruct((count, points * each, width), BF16),
        ],
        scratch_shapes=[
            pltpu.VMEM((points * each, points), BF16),
            pltpu.VMEM((fine, fine * each), BF16),
            pltpu.VMEM((points * each, fine * each), F32),
        ],
        compiler_params=params(24),
        cost_estimate=cost(4 * count * points * fine * each * each * width, 8 * MIB),
        name="mix_all",
    )(mix, *blocks, after)


def row_mix_kernel(each, mix, vectors, _, out, table, repeat, widen, same):
    points, group, width = vectors.shape
    count, rows = out.shape[:2]

    @pl.when(pl.program_id(0) == 0)
    def _():
        spread_parts(mix.shape[0], mix.shape[1], each, repeat, widen, same)
        table[...] = spread_table(mix[...], repeat, widen, same)

    value = vectors[...].astype(F32).reshape(points, group // each, each, width)
    parts = []
    for g in range(group // each):
        flat = value[:, g].reshape(points * each, width).astype(BF16)
        parts.append(dot(table[...], flat).reshape(count * rows, each, width))
    joined = jnp.concatenate(parts, axis=1).astype(BF16)
    out[...] = joined.reshape(out.shape)


def row_mix_all(mix, vectors, after):
    count, rows, points = mix.shape
    columns, width = vectors.shape[1:]
    each, group = 8, 16
    return pl.pallas_call(
        functools.partial(row_mix_kernel, each),
        grid=(columns // group,),
        in_specs=[
            whole((count * rows, points)),
            pl.BlockSpec((points, group, width), lambda g: (0, g, 0)),
            ANY,
        ],
        out_specs=pl.BlockSpec((count, rows, group, width), lambda g: (0, 0, g, 0)),
        out_shape=jax.ShapeDtypeStruct((count, rows, columns, width), BF16),
        scratch_shapes=[
            pltpu.VMEM((count * rows * each, points * each), BF16),
            pltpu.VMEM((count * rows * each, count * rows), BF16),
            pltpu.VMEM((points, points * each), BF16),
            pltpu.VMEM((count * rows * each, points * each), F32),
        ],
        compiler_params=params(24),
        cost_estimate=cost(2 * count * rows * each * points * columns * width, 8 * MIB),
        name="row_mix_all",
    )(mix.reshape(count * rows, points), vectors, after)


def row_through_kernel(vectors, *refs):
    *kernels, _, out = refs
    total, c = 0.0, 0
    for kernel in kernels:
        for k in range(kernel.shape[0]):
            total = total + dot(vectors[c], kernel[k])
            c += 1
    out[...] = total.astype(BF16)


def row_through(vectors, kernels, after):
    count, rows, width = vectors.shape
    vmem = pl.BlockSpec(memory_space=pltpu.VMEM)
    return pl.pallas_call(
        row_through_kernel,
        in_specs=[vmem] * (1 + len(kernels)) + [ANY],
        out_specs=vmem,
        out_shape=jax.ShapeDtypeStruct((rows, width), BF16),
        compiler_params=params(24),
        cost_estimate=cost(2 * count * rows * width * width, 6 * MIB),
        name="row_through",
    )(vectors, *kernels, after)


def start_kernel(each, pick, transform, trial, live, start, mine, my_trial, held):
    points, width, _ = transform.shape
    for k in range(points):
        here = slice(k * each, (k + 1) * each)
        block = trial[k * width : (k + 1) * width, :]
        my_trial[here] = dot(pick[...], block, NT)
        vectors = block.astype(F32).T * live[k : k + 1, :]
        turned = dot(vectors.astype(BF16), transform[k], NT).astype(BF16)
        start[k] = turned
        held[here] = dot(pick[...], turned)
    mine[...] = held[...].astype(BF16)


def start_call(pick, transform, trial, live):
    each, columns = pick.shape
    points, width, _ = transform.shape
    group = 8
    my_rows = pl.BlockSpec((group * each, width), lambda s: (s, 0))
    return pl.pallas_call(
        functools.partial(start_kernel, each),
        grid=(points // group,),
        in_specs=[
            whole((each, columns)),
            pl.BlockSpec((group, width, width), lambda s: (s, 0, 0)),
            pl.BlockSpec((group * width, columns), lambda s: (s, 0)),
            pl.BlockSpec((group, width), lambda s: (s, 0)),
        ],
        out_specs=[
            pl.BlockSpec((group, columns, width), lambda s: (s, 0, 0)),
            my_rows,
            my_rows,
        ],
        out_shape=[
            jax.ShapeDtypeStruct((points, columns, width), BF16),
            jax.ShapeDtypeStruct((points * each, width), BF16),
            jax.ShapeDtypeStruct((points * each, width), F32),
        ],
        scratch_shapes=[pltpu.VMEM((group * each, width), F32)],
        compiler_params=params(24),
        cost_estimate=cost(4 * points * columns * width * width, 8 * MIB),
        name="start_call",
    )(pick, transform, trial, live)


def fold_kernel(scale, each, transform, live, energy, my_trial, _, folded, shift):
    for k in range(transform.shape[0]):
        here = slice(k * each, (k + 1) * each)
        table = transform[k]
        masked = (table.astype(F32) * (scale * live[k : k + 1, :])).astype(BF16)
        folded[k] = dot(masked, table, NT).astype(BF16)
        vectors = my_trial[here] * (live[k : k + 1, :] * energy[k : k + 1, :])
        shift[here] = dot(vectors.astype(BF16), table, NT)


def fold_call(transform, live, energy, my_trial, scale, each, after):
    points, width, _ = transform.shape
    group = 8
    my_rows = pl.BlockSpec((group * each, width), lambda s: (s, 0))
    point_rows = pl.BlockSpec((group, width), lambda s: (s, 0))
    tables = pl.BlockSpec((group, width, width), lambda s: (s, 0, 0))
    return pl.pallas_call(
        functools.partial(fold_kernel, scale, each),
        grid=(points // group,),
        in_specs=[tables, point_rows, point_rows, my_rows, ANY],
        out_specs=[tables, my_rows],
        out_shape=[
            jax.ShapeDtypeStruct((points, width, width), BF16),
            jax.ShapeDtypeStruct((points * each, width), F32),
        ],
        compiler_params=params(24),
        cost_estimate=cost(3 * points * width * width * width, 8 * MIB),
        name="fold_call",
    )(transform, live, energy, my_trial, after)


def by_point(each, points, body, store):
    step = max(each, 8)
    group = step // each
    owner = lax.broadcasted_iota(jnp.int32, (step, 1), 0) // each
    for b in range(points // group):
        here = slice(b * step, (b + 1) * step)
        if group == 1:
            value = body(here, b)
        else:
            value = 0.0
            for p in range(group):
                value = value + jnp.where(owner == p, body(here, b * group + p), 0.0)
        store[here] = value


def through_kernel(first, count, each, last, *refs):
    mixed_at, *refs = refs
    packed, refs = refs[:count], refs[count:]
    if last:
        before, folded_at, shift, kernels, total, again, mixed, sems, folded, held = refs
    else:
        kernels, total, mixed, sems = refs
    load = pltpu.make_async_copy(mixed_at.at[pl.ds(first, count)], mixed, sems.at[0])
    load.start()
    if last:
        load_folded = pltpu.make_async_copy(folded_at, folded, sems.at[1])
        load_folded.start()
    for c in range(count):
        kernels[c] = unpack(packed[c][...])
    load.wait()
    value = before[...] if last else 0.0
    for c in range(count):
        value = value + dot(mixed[c], kernels[c])
    total[...] = value
    if last:
        load_folded.wait()

        def body(here, k):
            return dot(total[here].astype(BF16), folded[k]) + shift[here]

        by_point(each, folded.shape[0], body, held)
        again[...] = held[...].astype(BF16)


def through(mixed, first, packed, each, before=None, folded=None, shift=None):
    _, rows, width = mixed.shape
    count = len(packed)
    last = before is not None
    vmem = pl.BlockSpec(memory_space=pltpu.VMEM)
    rows_f32 = jax.ShapeDtypeStruct((rows, width), F32)
    out_shape = [jax.ShapeDtypeStruct((count, width, width), BF16), rows_f32]
    scratch = [pltpu.VMEM((count, rows, width), BF16), pltpu.SemaphoreType.DMA((2,))]
    operands = [mixed, *packed]
    in_specs = [ANY] + [vmem] * count
    if last:
        out_shape.append(jax.ShapeDtypeStruct((rows, width), BF16))
        scratch += [pltpu.VMEM(folded.shape, BF16), pltpu.VMEM((rows, width), F32)]
        operands += [before, folded, shift]
        in_specs += [vmem, ANY, vmem]
    return pl.pallas_call(
        functools.partial(through_kernel, first, count, each, last),
        in_specs=in_specs,
        out_specs=[vmem] * len(out_shape),
        out_shape=out_shape,
        scratch_shapes=scratch,
        compiler_params=params(24),
        cost_estimate=cost(8 * count * rows * width * width, 8 * MIB),
        name="through_last" if last else "through_early",
    )(*operands)


def energy_kernel(scale, each, transform_at, total, live, energy, trial, _, out, transform, sem):
    load = pltpu.make_async_copy(transform_at, transform, sem)
    load.start()
    load.wait()

    def body(here, k):
        turned = dot(total[here].astype(BF16), transform[k])
        row = energy[k : k + 1, :]
        value = turned * (scale * live[k : k + 1, :]) + row * trial[here]
        return value * row

    by_point(each, transform.shape[0], body, out)


def energy_call(transform, total, live, energy, my_trial, scale, each, after):
    rows, width = total.shape
    vmem = pl.BlockSpec(memory_space=pltpu.VMEM)
    return pl.pallas_call(
        functools.partial(energy_kernel, scale, each),
        in_specs=[ANY] + [vmem] * 4 + [ANY],
        out_specs=vmem,
        out_shape=jax.ShapeDtypeStruct((rows, width), F32),
        scratch_shapes=[pltpu.VMEM(transform.shape, BF16), pltpu.SemaphoreType.DMA],
        compiler_params=params(24),
        cost_estimate=cost(2 * rows * width * width, 5 * MIB),
        name="energy_call",
    )(transform, total, live, energy, my_trial, after)


def step_kernel(scale, at, each, group, parts, last, mixer_at, vectors, *refs):
    kernel_refs, refs = refs[:parts], refs[parts:]
    if last:
        before, transform_at, live, shift, out, mixer, sems, transform, total, held = refs
    else:
        out, mixer, sems = refs
    depth = vectors.shape[0]
    loads = []
    for g in range(mixer.shape[0] // group):
        part = pl.ds(g * group, group)
        loads.append(
            pltpu.make_async_copy(
                mixer_at.at[part, :, pl.ds(at * depth, depth)], mixer.at[part], sems.at[g]
            )
        )
        loads[-1].start()
    if last:
        load = pltpu.make_async_copy(transform_at, transform, sems.at[len(loads)])
        load.start()
    kernels = [(ref, c) for ref in kernel_refs for c in range(ref.shape[0])]
    value = before[...] if last else 0.0
    for c, (ref, k) in enumerate(kernels):
        if c % group == 0:
            loads[c // group].wait()
        value = value + dot(dot(mixer[c], vectors[...]).astype(BF16), ref[k])
    if not last:
        out[...] = value
        return
    total[...] = value
    load.wait()

    def body(here, k):
        turned = dot(total[here].astype(BF16), transform[k])
        return turned * (scale * live[k : k + 1, :]) + shift[here]

    by_point(each, transform.shape[0], body, held)
    out[...] = held[...].astype(BF16)


def step_call(mixer, vectors, at, kernels, scale, each, last=None):
    count, rows, _ = mixer.shape
    depth, width = vectors.shape
    group = 4
    vmem = pl.BlockSpec(memory_space=pltpu.VMEM)
    sems = count // group + (last is not None)
    scratch = [pltpu.VMEM((count, rows, depth), BF16), pltpu.SemaphoreType.DMA((sems,))]
    operands = [mixer, vectors, *kernels]
    in_specs = [ANY] + [vmem] * (1 + len(kernels))
    if last is not None:
        operands += list(last)
        in_specs += [vmem, ANY, vmem, vmem]
        scratch += [pltpu.VMEM(last[1].shape, BF16)] + [pltpu.VMEM((rows, width), F32)] * 2
    return pl.pallas_call(
        functools.partial(step_kernel, scale, at, each, group, len(kernels), last is not None),
        in_specs=in_specs,
        out_specs=vmem,
        out_shape=jax.ShapeDtypeStruct((rows, width), F32 if last is None else BF16),
        scratch_shapes=scratch,
        compiler_params=params(24),
        cost_estimate=cost(4 * count * rows * depth * width, 8 * MIB),
        name="step_part" if last is None else "step_last",
    )(*operands)


def last_kernel(each, order, trial, *refs):
    *blocks, out, held, sems = refs
    copies = [
        pltpu.make_async_copy(block, held.at[order[r]], sems.at[r])
        for r, block in enumerate(blocks)
    ]

    @pl.when(pl.program_id(0) == 0)
    def _():
        for copy in copies:
            copy.start()
        for copy in copies:
            copy.wait()

    width, columns = held.shape[2], trial.shape[1]
    points = trial.shape[0] // width
    size = points * each
    here = pl.ds(pl.multiple_of(pl.program_id(0) * size, size), size)
    part = held[:, here, :].astype(F32).reshape(len(blocks), points, each, width)
    for p in range(points):
        rows = part[:, p].reshape(columns, width)
        at = slice(p * width, (p + 1) * width)
        out[at] = 2.0 * rows.T - trial[at].astype(F32)


def last_call(blocks, order, trial, each, points):
    total, columns = trial.shape
    rows, width = blocks[0].shape
    if each % 8 != 0:
        place = jnp.zeros_like(order).at[order].set(jnp.arange(order.shape[0], dtype=jnp.int32))
        held = jnp.stack(blocks)[place].reshape(len(blocks), -1, each, width)
        summed = jnp.transpose(held, (1, 3, 0, 2)).reshape(total, columns)
        return 2.0 * summed.astype(F32) - trial.astype(F32)
    step = 8 * width
    row_block = pl.BlockSpec((step, columns), lambda s, o: (s, 0))
    return pl.pallas_call(
        functools.partial(last_kernel, each),
        grid_spec=pltpu.PrefetchScalarGridSpec(
            num_scalar_prefetch=1,
            grid=(total // step,),
            in_specs=[row_block] + [ANY] * len(blocks),
            out_specs=row_block,
            scratch_shapes=[
                pltpu.VMEM((len(blocks), rows, width), BF16),
                pltpu.SemaphoreType.DMA((len(blocks),)),
            ],
        ),
        out_shape=jax.ShapeDtypeStruct((total, columns), F32),
        compiler_params=params(24),
        cost_estimate=cost(2 * total * columns * width, 8 * MIB),
        name="last_call",
    )(order, trial, *blocks)


def shards(screened, density, transform, energy, trial, coarse_index, interp_weight, bands):
    pair_count = lax.axis_size("pair")
    plane_count = lax.axis_size("pw")
    row_index = lax.axis_index("pair")
    col_index = lax.axis_index("pw")
    transitions = density.shape[2]
    row_points, col_points, neighbours = coarse_index.shape
    fine_points = bands.shape[0]
    columns = trial.shape[1]
    each = columns // pair_count
    norm_scale = 1.0 / math.sqrt(fine_points * transitions)
    order = pair_order()

    density_blocks = plane_blocks(density[0])

    table = jnp.concatenate([coarse_index.astype(BF16), interp_weight], axis=2)
    table, rows_from = small_pair_blocks(table.reshape(row_points, -1))
    table = table.reshape(pair_count, -1)
    first_pair = (col_index * pair_count) // plane_count
    wanted = (jnp.arange(pair_count) + first_pair) % pair_count
    sort = (wanted[:, None] == rows_from[None, :]).astype(BF16)
    table = dot(sort, table).reshape(fine_points, col_points, -1)
    names = order.astype(F32)

    def coefficients(index, weight):
        hit = index.astype(F32)[..., None, :] == names[:, None]
        return jnp.sum(jnp.where(hit, weight.astype(F32)[..., None, :], 0.0), axis=-1)

    mix = coefficients(table[..., :neighbours], table[..., neighbours:])
    mix = jnp.transpose(mix, (2, 1, 0)).astype(BF16)
    row_mix = coefficients(coarse_index, interp_weight)
    row_mix = jnp.transpose(row_mix, (2, 0, 1)).astype(BF16)

    positions = jnp.arange(transitions) % NCOND
    live = (positions[None, :] < bands[:, None]).astype(F32)
    my_live = lax.dynamic_slice_in_dim(live, col_index * col_points, col_points, 0)
    energies = energy.reshape(col_points, transitions)
    pick = (
        jnp.arange(columns)[None, :] == row_index * each + jnp.arange(each)[:, None]
    ).astype(BF16)

    start, my_start, my_trial = start_call(pick, transform, trial, my_live)
    start_blocks = plane_blocks(my_start)

    planes = jnp.stack([(col_index + d) % plane_count for d in range(plane_count)])
    planes = planes.astype(jnp.int32)
    left, own = left_product(planes[:1], screened, density[0])
    packed = coarse_block(planes[1:], left, own, density_blocks[1:])

    folded, shift = fold_call(transform, my_live, energies, my_trial, norm_scale, each, packed)
    mixer, mixed = mix_all(mix, start_blocks, each, packed)
    row_mixed = row_mix_all(row_mix, start, packed)
    row_mixed = row_mixed.reshape(pair_count, row_points * columns, transitions)
    first_point = row_index * row_points
    wanted = lax.dynamic_slice_in_dim(transform, first_point % col_points, row_points, 0)
    wanted, _ = lax.optimization_barrier((wanted, packed))
    wanted_blocks = plane_blocks(wanted)
    root = first_point // col_points
    row_transform = wanted
    for step in range(1, plane_count):
        from_root = (col_index + step) % plane_count == root
        row_transform = jnp.where(from_root, wanted_blocks[step], row_transform)

    blocks = pair_blocks(plane_sum(packed).astype(BF16))
    early = len(pair_moves()[0])
    kernels_early, total = through(mixed, 0, blocks[:early], each)
    kernels_late, total, again = through(mixed, early, blocks[early:], each, total, folded, shift)
    kernels = [kernels_early, kernels_late]
    again_blocks = plane_blocks(again)
    energy_part = energy_call(
        transform, total, my_live, energies, my_trial, norm_scale, each, again
    )

    back = jnp.zeros(again.shape, F32)
    if again.shape[0] % 128 != 0:
        again_blocks = [jnp.concatenate(again_blocks, axis=0)]
    for step in range(len(again_blocks) - 1):
        part = step_call(mixer, again_blocks[step], step, kernels, norm_scale, each)
        back = part if step == 0 else back + part
    second = step_call(
        mixer, again_blocks[-1], len(again_blocks) - 1, kernels, norm_scale, each,
        (back, transform, my_live, energy_part),
    )
    second_blocks = pair_blocks(second)

    row_back = row_through(row_mixed, kernels, second)
    row_back = row_back.reshape(row_points, columns, transitions)
    row_part = jnp.einsum("ksv,kns->kvn", row_transform, row_back, preferred_element_type=F32)
    row_live = lax.dynamic_slice_in_dim(live, first_point, row_points, 0)
    row_energy = lax.dynamic_slice_in_dim(energies, first_point % col_points, row_points, 0)
    trial_blocks = trial.reshape(col_points, transitions, columns)
    row_trial = lax.dynamic_slice_in_dim(trial_blocks, first_point % col_points, row_points, 0)
    diagonal = jnp.where(root == col_index, row_energy[:, :, None] * row_trial.astype(F32), 0.0)
    row_part = row_part * norm_scale * row_live[:, :, None] + diagonal
    first_step = plane_sum(row_part.astype(BF16)).astype(BF16)
    first_step = first_step.reshape(row_points * transitions, columns)

    second_step = last_call(second_blocks, order.astype(jnp.int32), trial, each, col_points)
    return (first_step, second_step)


def solution(mesh):
    in_specs = (
        P("pair", "pw", None),
        P("pair", "pw", None),
        P("pw", None, None),
        P("pw"),
        P("pw", None),
        P("pair", "pw", None),
        P("pair", "pw", None),
        P(),
    )
    out_specs = (P("pair", None), P("pw", None))
    return jax.shard_map(shards, mesh=mesh, in_specs=in_specs, out_specs=out_specs, check_vma=False)
```

time: 169 us -> 128 us (0.76)
  matrix products: 48.9 us -> 0.71 us
  Pallas kernels: 0 us -> 47.1 us
  blocking collectives: 21.7 us -> 0 us
  waiting for transfers between devices: 39 us -> 18.3 us
  starting transfers between devices: 20.4 us -> 35.1 us
  other arithmetic: 12.3 us -> 5.73 us
  local copies, waits for them, and re-layouts: 24.7 us -> 19.4 us
    dot_general x13 -> x1, matrix products: 48.3 us -> 0.19 us  [dot(): return lax.dot_general(a, b, dims, preferred_element_type=F32)]
    pallas_call x0 -> x13, Pallas kernels: none -> 47.1 us  [the longest x1 12.9 us: left_product(): pl.pallas_call(left_kernel, grid_spec=pltpu.PrefetchScalarGridSpec(num_sc...]
    all_gather x1 -> x0, blocking collectives: 21.7 us -> none  [shards(): lax.all_gather(table.reshape(row_points, -1), 'pair', axis=0, tiled=True)]
    ppermute x12 -> x15, waiting for transfers between devices: 22.6 us -> 9.69 us  [from_ahead(): lax.ppermute(value, axis, [((s + step) % count, s) for s in range(count)])]
    ppermute x12 -> x15, starting transfers between devices: 12.4 us -> 21.4 us  [from_ahead(): lax.ppermute(value, axis, [((s + step) % count, s) for s in range(count)])]
    ppermute x24 -> x26, waiting for transfers between devices: 16.5 us -> 8.65 us  [flipped(): return lax.ppermute(value, axis, [(s, s ^ bit) for s in range(count)])]
    convert_element_type x1, local copies, waits for them, and re-layouts: 6.67 us -> 0.72 us  [shards(): row_mix = jnp.transpose(row_mix, (2, 0, 1)).astype(BF16)]
    ppermute x24 -> x26, starting transfers between devices: 8 us -> 13.7 us  [flipped(): return lax.ppermute(value, axis, [(s, s ^ bit) for s in range(count)])]
  transfers between devices with their start and end apart: 36 -> 41, of which waited for: 18 -> 11; matrix products, arithmetic and copies ran while one was open for 42% -> 9% of each run, Pallas kernels for 0% -> 32%
where the time goes in v2:
time: 128 us
  Pallas kernels  47.1 us (37%)
  starting transfers between devices  35.1 us (27%)
  local copies, waits for them, and re-layouts  19.4 us (15%)
  waiting for transfers between devices  18.3 us (14%)
  other arithmetic  5.73 us (4%)
  between operations  1.33 us (1%)
    ppermute x15, starting transfers between devices, from_ahead(): lax.ppermute(value, axis, [((s + step) % count, s) for s in range(count)])  21.4 us
    ppermute x26, starting transfers between devices, flipped(): return lax.ppermute(value, axis, [(s, s ^ bit) for s in range(count)])  13.7 us
    unnamed x41, local copies, waits for them, and re-layouts  13.2 us
    pallas_call x1, Pallas kernels, left_product(): pl.pallas_call(left_kernel, grid_spec=pltpu.PrefetchScalarGridSpec(num_sc...  12.9 us
    ppermute x15, waiting for transfers between devices, from_ahead(): lax.ppermute(value, axis, [((s + step) % count, s) for s in range(count)])  9.69 us
    ppermute x26, waiting for transfers between devices, flipped(): return lax.ppermute(value, axis, [(s, s ^ bit) for s in range(count)])  8.65 us
    pallas_call x1, Pallas kernels, last_call(): pl.pallas_call(functools.partial(last_kernel, each), grid_spec=pltpu.Pref...  6.49 us
    pallas_call x1, Pallas kernels, start_call(): pl.pallas_call(functools.partial(start_kernel, each), grid=(points // gro...  5.64 us
  transfers between devices with their start and end apart: 41, of which 11 were waited for; matrix products, arithmetic and copies ran while one was open for 9% of the time, Pallas kernels for 32%

profile of v2, /device:TPU:0, one launch (start us, length us, event | category | flops | bytes accessed | tf_op | source)
XLA Modules:
  0.0 127.7 jit_solution(205287746519468324)
XLA Ops:
  2.3 5.1 %collective-permute-start.2 = (bf16[4,256]{1,0:T(4,128)(2,1)S(1)}, bf16[4,256]{1,0:T(4,128)(2,1)S(1)}, u32[]{:S(2)}, u32[]{:S(2)}) collective-permute-start(bf16[4,256]{1,0:T(4,128)(2,1)S(1)} %reshape.207), channel_id=1, source_target_pairs={{8,0},{10,2},{12,4},{14,6},{16,8},{18,10},{20,12},{22,14},{24,16},... | collective-permute-start | bytes 6152 | tf_op jit(solution)/shard_map/ppermute | solution.py:41
  7.4 1.0 collective-permute-start.4
  8.4 1.5 %collective-permute-start = (bf16[2048,256]{1,0:T(8,128)(2,1)}, bf16[2048,256]{1,0:T(8,128)(2,1)S(1)}, u32[]{:S(2)}, u32[]{:S(2)}) collective-permute-start(bf16[2048,256]{1,0:T(8,128)(2,1)} %bitcast.56), channel_id=1, source_target_pairs={{1,0},{0,1},{3,2},{2,3},{5,4},{4,5},{7,6},{6,7},{9,8},{8,9},{11,10... | collective-permute-start | bytes 3145736 | tf_op jit(solution)/shard_map/ppermute | solution.py:41
  10.8 2.2 %copy-done = bf16[32,256,256]{2,1,0:T(8,128)(2,1)S(1)} copy-done((bf16[32,256,256]{2,1,0:T(8,128)(2,1)S(1)}, bf16[32,256,256]{2,1,0:T(8,128)(2,1)}, u32[]{:S(2)}) %copy-start) | copy-done | bytes 4194328
  13.0 1.6 %copy-done.6 = bf16[8192,128]{1,0:T(8,128)(2,1)S(1)} copy-done((bf16[8192,128]{1,0:T(8,128)(2,1)S(1)}, bf16[8192,128]{1,0:T(8,128)(2,1)}, u32[]{:S(2)}) %copy-start.6) | copy-done | bytes 2097176
  14.6 5.6 %start_call.1 = (bf16[32,128,256]{2,1,0:T(8,128)(2,1)S(1)}, bf16[256,256]{1,0:T(8,128)(2,1)S(1)}, f32[256,256]{1,0:T(8,128)S(1)}) custom-call(bf16[8,128]{1,0:T(8,128)(2,1)S(1)} %fusion.9.pick, bf16[32,256,256]{2,1,0:T(8,128)(2,1)S(1)} %copy-done, bf16[8192,128]{1,0:T(8,128)(2,1)S(1)} %copy-done.6, f32[32,256]{1,0:T(8,128)S(1)} %constant_dynamic-slice_fusion.1.live.refs_4_), custom_call_target="tpu_custom_call" | custom-call | flops 1073741824 | bytes 8388608 | tf_op jit(solution)/shard_map/start_call/pallas_call | solution.py:352
  20.2 1.4 %copy-done.9 = bf16[32,128,256]{2,1,0:T(8,128)(2,1)} copy-done((bf16[32,128,256]{2,1,0:T(8,128)(2,1)}, bf16[32,128,256]{2,1,0:T(8,128)(2,1)S(1)}, u32[]{:S(2)}) %copy-start.9) | copy-done | bytes 2097176
  22.5 1.1 constant_dynamic-slice_fusion.2
  23.6 12.9 %left_product.1 = (bf16[256,4096]{1,0:T(8,128)(2,1)}, f32[256,256]{1,0:T(8,128)}) custom-call(s32[1]{0:T(128)} %bitcast.1.plane, bf16[1,2048,4096]{2,1,0:T(8,128)(2,1)} %screened.1, bf16[2048,256]{1,0:T(8,128)(2,1)} %bitcast.57), custom_call_target="tpu_custom_call" | custom-call | flops 4294967296 | bytes 16777216 | tf_op jit(solution)/shard_map/left_product/pallas_call | solution.py:156
  37.3 1.6 %collective-permute-start.5 = (bf16[4,4,256]{2,1,0:T(4,128)(2,1)S(1)}, bf16[4,4,256]{2,1,0:T(4,128)(2,1)S(1)}, u32[]{:S(2)}, u32[]{:S(2)}) collective-permute-start(bf16[4,4,256]{2,1,0:T(4,128)(2,1)S(1)} %pad_maximum_fusion.1), channel_id=1, source_target_pairs={{0,4},{2,6},{4,0},{6,2},{8,12},{10,14},{12,8},{14,10},{16,20},{18,... | collective-permute-start | bytes 24584 | tf_op jit(solution)/shard_map/ppermute | solution.py:46
  38.8 2.1 %collective-permute-done.5 = bf16[4,4,256]{2,1,0:T(4,128)(2,1)S(1)} collective-permute-done((bf16[4,4,256]{2,1,0:T(4,128)(2,1)S(1)}, bf16[4,4,256]{2,1,0:T(4,128)(2,1)S(1)}, u32[]{:S(2)}, u32[]{:S(2)}) %collective-permute-start.5) | collective-permute-done | bytes 8224 | tf_op jit(solution)/shard_map/ppermute | solution.py:46
  42.5 1.6 %reshape.208 = f32[64,32,8]{2,1,0:T(8,128)} reshape(f32[16,1024]{1,0:T(8,128)S(1)} %fusion.5) | data formatting | bytes 131072 | tf_op jit(solution)/shard_map/reshape | solution.py:648
  44.0 1.6 %copy-done.8 = bf16[256,4096]{1,0:T(8,128)(2,1)S(1)} copy-done((bf16[256,4096]{1,0:T(8,128)(2,1)S(1)}, bf16[256,4096]{1,0:T(8,128)(2,1)}, u32[]{:S(2)}) %copy-start.8) | copy-done | bytes 2097176
  45.6 0.9 copy-done.11
  47.1 1.4 %collective-permute-start.8 = (bf16[272,128]{1,0:T(8,128)(2,1)S(1)}, bf16[272,128]{1,0:T(8,128)(2,1)S(1)}, u32[]{:S(2)}, u32[]{:S(2)}) collective-permute-start(bf16[272,128]{1,0:T(8,128)(2,1)S(1)} %coarse_block.1._.refs_2_), channel_id=1, source_target_pairs={{1,0},{0,1},{3,2},{2,3},{5,4},{4,5},{7,6},{6,7},{9,8},{8,9},{11,10... | collective-permute-start | bytes 208904 | tf_op jit(solution)/shard_map/ppermute | solution.py:41
  48.8 1.2 copy.23
  51.5 2.9 %collective-permute-start.9 = (bf16[272,128]{1,0:T(8,128)(2,1)S(1)}, bf16[272,128]{1,0:T(8,128)(2,1)S(1)}, u32[]{:S(2)}, u32[]{:S(2)}) collective-permute-start(bf16[272,128]{1,0:T(8,128)(2,1)S(1)} %add_convert_fusion.1.refs_1_), channel_id=1, source_target_pairs={{8,0},{10,2},{12,4},{14,6},{16,8},{18,10},{20,12},{22,14},{24,16},... | collective-permute-start | bytes 208904 | tf_op jit(solution)/shard_map/ppermute | solution.py:41
  54.4 1.1 select_reduce_fusion
  55.5 1.2 collective-permute-start.11
  56.7 1.5 %collective-permute-start.12 = (bf16[272,128]{1,0:T(8,128)(2,1)S(1)}, bf16[272,128]{1,0:T(8,128)(2,1)S(1)}, u32[]{:S(2)}, u32[]{:S(2)}) collective-permute-start(bf16[272,128]{1,0:T(8,128)(2,1)S(1)} %add_convert_fusion.1.refs_1_), channel_id=1, source_target_pairs={{0,4},{2,6},{4,0},{6,2},{8,12},{10,14},{12,8},{14,10},{16,20},{18,... | collective-permute-start | bytes 208904 | tf_op jit(solution)/shard_map/ppermute | solution.py:46
  58.7 1.8 %collective-permute-done.10.refs_3_ = bf16[272,128]{1,0:T(8,128)(2,1)S(1)} collective-permute-done((bf16[272,128]{1,0:T(8,128)(2,1)S(1)}, bf16[272,128]{1,0:T(8,128)(2,1)S(1)}, u32[]{:S(2)}, u32[]{:S(2)}) %collective-permute-start.10) | collective-permute-done | bytes 69664 | tf_op jit(solution)/shard_map/ppermute | solution.py:41
  60.5 5.4 %mix_all.1 = (bf16[16,256,512]{2,1,0:T(8,128)(2,1)S(1)}, bf16[16,256,256]{2,1,0:T(8,128)(2,1)S(1)}) custom-call(bf16[16,32,64]{2,1,0:T(8,128)(2,1)S(1)} %bitcast.54, bf16[256,256]{1,0:T(8,128)(2,1)S(1)} %get-tuple-element.21.refs_0_, bf16[256,256]{1,0:T(8,128)(2,1)S(1)} %collective-permute-done.7.refs_1_, bf16[272,128]{1,0:T(8,128)(2,1)S(1)} %coarse_block.1._.refs_2_), custom_call_target="tpu_custom_call" | custom-call | flops 2147483648 | bytes 8388608 | tf_op jit(solution)/shard_map/mix_all/pallas_call | solution.py:241
  65.9 2.0 %copy-done.4 = bf16[16,256,512]{2,1,0:T(8,128)(2,1)} copy-done((bf16[16,256,512]{2,1,0:T(8,128)(2,1)}, bf16[16,256,512]{2,1,0:T(8,128)(2,1)S(1)}, u32[]{:S(2)}) %copy-start.4) | copy-done | bytes 4194328
  67.9 1.5 %collective-permute-start.18 = (bf16[272,128]{1,0:T(8,128)(2,1)S(1)}, bf16[272,128]{1,0:T(8,128)(2,1)S(1)}, u32[]{:S(2)}, u32[]{:S(2)}) collective-permute-start(bf16[272,128]{1,0:T(8,128)(2,1)S(1)} %collective-permute-done.9.refs_2_), channel_id=1, source_target_pairs={{0,4},{2,6},{4,0},{6,2},{8,12},{10,14},{12,8},{14,10},{16,20},{18,... | collective-permute-start | bytes 208904 | tf_op jit(solution)/shard_map/ppermute | solution.py:46
  69.9 1.6 %collective-permute-start.22 = (bf16[272,128]{1,0:T(8,128)(2,1)S(1)}, bf16[272,128]{1,0:T(8,128)(2,1)S(1)}, u32[]{:S(2)}, u32[]{:S(2)}) collective-permute-start(bf16[272,128]{1,0:T(8,128)(2,1)S(1)} %collective-permute-done.11.refs_4_), channel_id=1, source_target_pairs={{0,4},{2,6},{4,0},{6,2},{8,12},{10,14},{12,8},{14,10},{16,20},{18,... | collective-permute-start | bytes 208904 | tf_op jit(solution)/shard_map/ppermute | solution.py:46
  71.7 3.0 %fold_call.1 = (bf16[32,256,256]{2,1,0:T(8,128)(2,1)S(1)}, f32[256,256]{1,0:T(8,128)S(1)}) custom-call(bf16[32,256,256]{2,1,0:T(8,128)(2,1)S(1)} %copy-done.1, f32[32,256]{1,0:T(8,128)S(1)} %constant_dynamic-slice_fusion.1.live.refs_4_, f32[32,256]{1,0:T(8,128)S(1)} %reshape.209.energy, f32[256,256]{1,0:T(8,128)S(1)} %get-tuple-element.25.my_trial.trial, ...), custom_call_target="tpu_custom_call" | custom-call | flops 1610612736 | bytes 8388608 | tf_op jit(solution)/shard_map/fold_call/pallas_call | solution.py:394
  74.6 1.4 %collective-permute-start.1 = (bf16[4,256,256]{2,1,0:T(8,128)(2,1)S(1)}, bf16[4,256,256]{2,1,0:T(8,128)(2,1)}, u32[]{:S(2)}, u32[]{:S(2)}) collective-permute-start(bf16[4,256,256]{2,1,0:T(8,128)(2,1)S(1)} %constant_dynamic-slice_fusion.2), channel_id=1, source_target_pairs={{1,0},{0,1},{3,2},{2,3},{5,4},{4,5},{7,6},{6,7},{9,8},{8,9},{11,10... | collective-permute-start | bytes 1572872 | tf_op jit(solution)/shard_map/ppermute | solution.py:41
  76.6 1.1 through_early.1
  77.8 1.7 %through_last.1 = (bf16[4,256,256]{2,1,0:T(8,128)(2,1)S(1)}, f32[256,256]{1,0:T(8,128)S(1)}, bf16[256,256]{1,0:T(8,128)(2,1)S(1)}) custom-call(bf16[16,256,256]{2,1,0:T(8,128)(2,1)S(1)} %get-tuple-element.22.refs_0_, bf16[272,128]{1,0:T(8,128)(2,1)S(1)} %collective-permute-done.20.refs_1_, bf16[272,128]{1,0:T(8,128)(2,1)S(1)} %collective-permute-done.21.refs_2_, ...), custom_call_target="tpu_custom_call" | custom-call | flops 536870912 | bytes 8388608 | tf_op jit(solution)/shard_map/through_last/pallas_call | solution.py:468
  81.8 2.2 %copy-done.2 = bf16[32,256,256]{2,1,0:T(8,128)(2,1)S(1)} copy-done((bf16[32,256,256]{2,1,0:T(8,128)(2,1)S(1)}, bf16[32,256,256]{2,1,0:T(8,128)(2,1)}, u32[]{:S(2)}) %copy-start.2) | copy-done | bytes 4194328
  83.9 1.0 energy_call.1.refs_5_
  84.9 1.2 copy-done.5
  86.1 2.1 %step_part.1.refs_2_ = f32[256,256]{1,0:T(8,128)S(1)} custom-call(bf16[16,256,512]{2,1,0:T(8,128)(2,1)S(1)} %copy-done.5, bf16[256,256]{1,0:T(8,128)(2,1)S(1)} %get-tuple-element.30.vectors._, bf16[12,256,256]{2,1,0:T(8,128)(2,1)S(1)} %get-tuple-element.23.refs_0_, bf16[4,256,256]{2,1,0:T(8,128)(2,1)S(1)} %get-tuple-element.28.refs_1_), custom_call_target="tpu_custom_call" | custom-call | flops 1073741824 | bytes 8388608 | tf_op jit(solution)/shard_map/step_part/pallas_call | solution.py:561
  88.2 3.5 %collective-permute-done.24.vectors = bf16[256,256]{1,0:T(8,128)(2,1)S(1)} collective-permute-done((bf16[256,256]{1,0:T(8,128)(2,1)S(1)}, bf16[256,256]{1,0:T(8,128)(2,1)S(1)}, u32[]{:S(2)}, u32[]{:S(2)}) %collective-permute-start.24) | collective-permute-done | bytes 131104 | tf_op jit(solution)/shard_map/ppermute | solution.py:41
  91.7 3.0 %step_last.1.refs_2_.refs_0_ = bf16[256,256]{1,0:T(8,128)(2,1)S(1)} custom-call(bf16[16,256,512]{2,1,0:T(8,128)(2,1)S(1)} %copy-done.5, bf16[256,256]{1,0:T(8,128)(2,1)S(1)} %collective-permute-done.24.vectors, bf16[12,256,256]{2,1,0:T(8,128)(2,1)S(1)} %get-tuple-element.23.refs_0_, bf16[4,256,256]{2,1,0:T(8,128)(2,1)S(1)} %get-tuple-element.28.refs_1_, ...), custom_call_target="tpu_custom_call" | custom-call | flops 1073741824 | bytes 8388608 | tf_op jit(solution)/shard_map/step_last/pallas_call | solution.py:561
  94.7 1.2 collective-permute-start.26
  95.9 3.2 %row_mix_all.1 = bf16[16,4,128,256]{3,2,1,0:T(8,128)(2,1)S(1)} custom-call(bf16[64,32]{1,0:T(8,128)(2,1)S(1)} %bitcast.55, bf16[32,128,256]{2,1,0:T(8,128)(2,1)S(1)} %copy-done.10, bf16[272,128]{1,0:T(8,128)(2,1)S(1)} %coarse_block.1._.refs_2_), custom_call_target="tpu_custom_call" | custom-call | flops 1073741824 | bytes 8388608 | tf_op jit(solution)/shard_map/row_mix_all/pallas_call | solution.py:288
  99.1 1.1 collective-permute-start.27
  100.2 1.9 %collective-permute-start.28 = (bf16[256,256]{1,0:T(8,128)(2,1)S(1)}, bf16[256,256]{1,0:T(8,128)(2,1)S(1)}, u32[]{:S(2)}, u32[]{:S(2)}) collective-permute-start(bf16[256,256]{1,0:T(8,128)(2,1)S(1)} %step_last.1.refs_2_.refs_0_), channel_id=1, source_target_pairs={{16,0},{18,2},{20,4},{22,6},{24,8},{26,10},{28,12},{30,14},{0,16},... | collective-permute-start | bytes 393224 | tf_op jit(solution)/shard_map/ppermute | solution.py:41
  102.6 1.2 row_through.1
  104.0 1.6 %collective-permute-start.35 = (bf16[256,256]{1,0:T(8,128)(2,1)S(1)}, bf16[256,256]{1,0:T(8,128)(2,1)S(1)}, u32[]{:S(2)}, u32[]{:S(2)}) collective-permute-start(bf16[256,256]{1,0:T(8,128)(2,1)S(1)} %collective-permute-done.26.refs_1_), channel_id=1, source_target_pairs={{0,4},{2,6},{4,0},{6,2},{8,12},{10,14},{12,8},{14,10},{16,20},{18,... | collective-permute-start | bytes 393224 | tf_op jit(solution)/shard_map/ppermute | solution.py:46
  106.1 1.3 %collective-permute-done.27.refs_2_ = bf16[256,256]{1,0:T(8,128)(2,1)S(1)} collective-permute-done((bf16[256,256]{1,0:T(8,128)(2,1)S(1)}, bf16[256,256]{1,0:T(8,128)(2,1)S(1)}, u32[]{:S(2)}, u32[]{:S(2)}) %collective-permute-start.27) | collective-permute-done | bytes 131104 | tf_op jit(solution)/shard_map/ppermute | solution.py:41
  107.4 1.4 %collective-permute-start.25 = (bf16[4,256,128]{2,1,0:T(8,128)(2,1)S(1)}, bf16[4,256,128]{2,1,0:T(8,128)(2,1)S(1)}, u32[]{:S(2)}, u32[]{:S(2)}) collective-permute-start(bf16[4,256,128]{2,1,0:T(8,128)(2,1)S(1)} %fusion.1), channel_id=1, source_target_pairs={{1,0},{0,1},{3,2},{2,3},{5,4},{4,5},{7,6},{6,7},{9,8},{8,9},{11,10... | collective-permute-start | bytes 786440 | tf_op jit(solution)/shard_map/ppermute | solution.py:41
  108.8 2.3 %collective-permute-done.28.refs_3_ = bf16[256,256]{1,0:T(8,128)(2,1)S(1)} collective-permute-done((bf16[256,256]{1,0:T(8,128)(2,1)S(1)}, bf16[256,256]{1,0:T(8,128)(2,1)S(1)}, u32[]{:S(2)}, u32[]{:S(2)}) %collective-permute-start.28) | collective-permute-done | bytes 131104 | tf_op jit(solution)/shard_map/ppermute | solution.py:41
  111.7 1.5 %collective-permute-start.39 = (bf16[256,256]{1,0:T(8,128)(2,1)S(1)}, bf16[256,256]{1,0:T(8,128)(2,1)S(1)}, u32[]{:S(2)}, u32[]{:S(2)}) collective-permute-start(bf16[256,256]{1,0:T(8,128)(2,1)S(1)} %collective-permute-done.28.refs_3_), channel_id=1, source_target_pairs={{0,4},{2,6},{4,0},{6,2},{8,12},{10,14},{12,8},{14,10},{16,20},{18,... | collective-permute-start | bytes 393224 | tf_op jit(solution)/shard_map/ppermute | solution.py:46
  113.7 3.9 %collective-permute-done.36.refs_11_ = bf16[256,256]{1,0:T(8,128)(2,1)S(1)} collective-permute-done((bf16[256,256]{1,0:T(8,128)(2,1)S(1)}, bf16[256,256]{1,0:T(8,128)(2,1)S(1)}, u32[]{:S(2)}, u32[]{:S(2)}) %collective-permute-start.36) | collective-permute-done | bytes 131104 | tf_op jit(solution)/shard_map/ppermute | solution.py:46
  117.5 1.4 %collective-permute-done.39.refs_14_ = bf16[256,256]{1,0:T(8,128)(2,1)S(1)} collective-permute-done((bf16[256,256]{1,0:T(8,128)(2,1)S(1)}, bf16[256,256]{1,0:T(8,128)(2,1)S(1)}, u32[]{:S(2)}, u32[]{:S(2)}) %collective-permute-start.39) | collective-permute-done | bytes 131104 | tf_op jit(solution)/shard_map/ppermute | solution.py:46
  121.0 6.5 %last_call.1 = f32[8192,128]{1,0:T(8,128)} custom-call(s32[16]{0:T(128)S(1)} %stack.87.order, bf16[8192,128]{1,0:T(8,128)(2,1)S(1)} %copy-done.7, bf16[256,256]{1,0:T(8,128)(2,1)S(1)} %step_last.1.refs_2_.refs_0_, bf16[256,256]{1,0:T(8,128)(2,1)S(1)} %collective-permute-done.26.refs_1_, bf16[256,256]{1,0:T(8,128)(2,1)S(1)} %collective-permute-done.27.refs_2_, ...), custom_call_target="tpu_custom_call" | custom-call | flops 536870912 | bytes 8388608 | tf_op jit(solution)/shard_map/last_call/pallas_call | solution.py:608
  (124 shorter events, 16.3 us)
Async XLA Ops:
  0.6 21.7 %copy-start.15 = (bf16[4,32,4]{1,2,0:T(4,128)(2,1)S(1)}, bf16[4,32,4]{1,2,0:T(4,128)(2,1)}, u32[]{:S(2)}) copy-start(bf16[4,32,4]{1,2,0:T(4,128)(2,1)} %param.14) | copy-start | bytes 3076
  2.3 34.9 %collective-permute-start.2 = (bf16[4,256]{1,0:T(4,128)(2,1)S(1)}, bf16[4,256]{1,0:T(4,128)(2,1)S(1)}, u32[]{:S(2)}, u32[]{:S(2)}) collective-permute-start(bf16[4,256]{1,0:T(4,128)(2,1)S(1)} %reshape.207), channel_id=1, source_target_pairs={{8,0},{10,2},{12,4},{14,6},{16,8},{18,10},{20,12},{22,14},{24,16},... | collective-permute-start | bytes 6152 | tf_op jit(solution)/shard_map/ppermute | solution.py:41
  7.4 29.8 %collective-permute-start.3 = (bf16[4,256]{1,0:T(4,128)(2,1)S(1)}, bf16[4,256]{1,0:T(4,128)(2,1)S(1)}, u32[]{:S(2)}, u32[]{:S(2)}) collective-permute-start(bf16[4,256]{1,0:T(4,128)(2,1)S(1)} %reshape.207), channel_id=1, source_target_pairs={{16,0},{18,2},{20,4},{22,6},{24,8},{26,10},{28,12},{30,14},{0,16},... | collective-permute-start | bytes 6152 | tf_op jit(solution)/shard_map/ppermute | solution.py:41
  7.4 29.8 %collective-permute-start.4 = (bf16[4,256]{1,0:T(4,128)(2,1)S(1)}, bf16[4,256]{1,0:T(4,128)(2,1)S(1)}, u32[]{:S(2)}, u32[]{:S(2)}) collective-permute-start(bf16[4,256]{1,0:T(4,128)(2,1)S(1)} %reshape.207), channel_id=1, source_target_pairs={{24,0},{26,2},{28,4},{30,6},{0,8},{2,10},{4,12},{6,14},{8,16},{10,... | collective-permute-start | bytes 6152 | tf_op jit(solution)/shard_map/ppermute | solution.py:41
  8.4 35.6 %collective-permute-start = (bf16[2048,256]{1,0:T(8,128)(2,1)}, bf16[2048,256]{1,0:T(8,128)(2,1)S(1)}, u32[]{:S(2)}, u32[]{:S(2)}) collective-permute-start(bf16[2048,256]{1,0:T(8,128)(2,1)} %bitcast.56), channel_id=1, source_target_pairs={{1,0},{0,1},{3,2},{2,3},{5,4},{4,5},{7,6},{6,7},{9,8},{8,9},{11,10... | collective-permute-start | bytes 3145736 | tf_op jit(solution)/shard_map/ppermute | solution.py:41
  10.8 25.7 %copy-start.13 = (f32[64,256]{1,0:T(8,128)}, f32[64,256]{1,0:T(8,128)S(1)}, u32[]{:S(2)}) copy-start(f32[64,256]{1,0:T(8,128)S(1)} %compare_convert_fusion) | copy-start | bytes 196612
  21.6 36.6 %collective-permute-start.7 = (bf16[256,256]{1,0:T(8,128)(2,1)S(1)}, bf16[256,256]{1,0:T(8,128)(2,1)S(1)}, u32[]{:S(2)}, u32[]{:S(2)}) collective-permute-start(bf16[256,256]{1,0:T(8,128)(2,1)S(1)} %get-tuple-element.21.refs_0_), channel_id=1, source_target_pairs={{1,0},{0,1},{3,2},{2,3},{5,4},{4,5},{7,6},{6,7},{9,8},{8,9},{11,10... | collective-permute-start | bytes 393224 | tf_op jit(solution)/shard_map/ppermute | solution.py:41
  23.6 17.7 %copy-start.14 = (f32[8192]{0:T(1024)S(1)}, f32[8192]{0:T(1024)}, u32[]{:S(2)}) copy-start(f32[8192]{0:T(1024)} %param.11) | copy-start | bytes 98308
  37.3 3.7 %collective-permute-start.5 = (bf16[4,4,256]{2,1,0:T(4,128)(2,1)S(1)}, bf16[4,4,256]{2,1,0:T(4,128)(2,1)S(1)}, u32[]{:S(2)}, u32[]{:S(2)}) collective-permute-start(bf16[4,4,256]{2,1,0:T(4,128)(2,1)S(1)} %pad_maximum_fusion.1), channel_id=1, source_target_pairs={{0,4},{2,6},{4,0},{6,2},{8,12},{10,14},{12,8},{14,10},{16,20},{18,... | collective-permute-start | bytes 24584 | tf_op jit(solution)/shard_map/ppermute | solution.py:46
  41.0 1.2 collective-permute-start.6
  47.1 4.4 %collective-permute-start.8 = (bf16[272,128]{1,0:T(8,128)(2,1)S(1)}, bf16[272,128]{1,0:T(8,128)(2,1)S(1)}, u32[]{:S(2)}, u32[]{:S(2)}) collective-permute-start(bf16[272,128]{1,0:T(8,128)(2,1)S(1)} %coarse_block.1._.refs_2_), channel_id=1, source_target_pairs={{1,0},{0,1},{3,2},{2,3},{5,4},{4,5},{7,6},{6,7},{9,8},{8,9},{11,10... | collective-permute-start | bytes 208904 | tf_op jit(solution)/shard_map/ppermute | solution.py:41
  51.5 20.2 %copy-start.1 = (bf16[32,256,256]{2,1,0:T(8,128)(2,1)S(1)}, bf16[32,256,256]{2,1,0:T(8,128)(2,1)}, u32[]{:S(2)}) copy-start(bf16[32,256,256]{2,1,0:T(8,128)(2,1)} %refs_3_.1) | copy-start | bytes 12582916
  51.5 6.7 %collective-permute-start.9 = (bf16[272,128]{1,0:T(8,128)(2,1)S(1)}, bf16[272,128]{1,0:T(8,128)(2,1)S(1)}, u32[]{:S(2)}, u32[]{:S(2)}) collective-permute-start(bf16[272,128]{1,0:T(8,128)(2,1)S(1)} %add_convert_fusion.1.refs_1_), channel_id=1, source_target_pairs={{8,0},{10,2},{12,4},{14,6},{16,8},{18,10},{20,12},{22,14},{24,16},... | collective-permute-start | bytes 208904 | tf_op jit(solution)/shard_map/ppermute | solution.py:41
  54.4 6.1 %collective-permute-start.10 = (bf16[272,128]{1,0:T(8,128)(2,1)S(1)}, bf16[272,128]{1,0:T(8,128)(2,1)S(1)}, u32[]{:S(2)}, u32[]{:S(2)}) collective-permute-start(bf16[272,128]{1,0:T(8,128)(2,1)S(1)} %add_convert_fusion.1.refs_1_), channel_id=1, source_target_pairs={{24,0},{26,2},{28,4},{30,6},{0,8},{2,10},{4,12},{6,14},{8,16},{10,... | collective-permute-start | bytes 208904 | tf_op jit(solution)/shard_map/ppermute | solution.py:41
  55.5 12.4 %collective-permute-start.11 = (bf16[272,128]{1,0:T(8,128)(2,1)S(1)}, bf16[272,128]{1,0:T(8,128)(2,1)S(1)}, u32[]{:S(2)}, u32[]{:S(2)}) collective-permute-start(bf16[272,128]{1,0:T(8,128)(2,1)S(1)} %add_convert_fusion.1.refs_1_), channel_id=1, source_target_pairs={{16,0},{18,2},{20,4},{22,6},{24,8},{26,10},{28,12},{30,14},{0,16},... | collective-permute-start | bytes 208904 | tf_op jit(solution)/shard_map/ppermute | solution.py:41
  56.7 12.7 %collective-permute-start.12 = (bf16[272,128]{1,0:T(8,128)(2,1)S(1)}, bf16[272,128]{1,0:T(8,128)(2,1)S(1)}, u32[]{:S(2)}, u32[]{:S(2)}) collective-permute-start(bf16[272,128]{1,0:T(8,128)(2,1)S(1)} %add_convert_fusion.1.refs_1_), channel_id=1, source_target_pairs={{0,4},{2,6},{4,0},{6,2},{8,12},{10,14},{12,8},{14,10},{16,20},{18,... | collective-permute-start | bytes 208904 | tf_op jit(solution)/shard_map/ppermute | solution.py:46
  58.2 11.8 %collective-permute-start.13 = (bf16[272,128]{1,0:T(8,128)(2,1)S(1)}, bf16[272,128]{1,0:T(8,128)(2,1)S(1)}, u32[]{:S(2)}, u32[]{:S(2)}) collective-permute-start(bf16[272,128]{1,0:T(8,128)(2,1)S(1)} %add_convert_fusion.1.refs_1_), channel_id=1, source_target_pairs={{0,2},{2,0},{4,6},{6,4},{8,10},{10,8},{12,14},{14,12},{16,18},{18,... | collective-permute-start | bytes 208904 | tf_op jit(solution)/shard_map/ppermute | solution.py:46
  58.2 11.8 %collective-permute-start.14 = (bf16[272,128]{1,0:T(8,128)(2,1)S(1)}, bf16[272,128]{1,0:T(8,128)(2,1)S(1)}, u32[]{:S(2)}, u32[]{:S(2)}) collective-permute-start(bf16[272,128]{1,0:T(8,128)(2,1)S(1)} %collective-permute-done.9.refs_2_), channel_id=1, source_target_pairs={{0,2},{2,0},{4,6},{6,4},{8,10},{10,8},{12,14},{14,12},{16,18},{18,... | collective-permute-start | bytes 208904 | tf_op jit(solution)/shard_map/ppermute | solution.py:46
  60.5 11.0 %collective-permute-start.15 = (bf16[272,128]{1,0:T(8,128)(2,1)S(1)}, bf16[272,128]{1,0:T(8,128)(2,1)S(1)}, u32[]{:S(2)}, u32[]{:S(2)}) collective-permute-start(bf16[272,128]{1,0:T(8,128)(2,1)S(1)} %collective-permute-done.10.refs_3_), channel_id=1, source_target_pairs={{0,2},{2,0},{4,6},{6,4},{8,10},{10,8},{12,14},{14,12},{16,18},{18,... | collective-permute-start | bytes 208904 | tf_op jit(solution)/shard_map/ppermute | solution.py:46
  67.9 8.1 %collective-permute-start.18 = (bf16[272,128]{1,0:T(8,128)(2,1)S(1)}, bf16[272,128]{1,0:T(8,128)(2,1)S(1)}, u32[]{:S(2)}, u32[]{:S(2)}) collective-permute-start(bf16[272,128]{1,0:T(8,128)(2,1)S(1)} %collective-permute-done.9.refs_2_), channel_id=1, source_target_pairs={{0,4},{2,6},{4,0},{6,2},{8,12},{10,14},{12,8},{14,10},{16,20},{18,... | collective-permute-start | bytes 208904 | tf_op jit(solution)/shard_map/ppermute | solution.py:46
  69.4 6.7 %collective-permute-start.19 = (bf16[272,128]{1,0:T(8,128)(2,1)S(1)}, bf16[272,128]{1,0:T(8,128)(2,1)S(1)}, u32[]{:S(2)}, u32[]{:S(2)}) collective-permute-start(bf16[272,128]{1,0:T(8,128)(2,1)S(1)} %collective-permute-done.10.refs_3_), channel_id=1, source_target_pairs={{0,4},{2,6},{4,0},{6,2},{8,12},{10,14},{12,8},{14,10},{16,20},{18,... | collective-permute-start | bytes 208904 | tf_op jit(solution)/shard_map/ppermute | solution.py:46
  69.9 4.7 %collective-permute-start.16 = (bf16[272,128]{1,0:T(8,128)(2,1)S(1)}, bf16[272,128]{1,0:T(8,128)(2,1)S(1)}, u32[]{:S(2)}, u32[]{:S(2)}) collective-permute-start(bf16[272,128]{1,0:T(8,128)(2,1)S(1)} %collective-permute-done.11.refs_4_), channel_id=1, source_target_pairs={{0,2},{2,0},{4,6},{6,4},{8,10},{10,8},{12,14},{14,12},{16,18},{18,... | collective-permute-start | bytes 208904 | tf_op jit(solution)/shard_map/ppermute | solution.py:46
  69.9 6.6 %collective-permute-start.22 = (bf16[272,128]{1,0:T(8,128)(2,1)S(1)}, bf16[272,128]{1,0:T(8,128)(2,1)S(1)}, u32[]{:S(2)}, u32[]{:S(2)}) collective-permute-start(bf16[272,128]{1,0:T(8,128)(2,1)S(1)} %collective-permute-done.11.refs_4_), channel_id=1, source_target_pairs={{0,4},{2,6},{4,0},{6,2},{8,12},{10,14},{12,8},{14,10},{16,20},{18,... | collective-permute-start | bytes 208904 | tf_op jit(solution)/shard_map/ppermute | solution.py:46
  71.5 5.1 %collective-permute-start.17 = (bf16[272,128]{1,0:T(8,128)(2,1)S(1)}, bf16[272,128]{1,0:T(8,128)(2,1)S(1)}, u32[]{:S(2)}, u32[]{:S(2)}) collective-permute-start(bf16[272,128]{1,0:T(8,128)(2,1)S(1)} %collective-permute-done.12.refs_5_), channel_id=1, source_target_pairs={{0,2},{2,0},{4,6},{6,4},{8,10},{10,8},{12,14},{14,12},{16,18},{18,... | collective-permute-start | bytes 208904 | tf_op jit(solution)/shard_map/ppermute | solution.py:46
  74.6 29.3 %collective-permute-start.1 = (bf16[4,256,256]{2,1,0:T(8,128)(2,1)S(1)}, bf16[4,256,256]{2,1,0:T(8,128)(2,1)}, u32[]{:S(2)}, u32[]{:S(2)}) collective-permute-start(bf16[4,256,256]{2,1,0:T(8,128)(2,1)S(1)} %constant_dynamic-slice_fusion.2), channel_id=1, source_target_pairs={{1,0},{0,1},{3,2},{2,3},{5,4},{4,5},{7,6},{6,7},{9,8},{8,9},{11,10... | collective-permute-start | bytes 1572872 | tf_op jit(solution)/shard_map/ppermute | solution.py:41
  76.0 1.7 %collective-permute-start.20 = (bf16[272,128]{1,0:T(8,128)(2,1)S(1)}, bf16[272,128]{1,0:T(8,128)(2,1)S(1)}, u32[]{:S(2)}, u32[]{:S(2)}) collective-permute-start(bf16[272,128]{1,0:T(8,128)(2,1)S(1)} %collective-permute-done.18.refs_11_), channel_id=1, source_target_pairs={{0,2},{2,0},{4,6},{6,4},{8,10},{10,8},{12,14},{14,12},{16,18},{18,... | collective-permute-start | bytes 208904 | tf_op jit(solution)/shard_map/ppermute | solution.py:46
  76.1 1.6 %collective-permute-start.21 = (bf16[272,128]{1,0:T(8,128)(2,1)S(1)}, bf16[272,128]{1,0:T(8,128)(2,1)S(1)}, u32[]{:S(2)}, u32[]{:S(2)}) collective-permute-start(bf16[272,128]{1,0:T(8,128)(2,1)S(1)} %collective-permute-done.19.refs_12_), channel_id=1, source_target_pairs={{0,2},{2,0},{4,6},{6,4},{8,10},{10,8},{12,14},{14,12},{16,18},{18,... | collective-permute-start | bytes 208904 | tf_op jit(solution)/shard_map/ppermute | solution.py:46
  76.5 1.3 collective-permute-start.23
  79.5 12.2 %collective-permute-start.24 = (bf16[256,256]{1,0:T(8,128)(2,1)S(1)}, bf16[256,256]{1,0:T(8,128)(2,1)S(1)}, u32[]{:S(2)}, u32[]{:S(2)}) collective-permute-start(bf16[256,256]{1,0:T(8,128)(2,1)S(1)} %get-tuple-element.30.vectors._), channel_id=1, source_target_pairs={{1,0},{0,1},{3,2},{2,3},{5,4},{4,5},{7,6},{6,7},{9,8},{8,9},{11,10... | collective-permute-start | bytes 393224 | tf_op jit(solution)/shard_map/ppermute | solution.py:41
  84.9 6.8 %copy-start.3 = (bf16[32,256,256]{2,1,0:T(8,128)(2,1)S(1)}, bf16[32,256,256]{2,1,0:T(8,128)(2,1)}, u32[]{:S(2)}) copy-start(bf16[32,256,256]{2,1,0:T(8,128)(2,1)} %refs_3_.1) | copy-start | bytes 12582916
  88.2 7.7 %copy-start.10 = (bf16[32,128,256]{2,1,0:T(8,128)(2,1)S(1)}, bf16[32,128,256]{2,1,0:T(8,128)(2,1)}, u32[]{:S(2)}) copy-start(bf16[32,128,256]{2,1,0:T(8,128)(2,1)} %copy-done.9) | copy-start | bytes 6291460
  94.7 9.3 %collective-permute-start.26 = (bf16[256,256]{1,0:T(8,128)(2,1)S(1)}, bf16[256,256]{1,0:T(8,128)(2,1)S(1)}, u32[]{:S(2)}, u32[]{:S(2)}) collective-permute-start(bf16[256,256]{1,0:T(8,128)(2,1)S(1)} %step_last.1.refs_2_.refs_0_), channel_id=1, source_target_pairs={{8,0},{10,2},{12,4},{14,6},{16,8},{18,10},{20,12},{22,14},{24,16},... | collective-permute-start | bytes 393224 | tf_op jit(solution)/shard_map/ppermute | solution.py:41
  99.1 6.5 %copy-start.7 = (bf16[8192,128]{1,0:T(8,128)(2,1)S(1)}, bf16[8192,128]{1,0:T(8,128)(2,1)}, u32[]{:S(2)}) copy-start(bf16[8192,128]{1,0:T(8,128)(2,1)} %trial.3) | copy-start | bytes 6291460
  99.1 8.3 %collective-permute-start.27 = (bf16[256,256]{1,0:T(8,128)(2,1)S(1)}, bf16[256,256]{1,0:T(8,128)(2,1)S(1)}, u32[]{:S(2)}, u32[]{:S(2)}) collective-permute-start(bf16[256,256]{1,0:T(8,128)(2,1)S(1)} %step_last.1.refs_2_.refs_0_), channel_id=1, source_target_pairs={{24,0},{26,2},{28,4},{30,6},{0,8},{2,10},{4,12},{6,14},{8,16},{10,... | collective-permute-start | bytes 393224 | tf_op jit(solution)/shard_map/ppermute | solution.py:41
  100.2 10.9 %collective-permute-start.28 = (bf16[256,256]{1,0:T(8,128)(2,1)S(1)}, bf16[256,256]{1,0:T(8,128)(2,1)S(1)}, u32[]{:S(2)}, u32[]{:S(2)}) collective-permute-start(bf16[256,256]{1,0:T(8,128)(2,1)S(1)} %step_last.1.refs_2_.refs_0_), channel_id=1, source_target_pairs={{16,0},{18,2},{20,4},{22,6},{24,8},{26,10},{28,12},{30,14},{0,16},... | collective-permute-start | bytes 393224 | tf_op jit(solution)/shard_map/ppermute | solution.py:41
  102.1 9.6 %collective-permute-start.29 = (bf16[256,256]{1,0:T(8,128)(2,1)S(1)}, bf16[256,256]{1,0:T(8,128)(2,1)S(1)}, u32[]{:S(2)}, u32[]{:S(2)}) collective-permute-start(bf16[256,256]{1,0:T(8,128)(2,1)S(1)} %step_last.1.refs_2_.refs_0_), channel_id=1, source_target_pairs={{0,4},{2,6},{4,0},{6,2},{8,12},{10,14},{12,8},{14,10},{16,20},{18,... | collective-permute-start | bytes 393224 | tf_op jit(solution)/shard_map/ppermute | solution.py:46
  103.9 9.3 %collective-permute-start.30 = (bf16[256,256]{1,0:T(8,128)(2,1)S(1)}, bf16[256,256]{1,0:T(8,128)(2,1)S(1)}, u32[]{:S(2)}, u32[]{:S(2)}) collective-permute-start(bf16[256,256]{1,0:T(8,128)(2,1)S(1)} %step_last.1.refs_2_.refs_0_), channel_id=1, source_target_pairs={{0,2},{2,0},{4,6},{6,4},{8,10},{10,8},{12,14},{14,12},{16,18},{18,... | collective-permute-start | bytes 393224 | tf_op jit(solution)/shard_map/ppermute | solution.py:46
  104.0 9.2 %collective-permute-start.35 = (bf16[256,256]{1,0:T(8,128)(2,1)S(1)}, bf16[256,256]{1,0:T(8,128)(2,1)S(1)}, u32[]{:S(2)}, u32[]{:S(2)}) collective-permute-start(bf16[256,256]{1,0:T(8,128)(2,1)S(1)} %collective-permute-done.26.refs_1_), channel_id=1, source_target_pairs={{0,4},{2,6},{4,0},{6,2},{8,12},{10,14},{12,8},{14,10},{16,20},{18,... | collective-permute-start | bytes 393224 | tf_op jit(solution)/shard_map/ppermute | solution.py:46
  107.4 12.2 %collective-permute-start.25 = (bf16[4,256,128]{2,1,0:T(8,128)(2,1)S(1)}, bf16[4,256,128]{2,1,0:T(8,128)(2,1)S(1)}, u32[]{:S(2)}, u32[]{:S(2)}) collective-permute-start(bf16[4,256,128]{2,1,0:T(8,128)(2,1)S(1)} %fusion.1), channel_id=1, source_target_pairs={{1,0},{0,1},{3,2},{2,3},{5,4},{4,5},{7,6},{6,7},{9,8},{8,9},{11,10... | collective-permute-start | bytes 786440 | tf_op jit(solution)/shard_map/ppermute | solution.py:41
  111.1 6.4 %collective-permute-start.36 = (bf16[256,256]{1,0:T(8,128)(2,1)S(1)}, bf16[256,256]{1,0:T(8,128)(2,1)S(1)}, u32[]{:S(2)}, u32[]{:S(2)}) collective-permute-start(bf16[256,256]{1,0:T(8,128)(2,1)S(1)} %collective-permute-done.27.refs_2_), channel_id=1, source_target_pairs={{0,4},{2,6},{4,0},{6,2},{8,12},{10,14},{12,8},{14,10},{16,20},{18,... | collective-permute-start | bytes 393224 | tf_op jit(solution)/shard_map/ppermute | solution.py:46
  111.7 7.3 %collective-permute-start.39 = (bf16[256,256]{1,0:T(8,128)(2,1)S(1)}, bf16[256,256]{1,0:T(8,128)(2,1)S(1)}, u32[]{:S(2)}, u32[]{:S(2)}) collective-permute-start(bf16[256,256]{1,0:T(8,128)(2,1)S(1)} %collective-permute-done.28.refs_3_), channel_id=1, source_target_pairs={{0,4},{2,6},{4,0},{6,2},{8,12},{10,14},{12,8},{14,10},{16,20},{18,... | collective-permute-start | bytes 393224 | tf_op jit(solution)/shard_map/ppermute | solution.py:46
  113.2 5.8 %collective-permute-start.31 = (bf16[256,256]{1,0:T(8,128)(2,1)S(1)}, bf16[256,256]{1,0:T(8,128)(2,1)S(1)}, u32[]{:S(2)}, u32[]{:S(2)}) collective-permute-start(bf16[256,256]{1,0:T(8,128)(2,1)S(1)} %collective-permute-done.26.refs_1_), channel_id=1, source_target_pairs={{0,2},{2,0},{4,6},{6,4},{8,10},{10,8},{12,14},{14,12},{16,18},{18,... | collective-permute-start | bytes 393224 | tf_op jit(solution)/shard_map/ppermute | solution.py:46
  113.2 6.3 %collective-permute-start.32 = (bf16[256,256]{1,0:T(8,128)(2,1)S(1)}, bf16[256,256]{1,0:T(8,128)(2,1)S(1)}, u32[]{:S(2)}, u32[]{:S(2)}) collective-permute-start(bf16[256,256]{1,0:T(8,128)(2,1)S(1)} %collective-permute-done.27.refs_2_), channel_id=1, source_target_pairs={{0,2},{2,0},{4,6},{6,4},{8,10},{10,8},{12,14},{14,12},{16,18},{18,... | collective-permute-start | bytes 393224 | tf_op jit(solution)/shard_map/ppermute | solution.py:46
  117.5 3.2 %collective-permute-start.33 = (bf16[256,256]{1,0:T(8,128)(2,1)S(1)}, bf16[256,256]{1,0:T(8,128)(2,1)S(1)}, u32[]{:S(2)}, u32[]{:S(2)}) collective-permute-start(bf16[256,256]{1,0:T(8,128)(2,1)S(1)} %collective-permute-done.28.refs_3_), channel_id=1, source_target_pairs={{0,2},{2,0},{4,6},{6,4},{8,10},{10,8},{12,14},{14,12},{16,18},{18,... | collective-permute-start | bytes 393224 | tf_op jit(solution)/shard_map/ppermute | solution.py:46
  118.9 1.8 %collective-permute-start.34 = (bf16[256,256]{1,0:T(8,128)(2,1)S(1)}, bf16[256,256]{1,0:T(8,128)(2,1)S(1)}, u32[]{:S(2)}, u32[]{:S(2)}) collective-permute-start(bf16[256,256]{1,0:T(8,128)(2,1)S(1)} %collective-permute-done.29.refs_4_), channel_id=1, source_target_pairs={{0,2},{2,0},{4,6},{6,4},{8,10},{10,8},{12,14},{14,12},{16,18},{18,... | collective-permute-start | bytes 393224 | tf_op jit(solution)/shard_map/ppermute | solution.py:46
  118.9 1.8 %collective-permute-start.37 = (bf16[256,256]{1,0:T(8,128)(2,1)S(1)}, bf16[256,256]{1,0:T(8,128)(2,1)S(1)}, u32[]{:S(2)}, u32[]{:S(2)}) collective-permute-start(bf16[256,256]{1,0:T(8,128)(2,1)S(1)} %collective-permute-done.35.refs_10_), channel_id=1, source_target_pairs={{0,2},{2,0},{4,6},{6,4},{8,10},{10,8},{12,14},{14,12},{16,18},{18,... | collective-permute-start | bytes 393224 | tf_op jit(solution)/shard_map/ppermute | solution.py:46
  119.5 1.3 %collective-permute-start.38 = (bf16[256,256]{1,0:T(8,128)(2,1)S(1)}, bf16[256,256]{1,0:T(8,128)(2,1)S(1)}, u32[]{:S(2)}, u32[]{:S(2)}) collective-permute-start(bf16[256,256]{1,0:T(8,128)(2,1)S(1)} %collective-permute-done.36.refs_11_), channel_id=1, source_target_pairs={{0,2},{2,0},{4,6},{6,4},{8,10},{10,8},{12,14},{14,12},{16,18},{18,... | collective-permute-start | bytes 393224 | tf_op jit(solution)/shard_map/ppermute | solution.py:46
  119.5 1.5 %collective-permute-start.40 = (bf16[256,256]{1,0:T(8,128)(2,1)S(1)}, bf16[256,256]{1,0:T(8,128)(2,1)S(1)}, u32[]{:S(2)}, u32[]{:S(2)}) collective-permute-start(bf16[256,256]{1,0:T(8,128)(2,1)S(1)} %collective-permute-done.39.refs_14_), channel_id=1, source_target_pairs={{0,2},{2,0},{4,6},{6,4},{8,10},{10,8},{12,14},{14,12},{16,18},{18,... | collective-permute-start | bytes 393224 | tf_op jit(solution)/shard_map/ppermute | solution.py:46
  (9 other events, 16.0 us)

commit v3 on v1

v3 whole, which is shorter than its diff:
```python
import functools
import math

import jax
import jax.numpy as jnp
from jax import lax
from jax.experimental import pallas as pl
from jax.experimental.pallas import tpu as pltpu
from jax.sharding import PartitionSpec as P

NCOND = 16
F32 = jnp.float32
BF16 = jnp.bfloat16
MIB = 1 << 20
NN = (((1,), (0,)), ((), ()))
NT = (((1,), (1,)), ((), ()))
TN = (((0,), (0,)), ((), ()))


def dot(a, b, dims=NN):
    return lax.dot_general(a, b, dims, preferred_element_type=F32)


def cost(flops, read):
    return pl.CostEstimate(flops=1, bytes_accessed=1, transcendentals=0)


def params(mib):
    return pltpu.CompilerParams(vmem_limit_bytes=mib * MIB)


def whole(shape):
    return pl.BlockSpec(shape, lambda *_: (0,) * len(shape))


ANY = pl.BlockSpec(memory_space=pl.ANY)
HBM = pl.BlockSpec(memory_space=pltpu.HBM)
VMEM = pl.BlockSpec(memory_space=pltpu.VMEM)
SMEM = pl.BlockSpec(memory_space=pltpu.SMEM)


def far(value):
    return pltpu.with_memory_space_constraint(value, pltpu.HBM)


def shaped(shape, dtype=BF16):
    return jax.ShapeDtypeStruct(shape, dtype)


def far_shaped(shape):
    return pltpu.HBM(shape, BF16)


def loads(source, target, sems, pieces, axis=0, first=0):
    size = target.shape[axis] // pieces
    copies = []
    for p in range(pieces):
        at = (slice(None),) * axis + (pl.ds(p * size, size),)
        copies.append(pltpu.make_async_copy(source.at[at], target.at[at], sems.at[first + p]))
        copies[-1].start()
    return copies


def store(source, target, at, sem, copies):
    copies.append(pltpu.make_async_copy(source.at[at], target.at[at], sem))
    copies[-1].start()


def finish(copies):
    for copy in copies:
        copy.wait()


def from_ahead(value, axis, step):
    count = lax.axis_size(axis)
    return lax.ppermute(value, axis, [((s + step) % count, s) for s in range(count)])


def flipped(value, axis, bit):
    count = lax.axis_size(axis)
    return lax.ppermute(value, axis, [(s, s ^ bit) for s in range(count)])


def plane_blocks(value):
    return [value] + [from_ahead(value, "pw", d) for d in range(1, lax.axis_size("pw"))]


def pair_moves():
    groups = lax.axis_size("pair") // 4
    far = sorted(range(groups), key=lambda d: min(d, groups - d))
    early = [(d, 0, 0) for d in far] + [(0, 1, 0)] + [(d, 0, 1) for d in far] + [(0, 1, 1)]
    early += [(d, 1, 0) for d in far[1:-1]]
    late = [(d, 1, 1) for d in far[1:-1]] + [(far[-1], 1, 0), (far[-1], 1, 1)]
    return early, late


def after(value, *others):
    return lax.optimization_barrier((value, *others))[0]


def pair_blocks(value, meanwhile=None):
    early, late = pair_moves()
    far_moves = [move for move in early if move[0] and not move[1] and not move[2]]
    held = {(0, 0, 0): value, (0, 1, 0): flipped(value, "pair", 2)}
    for move in far_moves:
        ready = value
        if meanwhile is None and move == far_moves[-1]:
            ready = after(value, *[held[other] for other in far_moves[:-1]])
        held[move] = from_ahead(ready, "pair", 4 * move[0])
    done = None
    if meanwhile is not None:
        held[0, 0, 1] = flipped(value, "pair", 1)
        done = meanwhile(held[0, 0, 1])
        for move in far_moves:
            held[move] = after(held[move], done)
    for move in early + late:
        far, side, core = move
        if core and move not in held:
            held[move] = flipped(held[far, side, 0], "pair", 1)
        elif side and far and not core:
            held[move] = flipped(held[far, 0, 0], "pair", 2)
    return [held[move] for move in early + late], done


def pair_order():
    early, late = pair_moves()
    me = lax.axis_index("pair")
    count = lax.axis_size("pair")
    return jnp.stack([((me + 4 * far) % count) ^ (2 * side + core) for far, side, core in early + late])


def small_pair_blocks(value, names):
    count = lax.axis_size("pair")
    steps = range(1, count // 4)
    value = jnp.concatenate([value] + [from_ahead(value, "pair", 4 * d) for d in steps])
    me = lax.axis_index("pair")
    index = jnp.stack([(me + 4 * d) % count for d in range(count // 4)])
    value = jnp.concatenate([value] + [flipped(value, "pair", bits) for bits in (2, 1, 3)])
    index = jnp.concatenate([index ^ bits for bits in (0, 2, 1, 3)])
    return value, names[index].reshape(-1)


def plane_sum(value):
    blocks = plane_blocks(value)
    if len(blocks) == 2:
        return blocks[0].astype(F32) + blocks[1].astype(F32)
    stacked = jnp.roll(jnp.stack(blocks), lax.axis_index("pw"), axis=0)
    return jnp.sum(stacked.astype(F32), axis=0)


def iotas(rows, cols):
    return (
        lax.broadcasted_iota(jnp.int32, (rows, cols), 0),
        lax.broadcasted_iota(jnp.int32, (rows, cols), 1),
    )


def pack(symmetric, out):
    half = symmetric.shape[0] // 2
    row, col = iotas(half, half)
    upper, lower = symmetric[:half, :half], symmetric[half:, half:]
    diagonal = jnp.sum(jnp.where(row == col, upper, 0.0), axis=0, keepdims=True)
    out[:half] = symmetric[:half, half:].astype(BF16)
    out[half : 2 * half] = jnp.where(row > col, upper, lower).astype(BF16)
    out[2 * half :] = jnp.broadcast_to(diagonal, (16, half)).astype(BF16)


def unpack(packed):
    half = packed.shape[1]
    row, col = iotas(half, half)
    corner = packed[:half]
    both = packed[half : 2 * half].astype(F32)
    diagonal = packed[2 * half : 2 * half + 1].astype(F32)
    other = both.T
    upper = jnp.where(row > col, both, jnp.where(row == col, diagonal, other))
    lower = jnp.where(row <= col, both, other)
    top = jnp.concatenate([upper.astype(BF16), corner], axis=1)
    bottom = jnp.concatenate([corner.T, lower.astype(BF16)], axis=1)
    return jnp.concatenate([top, bottom], axis=0)


def left_kernel(plane, screened_at, density, _, out_at, total, screened, turned, out, sems):
    pieces = sems.shape[0] // 2
    copies = loads(screened_at.at[0], screened, sems, pieces, axis=1)
    stores = []
    rows = density.shape[0]
    turned[...] = density[...].T
    size = out.shape[1] // pieces
    for p in range(pieces):
        copies[p].wait()
        at = slice(p * size, (p + 1) * size)
        out[:, at] = dot(turned[...], screened[:, at]).astype(BF16)
        at = (slice(None), pl.ds(p * size, size))
        store(out, out_at, at, sems.at[pieces + p], stores)
    at = pl.multiple_of(plane[0] * rows, rows)
    total[...] = dot(out[:, pl.ds(at, rows)], density[...])
    finish(stores)


def left_product(plane, screened, density, later):
    rows, width = density.shape
    depth = screened.shape[2]
    return pl.pallas_call(
        left_kernel,
        in_specs=[SMEM, HBM, VMEM, ANY],
        out_specs=[HBM, VMEM],
        out_shape=[far_shaped((width, depth)), shaped((width, width), F32)],
        scratch_shapes=[
            pltpu.VMEM((rows, depth), BF16),
            pltpu.VMEM((width, rows), BF16),
            pltpu.VMEM((width, depth), BF16),
            pltpu.SemaphoreType.DMA((16,)),
        ],
        compiler_params=params(24),
        cost_estimate=cost(2 * rows * depth * width, 2 * rows * depth),
        name="left_product",
    )(plane, far(screened), density, later)


def coarse_kernel(planes, left_at, total, *refs):
    *blocks, _, _, out, left, sems = refs
    copies = []
    for step, block in enumerate(blocks):
        rows = block.shape[0]
        at = pl.multiple_of(planes[step] * rows, rows)
        part = left_at.at[:, pl.ds(at, rows)]
        copies.append(pltpu.make_async_copy(part, left.at[step], sems.at[step]))
        copies[-1].start()
    raw = total[...]
    for step, block in enumerate(blocks):
        copies[step].wait()
        raw = raw + dot(left[step], block[...])
    pack(0.5 * (raw + raw.T), out)


def coarse_block(planes, left, total, density_blocks, later):
    width = left.shape[0]
    return pl.pallas_call(
        coarse_kernel,
        in_specs=[SMEM, HBM] + [VMEM] * (1 + len(density_blocks)) + [ANY] * 2,
        out_specs=VMEM,
        out_shape=shaped((width + 16, width // 2)),
        scratch_shapes=[
            pltpu.VMEM((len(density_blocks), width, density_blocks[0].shape[0]), BF16),
            pltpu.SemaphoreType.DMA((len(density_blocks),)),
        ],
        compiler_params=params(16),
        cost_estimate=cost(width * width * left.shape[1], 4 * MIB),
        name="coarse_block",
    )(planes, far(left), total, *density_blocks, *later)


def spread(table, each, same):
    rows, cols = table.shape
    tall = jnp.broadcast_to(table[:, None, :], (rows, each, cols)).reshape(rows * each, cols)
    return (tall * same).astype(BF16)


def same_column(rows, cols, each):
    row, col = iotas(rows, cols)
    return jnp.where(((row ^ col) & (each - 1)) == 0, 1.0, 0.0)


def widening(names, cols, each):
    col = lax.broadcasted_iota(jnp.int32, (names.shape[0], cols), 1)
    return jnp.where((col >= names * each) & (col < (names + 1) * each), 1.0, 0.0).astype(BF16)


def mix_kernel(each, points, order, table, names, *refs):
    *blocks, mixer_at, mixed, wide, same, mixer, sems = refs
    count, rows, cols = mixer.shape
    stores = []
    same[...] = same_column(rows, cols, each)
    chunks = wide.shape[0] // table.shape[1]
    row = lax.broadcasted_iota(jnp.int32, names.shape, 0)
    for p in range(chunks):
        here = jnp.where(row % chunks == p, names[...], -1)
        at = slice(p * table.shape[1], (p + 1) * table.shape[1])
        wide[at] = dot(table[...], widening(here, cols, each), TN)
    for c in range(count):
        at = pl.multiple_of(order[c] * points, points)
        part = spread(wide[pl.ds(at, points), :], each, same[...])
        mixer[c] = part
        total, at = 0.0, 0
        for block in blocks:
            depth = block.shape[0]
            total = total + dot(part[:, at : at + depth], block[...])
            at += depth
        mixed[c] = total.astype(BF16)
        if c % 2 == 1:
            store(mixer, mixer_at, pl.ds(c - 1, 2), sems.at[c // 2], stores)
    finish(stores)


def mix_all(order, table, names, blocks, points, each):
    count = order.shape[0]
    cols = sum(block.shape[0] for block in blocks)
    width = blocks[0].shape[1]
    mixer = (count, points * each, cols)
    mixed = (count, points * each, width)
    return pl.pallas_call(
        functools.partial(mix_kernel, each, points),
        in_specs=[SMEM, VMEM, VMEM] + [VMEM] * len(blocks),
        out_specs=[HBM, VMEM],
        out_shape=[far_shaped(mixer), shaped(mixed)],
        scratch_shapes=[
            pltpu.VMEM((count * points, cols), F32),
            pltpu.VMEM(mixer[1:], F32),
            pltpu.VMEM(mixer, BF16),
            pltpu.SemaphoreType.DMA((count // 2,)),
        ],
        compiler_params=params(16),
        cost_estimate=cost(4 * count * points * cols * each * width, 8 * MIB),
        name="mix_all",
    )(order, table, names, *blocks)


def row_kernel(each, parts, order, table, vectors_at, *refs):
    kernels, refs = refs[:parts], refs[parts:]
    _, out, vectors, mixed, sems = refs
    points, columns, width = vectors.shape
    count, rows = mixed.shape[:2]
    pieces = sems.shape[0]
    group = columns // pieces
    copies = loads(vectors_at, vectors, sems, pieces, axis=1)
    names = lax.broadcasted_iota(jnp.int32, (points, 1), 0)
    cols = points * each
    wide = dot(table[...], widening(names, cols, each))
    mixer = spread(wide, each, same_column(count * rows * each, cols, each))
    for p in range(pieces):
        copies[p].wait()
        at = slice(p * group, (p + 1) * group)
        value = vectors[:, at, :].astype(F32).reshape(points, group // each, each, width)
        parts = []
        for g in range(group // each):
            flat = value[:, g].reshape(cols, width).astype(BF16)
            parts.append(dot(mixer, flat).reshape(count * rows, each, width))
        joined = jnp.concatenate(parts, axis=1).astype(BF16)
        mixed[:, :, at, :] = joined.reshape(count, rows, group, width)
    total, c = 0.0, 0
    for kernel in kernels:
        for k in range(kernel.shape[0]):
            total = total + dot(mixed[order[c]].reshape(out.shape), kernel[k])
            c += 1
    out[...] = total.astype(BF16)


def row_call(order, mix, vectors, kernels, later):
    count, rows, points = mix.shape
    columns, width = vectors.shape[1:]
    each = 8
    return pl.pallas_call(
        functools.partial(row_kernel, each, len(kernels)),
        in_specs=[SMEM, VMEM, HBM] + [VMEM] * len(kernels) + [ANY],
        out_specs=VMEM,
        out_shape=shaped((rows * columns, width)),
        scratch_shapes=[
            pltpu.VMEM(vectors.shape, BF16),
            pltpu.VMEM((count, rows, columns, width), BF16),
            pltpu.SemaphoreType.DMA((columns // (2 * each),)),
        ],
        compiler_params=params(24),
        cost_estimate=cost(1, 1),
        name="row_call",
    )(order, mix.reshape(count * rows, points), far(vectors), *kernels, later)


def start_kernel(each, index, pick, transform_at, trial_at, live, table, *refs):
    start_at, mine, my_trial, table_out, transform, trial, start, held, rows, sems = refs
    pieces = 4
    load_trial = loads(trial_at, trial, sems, pieces)
    load_transform = loads(transform_at, transform, sems, pieces, first=pieces)
    table_out[...] = table[...]
    points, width, _ = transform.shape
    group = points // pieces
    at_mine = pl.ds(pl.multiple_of(index[0] * each, each), each)
    stores = []
    for p in range(pieces):
        load_trial[p].wait()
        load_transform[p].wait()
        for k in range(p * group, (p + 1) * group):
            here = slice(k * each, (k + 1) * each)
            block = trial[k * width : (k + 1) * width, :]
            turned_block = block.astype(F32).T
            vectors = turned_block * live[k : k + 1, :]
            turned = dot(vectors.astype(BF16), transform[k], NT)
            start[k] = turned.astype(BF16)
            if each % 8 == 0:
                rows[0] = turned_block
                rows[1] = turned
                my_trial[here] = rows[0, at_mine, :]
                held[here] = rows[1, at_mine, :]
            else:
                my_trial[here] = dot(pick[...], block, NT)
                held[here] = dot(pick[...], start[k])
        store(start, start_at, pl.ds(p * group, group), sems.at[2 * pieces + p], stores)
    mine[...] = held[...].astype(BF16)
    finish(stores)


def start_call(index, pick, transform, trial, live, table):
    each, columns = pick.shape
    points, width, _ = transform.shape
    mine = (points * each, width)
    return pl.pallas_call(
        functools.partial(start_kernel, each),
        in_specs=[SMEM, VMEM, HBM, HBM, VMEM, VMEM],
        out_specs=[HBM] + [VMEM] * 3,
        out_shape=[
            far_shaped((points, columns, width)),
            shaped(mine),
            shaped(mine, F32),
            shaped(table.shape),
        ],
        scratch_shapes=[
            pltpu.VMEM(transform.shape, BF16),
            pltpu.VMEM(trial.shape, BF16),
            pltpu.VMEM((points, columns, width), BF16),
            pltpu.VMEM(mine, F32),
            pltpu.VMEM((2, columns, width), F32),
            pltpu.SemaphoreType.DMA((12,)),
        ],
        compiler_params=params(16),
        cost_estimate=cost(4 * points * columns * width * width, 8 * MIB),
        name="start_call",
    )(index, pick, far(transform), far(trial), live, table)


def fold_kernel(scale, each, place, transform_at, live, energy, my_trial, *refs):
    folded_at, shift, wanted_at, transform, folded, sems = refs
    pieces = 4
    group = transform.shape[0] // pieces
    copies = loads(transform_at, transform, sems, pieces)
    stores = []
    for p in range(pieces):
        copies[p].wait()
        for k in range(p * group, (p + 1) * group):
            here = slice(k * each, (k + 1) * each)
            table = transform[k]
            masked = (table.astype(F32) * (scale * live[k : k + 1, :])).astype(BF16)
            folded[k] = dot(masked, table, NT).astype(BF16)
            vectors = my_trial[here] * (live[k : k + 1, :] * energy[k : k + 1, :])
            shift[here] = dot(vectors.astype(BF16), table, NT)
        store(folded, folded_at, pl.ds(p * group, group), sems.at[pieces + p], stores)
    wanted = transform.at[pl.ds(place[0], wanted_at.shape[0])]
    stores.append(pltpu.make_async_copy(wanted, wanted_at, sems.at[2 * pieces]))
    stores[-1].start()
    finish(stores)


def fold_call(place, rows, transform, live, energy, my_trial, scale, each):
    points, width, _ = transform.shape
    vectors = (points * each, width)
    return pl.pallas_call(
        functools.partial(fold_kernel, scale, each),
        in_specs=[SMEM, HBM] + [VMEM] * 3,
        out_specs=[HBM, VMEM, HBM],
        out_shape=[
            far_shaped(transform.shape),
            shaped(vectors, F32),
            far_shaped((rows, width, width)),
        ],
        scratch_shapes=[
            pltpu.VMEM(transform.shape, BF16),
            pltpu.VMEM(transform.shape, BF16),
            pltpu.SemaphoreType.DMA((9,)),
        ],
        compiler_params=params(16),
        cost_estimate=cost(3 * points * width * width * width, 8 * MIB),
        name="fold_call",
    )(place, far(transform), live, energy, my_trial)


def by_point(each, points, body, store):
    step = max(each, 8)
    group = step // each
    owner = lax.broadcasted_iota(jnp.int32, (step, 1), 0) // each
    for b in range(points // group):
        here = slice(b * step, (b + 1) * step)
        if group == 1:
            value = body(here, b)
        else:
            value = 0.0
            for p in range(group):
                value = value + jnp.where(owner == p, body(here, b * group + p), 0.0)
        store[here] = value


def through_kernel(first, count, each, last, mixed, *refs):
    packed, refs = refs[:count], refs[count:]
    if last:
        before, folded_at, shift, kernels, total, again, folded, held, sem = refs
        load_folded = pltpu.make_async_copy(folded_at, folded, sem)
        load_folded.start()
    else:
        kernels, total = refs
    value = before[...] if last else 0.0
    for c in range(count):
        kernels[c] = unpack(packed[c][...])
        value = value + dot(mixed[first + c], kernels[c])
    total[...] = value
    if last:
        load_folded.wait()

        def body(here, k):
            return dot(total[here].astype(BF16), folded[k]) + shift[here]

        by_point(each, folded.shape[0], body, held)
        again[...] = held[...].astype(BF16)


def through(mixed, first, packed, each, before=None, folded=None, shift=None):
    _, rows, width = mixed.shape
    count = len(packed)
    last = before is not None
    out_shape = [shaped((count, width, width)), shaped((rows, width), F32)]
    scratch = []
    operands = [mixed, *packed]
    in_specs = [VMEM] * (1 + count)
    if last:
        out_shape.append(shaped((rows, width)))
        scratch = [
            pltpu.VMEM(folded.shape, BF16),
            pltpu.VMEM((rows, width), F32),
            pltpu.SemaphoreType.DMA,
        ]
        operands += [before, far(folded), shift]
        in_specs += [VMEM, HBM, VMEM]
    return pl.pallas_call(
        functools.partial(through_kernel, first, count, each, last),
        in_specs=in_specs,
        out_specs=[VMEM] * len(out_shape),
        out_shape=out_shape,
        scratch_shapes=scratch,
        compiler_params=params(24),
        cost_estimate=cost(8 * count * rows * width * width, 8 * MIB),
        name="through_last" if last else "through_early",
    )(*operands)


def mix_and_through(mixer_at, mixer, vectors, at, kernel_refs, sems, next_load):
    depth = vectors.shape[0]
    pieces = sems.shape[0]
    columns = mixer_at.at[:, :, pl.ds(at, depth)]
    copies = loads(columns, mixer, sems, pieces)
    next_load.start()
    group = mixer.shape[0] // pieces
    value, c = 0.0, 0
    for ref in kernel_refs:
        for k in range(ref.shape[0]):
            if c % group == 0:
                copies[c // group].wait()
            mixed = dot(mixer[c], vectors[...]).astype(BF16)
            value = value + dot(mixed, ref[k])
            c += 1
    return value


def step_part_kernel(scale, each, parts, mixer_at, vectors, *refs):
    kernels, refs = refs[:parts], refs[parts:]
    transform_at, total, live, energy, trial, out, shift, mixer, transform, sems, sem = refs
    load = pltpu.make_async_copy(transform_at, transform, sem)
    out[...] = mix_and_through(mixer_at, mixer, vectors, 0, kernels, sems, load)
    load.wait()

    def body(here, k):
        turned = dot(total[here].astype(BF16), transform[k])
        row = energy[k : k + 1, :]
        return (turned * (scale * live[k : k + 1, :]) + row * trial[here]) * row

    by_point(each, transform.shape[0], body, shift)


def step_part(mixer, vectors, kernels, transform, total, live, energy, my_trial, scale, each):
    rows, width = total.shape
    operands = [far(mixer), vectors, *kernels, far(transform), total, live, energy, my_trial]
    return pl.pallas_call(
        functools.partial(step_part_kernel, scale, each, len(kernels)),
        in_specs=[HBM] + [VMEM] * (1 + len(kernels)) + [HBM] + [VMEM] * 4,
        out_specs=[VMEM, VMEM],
        out_shape=[shaped((rows, width), F32)] * 2,
        scratch_shapes=[
            pltpu.VMEM((mixer.shape[0], rows, vectors.shape[0]), BF16),
            pltpu.VMEM(transform.shape, BF16),
            pltpu.SemaphoreType.DMA((4,)),
            pltpu.SemaphoreType.DMA,
        ],
        compiler_params=params(24),
        cost_estimate=cost(1, 1),
        name="step_part",
    )(*operands)


def step_last_kernel(scale, at, each, parts, mixer_at, vectors, *refs):
    kernels, refs = refs[:parts], refs[parts:]
    before, transform_at, live, shift, out, total, held, mixer, transform, sems, sem = refs
    load = pltpu.make_async_copy(transform_at, transform, sem)
    value = mix_and_through(mixer_at, mixer, vectors, at, kernels, sems, load)
    total[...] = before[...] + value
    load.wait()

    def body(here, k):
        turned = dot(total[here].astype(BF16), transform[k])
        return turned * (scale * live[k : k + 1, :]) + shift[here]

    by_point(each, transform.shape[0], body, held)
    out[...] = held[...].astype(BF16)


def step_last(mixer, vectors, at, kernels, before, transform, live, shift, scale, each):
    rows, width = before.shape
    operands = [far(mixer), vectors, *kernels, before, far(transform), live, shift]
    return pl.pallas_call(
        functools.partial(step_last_kernel, scale, at, each, len(kernels)),
        in_specs=[HBM] + [VMEM] * (2 + len(kernels)) + [HBM, VMEM, VMEM],
        out_specs=VMEM,
        out_shape=shaped((rows, width)),
        scratch_shapes=[
            pltpu.VMEM((rows, width), F32),
            pltpu.VMEM((rows, width), F32),
            pltpu.VMEM((mixer.shape[0], rows, vectors.shape[0]), BF16),
            pltpu.VMEM(transform.shape, BF16),
            pltpu.SemaphoreType.DMA((4,)),
            pltpu.SemaphoreType.DMA,
        ],
        compiler_params=params(24),
        cost_estimate=cost(1, 1),
        name="step_last",
    )(*operands)


def last_kernel(each, order, trial_at, *refs):
    *blocks, out_at, held, trial, out, in_sems, out_sems, sems = refs
    pieces = out_sems.shape[0]
    copies = [
        pltpu.make_async_copy(block, held.at[order[r]], sems.at[r])
        for r, block in enumerate(blocks)
    ]
    for copy in copies:
        copy.start()
    load_trial = loads(trial_at, trial, in_sems, pieces)
    finish(copies)
    width, columns = held.shape[2], trial.shape[1]
    points = trial.shape[0] // width // pieces
    stores = []
    for p in range(pieces):
        load_trial[p].wait()
        part = held[:, p * points * each : (p + 1) * points * each, :].astype(F32)
        part = part.reshape(len(blocks), points, each, width)
        for k in range(points):
            rows = part[:, k].reshape(columns, width)
            first = (p * points + k) * width
            at = slice(first, first + width)
            out[at] = 2.0 * rows.T - trial[at].astype(F32)
        at = pl.ds(p * points * width, points * width)
        store(out, out_at, at, out_sems.at[p], stores)
    finish(stores)


def last_call(blocks, order, trial, each):
    total, columns = trial.shape
    rows, width = blocks[0].shape
    if each % 8 != 0:
        place = jnp.zeros_like(order).at[order].set(jnp.arange(order.shape[0], dtype=jnp.int32))
        held = jnp.stack(blocks)[place].reshape(len(blocks), -1, each, width)
        summed = jnp.transpose(held, (1, 3, 0, 2)).reshape(total, columns)
        return 2.0 * summed.astype(F32) - trial.astype(F32)
    pieces = 8
    return pl.pallas_call(
        functools.partial(last_kernel, each),
        in_specs=[SMEM, HBM] + [ANY] * len(blocks),
        out_specs=HBM,
        out_shape=shaped((total, columns), F32),
        scratch_shapes=[
            pltpu.VMEM((len(blocks), rows, width), BF16),
            pltpu.VMEM((total, columns), BF16),
            pltpu.VMEM((total, columns), F32),
            pltpu.SemaphoreType.DMA((pieces,)),
            pltpu.SemaphoreType.DMA((pieces,)),
            pltpu.SemaphoreType.DMA((len(blocks),)),
        ],
        compiler_params=params(24),
        cost_estimate=cost(2 * total * columns * width, 8 * MIB),
        name="last_call",
    )(order, far(trial), *blocks)


def shards(screened, density, transform, energy, trial, coarse_index, interp_weight, bands):
    pair_count = lax.axis_size("pair")
    plane_count = lax.axis_size("pw")
    row_index = lax.axis_index("pair")
    col_index = lax.axis_index("pw")
    transitions = density.shape[2]
    row_points, col_points, neighbours = coarse_index.shape
    fine_points = bands.shape[0]
    columns = trial.shape[1]
    each = columns // pair_count
    norm_scale = 1.0 / math.sqrt(fine_points * transitions)
    order = pair_order().astype(jnp.int32)

    density_blocks = plane_blocks(density[0])

    names = jnp.arange(pair_count, dtype=jnp.int32)
    hit = jnp.swapaxes(coarse_index, 1, 2)[:, None, :, :] == names[None, :, None, None]
    weight = jnp.swapaxes(interp_weight, 1, 2).astype(F32)[:, None, :, :]
    dense = jnp.sum(jnp.where(hit, weight, 0.0), axis=2).astype(BF16)

    positions = jnp.arange(transitions) % NCOND
    live = (positions[None, :] < bands[:, None]).astype(F32)
    my_live = lax.dynamic_slice_in_dim(live, col_index * col_points, col_points, 0)
    energies = energy.reshape(col_points, transitions)
    pick = (
        jnp.arange(columns)[None, :] == row_index * each + jnp.arange(each)[:, None]
    ).astype(BF16)

    table = dense.reshape(row_points, -1)
    chunks = table.shape[1] // 128
    start, my_start, my_trial, table = start_call(
        row_index[None].astype(jnp.int32), pick, transform, trial, my_live,
        table.reshape(row_points * chunks, 128),
    )

    points_of = jnp.arange(fine_points, dtype=jnp.int32).reshape(pair_count, row_points)
    points_of = (points_of - col_index * col_points) % fine_points
    points_of = jnp.repeat(points_of, chunks, axis=1)
    table, rows_from = small_pair_blocks(after(table, density_blocks[-1]), points_of)
    rows_from = rows_from[:, None]

    planes = jnp.stack([(col_index + d) % plane_count for d in range(plane_count)])
    planes = planes.astype(jnp.int32)
    first_point = row_index * row_points
    place = (first_point % col_points).astype(jnp.int32)
    left, own = left_product(planes[:1], screened, density[0], my_start)
    folded, shift, wanted = fold_call(
        place[None], row_points, transform, my_live, energies, my_trial, norm_scale, each
    )
    packed = coarse_block(planes[1:], left, own, density_blocks[1:], (shift, my_start))
    packed = plane_sum(packed).astype(BF16)

    start_blocks = plane_blocks(after(my_start, packed))
    blocks, _ = pair_blocks(packed)
    side_block = blocks[pair_moves()[0].index((1, 1, 0))]
    mixer, mixed = mix_all(
        order, after(table, side_block), rows_from, start_blocks, col_points, each
    )
    early = len(pair_moves()[0])
    kernels_early, total = through(mixed, 0, blocks[:early], each)
    kernels_late, total, again = through(mixed, early, blocks[early:], each, total, folded, shift)
    kernels = [kernels_early, kernels_late]
    again_blocks = plane_blocks(again)

    near_count = 1
    while near_count * again.shape[0] % 128 != 0:
        near_count += 1
    first_again = jnp.concatenate(again_blocks[:near_count], axis=0)
    other_again = jnp.concatenate(again_blocks[near_count:], axis=0)
    back, shift = step_part(
        mixer, first_again, kernels, transform, total, my_live, energies, my_trial,
        norm_scale, each,
    )
    second = step_last(
        mixer, other_again, first_again.shape[0], kernels, back, transform, my_live, shift,
        norm_scale, each,
    )
    by_point_first = jnp.swapaxes(dense, 0, 1)
    second_blocks, row_back = pair_blocks(
        second, lambda block: row_call(order, by_point_first, start, kernels, block)
    )

    wanted_blocks = plane_blocks(after(wanted, second))
    root = first_point // col_points
    row_transform = wanted
    for step in range(1, plane_count):
        from_root = (col_index + step) % plane_count == root
        row_transform = jnp.where(from_root, wanted_blocks[step], row_transform)
    row_back = row_back.reshape(row_points, columns, transitions)
    row_part = jnp.einsum("ksv,kns->kvn", row_transform, row_back, preferred_element_type=F32)
    row_live = lax.dynamic_slice_in_dim(live, first_point, row_points, 0)
    row_energy = lax.dynamic_slice_in_dim(energies, first_point % col_points, row_points, 0)
    trial_blocks = trial.reshape(col_points, transitions, columns)
    row_trial = lax.dynamic_slice_in_dim(trial_blocks, first_point % col_points, row_points, 0)
    diagonal = jnp.where(root == col_index, row_energy[:, :, None] * row_trial.astype(F32), 0.0)
    row_part = row_part * norm_scale * row_live[:, :, None] + diagonal
    first_step = plane_sum(row_part.astype(BF16)).astype(BF16)
    first_step = first_step.reshape(row_points * transitions, columns)

    second_step = last_call(second_blocks, order, trial, each)
    return (first_step, second_step)


def solution(mesh):
    in_specs = (
        P("pair", "pw", None),
        P("pair", "pw", None),
        P("pw", None, None),
        P("pw"),
        P("pw", None),
        P("pair", "pw", None),
        P("pair", "pw", None),
        P(),
    )
    out_specs = (P("pair", None), P("pw", None))
    return jax.shard_map(shards, mesh=mesh, in_specs=in_specs, out_specs=out_specs, check_vma=False)
```

time: 169 us -> 113 us (0.67)
  Pallas kernels: 0 us -> 50.3 us
  matrix products: 48.9 us -> 1.62 us
  local copies, waits for them, and re-layouts: 24.7 us -> 1.12 us
  blocking collectives: 21.7 us -> 0 us
  waiting for transfers between devices: 39 us -> 18.3 us
  starting transfers between devices: 20.4 us -> 36.8 us
  other arithmetic: 12.3 us -> 3.14 us
    pallas_call x0 -> x11, Pallas kernels: none -> 50.3 us  [the longest x1 8.41 us: left_product(): pl.pallas_call(left_kernel, in_specs=[SMEM, HBM, VMEM, ANY], out_specs=[H...]
    dot_general x13 -> x0, matrix products: 48.3 us -> none  [the longest x3 10.8 us: through(): jnp.einsum('crt,cts->rs', vectors, kernels, preferred_element_type=F32)]
    all_gather x1 -> x0, blocking collectives: 21.7 us -> none  [shards(): lax.all_gather(table.reshape(row_points, -1), 'pair', axis=0, tiled=True)]
    ppermute x12 -> x15, waiting for transfers between devices: 22.6 us -> 6.09 us  [from_ahead(): lax.ppermute(value, axis, [((s + step) % count, s) for s in range(count)])]
    ppermute x12 -> x15, starting transfers between devices: 12.4 us -> 25 us  [from_ahead(): lax.ppermute(value, axis, [((s + step) % count, s) for s in range(count)])]
    unnamed x57 -> x9, local copies, waits for them, and re-layouts: 11.3 us -> 0.04 us
    convert_element_type x1 -> x2, local copies, waits for them, and re-layouts: 6.67 us -> 0.1 us  [shards(): dense = jnp.sum(jnp.where(hit, weight, 0.0), axis=2).astype(BF16)]
    ppermute x24 -> x27, waiting for transfers between devices: 16.5 us -> 12.2 us  [flipped(): return lax.ppermute(value, axis, [(s, s ^ bit) for s in range(count)])]
  transfers between devices with their start and end apart: 36 -> 42, of which waited for: 18 -> 12; matrix products, arithmetic and copies ran while one was open for 42% -> 5% of each run, Pallas kernels for 0% -> 39%
where the time goes in v3:
time: 113 us; the launch traced here: 112 us
  Pallas kernels  50.3 us (45%)
  starting transfers between devices  36.8 us (33%)
  waiting for transfers between devices  18.3 us (16%)
  other arithmetic  3.14 us (3%)
  matrix products  1.62 us (1%)
    ppermute x15, starting transfers between devices, from_ahead(): lax.ppermute(value, axis, [((s + step) % count, s) for s in range(count)])  25 us
    ppermute x27, waiting for transfers between devices, flipped(): return lax.ppermute(value, axis, [(s, s ^ bit) for s in range(count)])  12.2 us
    ppermute x27, starting transfers between devices, flipped(): return lax.ppermute(value, axis, [(s, s ^ bit) for s in range(count)])  11.8 us
    pallas_call x1, Pallas kernels, left_product(): pl.pallas_call(left_kernel, in_specs=[SMEM, HBM, VMEM, ANY], out_specs=[H...  8.41 us
    pallas_call x1, Pallas kernels, row_call(): pl.pallas_call(functools.partial(row_kernel, each, len(kernels)), in_spec...  7.24 us
    pallas_call x1, Pallas kernels, last_call(): pl.pallas_call(functools.partial(last_kernel, each), in_specs=[SMEM, HBM]...  6.94 us
    ppermute x15, waiting for transfers between devices, from_ahead(): lax.ppermute(value, axis, [((s + step) % count, s) for s in range(count)])  6.09 us
    pallas_call x1, Pallas kernels, fold_call(): pl.pallas_call(functools.partial(fold_kernel, scale, each), in_specs=[SME...  5.41 us
  transfers between devices with their start and end apart: 42, of which 12 were waited for; matrix products, arithmetic and copies ran while one was open for 5% of the time, Pallas kernels for 39%

profile of v3, /device:TPU:0, one launch (start us, length us, event | category | flops | bytes accessed | tf_op | source)
XLA Modules:
  0.0 112.5 jit_solution(4768729779399622301)
XLA Ops:
  0.6 3.0 %collective-permute-start = (bf16[2048,256]{1,0:T(8,128)(2,1)}, bf16[2048,256]{1,0:T(8,128)(2,1)S(1)}, u32[]{:S(2)}, u32[]{:S(2)}) collective-permute-start(bf16[2048,256]{1,0:T(8,128)(2,1)} %bitcast.43), channel_id=1, source_target_pairs={{1,0},{0,1},{3,2},{2,3},{5,4},{4,5},{7,6},{6,7},{9,8},{8,9},{11,10... | collective-permute-start | bytes 3145736 | tf_op jit(solution)/shard_map/ppermute | solution.py:76
  3.7 0.7 convert_bitcast_fusion
  4.4 0.7 select_reduce_fusion
  5.1 0.7 compare_convert_fusion
  6.0 5.0 %start_call.1 = (bf16[32,128,256]{2,1,0:T(8,128)(2,1)}, bf16[256,256]{1,0:T(8,128)(2,1)S(1)}, f32[256,256]{1,0:T(8,128)S(1)}, bf16[16,128]{1,0:T(8,128)(2,1)S(1)}) custom-call(s32[1]{0:T(128)} %bitcast.1.index, bf16[8,128]{1,0:T(8,128)(2,1)S(1)} %fusion.4.pick, bf16[32,256,256]{2,1,0:T(8,128)(2,1)} %refs_3_.1, bf16[8192,128]{1,0:T(8,128)(2,1)} %trial_at.3, ...), custom_call_target="tpu_custom_call" | custom-call | flops 1 | bytes 1 | tf_op jit(solution)/shard_map/start_call/pallas_call | solution.py:405
  11.1 8.4 %left_product.1 = (bf16[256,4096]{1,0:T(8,128)(2,1)}, f32[256,256]{1,0:T(8,128)S(1)}) custom-call(s32[1]{0:T(128)} %bitcast.22.plane, bf16[1,2048,4096]{2,1,0:T(8,128)(2,1)} %screened_at.1, bf16[2048,256]{1,0:T(8,128)(2,1)S(1)} %bitcast.44, bf16[256,256]{1,0:T(8,128)(2,1)S(1)} %get-tuple-element.37._.refs_2_.refs_0_), custom_call_target="tpu_custom_call" | custom-call | flops 1 | bytes 1 | tf_op jit(solution)/shard_map/left_product/pallas_call | solution.py:203
  19.5 5.4 %fold_call.1 = (bf16[32,256,256]{2,1,0:T(8,128)(2,1)}, f32[256,256]{1,0:T(8,128)S(1)}, bf16[4,256,256]{2,1,0:T(8,128)(2,1)}) custom-call(s32[1]{0:T(128)} %bitcast.place, bf16[32,256,256]{2,1,0:T(8,128)(2,1)} %refs_3_.1, f32[32,256]{1,0:T(8,128)S(1)} %constant_dynamic-slice_fusion.1.live.refs_4_, f32[32,256]{1,0:T(8,128)S(1)} %reshape.556.energy.refs_5_, ...), custom_call_target="tpu_custom_call" | custom-call | flops 1 | bytes 1 | tf_op jit(solution)/shard_map/fold_call/pallas_call | solution.py:454
  25.2 1.8 %collective-permute-done.refs_0_ = bf16[2048,256]{1,0:T(8,128)(2,1)S(1)} collective-permute-done((bf16[2048,256]{1,0:T(8,128)(2,1)}, bf16[2048,256]{1,0:T(8,128)(2,1)S(1)}, u32[]{:S(2)}, u32[]{:S(2)}) %collective-permute-start) | collective-permute-done | bytes 1048608 | tf_op jit(solution)/shard_map/ppermute | solution.py:76
  27.0 1.8 %collective-permute-start.3 = (bf16[16,128]{1,0:T(8,128)(2,1)S(1)}, bf16[16,128]{1,0:T(8,128)(2,1)S(1)}, u32[]{:S(2)}, u32[]{:S(2)}) collective-permute-start(bf16[16,128]{1,0:T(8,128)(2,1)S(1)} %get-tuple-element.31), channel_id=1, source_target_pairs={{24,0},{26,2},{28,4},{30,6},{0,8},{2,10},{4,12},{6,14},{8,16},{10,... | collective-permute-start | bytes 12296 | tf_op jit(solution)/shard_map/ppermute | solution.py:76
  28.8 2.6 %collective-permute-start.2 = (bf16[16,128]{1,0:T(8,128)(2,1)S(1)}, bf16[16,128]{1,0:T(8,128)(2,1)S(1)}, u32[]{:S(2)}, u32[]{:S(2)}) collective-permute-start(bf16[16,128]{1,0:T(8,128)(2,1)S(1)} %get-tuple-element.31), channel_id=1, source_target_pairs={{16,0},{18,2},{20,4},{22,6},{24,8},{26,10},{28,12},{30,14},{0,16},... | collective-permute-start | bytes 12296 | tf_op jit(solution)/shard_map/ppermute | solution.py:76
  31.4 1.3 %collective-permute-start.1 = (bf16[16,128]{1,0:T(8,128)(2,1)S(1)}, bf16[16,128]{1,0:T(8,128)(2,1)S(1)}, u32[]{:S(2)}, u32[]{:S(2)}) collective-permute-start(bf16[16,128]{1,0:T(8,128)(2,1)S(1)} %get-tuple-element.31), channel_id=1, source_target_pairs={{8,0},{10,2},{12,4},{14,6},{16,8},{18,10},{20,12},{22,14},{24,16},... | collective-permute-start | bytes 12296 | tf_op jit(solution)/shard_map/ppermute | solution.py:76
  32.8 1.7 %coarse_block.1 = bf16[272,128]{1,0:T(8,128)(2,1)S(1)} custom-call(s32[1]{0:T(128)} %bitcast.21.planes, bf16[256,4096]{1,0:T(8,128)(2,1)} %get-tuple-element.33.left_at, f32[256,256]{1,0:T(8,128)S(1)} %get-tuple-element.34.total, bf16[2048,256]{1,0:T(8,128)(2,1)S(1)} %collective-permute-done.refs_0_, f32[256,256]{1,0:T(8,128)S(1)} %get-tuple-element.35.refs_1_.refs_6_, ...), custom_call_target="tpu_custom_call" | custom-call | flops 1 | bytes 1 | tf_op jit(solution)/shard_map/coarse_block/pallas_call | solution.py:238
  34.5 1.6 %collective-permute-start.7 = (bf16[272,128]{1,0:T(8,128)(2,1)S(1)}, bf16[272,128]{1,0:T(8,128)(2,1)S(1)}, u32[]{:S(2)}, u32[]{:S(2)}) collective-permute-start(bf16[272,128]{1,0:T(8,128)(2,1)S(1)} %coarse_block.1), channel_id=1, source_target_pairs={{1,0},{0,1},{3,2},{2,3},{5,4},{4,5},{7,6},{6,7},{9,8},{8,9},{11,10... | collective-permute-start | bytes 208904 | tf_op jit(solution)/shard_map/ppermute | solution.py:76
  36.2 1.6 %collective-permute-start.4 = (bf16[64,128]{1,0:T(8,128)(2,1)S(1)}, bf16[64,128]{1,0:T(8,128)(2,1)S(1)}, u32[]{:S(2)}, u32[]{:S(2)}) collective-permute-start(bf16[64,128]{1,0:T(8,128)(2,1)S(1)} %get-tuple-element.56), channel_id=1, source_target_pairs={{0,4},{2,6},{4,0},{6,2},{8,12},{10,14},{12,8},{14,10},{16,20},{18,... | collective-permute-start | bytes 49160 | tf_op jit(solution)/shard_map/ppermute | solution.py:81
  37.8 1.1 collective-permute-done.7
  38.9 0.7 collective-permute-start.12
  39.7 3.1 %collective-permute-start.8 = (bf16[272,128]{1,0:T(8,128)(2,1)S(1)}, bf16[272,128]{1,0:T(8,128)(2,1)S(1)}, u32[]{:S(2)}, u32[]{:S(2)}) collective-permute-start(bf16[272,128]{1,0:T(8,128)(2,1)S(1)} %add_convert_fusion.1.refs_0_), channel_id=1, source_target_pairs={{8,0},{10,2},{12,4},{14,6},{16,8},{18,10},{20,12},{22,14},{24,16},... | collective-permute-start | bytes 208904 | tf_op jit(solution)/shard_map/ppermute | solution.py:76
  42.8 1.5 %collective-permute-start.10 = (bf16[256,256]{1,0:T(8,128)(2,1)S(1)}, bf16[256,256]{1,0:T(8,128)(2,1)S(1)}, u32[]{:S(2)}, u32[]{:S(2)}) collective-permute-start(bf16[256,256]{1,0:T(8,128)(2,1)S(1)} %get-tuple-element.37._.refs_2_.refs_0_), channel_id=1, source_target_pairs={{1,0},{0,1},{3,2},{2,3},{5,4},{4,5},{7,6},{6,7},{9,8},{8,9},{11,10... | collective-permute-start | bytes 393224 | tf_op jit(solution)/shard_map/ppermute | solution.py:76
  44.4 0.6 gather_fusion
  45.8 1.5 %collective-permute-start.18 = (bf16[272,128]{1,0:T(8,128)(2,1)S(1)}, bf16[272,128]{1,0:T(8,128)(2,1)S(1)}, u32[]{:S(2)}, u32[]{:S(2)}) collective-permute-start(bf16[272,128]{1,0:T(8,128)(2,1)S(1)} %add_convert_fusion.1.refs_0_), channel_id=1, source_target_pairs={{0,4},{2,6},{4,0},{6,2},{8,12},{10,14},{12,8},{14,10},{16,20},{18,... | collective-permute-start | bytes 208904 | tf_op jit(solution)/shard_map/ppermute | solution.py:81
  47.3 0.6 collective-permute-start.15
  47.9 0.6 collective-permute-start.13
  48.5 1.6 %collective-permute-done.18.refs_4_ = bf16[272,128]{1,0:T(8,128)(2,1)S(1)} collective-permute-done((bf16[272,128]{1,0:T(8,128)(2,1)S(1)}, bf16[272,128]{1,0:T(8,128)(2,1)S(1)}, u32[]{:S(2)}, u32[]{:S(2)}) %collective-permute-start.18) | collective-permute-done | bytes 69664 | tf_op jit(solution)/shard_map/ppermute | solution.py:81
  50.1 1.5 %collective-permute-start.9 = (bf16[272,128]{1,0:T(8,128)(2,1)S(1)}, bf16[272,128]{1,0:T(8,128)(2,1)S(1)}, u32[]{:S(2)}, u32[]{:S(2)}) collective-permute-start(bf16[272,128]{1,0:T(8,128)(2,1)S(1)} %collective-permute-done.8.refs_1_), channel_id=1, source_target_pairs={{0,4},{2,6},{4,0},{6,2},{8,12},{10,14},{12,8},{14,10},{16,20},{18,... | collective-permute-start | bytes 208904 | tf_op jit(solution)/shard_map/ppermute | solution.py:81
  51.6 2.1 %collective-permute-done.15.refs_3_ = bf16[272,128]{1,0:T(8,128)(2,1)S(1)} collective-permute-done((bf16[272,128]{1,0:T(8,128)(2,1)S(1)}, bf16[272,128]{1,0:T(8,128)(2,1)S(1)}, u32[]{:S(2)}, u32[]{:S(2)}) %collective-permute-start.15) | collective-permute-done | bytes 69664 | tf_op jit(solution)/shard_map/ppermute | solution.py:76
  55.3 2.7 %collective-permute-done.16.refs_2_ = bf16[272,128]{1,0:T(8,128)(2,1)S(1)} collective-permute-done((bf16[272,128]{1,0:T(8,128)(2,1)S(1)}, bf16[272,128]{1,0:T(8,128)(2,1)S(1)}, u32[]{:S(2)}, u32[]{:S(2)}) %collective-permute-start.16) | collective-permute-done | bytes 69664 | tf_op jit(solution)/shard_map/ppermute | solution.py:81
  58.0 4.4 %mix_all.1 = (bf16[16,256,512]{2,1,0:T(8,128)(2,1)}, bf16[16,256,256]{2,1,0:T(8,128)(2,1)S(1)}) custom-call(s32[16]{0:T(128)S(1)} %stack.80.order, bf16[256,128]{1,0:T(8,128)(2,1)S(1)} %constant_dynamic-update-slice_fusion.4.table, s32[256,1]{1,0:T(8,128)S(1)} %broadcast_in_dim_reshape.4.names, bf16[256,256]{1,0:T(8,128)(2,1)S(1)} %get-tuple-element.37._.refs_2_.refs_0_, ...), custom_call_target="tpu_custom_call" | custom-call | flops 1 | bytes 1 | tf_op jit(solution)/shard_map/mix_all/pallas_call | solution.py:301
  62.5 0.8 through_early.1
  63.4 3.0 %through_last.1 = (bf16[4,256,256]{2,1,0:T(8,128)(2,1)S(1)}, f32[256,256]{1,0:T(8,128)S(1)}, bf16[256,256]{1,0:T(8,128)(2,1)S(1)}) custom-call(bf16[16,256,256]{2,1,0:T(8,128)(2,1)S(1)} %get-tuple-element.39.mixed, bf16[272,128]{1,0:T(8,128)(2,1)S(1)} %collective-permute-done.11.refs_0_, bf16[272,128]{1,0:T(8,128)(2,1)S(1)} %collective-permute-done.14.refs_1_, ...), custom_call_target="tpu_custom_call" | custom-call | flops 1 | bytes 1 | tf_op jit(solution)/shard_map/through_last/pallas_call | solution.py:529
  66.4 1.6 %collective-permute-start.24 = (bf16[256,256]{1,0:T(8,128)(2,1)S(1)}, bf16[256,256]{1,0:T(8,128)(2,1)S(1)}, u32[]{:S(2)}, u32[]{:S(2)}) collective-permute-start(bf16[256,256]{1,0:T(8,128)(2,1)S(1)} %get-tuple-element.43.vectors), channel_id=1, source_target_pairs={{1,0},{0,1},{3,2},{2,3},{5,4},{4,5},{7,6},{6,7},{9,8},{8,9},{11,10... | collective-permute-start | bytes 393224 | tf_op jit(solution)/shard_map/ppermute | solution.py:76
  68.0 3.7 %step_part.1 = (f32[256,256]{1,0:T(8,128)S(1)}, f32[256,256]{1,0:T(8,128)S(1)}) custom-call(bf16[16,256,512]{2,1,0:T(8,128)(2,1)} %get-tuple-element.38.mixer_at, bf16[256,256]{1,0:T(8,128)(2,1)S(1)} %get-tuple-element.43.vectors, bf16[12,256,256]{2,1,0:T(8,128)(2,1)S(1)} %get-tuple-element.44.refs_0_, bf16[4,256,256]{2,1,0:T(8,128)(2,1)S(1)} %get-tuple-element.45.refs_1_, ...), custom_call_target="tpu_custom_call" | custom-call | flops 1 | bytes 1 | tf_op jit(solution)/shard_map/step_part/pallas_call | solution.py:577
  71.6 0.7 collective-permute-done.24.vectors
  72.3 3.7 %step_last.1.refs_0_ = bf16[256,256]{1,0:T(8,128)(2,1)S(1)} custom-call(bf16[16,256,512]{2,1,0:T(8,128)(2,1)} %get-tuple-element.38.mixer_at, bf16[256,256]{1,0:T(8,128)(2,1)S(1)} %collective-permute-done.24.vectors, bf16[12,256,256]{2,1,0:T(8,128)(2,1)S(1)} %get-tuple-element.44.refs_0_, bf16[4,256,256]{2,1,0:T(8,128)(2,1)S(1)} %get-tuple-element.45.refs_1_, ...), custom_call_target="tpu_custom_call" | custom-call | flops 1 | bytes 1 | tf_op jit(solution)/shard_map/step_last/pallas_call | solution.py:613
  76.0 1.6 %collective-permute-start.25 = (bf16[4,256,256]{2,1,0:T(8,128)(2,1)}, bf16[4,256,256]{2,1,0:T(8,128)(2,1)}, u32[]{:S(2)}, u32[]{:S(2)}) collective-permute-start(bf16[4,256,256]{2,1,0:T(8,128)(2,1)} %get-tuple-element.49), channel_id=1, source_target_pairs={{1,0},{0,1},{3,2},{2,3},{5,4},{4,5},{7,6},{6,7},{9,8},{8,9},{11,10... | collective-permute-start | bytes 1572872 | tf_op jit(solution)/shard_map/ppermute | solution.py:76
  78.1 3.0 %collective-permute-start.29 = (bf16[256,256]{1,0:T(8,128)(2,1)S(1)}, bf16[256,256]{1,0:T(8,128)(2,1)S(1)}, u32[]{:S(2)}, u32[]{:S(2)}) collective-permute-start(bf16[256,256]{1,0:T(8,128)(2,1)S(1)} %step_last.1.refs_0_), channel_id=1, source_target_pairs={{24,0},{26,2},{28,4},{30,6},{0,8},{2,10},{4,12},{6,14},{8,16},{10,... | collective-permute-start | bytes 393224 | tf_op jit(solution)/shard_map/ppermute | solution.py:76
  81.1 1.4 %collective-permute-done.31.refs_4_ = bf16[256,256]{1,0:T(8,128)(2,1)S(1)} collective-permute-done((bf16[256,256]{1,0:T(8,128)(2,1)S(1)}, bf16[256,256]{1,0:T(8,128)(2,1)S(1)}, u32[]{:S(2)}, u32[]{:S(2)}) %collective-permute-start.31) | collective-permute-done | bytes 131104 | tf_op jit(solution)/shard_map/ppermute | solution.py:81
  82.6 2.0 %collective-permute-start.28 = (bf16[256,256]{1,0:T(8,128)(2,1)S(1)}, bf16[256,256]{1,0:T(8,128)(2,1)S(1)}, u32[]{:S(2)}, u32[]{:S(2)}) collective-permute-start(bf16[256,256]{1,0:T(8,128)(2,1)S(1)} %step_last.1.refs_0_), channel_id=1, source_target_pairs={{8,0},{10,2},{12,4},{14,6},{16,8},{18,10},{20,12},{22,14},{24,16},... | collective-permute-start | bytes 393224 | tf_op jit(solution)/shard_map/ppermute | solution.py:76
  84.6 7.2 %row_call.1 = bf16[512,256]{1,0:T(8,128)(2,1)S(1)} custom-call(s32[16]{0:T(128)S(1)} %stack.80.order, bf16[64,32]{1,0:T(8,128)(2,1)S(1)} %bitcast.46, bf16[32,128,256]{2,1,0:T(8,128)(2,1)} %get-tuple-element.50.vectors_at, bf16[12,256,256]{2,1,0:T(8,128)(2,1)S(1)} %get-tuple-element.44.refs_0_, bf16[4,256,256]{2,1,0:T(8,128)(2,1)S(1)} %get-tuple-element.45.refs_1_, ...), custom_call_target="tpu_custom_call" | custom-call | flops 1 | bytes 1 | tf_op jit(solution)/shard_map/row_call/pallas_call | solution.py:352
  92.2 1.1 %collective-permute-start.36 = (bf16[256,256]{1,0:T(8,128)(2,1)S(1)}, bf16[256,256]{1,0:T(8,128)(2,1)S(1)}, u32[]{:S(2)}, u32[]{:S(2)}) collective-permute-start(bf16[256,256]{1,0:T(8,128)(2,1)S(1)} %collective-permute-done.28.refs_1_), channel_id=1, source_target_pairs={{0,4},{2,6},{4,0},{6,2},{8,12},{10,14},{12,8},{14,10},{16,20},{18,... | collective-permute-start | bytes 393224 | tf_op jit(solution)/shard_map/ppermute | solution.py:81
  93.3 0.9 collective-permute-start.37
  94.4 1.1 %collective-permute-start.40 = (bf16[256,256]{1,0:T(8,128)(2,1)S(1)}, bf16[256,256]{1,0:T(8,128)(2,1)S(1)}, u32[]{:S(2)}, u32[]{:S(2)}) collective-permute-start(bf16[256,256]{1,0:T(8,128)(2,1)S(1)} %collective-permute-done.30.refs_3_), channel_id=1, source_target_pairs={{0,4},{2,6},{4,0},{6,2},{8,12},{10,14},{12,8},{14,10},{16,20},{18,... | collective-permute-start | bytes 393224 | tf_op jit(solution)/shard_map/ppermute | solution.py:81
  95.6 1.6 %fusion.1 = bf16[4,256,128]{2,1,0:T(8,128)(2,1)S(1)} fusion(bf16[4,128,256]{2,1,0:T(8,128)(2,1)S(1)} %bitcast.45, bf16[4,256,256]{2,1,0:T(8,128)(2,1)} %collective-permute-done.25, bf16[4,256,256]{2,1,0:T(8,128)(2,1)} %get-tuple-element.49, pred[]{:T(512)S(6)} %eq.63, bf16[32,256,128]{2,1,0:T(8,128)(2,1)} %bitcast.47, s32[]{:T(128)S(6)} %select_n.146, ...), kind=kOutput, calls=%fused_computation.3 | convolution fusion | flops 68157440 | bytes 1843206 | tf_op jit(solution)/shard_map/ksv,kns->kvn/dot_general | solution.py:777
  97.2 1.3 %collective-permute-done.36.refs_10_ = bf16[256,256]{1,0:T(8,128)(2,1)S(1)} collective-permute-done((bf16[256,256]{1,0:T(8,128)(2,1)S(1)}, bf16[256,256]{1,0:T(8,128)(2,1)S(1)}, u32[]{:S(2)}, u32[]{:S(2)}) %collective-permute-start.36) | collective-permute-done | bytes 131104 | tf_op jit(solution)/shard_map/ppermute | solution.py:81
  99.0 2.3 %collective-permute-done.37.refs_11_ = bf16[256,256]{1,0:T(8,128)(2,1)S(1)} collective-permute-done((bf16[256,256]{1,0:T(8,128)(2,1)S(1)}, bf16[256,256]{1,0:T(8,128)(2,1)S(1)}, u32[]{:S(2)}, u32[]{:S(2)}) %collective-permute-start.37) | collective-permute-done | bytes 131104 | tf_op jit(solution)/shard_map/ppermute | solution.py:81
  101.8 1.6 %collective-permute-done.40.refs_14_ = bf16[256,256]{1,0:T(8,128)(2,1)S(1)} collective-permute-done((bf16[256,256]{1,0:T(8,128)(2,1)S(1)}, bf16[256,256]{1,0:T(8,128)(2,1)S(1)}, u32[]{:S(2)}, u32[]{:S(2)}) %collective-permute-start.40) | collective-permute-done | bytes 131104 | tf_op jit(solution)/shard_map/ppermute | solution.py:81
  103.4 1.3 %collective-permute-done.41.refs_15_ = bf16[256,256]{1,0:T(8,128)(2,1)S(1)} collective-permute-done((bf16[256,256]{1,0:T(8,128)(2,1)S(1)}, bf16[256,256]{1,0:T(8,128)(2,1)S(1)}, u32[]{:S(2)}, u32[]{:S(2)}) %collective-permute-start.41) | collective-permute-done | bytes 131104 | tf_op jit(solution)/shard_map/ppermute | solution.py:81
  104.7 6.9 %last_call.1 = f32[8192,128]{1,0:T(8,128)} custom-call(s32[16]{0:T(128)S(1)} %stack.80.order, bf16[8192,128]{1,0:T(8,128)(2,1)} %trial_at.3, bf16[256,256]{1,0:T(8,128)(2,1)S(1)} %step_last.1.refs_0_, bf16[256,256]{1,0:T(8,128)(2,1)S(1)} %collective-permute-done.28.refs_1_, bf16[256,256]{1,0:T(8,128)(2,1)S(1)} %collective-permute-done.29.refs_2_, ...), custom_call_target="tpu_custom_call" | custom-call | flops 1 | bytes 1 | tf_op jit(solution)/shard_map/last_call/pallas_call | solution.py:669
  111.7 0.8 add_convert_fusion
  (84 shorter events, 5.1 us)
Async XLA Ops:
  0.6 26.4 %collective-permute-start = (bf16[2048,256]{1,0:T(8,128)(2,1)}, bf16[2048,256]{1,0:T(8,128)(2,1)S(1)}, u32[]{:S(2)}, u32[]{:S(2)}) collective-permute-start(bf16[2048,256]{1,0:T(8,128)(2,1)} %bitcast.43), channel_id=1, source_target_pairs={{1,0},{0,1},{3,2},{2,3},{5,4},{4,5},{7,6},{6,7},{9,8},{8,9},{11,10... | collective-permute-start | bytes 3145736 | tf_op jit(solution)/shard_map/ppermute | solution.py:76
  6.0 5.1 %copy-start = (bf16[1,2048,256]{2,1,0:T(8,128)(2,1)S(1)}, bf16[1,2048,256]{2,1,0:T(8,128)(2,1)}, u32[]{:S(2)}) copy-start(bf16[1,2048,256]{2,1,0:T(8,128)(2,1)} %param.9) | copy-start | bytes 3145732
  11.1 8.4 %copy-start.1 = (f32[8192]{0:T(1024)S(1)}, f32[8192]{0:T(1024)}, u32[]{:S(2)}) copy-start(f32[8192]{0:T(1024)} %param.11) | copy-start | bytes 98308
  27.0 9.1 %collective-permute-start.3 = (bf16[16,128]{1,0:T(8,128)(2,1)S(1)}, bf16[16,128]{1,0:T(8,128)(2,1)S(1)}, u32[]{:S(2)}, u32[]{:S(2)}) collective-permute-start(bf16[16,128]{1,0:T(8,128)(2,1)S(1)} %get-tuple-element.31), channel_id=1, source_target_pairs={{24,0},{26,2},{28,4},{30,6},{0,8},{2,10},{4,12},{6,14},{8,16},{10,... | collective-permute-start | bytes 12296 | tf_op jit(solution)/shard_map/ppermute | solution.py:76
  28.8 7.3 %collective-permute-start.2 = (bf16[16,128]{1,0:T(8,128)(2,1)S(1)}, bf16[16,128]{1,0:T(8,128)(2,1)S(1)}, u32[]{:S(2)}, u32[]{:S(2)}) collective-permute-start(bf16[16,128]{1,0:T(8,128)(2,1)S(1)} %get-tuple-element.31), channel_id=1, source_target_pairs={{16,0},{18,2},{20,4},{22,6},{24,8},{26,10},{28,12},{30,14},{0,16},... | collective-permute-start | bytes 12296 | tf_op jit(solution)/shard_map/ppermute | solution.py:76
  31.4 4.7 %collective-permute-start.1 = (bf16[16,128]{1,0:T(8,128)(2,1)S(1)}, bf16[16,128]{1,0:T(8,128)(2,1)S(1)}, u32[]{:S(2)}, u32[]{:S(2)}) collective-permute-start(bf16[16,128]{1,0:T(8,128)(2,1)S(1)} %get-tuple-element.31), channel_id=1, source_target_pairs={{8,0},{10,2},{12,4},{14,6},{16,8},{18,10},{20,12},{22,14},{24,16},... | collective-permute-start | bytes 12296 | tf_op jit(solution)/shard_map/ppermute | solution.py:76
  34.5 4.4 %collective-permute-start.7 = (bf16[272,128]{1,0:T(8,128)(2,1)S(1)}, bf16[272,128]{1,0:T(8,128)(2,1)S(1)}, u32[]{:S(2)}, u32[]{:S(2)}) collective-permute-start(bf16[272,128]{1,0:T(8,128)(2,1)S(1)} %coarse_block.1), channel_id=1, source_target_pairs={{1,0},{0,1},{3,2},{2,3},{5,4},{4,5},{7,6},{6,7},{9,8},{8,9},{11,10... | collective-permute-start | bytes 208904 | tf_op jit(solution)/shard_map/ppermute | solution.py:76
  36.2 9.6 %collective-permute-start.6 = (bf16[64,128]{1,0:T(8,128)(2,1)S(1)}, bf16[64,128]{1,0:T(8,128)(2,1)S(1)}, u32[]{:S(2)}, u32[]{:S(2)}) collective-permute-start(bf16[64,128]{1,0:T(8,128)(2,1)S(1)} %get-tuple-element.56), channel_id=1, source_target_pairs={{0,6},{2,4},{4,2},{6,0},{8,14},{10,12},{12,10},{14,8},{16,22},{18,... | collective-permute-start | bytes 49160 | tf_op jit(solution)/shard_map/ppermute | solution.py:81
  36.2 11.0 %collective-permute-start.4 = (bf16[64,128]{1,0:T(8,128)(2,1)S(1)}, bf16[64,128]{1,0:T(8,128)(2,1)S(1)}, u32[]{:S(2)}, u32[]{:S(2)}) collective-permute-start(bf16[64,128]{1,0:T(8,128)(2,1)S(1)} %get-tuple-element.56), channel_id=1, source_target_pairs={{0,4},{2,6},{4,0},{6,2},{8,12},{10,14},{12,8},{14,10},{16,20},{18,... | collective-permute-start | bytes 49160 | tf_op jit(solution)/shard_map/ppermute | solution.py:81
  38.9 6.3 %collective-permute-start.12 = (bf16[272,128]{1,0:T(8,128)(2,1)S(1)}, bf16[272,128]{1,0:T(8,128)(2,1)S(1)}, u32[]{:S(2)}, u32[]{:S(2)}) collective-permute-start(bf16[272,128]{1,0:T(8,128)(2,1)S(1)} %add_convert_fusion.1.refs_0_), channel_id=1, source_target_pairs={{24,0},{26,2},{28,4},{30,6},{0,8},{2,10},{4,12},{6,14},{8,16},{10,... | collective-permute-start | bytes 208904 | tf_op jit(solution)/shard_map/ppermute | solution.py:76
  39.7 5.6 %collective-permute-start.8 = (bf16[272,128]{1,0:T(8,128)(2,1)S(1)}, bf16[272,128]{1,0:T(8,128)(2,1)S(1)}, u32[]{:S(2)}, u32[]{:S(2)}) collective-permute-start(bf16[272,128]{1,0:T(8,128)(2,1)S(1)} %add_convert_fusion.1.refs_0_), channel_id=1, source_target_pairs={{8,0},{10,2},{12,4},{14,6},{16,8},{18,10},{20,12},{22,14},{24,16},... | collective-permute-start | bytes 208904 | tf_op jit(solution)/shard_map/ppermute | solution.py:76
  42.8 8.8 %collective-permute-start.10 = (bf16[256,256]{1,0:T(8,128)(2,1)S(1)}, bf16[256,256]{1,0:T(8,128)(2,1)S(1)}, u32[]{:S(2)}, u32[]{:S(2)}) collective-permute-start(bf16[256,256]{1,0:T(8,128)(2,1)S(1)} %get-tuple-element.37._.refs_2_.refs_0_), channel_id=1, source_target_pairs={{1,0},{0,1},{3,2},{2,3},{5,4},{4,5},{7,6},{6,7},{9,8},{8,9},{11,10... | collective-permute-start | bytes 393224 | tf_op jit(solution)/shard_map/ppermute | solution.py:76
  45.2 2.7 %collective-permute-start.5 = (bf16[64,128]{1,0:T(8,128)(2,1)S(1)}, bf16[64,128]{1,0:T(8,128)(2,1)S(1)}, u32[]{:S(2)}, u32[]{:S(2)}) collective-permute-start(bf16[64,128]{1,0:T(8,128)(2,1)S(1)} %get-tuple-element.56), channel_id=1, source_target_pairs={{0,2},{2,0},{4,6},{6,4},{8,10},{10,8},{12,14},{14,12},{16,18},{18,... | collective-permute-start | bytes 49160 | tf_op jit(solution)/shard_map/ppermute | solution.py:81
  45.3 2.6 %collective-permute-start.19 = (bf16[272,128]{1,0:T(8,128)(2,1)S(1)}, bf16[272,128]{1,0:T(8,128)(2,1)S(1)}, u32[]{:S(2)}, u32[]{:S(2)}) collective-permute-start(bf16[272,128]{1,0:T(8,128)(2,1)S(1)} %add_convert_fusion.1.refs_0_), channel_id=1, source_target_pairs={{0,2},{2,0},{4,6},{6,4},{8,10},{10,8},{12,14},{14,12},{16,18},{18,... | collective-permute-start | bytes 208904 | tf_op jit(solution)/shard_map/ppermute | solution.py:81
  45.8 4.3 %collective-permute-start.18 = (bf16[272,128]{1,0:T(8,128)(2,1)S(1)}, bf16[272,128]{1,0:T(8,128)(2,1)S(1)}, u32[]{:S(2)}, u32[]{:S(2)}) collective-permute-start(bf16[272,128]{1,0:T(8,128)(2,1)S(1)} %add_convert_fusion.1.refs_0_), channel_id=1, source_target_pairs={{0,4},{2,6},{4,0},{6,2},{8,12},{10,14},{12,8},{14,10},{16,20},{18,... | collective-permute-start | bytes 208904 | tf_op jit(solution)/shard_map/ppermute | solution.py:81
  47.3 6.5 %collective-permute-start.15 = (bf16[272,128]{1,0:T(8,128)(2,1)S(1)}, bf16[272,128]{1,0:T(8,128)(2,1)S(1)}, u32[]{:S(2)}, u32[]{:S(2)}) collective-permute-start(bf16[272,128]{1,0:T(8,128)(2,1)S(1)} %add_convert_fusion.1.refs_0_), channel_id=1, source_target_pairs={{16,0},{18,2},{20,4},{22,6},{24,8},{26,10},{28,12},{30,14},{0,16},... | collective-permute-start | bytes 208904 | tf_op jit(solution)/shard_map/ppermute | solution.py:76
  47.9 6.4 %collective-permute-start.21 = (bf16[272,128]{1,0:T(8,128)(2,1)S(1)}, bf16[272,128]{1,0:T(8,128)(2,1)S(1)}, u32[]{:S(2)}, u32[]{:S(2)}) collective-permute-start(bf16[272,128]{1,0:T(8,128)(2,1)S(1)} %collective-permute-done.12.refs_2_), channel_id=1, source_target_pairs={{0,2},{2,0},{4,6},{6,4},{8,10},{10,8},{12,14},{14,12},{16,18},{18,... | collective-permute-start | bytes 208904 | tf_op jit(solution)/shard_map/ppermute | solution.py:81
  47.9 6.9 %collective-permute-start.13 = (bf16[272,128]{1,0:T(8,128)(2,1)S(1)}, bf16[272,128]{1,0:T(8,128)(2,1)S(1)}, u32[]{:S(2)}, u32[]{:S(2)}) collective-permute-start(bf16[272,128]{1,0:T(8,128)(2,1)S(1)} %collective-permute-done.12.refs_2_), channel_id=1, source_target_pairs={{0,4},{2,6},{4,0},{6,2},{8,12},{10,14},{12,8},{14,10},{16,20},{18,... | collective-permute-start | bytes 208904 | tf_op jit(solution)/shard_map/ppermute | solution.py:81
  50.1 4.8 %collective-permute-start.9 = (bf16[272,128]{1,0:T(8,128)(2,1)S(1)}, bf16[272,128]{1,0:T(8,128)(2,1)S(1)}, u32[]{:S(2)}, u32[]{:S(2)}) collective-permute-start(bf16[272,128]{1,0:T(8,128)(2,1)S(1)} %collective-permute-done.8.refs_1_), channel_id=1, source_target_pairs={{0,4},{2,6},{4,0},{6,2},{8,12},{10,14},{12,8},{14,10},{16,20},{18,... | collective-permute-start | bytes 208904 | tf_op jit(solution)/shard_map/ppermute | solution.py:81
  51.6 2.6 %collective-permute-start.23 = (bf16[272,128]{1,0:T(8,128)(2,1)S(1)}, bf16[272,128]{1,0:T(8,128)(2,1)S(1)}, u32[]{:S(2)}, u32[]{:S(2)}) collective-permute-start(bf16[272,128]{1,0:T(8,128)(2,1)S(1)} %collective-permute-done.18.refs_4_), channel_id=1, source_target_pairs={{0,2},{2,0},{4,6},{6,4},{8,10},{10,8},{12,14},{14,12},{16,18},{18,... | collective-permute-start | bytes 208904 | tf_op jit(solution)/shard_map/ppermute | solution.py:81
  53.7 4.3 %collective-permute-start.16 = (bf16[272,128]{1,0:T(8,128)(2,1)S(1)}, bf16[272,128]{1,0:T(8,128)(2,1)S(1)}, u32[]{:S(2)}, u32[]{:S(2)}) collective-permute-start(bf16[272,128]{1,0:T(8,128)(2,1)S(1)} %collective-permute-done.15.refs_3_), channel_id=1, source_target_pairs={{0,4},{2,6},{4,0},{6,2},{8,12},{10,14},{12,8},{14,10},{16,20},{18,... | collective-permute-start | bytes 208904 | tf_op jit(solution)/shard_map/ppermute | solution.py:81
  54.3 8.2 %collective-permute-start.20 = (bf16[272,128]{1,0:T(8,128)(2,1)S(1)}, bf16[272,128]{1,0:T(8,128)(2,1)S(1)}, u32[]{:S(2)}, u32[]{:S(2)}) collective-permute-start(bf16[272,128]{1,0:T(8,128)(2,1)S(1)} %collective-permute-done.8.refs_1_), channel_id=1, source_target_pairs={{0,2},{2,0},{4,6},{6,4},{8,10},{10,8},{12,14},{14,12},{16,18},{18,... | collective-permute-start | bytes 208904 | tf_op jit(solution)/shard_map/ppermute | solution.py:81
  54.3 8.2 %collective-permute-start.22 = (bf16[272,128]{1,0:T(8,128)(2,1)S(1)}, bf16[272,128]{1,0:T(8,128)(2,1)S(1)}, u32[]{:S(2)}, u32[]{:S(2)}) collective-permute-start(bf16[272,128]{1,0:T(8,128)(2,1)S(1)} %collective-permute-done.15.refs_3_), channel_id=1, source_target_pairs={{0,2},{2,0},{4,6},{6,4},{8,10},{10,8},{12,14},{14,12},{16,18},{18,... | collective-permute-start | bytes 208904 | tf_op jit(solution)/shard_map/ppermute | solution.py:81
  54.8 8.5 %collective-permute-start.14 = (bf16[272,128]{1,0:T(8,128)(2,1)S(1)}, bf16[272,128]{1,0:T(8,128)(2,1)S(1)}, u32[]{:S(2)}, u32[]{:S(2)}) collective-permute-start(bf16[272,128]{1,0:T(8,128)(2,1)S(1)} %collective-permute-done.13.refs_11_), channel_id=1, source_target_pairs={{0,2},{2,0},{4,6},{6,4},{8,10},{10,8},{12,14},{14,12},{16,18},{18,... | collective-permute-start | bytes 208904 | tf_op jit(solution)/shard_map/ppermute | solution.py:81
  54.9 8.5 %collective-permute-start.11 = (bf16[272,128]{1,0:T(8,128)(2,1)S(1)}, bf16[272,128]{1,0:T(8,128)(2,1)S(1)}, u32[]{:S(2)}, u32[]{:S(2)}) collective-permute-start(bf16[272,128]{1,0:T(8,128)(2,1)S(1)} %collective-permute-done.9.refs_10_), channel_id=1, source_target_pairs={{0,2},{2,0},{4,6},{6,4},{8,10},{10,8},{12,14},{14,12},{16,18},{18,... | collective-permute-start | bytes 208904 | tf_op jit(solution)/shard_map/ppermute | solution.py:81
  58.0 5.3 %collective-permute-start.17 = (bf16[272,128]{1,0:T(8,128)(2,1)S(1)}, bf16[272,128]{1,0:T(8,128)(2,1)S(1)}, u32[]{:S(2)}, u32[]{:S(2)}) collective-permute-start(bf16[272,128]{1,0:T(8,128)(2,1)S(1)} %collective-permute-done.16.refs_2_), channel_id=1, source_target_pairs={{0,2},{2,0},{4,6},{6,4},{8,10},{10,8},{12,14},{14,12},{16,18},{18,... | collective-permute-start | bytes 208904 | tf_op jit(solution)/shard_map/ppermute | solution.py:81
  66.4 6.0 %collective-permute-start.24 = (bf16[256,256]{1,0:T(8,128)(2,1)S(1)}, bf16[256,256]{1,0:T(8,128)(2,1)S(1)}, u32[]{:S(2)}, u32[]{:S(2)}) collective-permute-start(bf16[256,256]{1,0:T(8,128)(2,1)S(1)} %get-tuple-element.43.vectors), channel_id=1, source_target_pairs={{1,0},{0,1},{3,2},{2,3},{5,4},{4,5},{7,6},{6,7},{9,8},{8,9},{11,10... | collective-permute-start | bytes 393224 | tf_op jit(solution)/shard_map/ppermute | solution.py:76
  76.0 18.4 %collective-permute-start.25 = (bf16[4,256,256]{2,1,0:T(8,128)(2,1)}, bf16[4,256,256]{2,1,0:T(8,128)(2,1)}, u32[]{:S(2)}, u32[]{:S(2)}) collective-permute-start(bf16[4,256,256]{2,1,0:T(8,128)(2,1)} %get-tuple-element.49), channel_id=1, source_target_pairs={{1,0},{0,1},{3,2},{2,3},{5,4},{4,5},{7,6},{6,7},{9,8},{8,9},{11,10... | collective-permute-start | bytes 1572872 | tf_op jit(solution)/shard_map/ppermute | solution.py:76
  77.6 5.0 %collective-permute-start.31 = (bf16[256,256]{1,0:T(8,128)(2,1)S(1)}, bf16[256,256]{1,0:T(8,128)(2,1)S(1)}, u32[]{:S(2)}, u32[]{:S(2)}) collective-permute-start(bf16[256,256]{1,0:T(8,128)(2,1)S(1)} %step_last.1.refs_0_), channel_id=1, source_target_pairs={{0,4},{2,6},{4,0},{6,2},{8,12},{10,14},{12,8},{14,10},{16,20},{18,... | collective-permute-start | bytes 393224 | tf_op jit(solution)/shard_map/ppermute | solution.py:81
  78.1 6.4 %collective-permute-start.26 = (bf16[256,256]{1,0:T(8,128)(2,1)S(1)}, bf16[256,256]{1,0:T(8,128)(2,1)S(1)}, u32[]{:S(2)}, u32[]{:S(2)}) collective-permute-start(bf16[256,256]{1,0:T(8,128)(2,1)S(1)} %step_last.1.refs_0_), channel_id=1, source_target_pairs={{0,2},{2,0},{4,6},{6,4},{8,10},{10,8},{12,14},{14,12},{16,18},{18,... | collective-permute-start | bytes 393224 | tf_op jit(solution)/shard_map/ppermute | solution.py:81
  78.1 15.2 %collective-permute-start.30 = (bf16[256,256]{1,0:T(8,128)(2,1)S(1)}, bf16[256,256]{1,0:T(8,128)(2,1)S(1)}, u32[]{:S(2)}, u32[]{:S(2)}) collective-permute-start(bf16[256,256]{1,0:T(8,128)(2,1)S(1)} %step_last.1.refs_0_), channel_id=1, source_target_pairs={{16,0},{18,2},{20,4},{22,6},{24,8},{26,10},{28,12},{30,14},{0,16},... | collective-permute-start | bytes 393224 | tf_op jit(solution)/shard_map/ppermute | solution.py:76
  78.1 15.2 %collective-permute-start.29 = (bf16[256,256]{1,0:T(8,128)(2,1)S(1)}, bf16[256,256]{1,0:T(8,128)(2,1)S(1)}, u32[]{:S(2)}, u32[]{:S(2)}) collective-permute-start(bf16[256,256]{1,0:T(8,128)(2,1)S(1)} %step_last.1.refs_0_), channel_id=1, source_target_pairs={{24,0},{26,2},{28,4},{30,6},{0,8},{2,10},{4,12},{6,14},{8,16},{10,... | collective-permute-start | bytes 393224 | tf_op jit(solution)/shard_map/ppermute | solution.py:76
  82.6 9.6 %collective-permute-start.28 = (bf16[256,256]{1,0:T(8,128)(2,1)S(1)}, bf16[256,256]{1,0:T(8,128)(2,1)S(1)}, u32[]{:S(2)}, u32[]{:S(2)}) collective-permute-start(bf16[256,256]{1,0:T(8,128)(2,1)S(1)} %step_last.1.refs_0_), channel_id=1, source_target_pairs={{8,0},{10,2},{12,4},{14,6},{16,8},{18,10},{20,12},{22,14},{24,16},... | collective-permute-start | bytes 393224 | tf_op jit(solution)/shard_map/ppermute | solution.py:76
  84.5 9.8 %collective-permute-start.35 = (bf16[256,256]{1,0:T(8,128)(2,1)S(1)}, bf16[256,256]{1,0:T(8,128)(2,1)S(1)}, u32[]{:S(2)}, u32[]{:S(2)}) collective-permute-start(bf16[256,256]{1,0:T(8,128)(2,1)S(1)} %collective-permute-done.31.refs_4_), channel_id=1, source_target_pairs={{0,2},{2,0},{4,6},{6,4},{8,10},{10,8},{12,14},{14,12},{16,18},{18,... | collective-permute-start | bytes 393224 | tf_op jit(solution)/shard_map/ppermute | solution.py:81
  92.2 6.3 %collective-permute-start.36 = (bf16[256,256]{1,0:T(8,128)(2,1)S(1)}, bf16[256,256]{1,0:T(8,128)(2,1)S(1)}, u32[]{:S(2)}, u32[]{:S(2)}) collective-permute-start(bf16[256,256]{1,0:T(8,128)(2,1)S(1)} %collective-permute-done.28.refs_1_), channel_id=1, source_target_pairs={{0,4},{2,6},{4,0},{6,2},{8,12},{10,14},{12,8},{14,10},{16,20},{18,... | collective-permute-start | bytes 393224 | tf_op jit(solution)/shard_map/ppermute | solution.py:81
  93.3 5.7 %collective-permute-start.32 = (bf16[256,256]{1,0:T(8,128)(2,1)S(1)}, bf16[256,256]{1,0:T(8,128)(2,1)S(1)}, u32[]{:S(2)}, u32[]{:S(2)}) collective-permute-start(bf16[256,256]{1,0:T(8,128)(2,1)S(1)} %collective-permute-done.28.refs_1_), channel_id=1, source_target_pairs={{0,2},{2,0},{4,6},{6,4},{8,10},{10,8},{12,14},{14,12},{16,18},{18,... | collective-permute-start | bytes 393224 | tf_op jit(solution)/shard_map/ppermute | solution.py:81
  93.3 8.0 %collective-permute-start.37 = (bf16[256,256]{1,0:T(8,128)(2,1)S(1)}, bf16[256,256]{1,0:T(8,128)(2,1)S(1)}, u32[]{:S(2)}, u32[]{:S(2)}) collective-permute-start(bf16[256,256]{1,0:T(8,128)(2,1)S(1)} %collective-permute-done.29.refs_2_), channel_id=1, source_target_pairs={{0,4},{2,6},{4,0},{6,2},{8,12},{10,14},{12,8},{14,10},{16,20},{18,... | collective-permute-start | bytes 393224 | tf_op jit(solution)/shard_map/ppermute | solution.py:81
  94.3 7.0 %collective-permute-start.33 = (bf16[256,256]{1,0:T(8,128)(2,1)S(1)}, bf16[256,256]{1,0:T(8,128)(2,1)S(1)}, u32[]{:S(2)}, u32[]{:S(2)}) collective-permute-start(bf16[256,256]{1,0:T(8,128)(2,1)S(1)} %collective-permute-done.29.refs_2_), channel_id=1, source_target_pairs={{0,2},{2,0},{4,6},{6,4},{8,10},{10,8},{12,14},{14,12},{16,18},{18,... | collective-permute-start | bytes 393224 | tf_op jit(solution)/shard_map/ppermute | solution.py:81
  94.4 9.0 %collective-permute-start.40 = (bf16[256,256]{1,0:T(8,128)(2,1)S(1)}, bf16[256,256]{1,0:T(8,128)(2,1)S(1)}, u32[]{:S(2)}, u32[]{:S(2)}) collective-permute-start(bf16[256,256]{1,0:T(8,128)(2,1)S(1)} %collective-permute-done.30.refs_3_), channel_id=1, source_target_pairs={{0,4},{2,6},{4,0},{6,2},{8,12},{10,14},{12,8},{14,10},{16,20},{18,... | collective-permute-start | bytes 393224 | tf_op jit(solution)/shard_map/ppermute | solution.py:81
  98.5 13.2 %collective-permute-start.27 = (bf16[4,256,128]{2,1,0:T(8,128)(2,1)S(1)}, bf16[4,256,128]{2,1,0:T(8,128)(2,1)S(1)}, u32[]{:S(2)}, u32[]{:S(2)}) collective-permute-start(bf16[4,256,128]{2,1,0:T(8,128)(2,1)S(1)} %fusion.1), channel_id=1, source_target_pairs={{1,0},{0,1},{3,2},{2,3},{5,4},{4,5},{7,6},{6,7},{9,8},{8,9},{11,10... | collective-permute-start | bytes 786440 | tf_op jit(solution)/shard_map/ppermute | solution.py:76
  99.0 4.4 %collective-permute-start.34 = (bf16[256,256]{1,0:T(8,128)(2,1)S(1)}, bf16[256,256]{1,0:T(8,128)(2,1)S(1)}, u32[]{:S(2)}, u32[]{:S(2)}) collective-permute-start(bf16[256,256]{1,0:T(8,128)(2,1)S(1)} %collective-permute-done.30.refs_3_), channel_id=1, source_target_pairs={{0,2},{2,0},{4,6},{6,4},{8,10},{10,8},{12,14},{14,12},{16,18},{18,... | collective-permute-start | bytes 393224 | tf_op jit(solution)/shard_map/ppermute | solution.py:81
  101.3 2.1 %collective-permute-start.38 = (bf16[256,256]{1,0:T(8,128)(2,1)S(1)}, bf16[256,256]{1,0:T(8,128)(2,1)S(1)}, u32[]{:S(2)}, u32[]{:S(2)}) collective-permute-start(bf16[256,256]{1,0:T(8,128)(2,1)S(1)} %collective-permute-done.36.refs_10_), channel_id=1, source_target_pairs={{0,2},{2,0},{4,6},{6,4},{8,10},{10,8},{12,14},{14,12},{16,18},{18,... | collective-permute-start | bytes 393224 | tf_op jit(solution)/shard_map/ppermute | solution.py:81
  101.3 2.1 %collective-permute-start.39 = (bf16[256,256]{1,0:T(8,128)(2,1)S(1)}, bf16[256,256]{1,0:T(8,128)(2,1)S(1)}, u32[]{:S(2)}, u32[]{:S(2)}) collective-permute-start(bf16[256,256]{1,0:T(8,128)(2,1)S(1)} %collective-permute-done.37.refs_11_), channel_id=1, source_target_pairs={{0,2},{2,0},{4,6},{6,4},{8,10},{10,8},{12,14},{14,12},{16,18},{18,... | collective-permute-start | bytes 393224 | tf_op jit(solution)/shard_map/ppermute | solution.py:81
  103.4 1.3 %collective-permute-start.41 = (bf16[256,256]{1,0:T(8,128)(2,1)S(1)}, bf16[256,256]{1,0:T(8,128)(2,1)S(1)}, u32[]{:S(2)}, u32[]{:S(2)}) collective-permute-start(bf16[256,256]{1,0:T(8,128)(2,1)S(1)} %collective-permute-done.40.refs_14_), channel_id=1, source_target_pairs={{0,2},{2,0},{4,6},{6,4},{8,10},{10,8},{12,14},{14,12},{16,18},{18,... | collective-permute-start | bytes 393224 | tf_op jit(solution)/shard_map/ppermute | solution.py:81

commit v4 on v3

--- a/solution.py
+++ b/solution.py
@@ -98,19 +98,18 @@
     return lax.optimization_barrier((value, *others))[0]
 
 
-def pair_blocks(value, meanwhile=None):
+def pair_blocks(value, meanwhile=None, first=()):
     early, late = pair_moves()
     far_moves = [move for move in early if move[0] and not move[1] and not move[2]]
     held = {(0, 0, 0): value, (0, 1, 0): flipped(value, "pair", 2)}
     for move in far_moves:
         ready = value
         if meanwhile is None and move == far_moves[-1]:
-            ready = after(value, *[held[other] for other in far_moves[:-1]])
+            ready = after(value, *[held[other] for other in far_moves[:-1]], *first)
         held[move] = from_ahead(ready, "pair", 4 * move[0])
     done = None
     if meanwhile is not None:
-        held[0, 0, 1] = flipped(value, "pair", 1)
-        done = meanwhile(held[0, 0, 1])
+        done = meanwhile(held[0, 1, 0])
         for move in far_moves:
             held[move] = after(held[move], done)
     for move in early + late:
@@ -127,17 +126,6 @@
     me = lax.axis_index("pair")
     count = lax.axis_size("pair")
     return jnp.stack([((me + 4 * far) % count) ^ (2 * side + core) for far, side, core in early + late])
-
-
-def small_pair_blocks(value, names):
-    count = lax.axis_size("pair")
-    steps = range(1, count // 4)
-    value = jnp.concatenate([value] + [from_ahead(value, "pair", 4 * d) for d in steps])
-    me = lax.axis_index("pair")
-    index = jnp.stack([(me + 4 * d) % count for d in range(count // 4)])
-    value = jnp.concatenate([value] + [flipped(value, "pair", bits) for bits in (2, 1, 3)])
-    index = jnp.concatenate([index ^ bits for bits in (0, 2, 1, 3)])
-    return value, names[index].reshape(-1)
 
 
 def plane_sum(value):
@@ -266,53 +254,40 @@
     return jnp.where((col >= names * each) & (col < (names + 1) * each), 1.0, 0.0).astype(BF16)
 
 
-def mix_kernel(each, points, order, table, names, *refs):
-    *blocks, mixer_at, mixed, wide, same, mixer, sems = refs
-    count, rows, cols = mixer.shape
-    stores = []
-    same[...] = same_column(rows, cols, each)
-    chunks = wide.shape[0] // table.shape[1]
+def gathered_weights(order, tables, names, fine, held, out):
+    rows = names.shape[0] // len(tables)
+    table = jnp.concatenate([ref[ref.shape[0] - rows :, :] for ref in tables], axis=0)
+    chunks = out.shape[0] // table.shape[1]
     row = lax.broadcasted_iota(jnp.int32, names.shape, 0)
+    col = lax.broadcasted_iota(jnp.int32, (names.shape[0], fine), 1)
     for p in range(chunks):
         here = jnp.where(row % chunks == p, names[...], -1)
+        place = jnp.where(col == here, 1.0, 0.0).astype(BF16)
         at = slice(p * table.shape[1], (p + 1) * table.shape[1])
-        wide[at] = dot(table[...], widening(here, cols, each), TN)
-    for c in range(count):
-        at = pl.multiple_of(order[c] * points, points)
-        part = spread(wide[pl.ds(at, points), :], each, same[...])
-        mixer[c] = part
-        total, at = 0.0, 0
-        for block in blocks:
-            depth = block.shape[0]
-            total = total + dot(part[:, at : at + depth], block[...])
-            at += depth
-        mixed[c] = total.astype(BF16)
-        if c % 2 == 1:
-            store(mixer, mixer_at, pl.ds(c - 1, 2), sems.at[c // 2], stores)
-    finish(stores)
-
-
-def mix_all(order, table, names, blocks, points, each):
-    count = order.shape[0]
-    cols = sum(block.shape[0] for block in blocks)
-    width = blocks[0].shape[1]
-    mixer = (count, points * each, cols)
-    mixed = (count, points * each, width)
-    return pl.pallas_call(
-        functools.partial(mix_kernel, each, points),
-        in_specs=[SMEM, VMEM, VMEM] + [VMEM] * len(blocks),
-        out_specs=[HBM, VMEM],
-        out_shape=[far_shaped(mixer), shaped(mixed)],
-        scratch_shapes=[
-            pltpu.VMEM((count * points, cols), F32),
-            pltpu.VMEM(mixer[1:], F32),
-            pltpu.VMEM(mixer, BF16),
-            pltpu.SemaphoreType.DMA((count // 2,)),
-        ],
-        compiler_params=params(16),
-        cost_estimate=cost(4 * count * points * cols * each * width, 8 * MIB),
-        name="mix_all",
-    )(order, table, names, *blocks)
+        held[at] = dot(table, place, TN)
+    points = out.shape[0] // order.shape[0]
+    for c in range(order.shape[0]):
+        at = pl.ds(pl.multiple_of(order[c] * points, points), points)
+        out[c * points : (c + 1) * points] = held[at, :].astype(BF16)
+
+
+def mix_vectors(weights, blocks, each, mixed):
+    points = blocks[0].shape[0] // each
+    count, _, width = mixed.shape
+    for n in range(each):
+        at = slice(n * points, (n + 1) * points)
+        vectors = jnp.concatenate([block[at] for block in blocks], axis=0)
+        value = dot(weights[...], vectors).astype(BF16)
+        mixed[:, at, :] = value.reshape(count, points, width)
+
+
+def through(mixed, kernel_refs):
+    total, c = 0.0, 0
+    for ref in kernel_refs:
+        for k in range(ref.shape[0]):
+            total = total + dot(mixed[c], ref[k])
+            c += 1
+    return total
 
 
 def row_kernel(each, parts, order, table, vectors_at, *refs):
@@ -365,12 +340,24 @@
     )(order, mix.reshape(count * rows, points), far(vectors), *kernels, later)
 
 
-def start_kernel(each, index, pick, transform_at, trial_at, live, table, *refs):
-    start_at, mine, my_trial, table_out, transform, trial, start, held, rows, sems = refs
+def split_rows(rows, width):
+    return pltpu.VMEM((width // 128, rows, 128), F32)
+
+
+def put(ref, value, at=slice(None)):
+    for h in range(ref.shape[0]):
+        ref[h, at, :] = value[:, h * 128 : (h + 1) * 128]
+
+
+def get(ref, at=slice(None)):
+    return jnp.concatenate([ref[h, at, :] for h in range(ref.shape[0])], axis=1)
+
+
+def start_kernel(each, index, pick, transform_at, trial_at, live, *refs):
+    start_at, mine, my_trial, transform, trial, start, held, rows, sems = refs
     pieces = 4
     load_trial = loads(trial_at, trial, sems, pieces)
     load_transform = loads(transform_at, transform, sems, pieces, first=pieces)
-    table_out[...] = table[...]
     points, width, _ = transform.shape
     group = points // pieces
     at_mine = pl.ds(pl.multiple_of(index[0] * each, each), each)
@@ -389,41 +376,40 @@
                 rows[0] = turned_block
                 rows[1] = turned
                 my_trial[here] = rows[0, at_mine, :]
-                held[here] = rows[1, at_mine, :]
+                put(held, rows[1, at_mine, :], pl.ds(k, each, stride=points))
             else:
                 my_trial[here] = dot(pick[...], block, NT)
-                held[here] = dot(pick[...], start[k])
+                put(held, dot(pick[...], start[k]), pl.ds(k, each, stride=points))
         store(start, start_at, pl.ds(p * group, group), sems.at[2 * pieces + p], stores)
-    mine[...] = held[...].astype(BF16)
+    mine[...] = get(held).astype(BF16)
     finish(stores)
 
 
-def start_call(index, pick, transform, trial, live, table):
+def start_call(index, pick, transform, trial, live):
     each, columns = pick.shape
     points, width, _ = transform.shape
     mine = (points * each, width)
     return pl.pallas_call(
         functools.partial(start_kernel, each),
-        in_specs=[SMEM, VMEM, HBM, HBM, VMEM, VMEM],
-        out_specs=[HBM] + [VMEM] * 3,
+        in_specs=[SMEM, VMEM, HBM, HBM, VMEM],
+        out_specs=[HBM] + [VMEM] * 2,
         out_shape=[
             far_shaped((points, columns, width)),
             shaped(mine),
             shaped(mine, F32),
-            shaped(table.shape),
         ],
         scratch_shapes=[
             pltpu.VMEM(transform.shape, BF16),
             pltpu.VMEM(trial.shape, BF16),
             pltpu.VMEM((points, columns, width), BF16),
-            pltpu.VMEM(mine, F32),
+            split_rows(*mine),
             pltpu.VMEM((2, columns, width), F32),
             pltpu.SemaphoreType.DMA((12,)),
         ],
         compiler_params=params(16),
         cost_estimate=cost(4 * points * columns * width * width, 8 * MIB),
         name="start_call",
-    )(index, pick, far(transform), far(trial), live, table)
+    )(index, pick, far(transform), far(trial), live)
 
 
 def fold_kernel(scale, each, place, transform_at, live, energy, my_trial, *refs):
@@ -471,161 +457,137 @@
     )(place, far(transform), live, energy, my_trial)
 
 
-def by_point(each, points, body, store):
-    step = max(each, 8)
-    group = step // each
-    owner = lax.broadcasted_iota(jnp.int32, (step, 1), 0) // each
-    for b in range(points // group):
-        here = slice(b * step, (b + 1) * step)
-        if group == 1:
-            value = body(here, b)
-        else:
-            value = 0.0
-            for p in range(group):
-                value = value + jnp.where(owner == p, body(here, b * group + p), 0.0)
-        store[here] = value
-
-
-def through_kernel(first, count, each, last, mixed, *refs):
+def unpack_kernel(*refs):
+    *packed, out = refs
+    for c, ref in enumerate(packed):
+        out[c] = unpack(ref[...])
+
+
+def unpack_call(packed, width):
+    return pl.pallas_call(
+        unpack_kernel,
+        in_specs=[VMEM] * len(packed),
+        out_specs=VMEM,
+        out_shape=shaped((len(packed), width, width)),
+        compiler_params=params(16),
+        cost_estimate=cost(1, 1),
+        name="unpack_call",
+    )(*packed)
+
+
+def first_kernel(each, count, planes, order, names, *refs):
+    blocks, refs = refs[:planes], refs[planes:]
     packed, refs = refs[:count], refs[count:]
-    if last:
-        before, folded_at, shift, kernels, total, again, folded, held, sem = refs
-        load_folded = pltpu.make_async_copy(folded_at, folded, sem)
-        load_folded.start()
-    else:
-        kernels, total = refs
-    value = before[...] if last else 0.0
-    for c in range(count):
-        kernels[c] = unpack(packed[c][...])
-        value = value + dot(mixed[first + c], kernels[c])
-    total[...] = value
-    if last:
-        load_folded.wait()
-
-        def body(here, k):
-            return dot(total[here].astype(BF16), folded[k]) + shift[here]
-
-        by_point(each, folded.shape[0], body, held)
-        again[...] = held[...].astype(BF16)
-
-
-def through(mixed, first, packed, each, before=None, folded=None, shift=None):
-    _, rows, width = mixed.shape
+    early, folded_at, shift, late, total, again, weights, *refs = refs
+    mixed, folded, held, wide, sems = refs
+    pieces = sems.shape[0]
+    copies = loads(folded_at, folded, sems, pieces)
+    gathered_weights(order, packed, names, weights.shape[1], wide, weights)
+    mix_vectors(weights, blocks, each, mixed)
+    for c in range(late.shape[0]):
+        late[c] = unpack(packed[early.shape[0] + c][...])
+    put(total, through(mixed, [early, late]))
+    points = folded.shape[0]
+    for k in range(points):
+        if k % (points // pieces) == 0:
+            copies[k // (points // pieces)].wait()
+        rows = pl.ds(k, each, stride=points)
+        value = dot(get(total, rows).astype(BF16), folded[k])
+        put(held, value + shift[k * each : (k + 1) * each], rows)
+    again[...] = get(held).astype(BF16)
+
+
+def first_call(order, names, blocks, packed, early, folded, shift, each):
     count = len(packed)
-    last = before is not None
-    out_shape = [shaped((count, width, width)), shaped((rows, width), F32)]
-    scratch = []
-    operands = [mixed, *packed]
-    in_specs = [VMEM] * (1 + count)
-    if last:
-        out_shape.append(shaped((rows, width)))
-        scratch = [
+    rows, width = blocks[0].shape
+    points = rows // each
+    fine = points * len(blocks)
+    operands = [names, *blocks, *packed, early, far(folded), shift]
+    return pl.pallas_call(
+        functools.partial(first_kernel, each, count, len(blocks)),
+        in_specs=[SMEM] + [VMEM] * (len(operands) - 2) + [HBM, VMEM],
+        out_specs=[VMEM] * 4,
+        out_shape=[
+            shaped((count - early.shape[0], width, width)),
+            shaped((width // 128, rows, 128), F32),
+            shaped((rows, width)),
+            shaped((count * points, fine)),
+        ],
+        scratch_shapes=[
+            pltpu.VMEM((count, rows, width), BF16),
             pltpu.VMEM(folded.shape, BF16),
-            pltpu.VMEM((rows, width), F32),
-            pltpu.SemaphoreType.DMA,
-        ]
-        operands += [before, far(folded), shift]
-        in_specs += [VMEM, HBM, VMEM]
-    return pl.pallas_call(
-        functools.partial(through_kernel, first, count, each, last),
-        in_specs=in_specs,
-        out_specs=[VMEM] * len(out_shape),
-        out_shape=out_shape,
-        scratch_shapes=scratch,
-        compiler_params=params(24),
-        cost_estimate=cost(8 * count * rows * width * width, 8 * MIB),
-        name="through_last" if last else "through_early",
-    )(*operands)
-
-
-def mix_and_through(mixer_at, mixer, vectors, at, kernel_refs, sems, next_load):
-    depth = vectors.shape[0]
+            split_rows(rows, width),
+            pltpu.VMEM((count * points, fine), F32),
+            pltpu.SemaphoreType.DMA((8,)),
+        ],
+        compiler_params=params(20),
+        cost_estimate=cost(1, 1),
+        name="first_call",
+    )(order, *operands)
+
+
+def energy_kernel(scale, each, transform_at, total, live, energy, trial, out, transform, sems):
     pieces = sems.shape[0]
-    columns = mixer_at.at[:, :, pl.ds(at, depth)]
-    copies = loads(columns, mixer, sems, pieces)
-    next_load.start()
-    group = mixer.shape[0] // pieces
-    value, c = 0.0, 0
-    for ref in kernel_refs:
-        for k in range(ref.shape[0]):
-            if c % group == 0:
-                copies[c // group].wait()
-            mixed = dot(mixer[c], vectors[...]).astype(BF16)
-            value = value + dot(mixed, ref[k])
-            c += 1
-    return value
-
-
-def step_part_kernel(scale, each, parts, mixer_at, vectors, *refs):
-    kernels, refs = refs[:parts], refs[parts:]
-    transform_at, total, live, energy, trial, out, shift, mixer, transform, sems, sem = refs
-    load = pltpu.make_async_copy(transform_at, transform, sem)
-    out[...] = mix_and_through(mixer_at, mixer, vectors, 0, kernels, sems, load)
-    load.wait()
-
-    def body(here, k):
-        turned = dot(total[here].astype(BF16), transform[k])
+    copies = loads(transform_at, transform, sems, pieces)
+    points = transform.shape[0]
+    for k in range(points):
+        if k % (points // pieces) == 0:
+            copies[k // (points // pieces)].wait()
+        here = slice(k * each, (k + 1) * each)
+        turned = dot(get(total, pl.ds(k, each, stride=points)).astype(BF16), transform[k])
         row = energy[k : k + 1, :]
-        return (turned * (scale * live[k : k + 1, :]) + row * trial[here]) * row
-
-    by_point(each, transform.shape[0], body, shift)
-
-
-def step_part(mixer, vectors, kernels, transform, total, live, energy, my_trial, scale, each):
-    rows, width = total.shape
-    operands = [far(mixer), vectors, *kernels, far(transform), total, live, energy, my_trial]
-    return pl.pallas_call(
-        functools.partial(step_part_kernel, scale, each, len(kernels)),
-        in_specs=[HBM] + [VMEM] * (1 + len(kernels)) + [HBM] + [VMEM] * 4,
-        out_specs=[VMEM, VMEM],
-        out_shape=[shaped((rows, width), F32)] * 2,
-        scratch_shapes=[
-            pltpu.VMEM((mixer.shape[0], rows, vectors.shape[0]), BF16),
-            pltpu.VMEM(transform.shape, BF16),
-            pltpu.SemaphoreType.DMA((4,)),
-            pltpu.SemaphoreType.DMA,
-        ],
-        compiler_params=params(24),
+        out[here] = (turned * (scale * live[k : k + 1, :]) + row * trial[here]) * row
+
+
+def energy_call(transform, total, live, energy, my_trial, scale, each):
+    return pl.pallas_call(
+        functools.partial(energy_kernel, scale, each),
+        in_specs=[HBM] + [VMEM] * 4,
+        out_specs=VMEM,
+        out_shape=shaped(my_trial.shape, F32),
+        scratch_shapes=[pltpu.VMEM(transform.shape, BF16), pltpu.SemaphoreType.DMA((4,))],
+        compiler_params=params(16),
         cost_estimate=cost(1, 1),
-        name="step_part",
-    )(*operands)
-
-
-def step_last_kernel(scale, at, each, parts, mixer_at, vectors, *refs):
-    kernels, refs = refs[:parts], refs[parts:]
-    before, transform_at, live, shift, out, total, held, mixer, transform, sems, sem = refs
-    load = pltpu.make_async_copy(transform_at, transform, sem)
-    value = mix_and_through(mixer_at, mixer, vectors, at, kernels, sems, load)
-    total[...] = before[...] + value
-    load.wait()
-
-    def body(here, k):
-        turned = dot(total[here].astype(BF16), transform[k])
-        return turned * (scale * live[k : k + 1, :]) + shift[here]
-
-    by_point(each, transform.shape[0], body, held)
+        name="energy_call",
+    )(far(transform), total, live, energy, my_trial)
+
+
+def second_kernel(scale, each, planes, weights, *refs):
+    blocks, refs = refs[:planes], refs[planes:]
+    early, late, transform_at, live, shift, out, mixed, transform, total, held, sems = refs
+    pieces = sems.shape[0]
+    copies = loads(transform_at, transform, sems, pieces)
+    mix_vectors(weights, blocks, each, mixed)
+    put(total, through(mixed, [early, late]))
+    points = transform.shape[0]
+    for k in range(points):
+        if k % (points // pieces) == 0:
+            copies[k // (points // pieces)].wait()
+        here = slice(k * each, (k + 1) * each)
+        turned = dot(get(total, pl.ds(k, each, stride=points)).astype(BF16), transform[k])
+        held[here] = turned * (scale * live[k : k + 1, :]) + shift[here]
     out[...] = held[...].astype(BF16)
 
 
-def step_last(mixer, vectors, at, kernels, before, transform, live, shift, scale, each):
-    rows, width = before.shape
-    operands = [far(mixer), vectors, *kernels, before, far(transform), live, shift]
-    return pl.pallas_call(
-        functools.partial(step_last_kernel, scale, at, each, len(kernels)),
-        in_specs=[HBM] + [VMEM] * (2 + len(kernels)) + [HBM, VMEM, VMEM],
+def second_call(weights, blocks, kernels, transform, live, shift, scale, each):
+    rows, width = shift.shape
+    count = sum(kernel.shape[0] for kernel in kernels)
+    operands = [weights, *blocks, *kernels, far(transform), live, shift]
+    return pl.pallas_call(
+        functools.partial(second_kernel, scale, each, len(blocks)),
+        in_specs=[VMEM] * (len(operands) - 3) + [HBM, VMEM, VMEM],
         out_specs=VMEM,
         out_shape=shaped((rows, width)),
         scratch_shapes=[
+            pltpu.VMEM((count, rows, width), BF16),
+            pltpu.VMEM(transform.shape, BF16),
+            split_rows(rows, width),
             pltpu.VMEM((rows, width), F32),
-            pltpu.VMEM((rows, width), F32),
-            pltpu.VMEM((mixer.shape[0], rows, vectors.shape[0]), BF16),
-            pltpu.VMEM(transform.shape, BF16),
-            pltpu.SemaphoreType.DMA((4,)),
-            pltpu.SemaphoreType.DMA,
-        ],
-        compiler_params=params(24),
+            pltpu.SemaphoreType.DMA((8,)),
+        ],
+        compiler_params=params(20),
         cost_estimate=cost(1, 1),
-        name="step_last",
+        name="second_call",
     )(*operands)
 
 
@@ -668,7 +630,7 @@
     pieces = 8
     return pl.pallas_call(
         functools.partial(last_kernel, each),
-        in_specs=[SMEM, HBM] + [ANY] * len(blocks),
+        in_specs=[SMEM, HBM] + [HBM] * len(blocks),
         out_specs=HBM,
         out_shape=shaped((total, columns), F32),
         scratch_shapes=[
@@ -682,7 +644,7 @@
         compiler_params=params(24),
         cost_estimate=cost(2 * total * columns * width, 8 * MIB),
         name="last_call",
-    )(order, far(trial), *blocks)
+    )(order, far(trial), *[far(block) for block in blocks])
 
 
 def shards(screened, density, transform, energy, trial, coarse_index, interp_weight, bands):
@@ -713,18 +675,9 @@
         jnp.arange(columns)[None, :] == row_index * each + jnp.arange(each)[:, None]
     ).astype(BF16)
 
-    table = dense.reshape(row_points, -1)
-    chunks = table.shape[1] // 128
-    start, my_start, my_trial, table = start_call(
-        row_index[None].astype(jnp.int32), pick, transform, trial, my_live,
-        table.reshape(row_points * chunks, 128),
+    start, my_start, my_trial = start_call(
+        row_index[None].astype(jnp.int32), pick, transform, trial, my_live
     )
-
-    points_of = jnp.arange(fine_points, dtype=jnp.int32).reshape(pair_count, row_points)
-    points_of = (points_of - col_index * col_points) % fine_points
-    points_of = jnp.repeat(points_of, chunks, axis=1)
-    table, rows_from = small_pair_blocks(after(table, density_blocks[-1]), points_of)
-    rows_from = rows_from[:, None]
 
     planes = jnp.stack([(col_index + d) % plane_count for d in range(plane_count)])
     planes = planes.astype(jnp.int32)
@@ -737,30 +690,25 @@
     packed = coarse_block(planes[1:], left, own, density_blocks[1:], (shift, my_start))
     packed = plane_sum(packed).astype(BF16)
 
+    table = dense.reshape(row_points, -1)
+    chunks = table.shape[1] // packed.shape[1]
+    table = table.reshape(row_points * chunks, packed.shape[1])
     start_blocks = plane_blocks(after(my_start, packed))
-    blocks, _ = pair_blocks(packed)
-    side_block = blocks[pair_moves()[0].index((1, 1, 0))]
-    mixer, mixed = mix_all(
-        order, after(table, side_block), rows_from, start_blocks, col_points, each
+    blocks, _ = pair_blocks(jnp.concatenate([packed, table], axis=0), first=start_blocks[1:])
+    names = jnp.arange(fine_points, dtype=jnp.int32).reshape(pair_count, row_points)[order]
+    names = (jnp.repeat(names, chunks, axis=1) - col_index * col_points) % fine_points
+    names = names.reshape(-1, 1)
+
+    early = unpack_call(blocks[: len(pair_moves()[0])], transitions)
+    late, total, again, weights = first_call(
+        order, names, start_blocks, blocks, early, folded, shift, each
     )
-    early = len(pair_moves()[0])
-    kernels_early, total = through(mixed, 0, blocks[:early], each)
-    kernels_late, total, again = through(mixed, early, blocks[early:], each, total, folded, shift)
-    kernels = [kernels_early, kernels_late]
+    kernels = [early, late]
     again_blocks = plane_blocks(again)
-
-    near_count = 1
-    while near_count * again.shape[0] % 128 != 0:
-        near_count += 1
-    first_again = jnp.concatenate(again_blocks[:near_count], axis=0)
-    other_again = jnp.concatenate(again_blocks[near_count:], axis=0)
-    back, shift = step_part(
-        mixer, first_again, kernels, transform, total, my_live, energies, my_trial,
-        norm_scale, each,
-    )
-    second = step_last(
-        mixer, other_again, first_again.shape[0], kernels, back, transform, my_live, shift,
-        norm_scale, each,
+    energy_part = energy_call(transform, total, my_live, energies, my_trial, norm_scale, each)
+
+    second = second_call(
+        weights, again_blocks, kernels, transform, my_live, energy_part, norm_scale, each
     )
     by_point_first = jnp.swapaxes(dense, 0, 1)
     second_blocks, row_back = pair_blocks(

time: 113 us -> 104 us (0.920)
  Pallas kernels: 50.3 us -> 46.3 us
  starting transfers between devices: 36.8 us -> 32.8 us
  other arithmetic: 3.14 us -> 1.71 us
    ppermute x15 -> x12, starting transfers between devices: 25 us -> 20 us  [from_ahead(): lax.ppermute(value, axis, [((s + step) % count, s) for s in range(count)])]
    ppermute x27 -> x24, waiting for transfers between devices: 12.2 us -> 7.31 us  [flipped(): return lax.ppermute(value, axis, [(s, s ^ bit) for s in range(count)])]
    ppermute x15 -> x12, waiting for transfers between devices: 6.09 us -> 10.7 us  [from_ahead(): lax.ppermute(value, axis, [((s + step) % count, s) for s in range(count)])]
    pallas_call x5 -> x4, Pallas kernels: 15.5 us -> 13.1 us  [the longest x1 5.61 us: first_call(): pl.pallas_call(functools.partial(first_kernel, each, count, len(blocks)),...]
    pallas_call x1, Pallas kernels: 6.94 us -> 5.19 us  [last_call(): pl.pallas_call(functools.partial(last_kernel, each), in_specs=[SMEM, HBM]...]
    ppermute x27 -> x24, starting transfers between devices: 11.8 us -> 12.7 us  [flipped(): return lax.ppermute(value, axis, [(s, s ^ bit) for s in range(count)])]
  transfers between devices with their start and end apart: 42 -> 36, of which waited for: 12 -> 17; matrix products, arithmetic and copies ran while one was open for 5% -> 3% of each run, Pallas kernels for 39% -> 33%
where the time goes in v4:
time: 104 us
  Pallas kernels  46.3 us (45%)
  starting transfers between devices  32.8 us (32%)
  waiting for transfers between devices  18 us (17%)
  local copies, waits for them, and re-layouts  2.12 us (2%)
  other arithmetic  1.71 us (2%)
  matrix products  1.46 us (1%)
  between operations  1.15 us (1%)
    ppermute x12, starting transfers between devices, from_ahead(): lax.ppermute(value, axis, [((s + step) % count, s) for s in range(count)])  20 us
    ppermute x24, starting transfers between devices, flipped(): return lax.ppermute(value, axis, [(s, s ^ bit) for s in range(count)])  12.7 us
    ppermute x12, waiting for transfers between devices, from_ahead(): lax.ppermute(value, axis, [((s + step) % count, s) for s in range(count)])  10.7 us
    pallas_call x1, Pallas kernels, left_product(): pl.pallas_call(left_kernel, in_specs=[SMEM, HBM, VMEM, ANY], out_specs=[H...  8.43 us
    ppermute x24, waiting for transfers between devices, flipped(): return lax.ppermute(value, axis, [(s, s ^ bit) for s in range(count)])  7.31 us
    pallas_call x1, Pallas kernels, row_call(): pl.pallas_call(functools.partial(row_kernel, each, len(kernels)), in_spec...  7.24 us
    pallas_call x1, Pallas kernels, first_call(): pl.pallas_call(functools.partial(first_kernel, each, count, len(blocks)),...  5.61 us
    pallas_call x1, Pallas kernels, fold_call(): pl.pallas_call(functools.partial(fold_kernel, scale, each), in_specs=[SME...  5.39 us
  transfers between devices with their start and end apart: 36, of which 17 were waited for; matrix products, arithmetic and copies ran while one was open for 3% of the time, Pallas kernels for 33%

profile of v4, /device:TPU:0, one launch (start us, length us, event | category | flops | bytes accessed | tf_op | source)
XLA Modules:
  0.0 103.5 jit_solution(7551274002522103315)
XLA Ops:
  0.6 3.0 %collective-permute-start = (bf16[2048,256]{1,0:T(8,128)(2,1)}, bf16[2048,256]{1,0:T(8,128)(2,1)S(1)}, u32[]{:S(2)}, u32[]{:S(2)}) collective-permute-start(bf16[2048,256]{1,0:T(8,128)(2,1)} %bitcast.48), channel_id=1, source_target_pairs={{1,0},{0,1},{3,2},{2,3},{5,4},{4,5},{7,6},{6,7},{9,8},{8,9},{11,10... | collective-permute-start | bytes 3145736 | tf_op jit(solution)/shard_map/ppermute | solution.py:76
  3.7 0.7 compare_convert_fusion
  4.5 5.2 %start_call.1 = (bf16[32,128,256]{2,1,0:T(8,128)(2,1)}, bf16[256,256]{1,0:T(8,128)(2,1)S(1)}, f32[256,256]{1,0:T(8,128)S(1)}) custom-call(s32[1]{0:T(128)} %bitcast.1.index, bf16[8,128]{1,0:T(8,128)(2,1)S(1)} %fusion.5.pick, bf16[32,256,256]{2,1,0:T(8,128)(2,1)} %refs_4_.1, bf16[8192,128]{1,0:T(8,128)(2,1)} %trial_at.3, ...), custom_call_target="tpu_custom_call" | custom-call | flops 1 | bytes 1 | tf_op jit(solution)/shard_map/start_call/pallas_call | solution.py:392
  9.7 8.4 %left_product.1 = (bf16[256,4096]{1,0:T(8,128)(2,1)}, f32[256,256]{1,0:T(8,128)S(1)}) custom-call(s32[1]{0:T(128)} %bitcast.36.plane, bf16[1,2048,4096]{2,1,0:T(8,128)(2,1)} %screened_at.1, bf16[2048,256]{1,0:T(8,128)(2,1)S(1)} %bitcast.49, bf16[256,256]{1,0:T(8,128)(2,1)S(1)} %get-tuple-element.26._.refs_2_.refs_0_), custom_call_target="tpu_custom_call" | custom-call | flops 1 | bytes 1 | tf_op jit(solution)/shard_map/left_product/pallas_call | solution.py:191
  18.2 5.4 %fold_call.1 = (bf16[32,256,256]{2,1,0:T(8,128)(2,1)}, f32[256,256]{1,0:T(8,128)S(1)}, bf16[4,256,256]{2,1,0:T(8,128)(2,1)}) custom-call(s32[1]{0:T(128)} %bitcast.place, bf16[32,256,256]{2,1,0:T(8,128)(2,1)} %refs_4_.1, f32[32,256]{1,0:T(8,128)S(1)} %constant_dynamic-slice_fusion.1.live.refs_5_, f32[32,256]{1,0:T(8,128)S(1)} %reshape.711.energy, ...), custom_call_target="tpu_custom_call" | custom-call | flops 1 | bytes 1 | tf_op jit(solution)/shard_map/fold_call/pallas_call | solution.py:440
  23.8 3.2 %collective-permute-done.refs_0_ = bf16[2048,256]{1,0:T(8,128)(2,1)S(1)} collective-permute-done((bf16[2048,256]{1,0:T(8,128)(2,1)}, bf16[2048,256]{1,0:T(8,128)(2,1)S(1)}, u32[]{:S(2)}, u32[]{:S(2)}) %collective-permute-start) | collective-permute-done | bytes 1048608 | tf_op jit(solution)/shard_map/ppermute | solution.py:76
  27.0 1.7 %coarse_block.1 = bf16[272,128]{1,0:T(8,128)(2,1)S(1)} custom-call(s32[1]{0:T(128)} %bitcast.35.planes, bf16[256,4096]{1,0:T(8,128)(2,1)} %get-tuple-element.23.left_at, f32[256,256]{1,0:T(8,128)S(1)} %get-tuple-element.24.total, bf16[2048,256]{1,0:T(8,128)(2,1)S(1)} %collective-permute-done.refs_0_, f32[256,256]{1,0:T(8,128)S(1)} %get-tuple-element.25.refs_1_.refs_20_, ...), custom_call_target="tpu_custom_call" | custom-call | flops 1 | bytes 1 | tf_op jit(solution)/shard_map/coarse_block/pallas_call | solution.py:226
  28.8 1.8 %collective-permute-start.1 = (bf16[272,128]{1,0:T(8,128)(2,1)S(1)}, bf16[272,128]{1,0:T(8,128)(2,1)S(1)}, u32[]{:S(2)}, u32[]{:S(2)}) collective-permute-start(bf16[272,128]{1,0:T(8,128)(2,1)S(1)} %coarse_block.1), channel_id=1, source_target_pairs={{1,0},{0,1},{3,2},{2,3},{5,4},{4,5},{7,6},{6,7},{9,8},{8,9},{11,10... | collective-permute-start | bytes 208904 | tf_op jit(solution)/shard_map/ppermute | solution.py:76
  30.7 2.5 %collective-permute-done.1 = bf16[272,128]{1,0:T(8,128)(2,1)S(1)} collective-permute-done((bf16[272,128]{1,0:T(8,128)(2,1)S(1)}, bf16[272,128]{1,0:T(8,128)(2,1)S(1)}, u32[]{:S(2)}, u32[]{:S(2)}) %collective-permute-start.1) | collective-permute-done | bytes 69664 | tf_op jit(solution)/shard_map/ppermute | solution.py:76
  33.2 1.8 %collective-permute-start.2 = (bf16[256,256]{1,0:T(8,128)(2,1)S(1)}, bf16[256,256]{1,0:T(8,128)(2,1)S(1)}, u32[]{:S(2)}, u32[]{:S(2)}) collective-permute-start(bf16[256,256]{1,0:T(8,128)(2,1)S(1)} %get-tuple-element.26._.refs_2_.refs_0_), channel_id=1, source_target_pairs={{1,0},{0,1},{3,2},{2,3},{5,4},{4,5},{7,6},{6,7},{9,8},{8,9},{11,10... | collective-permute-start | bytes 393224 | tf_op jit(solution)/shard_map/ppermute | solution.py:76
  35.0 1.6 %collective-permute-start.4 = (bf16[288,128]{1,0:T(8,128)(2,1)S(1)}, bf16[288,128]{1,0:T(8,128)(2,1)S(1)}, u32[]{:S(2)}, u32[]{:S(2)}) collective-permute-start(bf16[288,128]{1,0:T(8,128)(2,1)S(1)} %pad_maximum_fusion.refs_0_.refs_2_), channel_id=1, source_target_pairs={{24,0},{26,2},{28,4},{30,6},{0,8},{2,10},{4,12},{6,14},{8,16},{10,... | collective-permute-start | bytes 221192 | tf_op jit(solution)/shard_map/ppermute | solution.py:76
  36.6 2.3 %collective-permute-start.3 = (bf16[288,128]{1,0:T(8,128)(2,1)S(1)}, bf16[288,128]{1,0:T(8,128)(2,1)S(1)}, u32[]{:S(2)}, u32[]{:S(2)}) collective-permute-start(bf16[288,128]{1,0:T(8,128)(2,1)S(1)} %pad_maximum_fusion.refs_0_.refs_2_), channel_id=1, source_target_pairs={{8,0},{10,2},{12,4},{14,6},{16,8},{18,10},{20,12},{22,14},{24,16},... | collective-permute-start | bytes 221192 | tf_op jit(solution)/shard_map/ppermute | solution.py:76
  38.9 1.5 %collective-permute-start.6 = (bf16[288,128]{1,0:T(8,128)(2,1)S(1)}, bf16[288,128]{1,0:T(8,128)(2,1)S(1)}, u32[]{:S(2)}, u32[]{:S(2)}) collective-permute-start(bf16[288,128]{1,0:T(8,128)(2,1)S(1)} %pad_maximum_fusion.refs_0_.refs_2_), channel_id=1, source_target_pairs={{0,4},{2,6},{4,0},{6,2},{8,12},{10,14},{12,8},{14,10},{16,20},{18,... | collective-permute-start | bytes 221192 | tf_op jit(solution)/shard_map/ppermute | solution.py:81
  40.3 0.9 collective-permute-done.4.refs_2_.refs_4_
  41.3 0.5 collective-permute-done.3.refs_1_.refs_3_
  41.7 1.8 %collective-permute-start.5 = (bf16[288,128]{1,0:T(8,128)(2,1)S(1)}, bf16[288,128]{1,0:T(8,128)(2,1)S(1)}, u32[]{:S(2)}, u32[]{:S(2)}) collective-permute-start(bf16[288,128]{1,0:T(8,128)(2,1)S(1)} %pad_maximum_fusion.refs_0_.refs_2_), channel_id=1, source_target_pairs={{16,0},{18,2},{20,4},{22,6},{24,8},{26,10},{28,12},{30,14},{0,16},... | collective-permute-start | bytes 221192 | tf_op jit(solution)/shard_map/ppermute | solution.py:76
  43.5 0.6 gather_fusion
  44.1 2.1 %collective-permute-start.13 = (bf16[288,128]{1,0:T(8,128)(2,1)S(1)}, bf16[288,128]{1,0:T(8,128)(2,1)S(1)}, u32[]{:S(2)}, u32[]{:S(2)}) collective-permute-start(bf16[288,128]{1,0:T(8,128)(2,1)S(1)} %collective-permute-done.4.refs_2_.refs_4_), channel_id=1, source_target_pairs={{0,4},{2,6},{4,0},{6,2},{8,12},{10,14},{12,8},{14,10},{16,20},{18,... | collective-permute-start | bytes 221192 | tf_op jit(solution)/shard_map/ppermute | solution.py:81
  46.4 0.4 collective-permute-start.11
  46.8 1.0 collective-permute-done.5.refs_3_.refs_5_
  47.8 1.5 %collective-permute-start.16 = (bf16[288,128]{1,0:T(8,128)(2,1)S(1)}, bf16[288,128]{1,0:T(8,128)(2,1)S(1)}, u32[]{:S(2)}, u32[]{:S(2)}) collective-permute-start(bf16[288,128]{1,0:T(8,128)(2,1)S(1)} %collective-permute-done.5.refs_3_.refs_5_), channel_id=1, source_target_pairs={{0,4},{2,6},{4,0},{6,2},{8,12},{10,14},{12,8},{14,10},{16,20},{18,... | collective-permute-start | bytes 221192 | tf_op jit(solution)/shard_map/ppermute | solution.py:81
  49.6 0.5 collective-permute-start.15
  50.0 1.2 %collective-permute-done.12.refs_10_.refs_12_ = bf16[288,128]{1,0:T(8,128)(2,1)S(1)} collective-permute-done((bf16[288,128]{1,0:T(8,128)(2,1)S(1)}, bf16[288,128]{1,0:T(8,128)(2,1)S(1)}, u32[]{:S(2)}, u32[]{:S(2)}) %collective-permute-start.12) | collective-permute-done | bytes 73760 | tf_op jit(solution)/shard_map/ppermute | solution.py:81
  51.3 0.5 collective-permute-start.10
  51.8 0.7 collective-permute-done.16.refs_16_
  52.7 0.4 unpack_call.1.refs_18_.refs_2_.refs_0_
  53.1 0.6 collective-permute-done.17.refs_17_
  53.8 5.6 %first_call.1 = (bf16[4,256,256]{2,1,0:T(8,128)(2,1)S(1)}, f32[2,256,128]{2,1,0:T(8,128)S(1)}, bf16[256,256]{1,0:T(8,128)(2,1)S(1)}, bf16[512,64]{1,0:T(8,128)(2,1)S(1)}) custom-call(s32[16]{0:T(128)S(1)} %stack.107.order, s32[256,1]{1,0:T(8,128)S(1)} %add_select_fusion.names, bf16[256,256]{1,0:T(8,128)(2,1)S(1)} %get-tuple-element.26._.refs_2_.refs_0_, ...), custom_call_target="tpu_custom_call" | custom-call | flops 1 | bytes 1 | tf_op jit(solution)/shard_map/first_call/pallas_call | solution.py:506
  59.4 0.6 collective-permute-start.18
  59.9 2.5 %energy_call.1.refs_6_ = f32[256,256]{1,0:T(8,128)S(1)} custom-call(bf16[32,256,256]{2,1,0:T(8,128)(2,1)} %refs_4_.1, f32[2,256,128]{2,1,0:T(8,128)S(1)} %get-tuple-element.32.total, f32[32,256]{1,0:T(8,128)S(1)} %constant_dynamic-slice_fusion.1.live.refs_5_, f32[32,256]{1,0:T(8,128)S(1)} %reshape.711.energy, f32[256,256]{1,0:T(8,128)S(1)} %get-tuple-element.20.my_trial.trial), custom_call_target="tpu_custom_call" | custom-call | flops 1 | bytes 1 | tf_op jit(solution)/shard_map/energy_call/pallas_call | solution.py:543
  62.4 2.6 %collective-permute-done.18.refs_1_ = bf16[256,256]{1,0:T(8,128)(2,1)S(1)} collective-permute-done((bf16[256,256]{1,0:T(8,128)(2,1)S(1)}, bf16[256,256]{1,0:T(8,128)(2,1)S(1)}, u32[]{:S(2)}, u32[]{:S(2)}) %collective-permute-start.18) | collective-permute-done | bytes 131104 | tf_op jit(solution)/shard_map/ppermute | solution.py:76
  65.0 4.7 %second_call.1.refs_0_ = bf16[256,256]{1,0:T(8,128)(2,1)S(1)} custom-call(bf16[512,64]{1,0:T(8,128)(2,1)S(1)} %get-tuple-element.29.weights, bf16[256,256]{1,0:T(8,128)(2,1)S(1)} %get-tuple-element.30.refs_0_, bf16[256,256]{1,0:T(8,128)(2,1)S(1)} %collective-permute-done.18.refs_1_, bf16[12,256,256]{2,1,0:T(8,128)(2,1)S(1)} %unpack_call.1.refs_18_.refs_2_.refs_0_, ...), custom_call_target="tpu_custom_call" | custom-call | flops 1 | bytes 1 | tf_op jit(solution)/shard_map/second_call/pallas_call | solution.py:576
  69.7 0.6 collective-permute-start.19
  70.2 1.1 %collective-permute-start.20 = (bf16[256,256]{1,0:T(8,128)(2,1)S(1)}, bf16[256,256]{1,0:T(8,128)(2,1)S(1)}, u32[]{:S(2)}, u32[]{:S(2)}) collective-permute-start(bf16[256,256]{1,0:T(8,128)(2,1)S(1)} %second_call.1.refs_0_), channel_id=1, source_target_pairs={{0,4},{2,6},{4,0},{6,2},{8,12},{10,14},{12,8},{14,10},{16,20},{18,... | collective-permute-start | bytes 393224 | tf_op jit(solution)/shard_map/ppermute | solution.py:81
  71.4 3.3 %collective-permute-start.22 = (bf16[256,256]{1,0:T(8,128)(2,1)S(1)}, bf16[256,256]{1,0:T(8,128)(2,1)S(1)}, u32[]{:S(2)}, u32[]{:S(2)}) collective-permute-start(bf16[256,256]{1,0:T(8,128)(2,1)S(1)} %second_call.1.refs_0_), channel_id=1, source_target_pairs={{8,0},{10,2},{12,4},{14,6},{16,8},{18,10},{20,12},{22,14},{24,16},... | collective-permute-start | bytes 393224 | tf_op jit(solution)/shard_map/ppermute | solution.py:76
  74.8 0.4 collective-permute-done.20.refs_2_.refs_4_
  75.2 1.7 %collective-permute-start.23 = (bf16[256,256]{1,0:T(8,128)(2,1)S(1)}, bf16[256,256]{1,0:T(8,128)(2,1)S(1)}, u32[]{:S(2)}, u32[]{:S(2)}) collective-permute-start(bf16[256,256]{1,0:T(8,128)(2,1)S(1)} %second_call.1.refs_0_), channel_id=1, source_target_pairs={{24,0},{26,2},{28,4},{30,6},{0,8},{2,10},{4,12},{6,14},{8,16},{10,... | collective-permute-start | bytes 393224 | tf_op jit(solution)/shard_map/ppermute | solution.py:76
  76.9 7.2 %row_call.1 = bf16[512,256]{1,0:T(8,128)(2,1)S(1)} custom-call(s32[16]{0:T(128)S(1)} %stack.107.order, bf16[64,32]{1,0:T(8,128)(2,1)S(1)} %bitcast.51, bf16[32,128,256]{2,1,0:T(8,128)(2,1)} %get-tuple-element.34.vectors_at, bf16[12,256,256]{2,1,0:T(8,128)(2,1)S(1)} %unpack_call.1.refs_18_.refs_2_.refs_0_, ...), custom_call_target="tpu_custom_call" | custom-call | flops 1 | bytes 1 | tf_op jit(solution)/shard_map/row_call/pallas_call | solution.py:327
  84.2 1.2 %collective-permute-start.30 = (bf16[256,256]{1,0:T(8,128)(2,1)S(1)}, bf16[256,256]{1,0:T(8,128)(2,1)S(1)}, u32[]{:S(2)}, u32[]{:S(2)}) collective-permute-start(bf16[256,256]{1,0:T(8,128)(2,1)S(1)} %collective-permute-done.22.refs_1_), channel_id=1, source_target_pairs={{0,4},{2,6},{4,0},{6,2},{8,12},{10,14},{12,8},{14,10},{16,20},{18,... | collective-permute-start | bytes 393224 | tf_op jit(solution)/shard_map/ppermute | solution.py:81
  85.5 0.9 collective-permute-start.31
  86.6 3.2 %collective-permute-done.30.refs_10_ = bf16[256,256]{1,0:T(8,128)(2,1)S(1)} collective-permute-done((bf16[256,256]{1,0:T(8,128)(2,1)S(1)}, bf16[256,256]{1,0:T(8,128)(2,1)S(1)}, u32[]{:S(2)}, u32[]{:S(2)}) %collective-permute-start.30) | collective-permute-done | bytes 131104 | tf_op jit(solution)/shard_map/ppermute | solution.py:81
  89.8 1.4 %collective-permute-start.34 = (bf16[256,256]{1,0:T(8,128)(2,1)S(1)}, bf16[256,256]{1,0:T(8,128)(2,1)S(1)}, u32[]{:S(2)}, u32[]{:S(2)}) collective-permute-start(bf16[256,256]{1,0:T(8,128)(2,1)S(1)} %collective-permute-done.24.refs_3_), channel_id=1, source_target_pairs={{0,4},{2,6},{4,0},{6,2},{8,12},{10,14},{12,8},{14,10},{16,20},{18,... | collective-permute-start | bytes 393224 | tf_op jit(solution)/shard_map/ppermute | solution.py:81
  91.2 1.5 %fusion.1 = bf16[4,256,128]{2,1,0:T(8,128)(2,1)S(1)} fusion(bf16[4,128,256]{2,1,0:T(8,128)(2,1)S(1)} %bitcast.50, bf16[4,256,256]{2,1,0:T(8,128)(2,1)S(1)} %collective-permute-done.19, bf16[4,256,256]{2,1,0:T(8,128)(2,1)S(1)} %copy-done.20, pred[]{:T(512)S(6)} %eq.59, bf16[32,256,128]{2,1,0:T(8,128)(2,1)} %bitcast.52, s32[]{:T(128)S(6)} %select_n.145, ...), kind=kOutput, calls=%fused_computation.3 | convolution fusion | flops 68157440 | bytes 1843206 | tf_op jit(solution)/shard_map/ksv,kns->kvn/dot_general | solution.py:725
  92.7 1.6 %collective-permute-start.21 = (bf16[4,256,128]{2,1,0:T(8,128)(2,1)S(1)}, bf16[4,256,128]{2,1,0:T(8,128)(2,1)S(1)}, u32[]{:S(2)}, u32[]{:S(2)}) collective-permute-start(bf16[4,256,128]{2,1,0:T(8,128)(2,1)S(1)} %fusion.1), channel_id=1, source_target_pairs={{1,0},{0,1},{3,2},{2,3},{5,4},{4,5},{7,6},{6,7},{9,8},{8,9},{11,10... | collective-permute-start | bytes 786440 | tf_op jit(solution)/shard_map/ppermute | solution.py:76
  95.4 0.3 collective-permute-done.29.refs_9_
  96.9 0.6 copy-done.16
  97.5 5.2 %last_call.1 = f32[8192,128]{1,0:T(8,128)} custom-call(s32[16]{0:T(128)S(1)} %stack.107.order, bf16[8192,128]{1,0:T(8,128)(2,1)} %trial_at.3, bf16[256,256]{1,0:T(8,128)(2,1)} %copy-done.1, bf16[256,256]{1,0:T(8,128)(2,1)} %copy-done.3, bf16[256,256]{1,0:T(8,128)(2,1)} %copy-done.6, bf16[256,256]{1,0:T(8,128)(2,1)} %copy-done.4, bf16[256,256]{1,0:T(8,128)(2,1)} %copy-done.2, ...), custom_call_target="tpu_custom_call" | custom-call | flops 1 | bytes 1 | tf_op jit(solution)/shard_map/last_call/pallas_call | solution.py:631
  102.8 0.8 add_convert_fusion
  (101 shorter events, 3.8 us)
Async XLA Ops:
  0.6 26.4 %collective-permute-start = (bf16[2048,256]{1,0:T(8,128)(2,1)}, bf16[2048,256]{1,0:T(8,128)(2,1)S(1)}, u32[]{:S(2)}, u32[]{:S(2)}) collective-permute-start(bf16[2048,256]{1,0:T(8,128)(2,1)} %bitcast.48), channel_id=1, source_target_pairs={{1,0},{0,1},{3,2},{2,3},{5,4},{4,5},{7,6},{6,7},{9,8},{8,9},{11,10... | collective-permute-start | bytes 3145736 | tf_op jit(solution)/shard_map/ppermute | solution.py:76
  4.5 5.2 %copy-start = (bf16[1,2048,256]{2,1,0:T(8,128)(2,1)S(1)}, bf16[1,2048,256]{2,1,0:T(8,128)(2,1)}, u32[]{:S(2)}) copy-start(bf16[1,2048,256]{2,1,0:T(8,128)(2,1)} %param.9) | copy-start | bytes 3145732
  9.7 8.5 %copy-start.17 = (f32[8192]{0:T(1024)S(1)}, f32[8192]{0:T(1024)}, u32[]{:S(2)}) copy-start(f32[8192]{0:T(1024)} %param.11) | copy-start | bytes 98308
  18.2 5.6 %copy-start.19 = (bf16[4,32,4]{1,2,0:T(4,128)(2,1)S(1)}, bf16[4,32,4]{1,2,0:T(4,128)(2,1)}, u32[]{:S(2)}) copy-start(bf16[4,32,4]{1,2,0:T(4,128)(2,1)} %param.14) | copy-start | bytes 3076
  23.6 7.0 %copy-start.18 = (s32[4,32,4]{1,2,0:T(4,128)S(1)}, s32[4,32,4]{1,2,0:T(4,128)}, u32[]{:S(2)}) copy-start(s32[4,32,4]{1,2,0:T(4,128)} %param.13) | copy-start | bytes 6148
  28.8 4.4 %collective-permute-start.1 = (bf16[272,128]{1,0:T(8,128)(2,1)S(1)}, bf16[272,128]{1,0:T(8,128)(2,1)S(1)}, u32[]{:S(2)}, u32[]{:S(2)}) collective-permute-start(bf16[272,128]{1,0:T(8,128)(2,1)S(1)} %coarse_block.1), channel_id=1, source_target_pairs={{1,0},{0,1},{3,2},{2,3},{5,4},{4,5},{7,6},{6,7},{9,8},{8,9},{11,10... | collective-permute-start | bytes 208904 | tf_op jit(solution)/shard_map/ppermute | solution.py:76
  33.2 8.5 %collective-permute-start.2 = (bf16[256,256]{1,0:T(8,128)(2,1)S(1)}, bf16[256,256]{1,0:T(8,128)(2,1)S(1)}, u32[]{:S(2)}, u32[]{:S(2)}) collective-permute-start(bf16[256,256]{1,0:T(8,128)(2,1)S(1)} %get-tuple-element.26._.refs_2_.refs_0_), channel_id=1, source_target_pairs={{1,0},{0,1},{3,2},{2,3},{5,4},{4,5},{7,6},{6,7},{9,8},{8,9},{11,10... | collective-permute-start | bytes 393224 | tf_op jit(solution)/shard_map/ppermute | solution.py:76
  35.0 6.3 %collective-permute-start.4 = (bf16[288,128]{1,0:T(8,128)(2,1)S(1)}, bf16[288,128]{1,0:T(8,128)(2,1)S(1)}, u32[]{:S(2)}, u32[]{:S(2)}) collective-permute-start(bf16[288,128]{1,0:T(8,128)(2,1)S(1)} %pad_maximum_fusion.refs_0_.refs_2_), channel_id=1, source_target_pairs={{24,0},{26,2},{28,4},{30,6},{0,8},{2,10},{4,12},{6,14},{8,16},{10,... | collective-permute-start | bytes 221192 | tf_op jit(solution)/shard_map/ppermute | solution.py:76
  36.6 5.1 %collective-permute-start.3 = (bf16[288,128]{1,0:T(8,128)(2,1)S(1)}, bf16[288,128]{1,0:T(8,128)(2,1)S(1)}, u32[]{:S(2)}, u32[]{:S(2)}) collective-permute-start(bf16[288,128]{1,0:T(8,128)(2,1)S(1)} %pad_maximum_fusion.refs_0_.refs_2_), channel_id=1, source_target_pairs={{8,0},{10,2},{12,4},{14,6},{16,8},{18,10},{20,12},{22,14},{24,16},... | collective-permute-start | bytes 221192 | tf_op jit(solution)/shard_map/ppermute | solution.py:76
  38.8 7.4 %collective-permute-start.7 = (bf16[288,128]{1,0:T(8,128)(2,1)S(1)}, bf16[288,128]{1,0:T(8,128)(2,1)S(1)}, u32[]{:S(2)}, u32[]{:S(2)}) collective-permute-start(bf16[288,128]{1,0:T(8,128)(2,1)S(1)} %pad_maximum_fusion.refs_0_.refs_2_), channel_id=1, source_target_pairs={{0,2},{2,0},{4,6},{6,4},{8,10},{10,8},{12,14},{14,12},{16,18},{18,... | collective-permute-start | bytes 221192 | tf_op jit(solution)/shard_map/ppermute | solution.py:81
  38.9 7.5 %collective-permute-start.6 = (bf16[288,128]{1,0:T(8,128)(2,1)S(1)}, bf16[288,128]{1,0:T(8,128)(2,1)S(1)}, u32[]{:S(2)}, u32[]{:S(2)}) collective-permute-start(bf16[288,128]{1,0:T(8,128)(2,1)S(1)} %pad_maximum_fusion.refs_0_.refs_2_), channel_id=1, source_target_pairs={{0,4},{2,6},{4,0},{6,2},{8,12},{10,14},{12,8},{14,10},{16,20},{18,... | collective-permute-start | bytes 221192 | tf_op jit(solution)/shard_map/ppermute | solution.py:81
  41.7 6.0 %collective-permute-start.5 = (bf16[288,128]{1,0:T(8,128)(2,1)S(1)}, bf16[288,128]{1,0:T(8,128)(2,1)S(1)}, u32[]{:S(2)}, u32[]{:S(2)}) collective-permute-start(bf16[288,128]{1,0:T(8,128)(2,1)S(1)} %pad_maximum_fusion.refs_0_.refs_2_), channel_id=1, source_target_pairs={{16,0},{18,2},{20,4},{22,6},{24,8},{26,10},{28,12},{30,14},{0,16},... | collective-permute-start | bytes 221192 | tf_op jit(solution)/shard_map/ppermute | solution.py:76
  44.1 5.5 %collective-permute-start.13 = (bf16[288,128]{1,0:T(8,128)(2,1)S(1)}, bf16[288,128]{1,0:T(8,128)(2,1)S(1)}, u32[]{:S(2)}, u32[]{:S(2)}) collective-permute-start(bf16[288,128]{1,0:T(8,128)(2,1)S(1)} %collective-permute-done.4.refs_2_.refs_4_), channel_id=1, source_target_pairs={{0,4},{2,6},{4,0},{6,2},{8,12},{10,14},{12,8},{14,10},{16,20},{18,... | collective-permute-start | bytes 221192 | tf_op jit(solution)/shard_map/ppermute | solution.py:81
  46.2 5.1 %collective-permute-start.9 = (bf16[288,128]{1,0:T(8,128)(2,1)S(1)}, bf16[288,128]{1,0:T(8,128)(2,1)S(1)}, u32[]{:S(2)}, u32[]{:S(2)}) collective-permute-start(bf16[288,128]{1,0:T(8,128)(2,1)S(1)} %collective-permute-done.4.refs_2_.refs_4_), channel_id=1, source_target_pairs={{0,2},{2,0},{4,6},{6,4},{8,10},{10,8},{12,14},{14,12},{16,18},{18,... | collective-permute-start | bytes 221192 | tf_op jit(solution)/shard_map/ppermute | solution.py:81
  46.2 5.1 %collective-permute-start.12 = (bf16[288,128]{1,0:T(8,128)(2,1)S(1)}, bf16[288,128]{1,0:T(8,128)(2,1)S(1)}, u32[]{:S(2)}, u32[]{:S(2)}) collective-permute-start(bf16[288,128]{1,0:T(8,128)(2,1)S(1)} %collective-permute-done.3.refs_1_.refs_3_), channel_id=1, source_target_pairs={{0,4},{2,6},{4,0},{6,2},{8,12},{10,14},{12,8},{14,10},{16,20},{18,... | collective-permute-start | bytes 221192 | tf_op jit(solution)/shard_map/ppermute | solution.py:81
  46.4 3.1 %collective-permute-start.11 = (bf16[288,128]{1,0:T(8,128)(2,1)S(1)}, bf16[288,128]{1,0:T(8,128)(2,1)S(1)}, u32[]{:S(2)}, u32[]{:S(2)}) collective-permute-start(bf16[288,128]{1,0:T(8,128)(2,1)S(1)} %collective-permute-done.6.refs_4_.refs_6_), channel_id=1, source_target_pairs={{0,2},{2,0},{4,6},{6,4},{8,10},{10,8},{12,14},{14,12},{16,18},{18,... | collective-permute-start | bytes 221192 | tf_op jit(solution)/shard_map/ppermute | solution.py:81
  47.8 4.7 %collective-permute-start.16 = (bf16[288,128]{1,0:T(8,128)(2,1)S(1)}, bf16[288,128]{1,0:T(8,128)(2,1)S(1)}, u32[]{:S(2)}, u32[]{:S(2)}) collective-permute-start(bf16[288,128]{1,0:T(8,128)(2,1)S(1)} %collective-permute-done.5.refs_3_.refs_5_), channel_id=1, source_target_pairs={{0,4},{2,6},{4,0},{6,2},{8,12},{10,14},{12,8},{14,10},{16,20},{18,... | collective-permute-start | bytes 221192 | tf_op jit(solution)/shard_map/ppermute | solution.py:81
  49.5 3.2 %collective-permute-start.8 = (bf16[288,128]{1,0:T(8,128)(2,1)S(1)}, bf16[288,128]{1,0:T(8,128)(2,1)S(1)}, u32[]{:S(2)}, u32[]{:S(2)}) collective-permute-start(bf16[288,128]{1,0:T(8,128)(2,1)S(1)} %collective-permute-done.3.refs_1_.refs_3_), channel_id=1, source_target_pairs={{0,2},{2,0},{4,6},{6,4},{8,10},{10,8},{12,14},{14,12},{16,18},{18,... | collective-permute-start | bytes 221192 | tf_op jit(solution)/shard_map/ppermute | solution.py:81
  49.6 3.6 %collective-permute-start.15 = (bf16[288,128]{1,0:T(8,128)(2,1)S(1)}, bf16[288,128]{1,0:T(8,128)(2,1)S(1)}, u32[]{:S(2)}, u32[]{:S(2)}) collective-permute-start(bf16[288,128]{1,0:T(8,128)(2,1)S(1)} %collective-permute-done.13.refs_11_.refs_13_), channel_id=1, source_target_pairs={{0,2},{2,0},{4,6},{6,4},{8,10},{10,8},{12,14},{14,12},{16,18},{18,... | collective-permute-start | bytes 221192 | tf_op jit(solution)/shard_map/ppermute | solution.py:81
  51.3 1.8 %collective-permute-start.14 = (bf16[288,128]{1,0:T(8,128)(2,1)S(1)}, bf16[288,128]{1,0:T(8,128)(2,1)S(1)}, u32[]{:S(2)}, u32[]{:S(2)}) collective-permute-start(bf16[288,128]{1,0:T(8,128)(2,1)S(1)} %collective-permute-done.12.refs_10_.refs_12_), channel_id=1, source_target_pairs={{0,2},{2,0},{4,6},{6,4},{8,10},{10,8},{12,14},{14,12},{16,18},{18,... | collective-permute-start | bytes 221192 | tf_op jit(solution)/shard_map/ppermute | solution.py:81
  51.3 1.4 %collective-permute-start.10 = (bf16[288,128]{1,0:T(8,128)(2,1)S(1)}, bf16[288,128]{1,0:T(8,128)(2,1)S(1)}, u32[]{:S(2)}, u32[]{:S(2)}) collective-permute-start(bf16[288,128]{1,0:T(8,128)(2,1)S(1)} %collective-permute-done.5.refs_3_.refs_5_), channel_id=1, source_target_pairs={{0,2},{2,0},{4,6},{6,4},{8,10},{10,8},{12,14},{14,12},{16,18},{18,... | collective-permute-start | bytes 221192 | tf_op jit(solution)/shard_map/ppermute | solution.py:81
  52.5 1.3 %collective-permute-start.17 = (bf16[288,128]{1,0:T(8,128)(2,1)S(1)}, bf16[288,128]{1,0:T(8,128)(2,1)S(1)}, u32[]{:S(2)}, u32[]{:S(2)}) collective-permute-start(bf16[288,128]{1,0:T(8,128)(2,1)S(1)} %collective-permute-done.16.refs_16_), channel_id=1, source_target_pairs={{0,2},{2,0},{4,6},{6,4},{8,10},{10,8},{12,14},{14,12},{16,18},{18,... | collective-permute-start | bytes 221192 | tf_op jit(solution)/shard_map/ppermute | solution.py:81
  59.4 5.6 %collective-permute-start.18 = (bf16[256,256]{1,0:T(8,128)(2,1)S(1)}, bf16[256,256]{1,0:T(8,128)(2,1)S(1)}, u32[]{:S(2)}, u32[]{:S(2)}) collective-permute-start(bf16[256,256]{1,0:T(8,128)(2,1)S(1)} %get-tuple-element.30.refs_0_), channel_id=1, source_target_pairs={{1,0},{0,1},{3,2},{2,3},{5,4},{4,5},{7,6},{6,7},{9,8},{8,9},{11,10... | collective-permute-start | bytes 393224 | tf_op jit(solution)/shard_map/ppermute | solution.py:76
  65.0 4.7 %copy-start.20 = (bf16[4,256,256]{2,1,0:T(8,128)(2,1)S(1)}, bf16[4,256,256]{2,1,0:T(8,128)(2,1)}, u32[]{:S(2)}) copy-start(bf16[4,256,256]{2,1,0:T(8,128)(2,1)} %get-tuple-element.33) | copy-start | bytes 1572868
  69.7 14.5 %copy-start.1 = (bf16[256,256]{1,0:T(8,128)(2,1)}, bf16[256,256]{1,0:T(8,128)(2,1)S(1)}, u32[]{:S(2)}) copy-start(bf16[256,256]{1,0:T(8,128)(2,1)S(1)} %second_call.1.refs_0_) | copy-start | bytes 393220
  69.7 21.6 %collective-permute-start.19 = (bf16[4,256,256]{2,1,0:T(8,128)(2,1)S(1)}, bf16[4,256,256]{2,1,0:T(8,128)(2,1)S(1)}, u32[]{:S(2)}, u32[]{:S(2)}) collective-permute-start(bf16[4,256,256]{2,1,0:T(8,128)(2,1)S(1)} %copy-done.20), channel_id=1, source_target_pairs={{1,0},{0,1},{3,2},{2,3},{5,4},{4,5},{7,6},{6,7},{9,8},{8,9},{11,10... | collective-permute-start | bytes 1572872 | tf_op jit(solution)/shard_map/ppermute | solution.py:76
  70.2 5.0 %collective-permute-start.20 = (bf16[256,256]{1,0:T(8,128)(2,1)S(1)}, bf16[256,256]{1,0:T(8,128)(2,1)S(1)}, u32[]{:S(2)}, u32[]{:S(2)}) collective-permute-start(bf16[256,256]{1,0:T(8,128)(2,1)S(1)} %second_call.1.refs_0_), channel_id=1, source_target_pairs={{0,4},{2,6},{4,0},{6,2},{8,12},{10,14},{12,8},{14,10},{16,20},{18,... | collective-permute-start | bytes 393224 | tf_op jit(solution)/shard_map/ppermute | solution.py:81
  71.4 12.8 %collective-permute-start.22 = (bf16[256,256]{1,0:T(8,128)(2,1)S(1)}, bf16[256,256]{1,0:T(8,128)(2,1)S(1)}, u32[]{:S(2)}, u32[]{:S(2)}) collective-permute-start(bf16[256,256]{1,0:T(8,128)(2,1)S(1)} %second_call.1.refs_0_), channel_id=1, source_target_pairs={{8,0},{10,2},{12,4},{14,6},{16,8},{18,10},{20,12},{22,14},{24,16},... | collective-permute-start | bytes 393224 | tf_op jit(solution)/shard_map/ppermute | solution.py:76
  74.7 10.8 %collective-permute-start.24 = (bf16[256,256]{1,0:T(8,128)(2,1)S(1)}, bf16[256,256]{1,0:T(8,128)(2,1)S(1)}, u32[]{:S(2)}, u32[]{:S(2)}) collective-permute-start(bf16[256,256]{1,0:T(8,128)(2,1)S(1)} %second_call.1.refs_0_), channel_id=1, source_target_pairs={{16,0},{18,2},{20,4},{22,6},{24,8},{26,10},{28,12},{30,14},{0,16},... | collective-permute-start | bytes 393224 | tf_op jit(solution)/shard_map/ppermute | solution.py:76
  74.7 11.7 %collective-permute-start.25 = (bf16[256,256]{1,0:T(8,128)(2,1)S(1)}, bf16[256,256]{1,0:T(8,128)(2,1)S(1)}, u32[]{:S(2)}, u32[]{:S(2)}) collective-permute-start(bf16[256,256]{1,0:T(8,128)(2,1)S(1)} %second_call.1.refs_0_), channel_id=1, source_target_pairs={{0,2},{2,0},{4,6},{6,4},{8,10},{10,8},{12,14},{14,12},{16,18},{18,... | collective-permute-start | bytes 393224 | tf_op jit(solution)/shard_map/ppermute | solution.py:81
  75.2 19.1 %copy-start.2 = (bf16[256,256]{1,0:T(8,128)(2,1)}, bf16[256,256]{1,0:T(8,128)(2,1)S(1)}, u32[]{:S(2)}) copy-start(bf16[256,256]{1,0:T(8,128)(2,1)S(1)} %collective-permute-done.20.refs_2_.refs_4_) | copy-start | bytes 393220
  75.2 10.3 %collective-permute-start.23 = (bf16[256,256]{1,0:T(8,128)(2,1)S(1)}, bf16[256,256]{1,0:T(8,128)(2,1)S(1)}, u32[]{:S(2)}, u32[]{:S(2)}) collective-permute-start(bf16[256,256]{1,0:T(8,128)(2,1)S(1)} %second_call.1.refs_0_), channel_id=1, source_target_pairs={{24,0},{26,2},{28,4},{30,6},{0,8},{2,10},{4,12},{6,14},{8,16},{10,... | collective-permute-start | bytes 393224 | tf_op jit(solution)/shard_map/ppermute | solution.py:76
  84.2 12.3 %copy-start.3 = (bf16[256,256]{1,0:T(8,128)(2,1)}, bf16[256,256]{1,0:T(8,128)(2,1)S(1)}, u32[]{:S(2)}) copy-start(bf16[256,256]{1,0:T(8,128)(2,1)S(1)} %collective-permute-done.22.refs_1_) | copy-start | bytes 393220
  84.2 5.6 %collective-permute-start.30 = (bf16[256,256]{1,0:T(8,128)(2,1)S(1)}, bf16[256,256]{1,0:T(8,128)(2,1)S(1)}, u32[]{:S(2)}, u32[]{:S(2)}) collective-permute-start(bf16[256,256]{1,0:T(8,128)(2,1)S(1)} %collective-permute-done.22.refs_1_), channel_id=1, source_target_pairs={{0,4},{2,6},{4,0},{6,2},{8,12},{10,14},{12,8},{14,10},{16,20},{18,... | collective-permute-start | bytes 393224 | tf_op jit(solution)/shard_map/ppermute | solution.py:81
  85.5 11.0 %copy-start.4 = (bf16[256,256]{1,0:T(8,128)(2,1)}, bf16[256,256]{1,0:T(8,128)(2,1)S(1)}, u32[]{:S(2)}) copy-start(bf16[256,256]{1,0:T(8,128)(2,1)S(1)} %collective-permute-done.24.refs_3_) | copy-start | bytes 393220
  85.5 7.2 %collective-permute-start.26 = (bf16[256,256]{1,0:T(8,128)(2,1)S(1)}, bf16[256,256]{1,0:T(8,128)(2,1)S(1)}, u32[]{:S(2)}, u32[]{:S(2)}) collective-permute-start(bf16[256,256]{1,0:T(8,128)(2,1)S(1)} %collective-permute-done.22.refs_1_), channel_id=1, source_target_pairs={{0,2},{2,0},{4,6},{6,4},{8,10},{10,8},{12,14},{14,12},{16,18},{18,... | collective-permute-start | bytes 393224 | tf_op jit(solution)/shard_map/ppermute | solution.py:81
  85.5 11.0 %copy-start.6 = (bf16[256,256]{1,0:T(8,128)(2,1)}, bf16[256,256]{1,0:T(8,128)(2,1)S(1)}, u32[]{:S(2)}) copy-start(bf16[256,256]{1,0:T(8,128)(2,1)S(1)} %collective-permute-done.23.refs_2_) | copy-start | bytes 393220
  85.5 8.8 %collective-permute-start.31 = (bf16[256,256]{1,0:T(8,128)(2,1)S(1)}, bf16[256,256]{1,0:T(8,128)(2,1)S(1)}, u32[]{:S(2)}, u32[]{:S(2)}) collective-permute-start(bf16[256,256]{1,0:T(8,128)(2,1)S(1)} %collective-permute-done.23.refs_2_), channel_id=1, source_target_pairs={{0,4},{2,6},{4,0},{6,2},{8,12},{10,14},{12,8},{14,10},{16,20},{18,... | collective-permute-start | bytes 393224 | tf_op jit(solution)/shard_map/ppermute | solution.py:81
  86.5 10.0 %copy-start.5 = (bf16[256,256]{1,0:T(8,128)(2,1)}, bf16[256,256]{1,0:T(8,128)(2,1)S(1)}, u32[]{:S(2)}) copy-start(bf16[256,256]{1,0:T(8,128)(2,1)S(1)} %collective-permute-done.25.refs_5_) | copy-start | bytes 393220
  86.5 8.2 %collective-permute-start.27 = (bf16[256,256]{1,0:T(8,128)(2,1)S(1)}, bf16[256,256]{1,0:T(8,128)(2,1)S(1)}, u32[]{:S(2)}, u32[]{:S(2)}) collective-permute-start(bf16[256,256]{1,0:T(8,128)(2,1)S(1)} %collective-permute-done.23.refs_2_), channel_id=1, source_target_pairs={{0,2},{2,0},{4,6},{6,4},{8,10},{10,8},{12,14},{14,12},{16,18},{18,... | collective-permute-start | bytes 393224 | tf_op jit(solution)/shard_map/ppermute | solution.py:81
  89.8 6.7 %copy-start.7 = (bf16[256,256]{1,0:T(8,128)(2,1)}, bf16[256,256]{1,0:T(8,128)(2,1)S(1)}, u32[]{:S(2)}) copy-start(bf16[256,256]{1,0:T(8,128)(2,1)S(1)} %collective-permute-done.30.refs_10_) | copy-start | bytes 393220
  89.8 5.1 %collective-permute-start.34 = (bf16[256,256]{1,0:T(8,128)(2,1)S(1)}, bf16[256,256]{1,0:T(8,128)(2,1)S(1)}, u32[]{:S(2)}, u32[]{:S(2)}) collective-permute-start(bf16[256,256]{1,0:T(8,128)(2,1)S(1)} %collective-permute-done.24.refs_3_), channel_id=1, source_target_pairs={{0,4},{2,6},{4,0},{6,2},{8,12},{10,14},{12,8},{14,10},{16,20},{18,... | collective-permute-start | bytes 393224 | tf_op jit(solution)/shard_map/ppermute | solution.py:81
  91.2 3.9 %collective-permute-start.28 = (bf16[256,256]{1,0:T(8,128)(2,1)S(1)}, bf16[256,256]{1,0:T(8,128)(2,1)S(1)}, u32[]{:S(2)}, u32[]{:S(2)}) collective-permute-start(bf16[256,256]{1,0:T(8,128)(2,1)S(1)} %collective-permute-done.24.refs_3_), channel_id=1, source_target_pairs={{0,2},{2,0},{4,6},{6,4},{8,10},{10,8},{12,14},{14,12},{16,18},{18,... | collective-permute-start | bytes 393224 | tf_op jit(solution)/shard_map/ppermute | solution.py:81
  92.7 10.0 %collective-permute-start.21 = (bf16[4,256,128]{2,1,0:T(8,128)(2,1)S(1)}, bf16[4,256,128]{2,1,0:T(8,128)(2,1)S(1)}, u32[]{:S(2)}, u32[]{:S(2)}) collective-permute-start(bf16[4,256,128]{2,1,0:T(8,128)(2,1)S(1)} %fusion.1), channel_id=1, source_target_pairs={{1,0},{0,1},{3,2},{2,3},{5,4},{4,5},{7,6},{6,7},{9,8},{8,9},{11,10... | collective-permute-start | bytes 786440 | tf_op jit(solution)/shard_map/ppermute | solution.py:76
  94.3 1.4 %collective-permute-start.29 = (bf16[256,256]{1,0:T(8,128)(2,1)S(1)}, bf16[256,256]{1,0:T(8,128)(2,1)S(1)}, u32[]{:S(2)}, u32[]{:S(2)}) collective-permute-start(bf16[256,256]{1,0:T(8,128)(2,1)S(1)} %collective-permute-done.20.refs_2_.refs_4_), channel_id=1, source_target_pairs={{0,2},{2,0},{4,6},{6,4},{8,10},{10,8},{12,14},{14,12},{16,18},{18,... | collective-permute-start | bytes 393224 | tf_op jit(solution)/shard_map/ppermute | solution.py:81
  94.6 1.3 %collective-permute-start.32 = (bf16[256,256]{1,0:T(8,128)(2,1)S(1)}, bf16[256,256]{1,0:T(8,128)(2,1)S(1)}, u32[]{:S(2)}, u32[]{:S(2)}) collective-permute-start(bf16[256,256]{1,0:T(8,128)(2,1)S(1)} %collective-permute-done.30.refs_10_), channel_id=1, source_target_pairs={{0,2},{2,0},{4,6},{6,4},{8,10},{10,8},{12,14},{14,12},{16,18},{18,... | collective-permute-start | bytes 393224 | tf_op jit(solution)/shard_map/ppermute | solution.py:81
  94.9 1.3 %collective-permute-start.33 = (bf16[256,256]{1,0:T(8,128)(2,1)S(1)}, bf16[256,256]{1,0:T(8,128)(2,1)S(1)}, u32[]{:S(2)}, u32[]{:S(2)}) collective-permute-start(bf16[256,256]{1,0:T(8,128)(2,1)S(1)} %collective-permute-done.31.refs_11_), channel_id=1, source_target_pairs={{0,2},{2,0},{4,6},{6,4},{8,10},{10,8},{12,14},{14,12},{16,18},{18,... | collective-permute-start | bytes 393224 | tf_op jit(solution)/shard_map/ppermute | solution.py:81
  95.1 1.3 %collective-permute-start.35 = (bf16[256,256]{1,0:T(8,128)(2,1)S(1)}, bf16[256,256]{1,0:T(8,128)(2,1)S(1)}, u32[]{:S(2)}, u32[]{:S(2)}) collective-permute-start(bf16[256,256]{1,0:T(8,128)(2,1)S(1)} %collective-permute-done.34.refs_14_), channel_id=1, source_target_pairs={{0,2},{2,0},{4,6},{6,4},{8,10},{10,8},{12,14},{14,12},{16,18},{18,... | collective-permute-start | bytes 393224 | tf_op jit(solution)/shard_map/ppermute | solution.py:81
  (9 other events, 13.8 us)

commit v5 on v4

--- a/solution.py
+++ b/solution.py
@@ -105,8 +105,10 @@
     for move in far_moves:
         ready = value
         if meanwhile is None and move == far_moves[-1]:
-            ready = after(value, *[held[other] for other in far_moves[:-1]], *first)
+            ready = after(value, *[held[other] for other in far_moves[:-1]])
         held[move] = from_ahead(ready, "pair", 4 * move[0])
+    if first:
+        held[far_moves[-1]] = after(held[far_moves[-1]], *first)
     done = None
     if meanwhile is not None:
         done = meanwhile(held[0, 1, 0])
@@ -167,75 +169,62 @@
     return jnp.concatenate([top, bottom], axis=0)
 
 
-def left_kernel(plane, screened_at, density, _, out_at, total, screened, turned, out, sems):
-    pieces = sems.shape[0] // 2
+def left_kernel(planes, screened_at, density, _, out, total, screened, turned, left, sems):
+    pieces = sems.shape[0]
     copies = loads(screened_at.at[0], screened, sems, pieces, axis=1)
-    stores = []
     rows = density.shape[0]
     turned[...] = density[...].T
-    size = out.shape[1] // pieces
+    size = left.shape[1] // pieces
     for p in range(pieces):
         copies[p].wait()
         at = slice(p * size, (p + 1) * size)
-        out[:, at] = dot(turned[...], screened[:, at]).astype(BF16)
-        at = (slice(None), pl.ds(p * size, size))
-        store(out, out_at, at, sems.at[pieces + p], stores)
-    at = pl.multiple_of(plane[0] * rows, rows)
-    total[...] = dot(out[:, pl.ds(at, rows)], density[...])
-    finish(stores)
-
-
-def left_product(plane, screened, density, later):
+        left[:, at] = dot(turned[...], screened[:, at]).astype(BF16)
+    at = pl.multiple_of(planes[0] * rows, rows)
+    total[...] = dot(left[:, pl.ds(at, rows)], density[...])
+    for step in range(out.shape[0]):
+        at = pl.multiple_of(planes[step + 1] * rows, rows)
+        out[step] = left[:, pl.ds(at, rows)]
+
+
+def left_product(planes, screened, density, later):
     rows, width = density.shape
     depth = screened.shape[2]
     return pl.pallas_call(
         left_kernel,
         in_specs=[SMEM, HBM, VMEM, ANY],
-        out_specs=[HBM, VMEM],
-        out_shape=[far_shaped((width, depth)), shaped((width, width), F32)],
+        out_specs=[VMEM, VMEM],
+        out_shape=[shaped((depth // rows - 1, width, rows)), shaped((width, width), F32)],
         scratch_shapes=[
             pltpu.VMEM((rows, depth), BF16),
             pltpu.VMEM((width, rows), BF16),
             pltpu.VMEM((width, depth), BF16),
-            pltpu.SemaphoreType.DMA((16,)),
+            pltpu.SemaphoreType.DMA((8,)),
         ],
         compiler_params=params(24),
-        cost_estimate=cost(2 * rows * depth * width, 2 * rows * depth),
+        cost_estimate=cost(1, 1),
         name="left_product",
-    )(plane, far(screened), density, later)
-
-
-def coarse_kernel(planes, left_at, total, *refs):
-    *blocks, _, _, out, left, sems = refs
-    copies = []
-    for step, block in enumerate(blocks):
-        rows = block.shape[0]
-        at = pl.multiple_of(planes[step] * rows, rows)
-        part = left_at.at[:, pl.ds(at, rows)]
-        copies.append(pltpu.make_async_copy(part, left.at[step], sems.at[step]))
-        copies[-1].start()
+    )(planes, far(screened), density, later)
+
+
+def coarse_kernel(left, total, *refs):
+    *blocks, _, _, out = refs
     raw = total[...]
     for step, block in enumerate(blocks):
-        copies[step].wait()
         raw = raw + dot(left[step], block[...])
     pack(0.5 * (raw + raw.T), out)
 
 
-def coarse_block(planes, left, total, density_blocks, later):
-    width = left.shape[0]
+def coarse_block(left, total, density_blocks, later):
+    width = left.shape[1]
     return pl.pallas_call(
         coarse_kernel,
-        in_specs=[SMEM, HBM] + [VMEM] * (1 + len(density_blocks)) + [ANY] * 2,
+        in_specs=[VMEM] * (2 + len(density_blocks)) + [ANY] * 2,
         out_specs=VMEM,
         out_shape=shaped((width + 16, width // 2)),
-        scratch_shapes=[
-            pltpu.VMEM((len(density_blocks), width, density_blocks[0].shape[0]), BF16),
-            pltpu.SemaphoreType.DMA((len(density_blocks),)),
-        ],
         compiler_params=params(16),
-        cost_estimate=cost(width * width * left.shape[1], 4 * MIB),
+        cost_estimate=cost(1, 1),
         name="coarse_block",
-    )(planes, far(left), total, *density_blocks, *later)
+    )(left, total, *density_blocks, *later)
 
 
 def spread(table, each, same):
@@ -292,30 +281,34 @@
 
 def row_kernel(each, parts, order, table, vectors_at, *refs):
     kernels, refs = refs[:parts], refs[parts:]
-    _, out, vectors, mixed, sems = refs
+    _, out, vectors, mixed, held, mixer, sems = refs
     points, columns, width = vectors.shape
     count, rows = mixed.shape[:2]
-    pieces = sems.shape[0]
+    pieces = columns // (2 * each)
     group = columns // pieces
-    copies = loads(vectors_at, vectors, sems, pieces, axis=1)
+    copies = loads(vectors_at, vectors, sems, sems.shape[0])
     names = lax.broadcasted_iota(jnp.int32, (points, 1), 0)
     cols = points * each
     wide = dot(table[...], widening(names, cols, each))
-    mixer = spread(wide, each, same_column(count * rows * each, cols, each))
+    held[...] = spread(wide, each, same_column(count * rows * each, cols, each)).astype(F32)
+    size = rows * each
+    for c in range(count):
+        at = pl.ds(pl.multiple_of(order[c] * size, size), size)
+        mixer[c * size : (c + 1) * size] = held[at, :].astype(BF16)
+    finish(copies)
     for p in range(pieces):
-        copies[p].wait()
         at = slice(p * group, (p + 1) * group)
         value = vectors[:, at, :].astype(F32).reshape(points, group // each, each, width)
         parts = []
         for g in range(group // each):
             flat = value[:, g].reshape(cols, width).astype(BF16)
-            parts.append(dot(mixer, flat).reshape(count * rows, each, width))
+            parts.append(dot(mixer[...], flat).reshape(count * rows, each, width))
         joined = jnp.concatenate(parts, axis=1).astype(BF16)
         mixed[:, :, at, :] = joined.reshape(count, rows, group, width)
     total, c = 0.0, 0
     for kernel in kernels:
         for k in range(kernel.shape[0]):
-            total = total + dot(mixed[order[c]].reshape(out.shape), kernel[k])
+            total = total + dot(mixed[c].reshape(out.shape), kernel[k])
             c += 1
     out[...] = total.astype(BF16)
 
@@ -332,7 +325,9 @@
         scratch_shapes=[
             pltpu.VMEM(vectors.shape, BF16),
             pltpu.VMEM((count, rows, columns, width), BF16),
-            pltpu.SemaphoreType.DMA((columns // (2 * each),)),
+            pltpu.VMEM((count * rows * each, points * each), F32),
+            pltpu.VMEM((count * rows * each, points * each), BF16),
+            pltpu.SemaphoreType.DMA((4,)),
         ],
         compiler_params=params(24),
         cost_estimate=cost(1, 1),
@@ -619,7 +614,7 @@
     finish(stores)
 
 
-def last_call(blocks, order, trial, each):
+def last_call(blocks, at_hand, order, trial, each):
     total, columns = trial.shape
     rows, width = blocks[0].shape
     if each % 8 != 0:
@@ -630,7 +625,7 @@
     pieces = 8
     return pl.pallas_call(
         functools.partial(last_kernel, each),
-        in_specs=[SMEM, HBM] + [HBM] * len(blocks),
+        in_specs=[SMEM, HBM] + [ANY] * len(blocks),
         out_specs=HBM,
         out_shape=shaped((total, columns), F32),
         scratch_shapes=[
@@ -644,7 +639,7 @@
         compiler_params=params(24),
         cost_estimate=cost(2 * total * columns * width, 8 * MIB),
         name="last_call",
-    )(order, far(trial), *[far(block) for block in blocks])
+    )(order, far(trial), *[b if i in at_hand else far(b) for i, b in enumerate(blocks)])
 
 
 def shards(screened, density, transform, energy, trial, coarse_index, interp_weight, bands):
@@ -683,11 +678,11 @@
     planes = planes.astype(jnp.int32)
     first_point = row_index * row_points
     place = (first_point % col_points).astype(jnp.int32)
-    left, own = left_product(planes[:1], screened, density[0], my_start)
+    left, own = left_product(planes, screened, density[0], my_start)
     folded, shift, wanted = fold_call(
         place[None], row_points, transform, my_live, energies, my_trial, norm_scale, each
     )
-    packed = coarse_block(planes[1:], left, own, density_blocks[1:], (shift, my_start))
+    packed = coarse_block(left, own, density_blocks[1:], (shift, my_start))
     packed = plane_sum(packed).astype(BF16)
 
     table = dense.reshape(row_points, -1)
@@ -695,9 +690,9 @@
     table = table.reshape(row_points * chunks, packed.shape[1])
     start_blocks = plane_blocks(after(my_start, packed))
     blocks, _ = pair_blocks(jnp.concatenate([packed, table], axis=0), first=start_blocks[1:])
-    names = jnp.arange(fine_points, dtype=jnp.int32).reshape(pair_count, row_points)[order]
-    names = (jnp.repeat(names, chunks, axis=1) - col_index * col_points) % fine_points
-    names = names.reshape(-1, 1)
+    names = order[:, None] * row_points + jnp.arange(row_points * chunks)[None, :] // chunks
+    names = (names - col_index * col_points) % fine_points
+    names = names.astype(jnp.int32).reshape(-1, 1)
 
     early = unpack_call(blocks[: len(pair_moves()[0])], transitions)
     late, total, again, weights = first_call(
@@ -732,7 +727,9 @@
     first_step = plane_sum(row_part.astype(BF16)).astype(BF16)
     first_step = first_step.reshape(row_points * transitions, columns)
 
-    second_step = last_call(second_blocks, order, trial, each)
+    early_moves = pair_moves()[0]
+    at_hand = (early_moves.index((0, 0, 0)), early_moves.index((0, 1, 0)))
+    second_step = last_call(second_blocks, at_hand, order, trial, each)
     return (first_step, second_step)
 
 

time: 104 us -> 101 us (0.971)
  starting transfers between devices: 32.8 us -> 30.6 us
  local copies, waits for them, and re-layouts: 2.12 us -> 4.21 us
  waiting for transfers between devices: 18 us -> 16.1 us
  Pallas kernels: 46.3 us -> 45 us
    ppermute x12, waiting for transfers between devices: 10.7 us -> 7.53 us  [from_ahead(): lax.ppermute(value, axis, [((s + step) % count, s) for s in range(count)])]
    unnamed x42 -> x48, local copies, waits for them, and re-layouts: 1.04 us -> 3.13 us
    ppermute x24, waiting for transfers between devices: 7.31 us -> 8.57 us  [flipped(): return lax.ppermute(value, axis, [(s, s ^ bit) for s in range(count)])]
    ppermute x12, starting transfers between devices: 20 us -> 18.9 us  [from_ahead(): lax.ppermute(value, axis, [((s + step) % count, s) for s in range(count)])]
    ppermute x24, starting transfers between devices: 12.7 us -> 11.7 us  [flipped(): return lax.ppermute(value, axis, [(s, s ^ bit) for s in range(count)])]
  transfers between devices with their start and end apart: 36 -> 36, of which waited for: 17 -> 15; matrix products, arithmetic and copies ran while one was open for 3% -> 4% of each run, Pallas kernels for 33% -> 34%
where the time goes in v5:
time: 101 us
  Pallas kernels  45 us (45%)
  starting transfers between devices  30.6 us (30%)
  waiting for transfers between devices  16.1 us (16%)
  local copies, waits for them, and re-layouts  4.21 us (4%)
  other arithmetic  2.54 us (3%)
  matrix products  1.47 us (1%)
  between operations  1.11 us (1%)
    ppermute x12, starting transfers between devices, from_ahead(): lax.ppermute(value, axis, [((s + step) % count, s) for s in range(count)])  18.9 us
    ppermute x24, starting transfers between devices, flipped(): return lax.ppermute(value, axis, [(s, s ^ bit) for s in range(count)])  11.7 us
    pallas_call x1, Pallas kernels, left_product(): pl.pallas_call(left_kernel, in_specs=[SMEM, HBM, VMEM, ANY], out_specs=[V...  8.9 us
    ppermute x24, waiting for transfers between devices, flipped(): return lax.ppermute(value, axis, [(s, s ^ bit) for s in range(count)])  8.57 us
    ppermute x12, waiting for transfers between devices, from_ahead(): lax.ppermute(value, axis, [((s + step) % count, s) for s in range(count)])  7.53 us
    pallas_call x1, Pallas kernels, row_call(): pl.pallas_call(functools.partial(row_kernel, each, len(kernels)), in_spec...  6.55 us
    pallas_call x1, Pallas kernels, first_call(): pl.pallas_call(functools.partial(first_kernel, each, count, len(blocks)),...  5.64 us
    pallas_call x1, Pallas kernels, fold_call(): pl.pallas_call(functools.partial(fold_kernel, scale, each), in_specs=[SME...  5.42 us
  transfers between devices with their start and end apart: 36, of which 15 were waited for; matrix products, arithmetic and copies ran while one was open for 4% of the time, Pallas kernels for 34%

profile of v5, /device:TPU:0, one launch (start us, length us, event | category | flops | bytes accessed | tf_op | source)
XLA Modules:
  0.0 101.0 jit_solution(8514393915939952671)
XLA Ops:
  0.6 3.0 %collective-permute-start = (bf16[2048,256]{1,0:T(8,128)(2,1)}, bf16[2048,256]{1,0:T(8,128)(2,1)S(1)}, u32[]{:S(2)}, u32[]{:S(2)}) collective-permute-start(bf16[2048,256]{1,0:T(8,128)(2,1)} %bitcast.30), channel_id=1, source_target_pairs={{1,0},{0,1},{3,2},{2,3},{5,4},{4,5},{7,6},{6,7},{9,8},{8,9},{11,10... | collective-permute-start | bytes 3145736 | tf_op jit(solution)/shard_map/ppermute | solution.py:76
  3.7 0.7 compare_convert_fusion
  4.4 0.6 copy-done.6
  5.1 5.1 %start_call.1 = (bf16[32,128,256]{2,1,0:T(8,128)(2,1)}, bf16[256,256]{1,0:T(8,128)(2,1)S(1)}, f32[256,256]{1,0:T(8,128)S(1)}) custom-call(s32[1]{0:T(128)} %bitcast.1.index, bf16[8,128]{1,0:T(8,128)(2,1)S(1)} %fusion.5.pick, bf16[32,256,256]{2,1,0:T(8,128)(2,1)} %refs_4_.1, bf16[8192,128]{1,0:T(8,128)(2,1)} %trial_at.3, ...), custom_call_target="tpu_custom_call" | custom-call | flops 1 | bytes 1 | tf_op jit(solution)/shard_map/start_call/pallas_call | solution.py:387
  10.3 8.9 %left_product.1 = (bf16[1,256,2048]{2,1,0:T(8,128)(2,1)S(1)}, f32[256,256]{1,0:T(8,128)S(1)}) custom-call(s32[2]{0:T(128)S(1)} %pad_add_fusion.planes, bf16[1,2048,4096]{2,1,0:T(8,128)(2,1)} %screened_at.1, bf16[2048,256]{1,0:T(8,128)(2,1)S(1)} %bitcast.31, bf16[256,256]{1,0:T(8,128)(2,1)S(1)} %get-tuple-element.27._.refs_2_.refs_0_), custom_call_target="tpu_custom_call" | custom-call | flops 1 | bytes 1 | tf_op jit(solution)/shard_map/left_product/pallas_call | solution.py:192
  19.3 0.7 copy-done.4
  20.0 0.8 reshape.268.energy
  20.8 0.7 copy-done.2
  21.5 5.4 %fold_call.1 = (bf16[32,256,256]{2,1,0:T(8,128)(2,1)}, f32[256,256]{1,0:T(8,128)S(1)}, bf16[4,256,256]{2,1,0:T(8,128)(2,1)}) custom-call(s32[1]{0:T(128)} %bitcast.place, bf16[32,256,256]{2,1,0:T(8,128)(2,1)} %refs_4_.1, f32[32,256]{1,0:T(8,128)S(1)} %copy-done.2, f32[32,256]{1,0:T(8,128)S(1)} %reshape.268.energy, ...), custom_call_target="tpu_custom_call" | custom-call | flops 1 | bytes 1 | tf_op jit(solution)/shard_map/fold_call/pallas_call | solution.py:435
  27.0 0.5 coarse_block.1
  27.6 1.8 %collective-permute-start.1 = (bf16[272,128]{1,0:T(8,128)(2,1)S(1)}, bf16[272,128]{1,0:T(8,128)(2,1)S(1)}, u32[]{:S(2)}, u32[]{:S(2)}) collective-permute-start(bf16[272,128]{1,0:T(8,128)(2,1)S(1)} %coarse_block.1), channel_id=1, source_target_pairs={{1,0},{0,1},{3,2},{2,3},{5,4},{4,5},{7,6},{6,7},{9,8},{8,9},{11,10... | collective-permute-start | bytes 208904 | tf_op jit(solution)/shard_map/ppermute | solution.py:76
  29.5 2.5 %collective-permute-done.1 = bf16[272,128]{1,0:T(8,128)(2,1)S(1)} collective-permute-done((bf16[272,128]{1,0:T(8,128)(2,1)S(1)}, bf16[272,128]{1,0:T(8,128)(2,1)S(1)}, u32[]{:S(2)}, u32[]{:S(2)}) %collective-permute-start.1) | collective-permute-done | bytes 69664 | tf_op jit(solution)/shard_map/ppermute | solution.py:76
  32.0 1.9 %collective-permute-start.4 = (bf16[288,128]{1,0:T(8,128)(2,1)S(1)}, bf16[288,128]{1,0:T(8,128)(2,1)S(1)}, u32[]{:S(2)}, u32[]{:S(2)}) collective-permute-start(bf16[288,128]{1,0:T(8,128)(2,1)S(1)} %pad_maximum_fusion.refs_0_.refs_2_), channel_id=1, source_target_pairs={{24,0},{26,2},{28,4},{30,6},{0,8},{2,10},{4,12},{6,14},{8,16},{10,... | collective-permute-start | bytes 221192 | tf_op jit(solution)/shard_map/ppermute | solution.py:76
  33.8 2.3 %collective-permute-start.3 = (bf16[288,128]{1,0:T(8,128)(2,1)S(1)}, bf16[288,128]{1,0:T(8,128)(2,1)S(1)}, u32[]{:S(2)}, u32[]{:S(2)}) collective-permute-start(bf16[288,128]{1,0:T(8,128)(2,1)S(1)} %pad_maximum_fusion.refs_0_.refs_2_), channel_id=1, source_target_pairs={{8,0},{10,2},{12,4},{14,6},{16,8},{18,10},{20,12},{22,14},{24,16},... | collective-permute-start | bytes 221192 | tf_op jit(solution)/shard_map/ppermute | solution.py:76
  36.3 1.6 %collective-permute-start.6 = (bf16[288,128]{1,0:T(8,128)(2,1)S(1)}, bf16[288,128]{1,0:T(8,128)(2,1)S(1)}, u32[]{:S(2)}, u32[]{:S(2)}) collective-permute-start(bf16[288,128]{1,0:T(8,128)(2,1)S(1)} %pad_maximum_fusion.refs_0_.refs_2_), channel_id=1, source_target_pairs={{0,4},{2,6},{4,0},{6,2},{8,12},{10,14},{12,8},{14,10},{16,20},{18,... | collective-permute-start | bytes 221192 | tf_op jit(solution)/shard_map/ppermute | solution.py:81
  37.8 1.5 %collective-permute-start.2 = (bf16[256,256]{1,0:T(8,128)(2,1)S(1)}, bf16[256,256]{1,0:T(8,128)(2,1)S(1)}, u32[]{:S(2)}, u32[]{:S(2)}) collective-permute-start(bf16[256,256]{1,0:T(8,128)(2,1)S(1)} %get-tuple-element.27._.refs_2_.refs_0_), channel_id=1, source_target_pairs={{1,0},{0,1},{3,2},{2,3},{5,4},{4,5},{7,6},{6,7},{9,8},{8,9},{11,10... | collective-permute-start | bytes 393224 | tf_op jit(solution)/shard_map/ppermute | solution.py:76
  39.4 1.4 %collective-permute-start.5 = (bf16[288,128]{1,0:T(8,128)(2,1)S(1)}, bf16[288,128]{1,0:T(8,128)(2,1)S(1)}, u32[]{:S(2)}, u32[]{:S(2)}) collective-permute-start(bf16[288,128]{1,0:T(8,128)(2,1)S(1)} %pad_maximum_fusion.refs_0_.refs_2_), channel_id=1, source_target_pairs={{16,0},{18,2},{20,4},{22,6},{24,8},{26,10},{28,12},{30,14},{0,16},... | collective-permute-start | bytes 221192 | tf_op jit(solution)/shard_map/ppermute | solution.py:76
  40.8 1.5 %collective-permute-start.13 = (bf16[288,128]{1,0:T(8,128)(2,1)S(1)}, bf16[288,128]{1,0:T(8,128)(2,1)S(1)}, u32[]{:S(2)}, u32[]{:S(2)}) collective-permute-start(bf16[288,128]{1,0:T(8,128)(2,1)S(1)} %collective-permute-done.4.refs_2_.refs_4_), channel_id=1, source_target_pairs={{0,4},{2,6},{4,0},{6,2},{8,12},{10,14},{12,8},{14,10},{16,20},{18,... | collective-permute-start | bytes 221192 | tf_op jit(solution)/shard_map/ppermute | solution.py:81
  42.3 1.1 %collective-permute-done.2.refs_1_ = bf16[256,256]{1,0:T(8,128)(2,1)S(1)} collective-permute-done((bf16[256,256]{1,0:T(8,128)(2,1)S(1)}, bf16[256,256]{1,0:T(8,128)(2,1)S(1)}, u32[]{:S(2)}, u32[]{:S(2)}) %collective-permute-start.2) | collective-permute-done | bytes 131104 | tf_op jit(solution)/shard_map/ppermute | solution.py:76
  43.4 0.5 collective-permute-start.12
  43.9 1.4 %collective-permute-done.5.refs_3_.refs_5_ = bf16[288,128]{1,0:T(8,128)(2,1)S(1)} collective-permute-done((bf16[288,128]{1,0:T(8,128)(2,1)S(1)}, bf16[288,128]{1,0:T(8,128)(2,1)S(1)}, u32[]{:S(2)}, u32[]{:S(2)}) %collective-permute-start.5) | collective-permute-done | bytes 73760 | tf_op jit(solution)/shard_map/ppermute | solution.py:76
  45.4 1.1 %collective-permute-start.16 = (bf16[288,128]{1,0:T(8,128)(2,1)S(1)}, bf16[288,128]{1,0:T(8,128)(2,1)S(1)}, u32[]{:S(2)}, u32[]{:S(2)}) collective-permute-start(bf16[288,128]{1,0:T(8,128)(2,1)S(1)} %collective-permute-done.5.refs_3_.refs_5_), channel_id=1, source_target_pairs={{0,4},{2,6},{4,0},{6,2},{8,12},{10,14},{12,8},{14,10},{16,20},{18,... | collective-permute-start | bytes 221192 | tf_op jit(solution)/shard_map/ppermute | solution.py:81
  47.8 2.3 %collective-permute-done.16.refs_16_ = bf16[288,128]{1,0:T(8,128)(2,1)S(1)} collective-permute-done((bf16[288,128]{1,0:T(8,128)(2,1)S(1)}, bf16[288,128]{1,0:T(8,128)(2,1)S(1)}, u32[]{:S(2)}, u32[]{:S(2)}) %collective-permute-start.16) | collective-permute-done | bytes 73760 | tf_op jit(solution)/shard_map/ppermute | solution.py:81
  50.5 0.8 collective-permute-done.17.refs_17_
  51.3 5.6 %first_call.1 = (bf16[4,256,256]{2,1,0:T(8,128)(2,1)S(1)}, f32[2,256,128]{2,1,0:T(8,128)S(1)}, bf16[256,256]{1,0:T(8,128)(2,1)S(1)}, bf16[512,64]{1,0:T(8,128)(2,1)S(1)}) custom-call(s32[16]{0:T(128)S(1)} %stack.76.order, s32[256,1]{1,0:T(8,128)S(1)} %add_select_fusion.names, bf16[256,256]{1,0:T(8,128)(2,1)S(1)} %get-tuple-element.27._.refs_2_.refs_0_, ...), custom_call_target="tpu_custom_call" | custom-call | flops 1 | bytes 1 | tf_op jit(solution)/shard_map/first_call/pallas_call | solution.py:501
  57.0 1.2 %collective-permute-start.18 = (bf16[256,256]{1,0:T(8,128)(2,1)S(1)}, bf16[256,256]{1,0:T(8,128)(2,1)S(1)}, u32[]{:S(2)}, u32[]{:S(2)}) collective-permute-start(bf16[256,256]{1,0:T(8,128)(2,1)S(1)} %get-tuple-element.32.refs_0_), channel_id=1, source_target_pairs={{1,0},{0,1},{3,2},{2,3},{5,4},{4,5},{7,6},{6,7},{9,8},{8,9},{11,10... | collective-permute-start | bytes 393224 | tf_op jit(solution)/shard_map/ppermute | solution.py:76
  58.2 2.5 %energy_call.1.refs_6_ = f32[256,256]{1,0:T(8,128)S(1)} custom-call(bf16[32,256,256]{2,1,0:T(8,128)(2,1)} %refs_4_.1, f32[2,256,128]{2,1,0:T(8,128)S(1)} %get-tuple-element.34.total, f32[32,256]{1,0:T(8,128)S(1)} %copy-done.3, f32[32,256]{1,0:T(8,128)S(1)} %reshape.268.energy, f32[256,256]{1,0:T(8,128)S(1)} %get-tuple-element.21.my_trial.trial), custom_call_target="tpu_custom_call" | custom-call | flops 1 | bytes 1 | tf_op jit(solution)/shard_map/energy_call/pallas_call | solution.py:538
  60.7 1.9 %collective-permute-done.18.refs_1_ = bf16[256,256]{1,0:T(8,128)(2,1)S(1)} collective-permute-done((bf16[256,256]{1,0:T(8,128)(2,1)S(1)}, bf16[256,256]{1,0:T(8,128)(2,1)S(1)}, u32[]{:S(2)}, u32[]{:S(2)}) %collective-permute-start.18) | collective-permute-done | bytes 131104 | tf_op jit(solution)/shard_map/ppermute | solution.py:76
  62.6 4.7 %second_call.1.refs_0_ = bf16[256,256]{1,0:T(8,128)(2,1)S(1)} custom-call(bf16[512,64]{1,0:T(8,128)(2,1)S(1)} %get-tuple-element.31.weights, bf16[256,256]{1,0:T(8,128)(2,1)S(1)} %get-tuple-element.32.refs_0_, bf16[256,256]{1,0:T(8,128)(2,1)S(1)} %collective-permute-done.18.refs_1_, bf16[12,256,256]{2,1,0:T(8,128)(2,1)S(1)} %unpack_call.1.refs_18_.refs_2_.refs_0_, ...), custom_call_target="tpu_custom_call" | custom-call | flops 1 | bytes 1 | tf_op jit(solution)/shard_map/second_call/pallas_call | solution.py:571
  67.3 1.2 %collective-permute-start.19 = (bf16[4,256,256]{2,1,0:T(8,128)(2,1)S(1)}, bf16[4,256,256]{2,1,0:T(8,128)(2,1)S(1)}, u32[]{:S(2)}, u32[]{:S(2)}) collective-permute-start(bf16[4,256,256]{2,1,0:T(8,128)(2,1)S(1)} %copy-done.23), channel_id=1, source_target_pairs={{1,0},{0,1},{3,2},{2,3},{5,4},{4,5},{7,6},{6,7},{9,8},{8,9},{11,10... | collective-permute-start | bytes 1572872 | tf_op jit(solution)/shard_map/ppermute | solution.py:76
  68.5 1.5 %collective-permute-start.20 = (bf16[256,256]{1,0:T(8,128)(2,1)S(1)}, bf16[256,256]{1,0:T(8,128)(2,1)S(1)}, u32[]{:S(2)}, u32[]{:S(2)}) collective-permute-start(bf16[256,256]{1,0:T(8,128)(2,1)S(1)} %second_call.1.refs_0_), channel_id=1, source_target_pairs={{0,4},{2,6},{4,0},{6,2},{8,12},{10,14},{12,8},{14,10},{16,20},{18,... | collective-permute-start | bytes 393224 | tf_op jit(solution)/shard_map/ppermute | solution.py:81
  70.0 3.0 %collective-permute-start.22 = (bf16[256,256]{1,0:T(8,128)(2,1)S(1)}, bf16[256,256]{1,0:T(8,128)(2,1)S(1)}, u32[]{:S(2)}, u32[]{:S(2)}) collective-permute-start(bf16[256,256]{1,0:T(8,128)(2,1)S(1)} %second_call.1.refs_0_), channel_id=1, source_target_pairs={{8,0},{10,2},{12,4},{14,6},{16,8},{18,10},{20,12},{22,14},{24,16},... | collective-permute-start | bytes 393224 | tf_op jit(solution)/shard_map/ppermute | solution.py:76
  73.5 0.9 collective-permute-start.23
  74.3 6.5 %row_call.1 = bf16[512,256]{1,0:T(8,128)(2,1)S(1)} custom-call(s32[16]{0:T(128)S(1)} %stack.76.order, bf16[64,32]{1,0:T(8,128)(2,1)S(1)} %bitcast.33, bf16[32,128,256]{2,1,0:T(8,128)(2,1)} %get-tuple-element.36.vectors_at, bf16[12,256,256]{2,1,0:T(8,128)(2,1)S(1)} %unpack_call.1.refs_18_.refs_2_.refs_0_, ...), custom_call_target="tpu_custom_call" | custom-call | flops 1 | bytes 1 | tf_op jit(solution)/shard_map/row_call/pallas_call | solution.py:320
  80.9 1.3 %collective-permute-start.30 = (bf16[256,256]{1,0:T(8,128)(2,1)S(1)}, bf16[256,256]{1,0:T(8,128)(2,1)S(1)}, u32[]{:S(2)}, u32[]{:S(2)}) collective-permute-start(bf16[256,256]{1,0:T(8,128)(2,1)S(1)} %collective-permute-done.22.refs_1_), channel_id=1, source_target_pairs={{0,4},{2,6},{4,0},{6,2},{8,12},{10,14},{12,8},{14,10},{16,20},{18,... | collective-permute-start | bytes 393224 | tf_op jit(solution)/shard_map/ppermute | solution.py:81
  82.2 0.7 dynamic-slice_multiply_fusion
  82.9 0.5 collective-permute-done.24.refs_3_
  83.5 0.8 collective-permute-start.31
  84.4 1.6 %collective-permute-done.30.refs_10_ = bf16[256,256]{1,0:T(8,128)(2,1)S(1)} collective-permute-done((bf16[256,256]{1,0:T(8,128)(2,1)S(1)}, bf16[256,256]{1,0:T(8,128)(2,1)S(1)}, u32[]{:S(2)}, u32[]{:S(2)}) %collective-permute-start.30) | collective-permute-done | bytes 131104 | tf_op jit(solution)/shard_map/ppermute | solution.py:81
  86.0 1.2 %collective-permute-start.34 = (bf16[256,256]{1,0:T(8,128)(2,1)S(1)}, bf16[256,256]{1,0:T(8,128)(2,1)S(1)}, u32[]{:S(2)}, u32[]{:S(2)}) collective-permute-start(bf16[256,256]{1,0:T(8,128)(2,1)S(1)} %collective-permute-done.24.refs_3_), channel_id=1, source_target_pairs={{0,4},{2,6},{4,0},{6,2},{8,12},{10,14},{12,8},{14,10},{16,20},{18,... | collective-permute-start | bytes 393224 | tf_op jit(solution)/shard_map/ppermute | solution.py:81
  87.2 1.5 %fusion.1 = bf16[4,256,128]{2,1,0:T(8,128)(2,1)S(1)} fusion(bf16[4,128,256]{2,1,0:T(8,128)(2,1)S(1)} %bitcast.32, bf16[4,256,256]{2,1,0:T(8,128)(2,1)S(1)} %collective-permute-done.19, bf16[4,256,256]{2,1,0:T(8,128)(2,1)S(1)} %copy-done.23, pred[]{:T(512)S(6)} %eq.59, bf16[32,256,128]{2,1,0:T(8,128)(2,1)} %bitcast.34, s32[]{:T(128)S(6)} %select_n.145, ...), kind=kOutput, calls=%fused_computation.2 | convolution fusion | flops 68157440 | bytes 1843206 | tf_op jit(solution)/shard_map/ksv,kns->kvn/dot_general | solution.py:720
  88.7 0.6 collective-permute-start.21
  89.3 0.6 collective-permute-done.31.refs_11_
  90.4 1.8 %collective-permute-done.34.refs_14_ = bf16[256,256]{1,0:T(8,128)(2,1)S(1)} collective-permute-done((bf16[256,256]{1,0:T(8,128)(2,1)S(1)}, bf16[256,256]{1,0:T(8,128)(2,1)S(1)}, u32[]{:S(2)}, u32[]{:S(2)}) %collective-permute-start.34) | collective-permute-done | bytes 131104 | tf_op jit(solution)/shard_map/ppermute | solution.py:81
  92.7 0.8 collective-permute-done.33.refs_13_
  94.2 0.6 copy-done.20
  94.8 5.4 %last_call.1 = f32[8192,128]{1,0:T(8,128)} custom-call(s32[16]{0:T(128)S(1)} %stack.76.order, bf16[8192,128]{1,0:T(8,128)(2,1)} %trial_at.3, bf16[256,256]{1,0:T(8,128)(2,1)S(1)} %second_call.1.refs_0_, bf16[256,256]{1,0:T(8,128)(2,1)} %copy-done.7, bf16[256,256]{1,0:T(8,128)(2,1)} %copy-done.10, bf16[256,256]{1,0:T(8,128)(2,1)} %copy-done.8, ...), custom_call_target="tpu_custom_call" | custom-call | flops 1 | bytes 1 | tf_op jit(solution)/shard_map/last_call/pallas_call | solution.py:626
  100.2 0.8 add_convert_fusion
  (103 shorter events, 4.5 us)
Async XLA Ops:
  0.6 9.7 %copy-start = (bf16[1,2048,256]{2,1,0:T(8,128)(2,1)S(1)}, bf16[1,2048,256]{2,1,0:T(8,128)(2,1)}, u32[]{:S(2)}) copy-start(bf16[1,2048,256]{2,1,0:T(8,128)(2,1)} %param.9) | copy-start | bytes 3145732
  0.6 26.4 %collective-permute-start = (bf16[2048,256]{1,0:T(8,128)(2,1)}, bf16[2048,256]{1,0:T(8,128)(2,1)S(1)}, u32[]{:S(2)}, u32[]{:S(2)}) collective-permute-start(bf16[2048,256]{1,0:T(8,128)(2,1)} %bitcast.30), channel_id=1, source_target_pairs={{1,0},{0,1},{3,2},{2,3},{5,4},{4,5},{7,6},{6,7},{9,8},{8,9},{11,10... | collective-permute-start | bytes 3145736 | tf_op jit(solution)/shard_map/ppermute | solution.py:76
  5.0 5.3 %copy-start.1 = (f32[32,256]{1,0:T(8,128)}, f32[32,256]{1,0:T(8,128)S(1)}, u32[]{:S(2)}) copy-start(f32[32,256]{1,0:T(8,128)S(1)} %constant_dynamic-slice_fusion.1.live.refs_5_) | copy-start | bytes 98308
  20.0 7.0 %copy-start.22 = (bf16[4,32,4]{1,2,0:T(4,128)(2,1)S(1)}, bf16[4,32,4]{1,2,0:T(4,128)(2,1)}, u32[]{:S(2)}) copy-start(bf16[4,32,4]{1,2,0:T(4,128)(2,1)} %param.14) | copy-start | bytes 3076
  20.0 9.4 %copy-start.21 = (s32[4,32,4]{1,2,0:T(4,128)S(1)}, s32[4,32,4]{1,2,0:T(4,128)}, u32[]{:S(2)}) copy-start(s32[4,32,4]{1,2,0:T(4,128)} %param.13) | copy-start | bytes 6148
  21.5 5.5 %copy-start.5 = (f32[256,256]{1,0:T(8,128)S(1)}, f32[256,256]{1,0:T(8,128)}, u32[]{:S(2)}) copy-start(f32[256,256]{1,0:T(8,128)} %copy-done.4) | copy-start | bytes 786436
  27.6 4.4 %collective-permute-start.1 = (bf16[272,128]{1,0:T(8,128)(2,1)S(1)}, bf16[272,128]{1,0:T(8,128)(2,1)S(1)}, u32[]{:S(2)}, u32[]{:S(2)}) collective-permute-start(bf16[272,128]{1,0:T(8,128)(2,1)S(1)} %coarse_block.1), channel_id=1, source_target_pairs={{1,0},{0,1},{3,2},{2,3},{5,4},{4,5},{7,6},{6,7},{9,8},{8,9},{11,10... | collective-permute-start | bytes 208904 | tf_op jit(solution)/shard_map/ppermute | solution.py:76
  32.0 7.4 %collective-permute-start.4 = (bf16[288,128]{1,0:T(8,128)(2,1)S(1)}, bf16[288,128]{1,0:T(8,128)(2,1)S(1)}, u32[]{:S(2)}, u32[]{:S(2)}) collective-permute-start(bf16[288,128]{1,0:T(8,128)(2,1)S(1)} %pad_maximum_fusion.refs_0_.refs_2_), channel_id=1, source_target_pairs={{24,0},{26,2},{28,4},{30,6},{0,8},{2,10},{4,12},{6,14},{8,16},{10,... | collective-permute-start | bytes 221192 | tf_op jit(solution)/shard_map/ppermute | solution.py:76
  33.8 5.5 %collective-permute-start.3 = (bf16[288,128]{1,0:T(8,128)(2,1)S(1)}, bf16[288,128]{1,0:T(8,128)(2,1)S(1)}, u32[]{:S(2)}, u32[]{:S(2)}) collective-permute-start(bf16[288,128]{1,0:T(8,128)(2,1)S(1)} %pad_maximum_fusion.refs_0_.refs_2_), channel_id=1, source_target_pairs={{8,0},{10,2},{12,4},{14,6},{16,8},{18,10},{20,12},{22,14},{24,16},... | collective-permute-start | bytes 221192 | tf_op jit(solution)/shard_map/ppermute | solution.py:76
  36.2 9.2 %collective-permute-start.7 = (bf16[288,128]{1,0:T(8,128)(2,1)S(1)}, bf16[288,128]{1,0:T(8,128)(2,1)S(1)}, u32[]{:S(2)}, u32[]{:S(2)}) collective-permute-start(bf16[288,128]{1,0:T(8,128)(2,1)S(1)} %pad_maximum_fusion.refs_0_.refs_2_), channel_id=1, source_target_pairs={{0,2},{2,0},{4,6},{6,4},{8,10},{10,8},{12,14},{14,12},{16,18},{18,... | collective-permute-start | bytes 221192 | tf_op jit(solution)/shard_map/ppermute | solution.py:81
  36.3 6.0 %collective-permute-start.6 = (bf16[288,128]{1,0:T(8,128)(2,1)S(1)}, bf16[288,128]{1,0:T(8,128)(2,1)S(1)}, u32[]{:S(2)}, u32[]{:S(2)}) collective-permute-start(bf16[288,128]{1,0:T(8,128)(2,1)S(1)} %pad_maximum_fusion.refs_0_.refs_2_), channel_id=1, source_target_pairs={{0,4},{2,6},{4,0},{6,2},{8,12},{10,14},{12,8},{14,10},{16,20},{18,... | collective-permute-start | bytes 221192 | tf_op jit(solution)/shard_map/ppermute | solution.py:81
  37.8 5.6 %collective-permute-start.2 = (bf16[256,256]{1,0:T(8,128)(2,1)S(1)}, bf16[256,256]{1,0:T(8,128)(2,1)S(1)}, u32[]{:S(2)}, u32[]{:S(2)}) collective-permute-start(bf16[256,256]{1,0:T(8,128)(2,1)S(1)} %get-tuple-element.27._.refs_2_.refs_0_), channel_id=1, source_target_pairs={{1,0},{0,1},{3,2},{2,3},{5,4},{4,5},{7,6},{6,7},{9,8},{8,9},{11,10... | collective-permute-start | bytes 393224 | tf_op jit(solution)/shard_map/ppermute | solution.py:76
  39.4 6.0 %collective-permute-start.5 = (bf16[288,128]{1,0:T(8,128)(2,1)S(1)}, bf16[288,128]{1,0:T(8,128)(2,1)S(1)}, u32[]{:S(2)}, u32[]{:S(2)}) collective-permute-start(bf16[288,128]{1,0:T(8,128)(2,1)S(1)} %pad_maximum_fusion.refs_0_.refs_2_), channel_id=1, source_target_pairs={{16,0},{18,2},{20,4},{22,6},{24,8},{26,10},{28,12},{30,14},{0,16},... | collective-permute-start | bytes 221192 | tf_op jit(solution)/shard_map/ppermute | solution.py:76
  40.8 6.2 %collective-permute-start.13 = (bf16[288,128]{1,0:T(8,128)(2,1)S(1)}, bf16[288,128]{1,0:T(8,128)(2,1)S(1)}, u32[]{:S(2)}, u32[]{:S(2)}) collective-permute-start(bf16[288,128]{1,0:T(8,128)(2,1)S(1)} %collective-permute-done.4.refs_2_.refs_4_), channel_id=1, source_target_pairs={{0,4},{2,6},{4,0},{6,2},{8,12},{10,14},{12,8},{14,10},{16,20},{18,... | collective-permute-start | bytes 221192 | tf_op jit(solution)/shard_map/ppermute | solution.py:81
  42.3 5.0 %collective-permute-start.9 = (bf16[288,128]{1,0:T(8,128)(2,1)S(1)}, bf16[288,128]{1,0:T(8,128)(2,1)S(1)}, u32[]{:S(2)}, u32[]{:S(2)}) collective-permute-start(bf16[288,128]{1,0:T(8,128)(2,1)S(1)} %collective-permute-done.4.refs_2_.refs_4_), channel_id=1, source_target_pairs={{0,2},{2,0},{4,6},{6,4},{8,10},{10,8},{12,14},{14,12},{16,18},{18,... | collective-permute-start | bytes 221192 | tf_op jit(solution)/shard_map/ppermute | solution.py:81
  43.4 4.4 %collective-permute-start.12 = (bf16[288,128]{1,0:T(8,128)(2,1)S(1)}, bf16[288,128]{1,0:T(8,128)(2,1)S(1)}, u32[]{:S(2)}, u32[]{:S(2)}) collective-permute-start(bf16[288,128]{1,0:T(8,128)(2,1)S(1)} %collective-permute-done.3.refs_1_.refs_3_), channel_id=1, source_target_pairs={{0,4},{2,6},{4,0},{6,2},{8,12},{10,14},{12,8},{14,10},{16,20},{18,... | collective-permute-start | bytes 221192 | tf_op jit(solution)/shard_map/ppermute | solution.py:81
  45.4 1.3 %collective-permute-start.11 = (bf16[288,128]{1,0:T(8,128)(2,1)S(1)}, bf16[288,128]{1,0:T(8,128)(2,1)S(1)}, u32[]{:S(2)}, u32[]{:S(2)}) collective-permute-start(bf16[288,128]{1,0:T(8,128)(2,1)S(1)} %collective-permute-done.6.refs_4_.refs_6_), channel_id=1, source_target_pairs={{0,2},{2,0},{4,6},{6,4},{8,10},{10,8},{12,14},{14,12},{16,18},{18,... | collective-permute-start | bytes 221192 | tf_op jit(solution)/shard_map/ppermute | solution.py:81
  45.4 4.7 %collective-permute-start.16 = (bf16[288,128]{1,0:T(8,128)(2,1)S(1)}, bf16[288,128]{1,0:T(8,128)(2,1)S(1)}, u32[]{:S(2)}, u32[]{:S(2)}) collective-permute-start(bf16[288,128]{1,0:T(8,128)(2,1)S(1)} %collective-permute-done.5.refs_3_.refs_5_), channel_id=1, source_target_pairs={{0,4},{2,6},{4,0},{6,2},{8,12},{10,14},{12,8},{14,10},{16,20},{18,... | collective-permute-start | bytes 221192 | tf_op jit(solution)/shard_map/ppermute | solution.py:81
  46.7 3.4 %collective-permute-start.8 = (bf16[288,128]{1,0:T(8,128)(2,1)S(1)}, bf16[288,128]{1,0:T(8,128)(2,1)S(1)}, u32[]{:S(2)}, u32[]{:S(2)}) collective-permute-start(bf16[288,128]{1,0:T(8,128)(2,1)S(1)} %collective-permute-done.3.refs_1_.refs_3_), channel_id=1, source_target_pairs={{0,2},{2,0},{4,6},{6,4},{8,10},{10,8},{12,14},{14,12},{16,18},{18,... | collective-permute-start | bytes 221192 | tf_op jit(solution)/shard_map/ppermute | solution.py:81
  47.0 3.1 %collective-permute-start.10 = (bf16[288,128]{1,0:T(8,128)(2,1)S(1)}, bf16[288,128]{1,0:T(8,128)(2,1)S(1)}, u32[]{:S(2)}, u32[]{:S(2)}) collective-permute-start(bf16[288,128]{1,0:T(8,128)(2,1)S(1)} %collective-permute-done.5.refs_3_.refs_5_), channel_id=1, source_target_pairs={{0,2},{2,0},{4,6},{6,4},{8,10},{10,8},{12,14},{14,12},{16,18},{18,... | collective-permute-start | bytes 221192 | tf_op jit(solution)/shard_map/ppermute | solution.py:81
  47.3 3.2 %collective-permute-start.15 = (bf16[288,128]{1,0:T(8,128)(2,1)S(1)}, bf16[288,128]{1,0:T(8,128)(2,1)S(1)}, u32[]{:S(2)}, u32[]{:S(2)}) collective-permute-start(bf16[288,128]{1,0:T(8,128)(2,1)S(1)} %collective-permute-done.13.refs_11_.refs_13_), channel_id=1, source_target_pairs={{0,2},{2,0},{4,6},{6,4},{8,10},{10,8},{12,14},{14,12},{16,18},{18,... | collective-permute-start | bytes 221192 | tf_op jit(solution)/shard_map/ppermute | solution.py:81
  47.8 2.8 %collective-permute-start.14 = (bf16[288,128]{1,0:T(8,128)(2,1)S(1)}, bf16[288,128]{1,0:T(8,128)(2,1)S(1)}, u32[]{:S(2)}, u32[]{:S(2)}) collective-permute-start(bf16[288,128]{1,0:T(8,128)(2,1)S(1)} %collective-permute-done.12.refs_10_.refs_12_), channel_id=1, source_target_pairs={{0,2},{2,0},{4,6},{6,4},{8,10},{10,8},{12,14},{14,12},{16,18},{18,... | collective-permute-start | bytes 221192 | tf_op jit(solution)/shard_map/ppermute | solution.py:81
  50.1 1.3 %collective-permute-start.17 = (bf16[288,128]{1,0:T(8,128)(2,1)S(1)}, bf16[288,128]{1,0:T(8,128)(2,1)S(1)}, u32[]{:S(2)}, u32[]{:S(2)}) collective-permute-start(bf16[288,128]{1,0:T(8,128)(2,1)S(1)} %collective-permute-done.16.refs_16_), channel_id=1, source_target_pairs={{0,2},{2,0},{4,6},{6,4},{8,10},{10,8},{12,14},{14,12},{16,18},{18,... | collective-permute-start | bytes 221192 | tf_op jit(solution)/shard_map/ppermute | solution.py:81
  50.5 7.7 %copy-start.3 = (f32[32,256]{1,0:T(8,128)S(1)}, f32[32,256]{1,0:T(8,128)}, u32[]{:S(2)}) copy-start(f32[32,256]{1,0:T(8,128)} %copy-done.1) | copy-start | bytes 98308
  57.0 5.6 %collective-permute-start.18 = (bf16[256,256]{1,0:T(8,128)(2,1)S(1)}, bf16[256,256]{1,0:T(8,128)(2,1)S(1)}, u32[]{:S(2)}, u32[]{:S(2)}) collective-permute-start(bf16[256,256]{1,0:T(8,128)(2,1)S(1)} %get-tuple-element.32.refs_0_), channel_id=1, source_target_pairs={{1,0},{0,1},{3,2},{2,3},{5,4},{4,5},{7,6},{6,7},{9,8},{8,9},{11,10... | collective-permute-start | bytes 393224 | tf_op jit(solution)/shard_map/ppermute | solution.py:76
  60.7 6.6 %copy-start.23 = (bf16[4,256,256]{2,1,0:T(8,128)(2,1)S(1)}, bf16[4,256,256]{2,1,0:T(8,128)(2,1)}, u32[]{:S(2)}) copy-start(bf16[4,256,256]{2,1,0:T(8,128)(2,1)} %get-tuple-element.35) | copy-start | bytes 1572868
  67.3 19.9 %collective-permute-start.19 = (bf16[4,256,256]{2,1,0:T(8,128)(2,1)S(1)}, bf16[4,256,256]{2,1,0:T(8,128)(2,1)S(1)}, u32[]{:S(2)}, u32[]{:S(2)}) collective-permute-start(bf16[4,256,256]{2,1,0:T(8,128)(2,1)S(1)} %copy-done.23), channel_id=1, source_target_pairs={{1,0},{0,1},{3,2},{2,3},{5,4},{4,5},{7,6},{6,7},{9,8},{8,9},{11,10... | collective-permute-start | bytes 1572872 | tf_op jit(solution)/shard_map/ppermute | solution.py:76
  68.5 5.0 %collective-permute-start.20 = (bf16[256,256]{1,0:T(8,128)(2,1)S(1)}, bf16[256,256]{1,0:T(8,128)(2,1)S(1)}, u32[]{:S(2)}, u32[]{:S(2)}) collective-permute-start(bf16[256,256]{1,0:T(8,128)(2,1)S(1)} %second_call.1.refs_0_), channel_id=1, source_target_pairs={{0,4},{2,6},{4,0},{6,2},{8,12},{10,14},{12,8},{14,10},{16,20},{18,... | collective-permute-start | bytes 393224 | tf_op jit(solution)/shard_map/ppermute | solution.py:81
  70.0 10.9 %collective-permute-start.22 = (bf16[256,256]{1,0:T(8,128)(2,1)S(1)}, bf16[256,256]{1,0:T(8,128)(2,1)S(1)}, u32[]{:S(2)}, u32[]{:S(2)}) collective-permute-start(bf16[256,256]{1,0:T(8,128)(2,1)S(1)} %second_call.1.refs_0_), channel_id=1, source_target_pairs={{8,0},{10,2},{12,4},{14,6},{16,8},{18,10},{20,12},{22,14},{24,16},... | collective-permute-start | bytes 393224 | tf_op jit(solution)/shard_map/ppermute | solution.py:76
  73.0 10.4 %collective-permute-start.24 = (bf16[256,256]{1,0:T(8,128)(2,1)S(1)}, bf16[256,256]{1,0:T(8,128)(2,1)S(1)}, u32[]{:S(2)}, u32[]{:S(2)}) collective-permute-start(bf16[256,256]{1,0:T(8,128)(2,1)S(1)} %second_call.1.refs_0_), channel_id=1, source_target_pairs={{16,0},{18,2},{20,4},{22,6},{24,8},{26,10},{28,12},{30,14},{0,16},... | collective-permute-start | bytes 393224 | tf_op jit(solution)/shard_map/ppermute | solution.py:76
  73.1 11.1 %collective-permute-start.25 = (bf16[256,256]{1,0:T(8,128)(2,1)S(1)}, bf16[256,256]{1,0:T(8,128)(2,1)S(1)}, u32[]{:S(2)}, u32[]{:S(2)}) collective-permute-start(bf16[256,256]{1,0:T(8,128)(2,1)S(1)} %second_call.1.refs_0_), channel_id=1, source_target_pairs={{0,2},{2,0},{4,6},{6,4},{8,10},{10,8},{12,14},{14,12},{16,18},{18,... | collective-permute-start | bytes 393224 | tf_op jit(solution)/shard_map/ppermute | solution.py:81
  73.5 10.0 %collective-permute-start.23 = (bf16[256,256]{1,0:T(8,128)(2,1)S(1)}, bf16[256,256]{1,0:T(8,128)(2,1)S(1)}, u32[]{:S(2)}, u32[]{:S(2)}) collective-permute-start(bf16[256,256]{1,0:T(8,128)(2,1)S(1)} %second_call.1.refs_0_), channel_id=1, source_target_pairs={{24,0},{26,2},{28,4},{30,6},{0,8},{2,10},{4,12},{6,14},{8,16},{10,... | collective-permute-start | bytes 393224 | tf_op jit(solution)/shard_map/ppermute | solution.py:76
  80.9 12.8 %copy-start.7 = (bf16[256,256]{1,0:T(8,128)(2,1)}, bf16[256,256]{1,0:T(8,128)(2,1)S(1)}, u32[]{:S(2)}) copy-start(bf16[256,256]{1,0:T(8,128)(2,1)S(1)} %collective-permute-done.22.refs_1_) | copy-start | bytes 393220
  80.9 5.0 %collective-permute-start.30 = (bf16[256,256]{1,0:T(8,128)(2,1)S(1)}, bf16[256,256]{1,0:T(8,128)(2,1)S(1)}, u32[]{:S(2)}, u32[]{:S(2)}) collective-permute-start(bf16[256,256]{1,0:T(8,128)(2,1)S(1)} %collective-permute-done.22.refs_1_), channel_id=1, source_target_pairs={{0,4},{2,6},{4,0},{6,2},{8,12},{10,14},{12,8},{14,10},{16,20},{18,... | collective-permute-start | bytes 393224 | tf_op jit(solution)/shard_map/ppermute | solution.py:81
  83.5 10.3 %copy-start.8 = (bf16[256,256]{1,0:T(8,128)(2,1)}, bf16[256,256]{1,0:T(8,128)(2,1)S(1)}, u32[]{:S(2)}) copy-start(bf16[256,256]{1,0:T(8,128)(2,1)S(1)} %collective-permute-done.24.refs_3_) | copy-start | bytes 393220
  83.5 5.2 %collective-permute-start.26 = (bf16[256,256]{1,0:T(8,128)(2,1)S(1)}, bf16[256,256]{1,0:T(8,128)(2,1)S(1)}, u32[]{:S(2)}, u32[]{:S(2)}) collective-permute-start(bf16[256,256]{1,0:T(8,128)(2,1)S(1)} %collective-permute-done.22.refs_1_), channel_id=1, source_target_pairs={{0,2},{2,0},{4,6},{6,4},{8,10},{10,8},{12,14},{14,12},{16,18},{18,... | collective-permute-start | bytes 393224 | tf_op jit(solution)/shard_map/ppermute | solution.py:81
  83.5 10.3 %copy-start.10 = (bf16[256,256]{1,0:T(8,128)(2,1)}, bf16[256,256]{1,0:T(8,128)(2,1)S(1)}, u32[]{:S(2)}) copy-start(bf16[256,256]{1,0:T(8,128)(2,1)S(1)} %collective-permute-done.23.refs_2_) | copy-start | bytes 393220
  83.5 6.4 %collective-permute-start.31 = (bf16[256,256]{1,0:T(8,128)(2,1)S(1)}, bf16[256,256]{1,0:T(8,128)(2,1)S(1)}, u32[]{:S(2)}, u32[]{:S(2)}) collective-permute-start(bf16[256,256]{1,0:T(8,128)(2,1)S(1)} %collective-permute-done.23.refs_2_), channel_id=1, source_target_pairs={{0,4},{2,6},{4,0},{6,2},{8,12},{10,14},{12,8},{14,10},{16,20},{18,... | collective-permute-start | bytes 393224 | tf_op jit(solution)/shard_map/ppermute | solution.py:81
  84.2 9.5 %copy-start.9 = (bf16[256,256]{1,0:T(8,128)(2,1)}, bf16[256,256]{1,0:T(8,128)(2,1)S(1)}, u32[]{:S(2)}) copy-start(bf16[256,256]{1,0:T(8,128)(2,1)S(1)} %collective-permute-done.25.refs_5_) | copy-start | bytes 393220
  84.2 5.6 %collective-permute-start.27 = (bf16[256,256]{1,0:T(8,128)(2,1)S(1)}, bf16[256,256]{1,0:T(8,128)(2,1)S(1)}, u32[]{:S(2)}, u32[]{:S(2)}) collective-permute-start(bf16[256,256]{1,0:T(8,128)(2,1)S(1)} %collective-permute-done.23.refs_2_), channel_id=1, source_target_pairs={{0,2},{2,0},{4,6},{6,4},{8,10},{10,8},{12,14},{14,12},{16,18},{18,... | collective-permute-start | bytes 393224 | tf_op jit(solution)/shard_map/ppermute | solution.py:81
  86.0 7.8 %copy-start.11 = (bf16[256,256]{1,0:T(8,128)(2,1)}, bf16[256,256]{1,0:T(8,128)(2,1)S(1)}, u32[]{:S(2)}) copy-start(bf16[256,256]{1,0:T(8,128)(2,1)S(1)} %collective-permute-done.30.refs_10_) | copy-start | bytes 393220
  86.0 6.2 %collective-permute-start.34 = (bf16[256,256]{1,0:T(8,128)(2,1)S(1)}, bf16[256,256]{1,0:T(8,128)(2,1)S(1)}, u32[]{:S(2)}, u32[]{:S(2)}) collective-permute-start(bf16[256,256]{1,0:T(8,128)(2,1)S(1)} %collective-permute-done.24.refs_3_), channel_id=1, source_target_pairs={{0,4},{2,6},{4,0},{6,2},{8,12},{10,14},{12,8},{14,10},{16,20},{18,... | collective-permute-start | bytes 393224 | tf_op jit(solution)/shard_map/ppermute | solution.py:81
  87.2 5.0 %collective-permute-start.28 = (bf16[256,256]{1,0:T(8,128)(2,1)S(1)}, bf16[256,256]{1,0:T(8,128)(2,1)S(1)}, u32[]{:S(2)}, u32[]{:S(2)}) collective-permute-start(bf16[256,256]{1,0:T(8,128)(2,1)S(1)} %collective-permute-done.24.refs_3_), channel_id=1, source_target_pairs={{0,2},{2,0},{4,6},{6,4},{8,10},{10,8},{12,14},{14,12},{16,18},{18,... | collective-permute-start | bytes 393224 | tf_op jit(solution)/shard_map/ppermute | solution.py:81
  88.7 11.5 %collective-permute-start.21 = (bf16[4,256,128]{2,1,0:T(8,128)(2,1)S(1)}, bf16[4,256,128]{2,1,0:T(8,128)(2,1)S(1)}, u32[]{:S(2)}, u32[]{:S(2)}) collective-permute-start(bf16[4,256,128]{2,1,0:T(8,128)(2,1)S(1)} %fusion.1), channel_id=1, source_target_pairs={{1,0},{0,1},{3,2},{2,3},{5,4},{4,5},{7,6},{6,7},{9,8},{8,9},{11,10... | collective-permute-start | bytes 786440 | tf_op jit(solution)/shard_map/ppermute | solution.py:76
  89.8 2.9 %collective-permute-start.29 = (bf16[256,256]{1,0:T(8,128)(2,1)S(1)}, bf16[256,256]{1,0:T(8,128)(2,1)S(1)}, u32[]{:S(2)}, u32[]{:S(2)}) collective-permute-start(bf16[256,256]{1,0:T(8,128)(2,1)S(1)} %collective-permute-done.20.refs_2_.refs_4_), channel_id=1, source_target_pairs={{0,2},{2,0},{4,6},{6,4},{8,10},{10,8},{12,14},{14,12},{16,18},{18,... | collective-permute-start | bytes 393224 | tf_op jit(solution)/shard_map/ppermute | solution.py:81
  89.9 2.9 %collective-permute-start.32 = (bf16[256,256]{1,0:T(8,128)(2,1)S(1)}, bf16[256,256]{1,0:T(8,128)(2,1)S(1)}, u32[]{:S(2)}, u32[]{:S(2)}) collective-permute-start(bf16[256,256]{1,0:T(8,128)(2,1)S(1)} %collective-permute-done.30.refs_10_), channel_id=1, source_target_pairs={{0,2},{2,0},{4,6},{6,4},{8,10},{10,8},{12,14},{14,12},{16,18},{18,... | collective-permute-start | bytes 393224 | tf_op jit(solution)/shard_map/ppermute | solution.py:81
  92.2 1.3 %collective-permute-start.33 = (bf16[256,256]{1,0:T(8,128)(2,1)S(1)}, bf16[256,256]{1,0:T(8,128)(2,1)S(1)}, u32[]{:S(2)}, u32[]{:S(2)}) collective-permute-start(bf16[256,256]{1,0:T(8,128)(2,1)S(1)} %collective-permute-done.31.refs_11_), channel_id=1, source_target_pairs={{0,2},{2,0},{4,6},{6,4},{8,10},{10,8},{12,14},{14,12},{16,18},{18,... | collective-permute-start | bytes 393224 | tf_op jit(solution)/shard_map/ppermute | solution.py:81
  92.2 1.5 %collective-permute-start.35 = (bf16[256,256]{1,0:T(8,128)(2,1)S(1)}, bf16[256,256]{1,0:T(8,128)(2,1)S(1)}, u32[]{:S(2)}, u32[]{:S(2)}) collective-permute-start(bf16[256,256]{1,0:T(8,128)(2,1)S(1)} %collective-permute-done.34.refs_14_), channel_id=1, source_target_pairs={{0,2},{2,0},{4,6},{6,4},{8,10},{10,8},{12,14},{14,12},{16,18},{18,... | collective-permute-start | bytes 393224 | tf_op jit(solution)/shard_map/ppermute | solution.py:81
  (12 other events, 21.7 us)

commit v6 on v5

--- a/solution.py
+++ b/solution.py
@@ -587,16 +587,11 @@
 
 
 def last_kernel(each, order, trial_at, *refs):
-    *blocks, out_at, held, trial, out, in_sems, out_sems, sems = refs
+    *blocks, out_at, held, trial, out, in_sems, out_sems = refs
     pieces = out_sems.shape[0]
-    copies = [
-        pltpu.make_async_copy(block, held.at[order[r]], sems.at[r])
-        for r, block in enumerate(blocks)
-    ]
-    for copy in copies:
-        copy.start()
     load_trial = loads(trial_at, trial, in_sems, pieces)
-    finish(copies)
+    for r, block in enumerate(blocks):
+        held[order[r]] = block[...]
     width, columns = held.shape[2], trial.shape[1]
     points = trial.shape[0] // width // pieces
     stores = []
@@ -614,7 +609,7 @@
     finish(stores)
 
 
-def last_call(blocks, at_hand, order, trial, each):
+def last_call(blocks, order, trial, each):
     total, columns = trial.shape
     rows, width = blocks[0].shape
     if each % 8 != 0:
@@ -625,7 +620,7 @@
     pieces = 8
     return pl.pallas_call(
         functools.partial(last_kernel, each),
-        in_specs=[SMEM, HBM] + [ANY] * len(blocks),
+        in_specs=[SMEM, HBM] + [VMEM] * len(blocks),
         out_specs=HBM,
         out_shape=shaped((total, columns), F32),
         scratch_shapes=[
@@ -634,12 +629,11 @@
             pltpu.VMEM((total, columns), F32),
             pltpu.SemaphoreType.DMA((pieces,)),
             pltpu.SemaphoreType.DMA((pieces,)),
-            pltpu.SemaphoreType.DMA((len(blocks),)),
         ],
         compiler_params=params(24),
         cost_estimate=cost(2 * total * columns * width, 8 * MIB),
         name="last_call",
-    )(order, far(trial), *[b if i in at_hand else far(b) for i, b in enumerate(blocks)])
+    )(order, far(trial), *blocks)
 
 
 def shards(screened, density, transform, energy, trial, coarse_index, interp_weight, bands):
@@ -727,9 +721,7 @@
     first_step = plane_sum(row_part.astype(BF16)).astype(BF16)
     first_step = first_step.reshape(row_points * transitions, columns)
 
-    early_moves = pair_moves()[0]
-    at_hand = (early_moves.index((0, 0, 0)), early_moves.index((0, 1, 0)))
-    second_step = last_call(second_blocks, at_hand, order, trial, each)
+    second_step = last_call(second_blocks, order, trial, each)
     return (first_step, second_step)
 
 

time: 101 us -> 98.7 us (0.977)
  Pallas kernels: 45 us -> 43.4 us
  local copies, waits for them, and re-layouts: 4.21 us -> 3.18 us
    pallas_call x1, Pallas kernels: 5.35 us -> 3.78 us  [last_call(): pl.pallas_call(functools.partial(last_kernel, each), in_specs=[SMEM, HBM]...]
    unnamed x48 -> x20, local copies, waits for them, and re-layouts: 3.13 us -> 2.1 us
  transfers between devices with their start and end apart: 36 -> 36, of which waited for: 15 -> 14; matrix products, arithmetic and copies ran while one was open for 4% -> 4% of each run, Pallas kernels for 34% -> 33%
where the time goes in v6:
time: 98.7 us; the launch traced here: 98.3 us
  Pallas kernels  43.4 us (44%)
  starting transfers between devices  30.6 us (31%)
  waiting for transfers between devices  16.1 us (16%)
  local copies, waits for them, and re-layouts  3.18 us (3%)
  other arithmetic  2.54 us (3%)
  matrix products  1.47 us (1%)
    ppermute x12, starting transfers between devices, from_ahead(): lax.ppermute(value, axis, [((s + step) % count, s) for s in range(count)])  18.9 us
    ppermute x24, starting transfers between devices, flipped(): return lax.ppermute(value, axis, [(s, s ^ bit) for s in range(count)])  11.7 us
    pallas_call x1, Pallas kernels, left_product(): pl.pallas_call(left_kernel, in_specs=[SMEM, HBM, VMEM, ANY], out_specs=[V...  8.9 us
    ppermute x24, waiting for transfers between devices, flipped(): return lax.ppermute(value, axis, [(s, s ^ bit) for s in range(count)])  8.6 us
    ppermute x12, waiting for transfers between devices, from_ahead(): lax.ppermute(value, axis, [((s + step) % count, s) for s in range(count)])  7.51 us
    pallas_call x1, Pallas kernels, row_call(): pl.pallas_call(functools.partial(row_kernel, each, len(kernels)), in_spec...  6.55 us
    pallas_call x1, Pallas kernels, first_call(): pl.pallas_call(functools.partial(first_kernel, each, count, len(blocks)),...  5.64 us
    pallas_call x1, Pallas kernels, fold_call(): pl.pallas_call(functools.partial(fold_kernel, scale, each), in_specs=[SME...  5.43 us
  transfers between devices with their start and end apart: 36, of which 14 were waited for; matrix products, arithmetic and copies ran while one was open for 4% of the time, Pallas kernels for 33%

profile of v6, /device:TPU:0, one launch (start us, length us, event | category | flops | bytes accessed | tf_op | source)
XLA Modules:
  0.0 98.3 jit_solution(2890326502724897673)
XLA Ops:
  0.6 3.0 %collective-permute-start = (bf16[2048,256]{1,0:T(8,128)(2,1)}, bf16[2048,256]{1,0:T(8,128)(2,1)S(1)}, u32[]{:S(2)}, u32[]{:S(2)}) collective-permute-start(bf16[2048,256]{1,0:T(8,128)(2,1)} %bitcast.30), channel_id=1, source_target_pairs={{1,0},{0,1},{3,2},{2,3},{5,4},{4,5},{7,6},{6,7},{9,8},{8,9},{11,10... | collective-permute-start | bytes 3145736 | tf_op jit(solution)/shard_map/ppermute | solution.py:76
  3.7 0.7 compare_convert_fusion
  4.4 0.6 copy-done.6
  5.1 5.1 %start_call.1 = (bf16[32,128,256]{2,1,0:T(8,128)(2,1)}, bf16[256,256]{1,0:T(8,128)(2,1)S(1)}, f32[256,256]{1,0:T(8,128)S(1)}) custom-call(s32[1]{0:T(128)} %bitcast.1.index, bf16[8,128]{1,0:T(8,128)(2,1)S(1)} %fusion.5.pick, bf16[32,256,256]{2,1,0:T(8,128)(2,1)} %refs_4_.1, bf16[8192,128]{1,0:T(8,128)(2,1)} %trial_at.3, ...), custom_call_target="tpu_custom_call" | custom-call | flops 1 | bytes 1 | tf_op jit(solution)/shard_map/start_call/pallas_call | solution.py:387
  10.4 8.9 %left_product.1 = (bf16[1,256,2048]{2,1,0:T(8,128)(2,1)S(1)}, f32[256,256]{1,0:T(8,128)S(1)}) custom-call(s32[2]{0:T(128)S(1)} %pad_add_fusion.planes, bf16[1,2048,4096]{2,1,0:T(8,128)(2,1)} %screened_at.1, bf16[2048,256]{1,0:T(8,128)(2,1)S(1)} %bitcast.31, bf16[256,256]{1,0:T(8,128)(2,1)S(1)} %get-tuple-element.27._.refs_2_.refs_0_), custom_call_target="tpu_custom_call" | custom-call | flops 1 | bytes 1 | tf_op jit(solution)/shard_map/left_product/pallas_call | solution.py:192
  19.3 0.7 copy-done.4
  20.0 0.8 reshape.268.energy
  20.8 0.7 copy-done.2
  21.5 5.4 %fold_call.1 = (bf16[32,256,256]{2,1,0:T(8,128)(2,1)}, f32[256,256]{1,0:T(8,128)S(1)}, bf16[4,256,256]{2,1,0:T(8,128)(2,1)}) custom-call(s32[1]{0:T(128)} %bitcast.place, bf16[32,256,256]{2,1,0:T(8,128)(2,1)} %refs_4_.1, f32[32,256]{1,0:T(8,128)S(1)} %copy-done.2, f32[32,256]{1,0:T(8,128)S(1)} %reshape.268.energy, ...), custom_call_target="tpu_custom_call" | custom-call | flops 1 | bytes 1 | tf_op jit(solution)/shard_map/fold_call/pallas_call | solution.py:435
  27.0 0.5 coarse_block.1
  27.6 1.8 %collective-permute-start.1 = (bf16[272,128]{1,0:T(8,128)(2,1)S(1)}, bf16[272,128]{1,0:T(8,128)(2,1)S(1)}, u32[]{:S(2)}, u32[]{:S(2)}) collective-permute-start(bf16[272,128]{1,0:T(8,128)(2,1)S(1)} %coarse_block.1), channel_id=1, source_target_pairs={{1,0},{0,1},{3,2},{2,3},{5,4},{4,5},{7,6},{6,7},{9,8},{8,9},{11,10... | collective-permute-start | bytes 208904 | tf_op jit(solution)/shard_map/ppermute | solution.py:76
  29.5 2.5 %collective-permute-done.1 = bf16[272,128]{1,0:T(8,128)(2,1)S(1)} collective-permute-done((bf16[272,128]{1,0:T(8,128)(2,1)S(1)}, bf16[272,128]{1,0:T(8,128)(2,1)S(1)}, u32[]{:S(2)}, u32[]{:S(2)}) %collective-permute-start.1) | collective-permute-done | bytes 69664 | tf_op jit(solution)/shard_map/ppermute | solution.py:76
  32.0 1.9 %collective-permute-start.4 = (bf16[288,128]{1,0:T(8,128)(2,1)S(1)}, bf16[288,128]{1,0:T(8,128)(2,1)S(1)}, u32[]{:S(2)}, u32[]{:S(2)}) collective-permute-start(bf16[288,128]{1,0:T(8,128)(2,1)S(1)} %pad_maximum_fusion.refs_0_.refs_2_), channel_id=1, source_target_pairs={{24,0},{26,2},{28,4},{30,6},{0,8},{2,10},{4,12},{6,14},{8,16},{10,... | collective-permute-start | bytes 221192 | tf_op jit(solution)/shard_map/ppermute | solution.py:76
  33.8 2.3 %collective-permute-start.3 = (bf16[288,128]{1,0:T(8,128)(2,1)S(1)}, bf16[288,128]{1,0:T(8,128)(2,1)S(1)}, u32[]{:S(2)}, u32[]{:S(2)}) collective-permute-start(bf16[288,128]{1,0:T(8,128)(2,1)S(1)} %pad_maximum_fusion.refs_0_.refs_2_), channel_id=1, source_target_pairs={{8,0},{10,2},{12,4},{14,6},{16,8},{18,10},{20,12},{22,14},{24,16},... | collective-permute-start | bytes 221192 | tf_op jit(solution)/shard_map/ppermute | solution.py:76
  36.3 1.6 %collective-permute-start.6 = (bf16[288,128]{1,0:T(8,128)(2,1)S(1)}, bf16[288,128]{1,0:T(8,128)(2,1)S(1)}, u32[]{:S(2)}, u32[]{:S(2)}) collective-permute-start(bf16[288,128]{1,0:T(8,128)(2,1)S(1)} %pad_maximum_fusion.refs_0_.refs_2_), channel_id=1, source_target_pairs={{0,4},{2,6},{4,0},{6,2},{8,12},{10,14},{12,8},{14,10},{16,20},{18,... | collective-permute-start | bytes 221192 | tf_op jit(solution)/shard_map/ppermute | solution.py:81
  37.8 1.5 %collective-permute-start.2 = (bf16[256,256]{1,0:T(8,128)(2,1)S(1)}, bf16[256,256]{1,0:T(8,128)(2,1)S(1)}, u32[]{:S(2)}, u32[]{:S(2)}) collective-permute-start(bf16[256,256]{1,0:T(8,128)(2,1)S(1)} %get-tuple-element.27._.refs_2_.refs_0_), channel_id=1, source_target_pairs={{1,0},{0,1},{3,2},{2,3},{5,4},{4,5},{7,6},{6,7},{9,8},{8,9},{11,10... | collective-permute-start | bytes 393224 | tf_op jit(solution)/shard_map/ppermute | solution.py:76
  39.4 1.4 %collective-permute-start.5 = (bf16[288,128]{1,0:T(8,128)(2,1)S(1)}, bf16[288,128]{1,0:T(8,128)(2,1)S(1)}, u32[]{:S(2)}, u32[]{:S(2)}) collective-permute-start(bf16[288,128]{1,0:T(8,128)(2,1)S(1)} %pad_maximum_fusion.refs_0_.refs_2_), channel_id=1, source_target_pairs={{16,0},{18,2},{20,4},{22,6},{24,8},{26,10},{28,12},{30,14},{0,16},... | collective-permute-start | bytes 221192 | tf_op jit(solution)/shard_map/ppermute | solution.py:76
  40.8 1.5 %collective-permute-start.13 = (bf16[288,128]{1,0:T(8,128)(2,1)S(1)}, bf16[288,128]{1,0:T(8,128)(2,1)S(1)}, u32[]{:S(2)}, u32[]{:S(2)}) collective-permute-start(bf16[288,128]{1,0:T(8,128)(2,1)S(1)} %collective-permute-done.4.refs_2_.refs_4_), channel_id=1, source_target_pairs={{0,4},{2,6},{4,0},{6,2},{8,12},{10,14},{12,8},{14,10},{16,20},{18,... | collective-permute-start | bytes 221192 | tf_op jit(solution)/shard_map/ppermute | solution.py:81
  42.3 1.1 %collective-permute-done.2.refs_1_ = bf16[256,256]{1,0:T(8,128)(2,1)S(1)} collective-permute-done((bf16[256,256]{1,0:T(8,128)(2,1)S(1)}, bf16[256,256]{1,0:T(8,128)(2,1)S(1)}, u32[]{:S(2)}, u32[]{:S(2)}) %collective-permute-start.2) | collective-permute-done | bytes 131104 | tf_op jit(solution)/shard_map/ppermute | solution.py:76
  43.4 0.5 collective-permute-start.12
  43.9 1.4 %collective-permute-done.5.refs_3_.refs_5_ = bf16[288,128]{1,0:T(8,128)(2,1)S(1)} collective-permute-done((bf16[288,128]{1,0:T(8,128)(2,1)S(1)}, bf16[288,128]{1,0:T(8,128)(2,1)S(1)}, u32[]{:S(2)}, u32[]{:S(2)}) %collective-permute-start.5) | collective-permute-done | bytes 73760 | tf_op jit(solution)/shard_map/ppermute | solution.py:76
  45.4 1.1 %collective-permute-start.16 = (bf16[288,128]{1,0:T(8,128)(2,1)S(1)}, bf16[288,128]{1,0:T(8,128)(2,1)S(1)}, u32[]{:S(2)}, u32[]{:S(2)}) collective-permute-start(bf16[288,128]{1,0:T(8,128)(2,1)S(1)} %collective-permute-done.5.refs_3_.refs_5_), channel_id=1, source_target_pairs={{0,4},{2,6},{4,0},{6,2},{8,12},{10,14},{12,8},{14,10},{16,20},{18,... | collective-permute-start | bytes 221192 | tf_op jit(solution)/shard_map/ppermute | solution.py:81
  47.8 2.3 %collective-permute-done.16.refs_16_ = bf16[288,128]{1,0:T(8,128)(2,1)S(1)} collective-permute-done((bf16[288,128]{1,0:T(8,128)(2,1)S(1)}, bf16[288,128]{1,0:T(8,128)(2,1)S(1)}, u32[]{:S(2)}, u32[]{:S(2)}) %collective-permute-start.16) | collective-permute-done | bytes 73760 | tf_op jit(solution)/shard_map/ppermute | solution.py:81
  50.5 0.8 collective-permute-done.17.refs_17_
  51.3 5.6 %first_call.1 = (bf16[4,256,256]{2,1,0:T(8,128)(2,1)S(1)}, f32[2,256,128]{2,1,0:T(8,128)S(1)}, bf16[256,256]{1,0:T(8,128)(2,1)S(1)}, bf16[512,64]{1,0:T(8,128)(2,1)S(1)}) custom-call(s32[16]{0:T(128)S(1)} %stack.76.order, s32[256,1]{1,0:T(8,128)S(1)} %add_select_fusion.names, bf16[256,256]{1,0:T(8,128)(2,1)S(1)} %get-tuple-element.27._.refs_2_.refs_0_, ...), custom_call_target="tpu_custom_call" | custom-call | flops 1 | bytes 1 | tf_op jit(solution)/shard_map/first_call/pallas_call | solution.py:501
  57.0 1.2 %collective-permute-start.18 = (bf16[256,256]{1,0:T(8,128)(2,1)S(1)}, bf16[256,256]{1,0:T(8,128)(2,1)S(1)}, u32[]{:S(2)}, u32[]{:S(2)}) collective-permute-start(bf16[256,256]{1,0:T(8,128)(2,1)S(1)} %get-tuple-element.32.refs_0_), channel_id=1, source_target_pairs={{1,0},{0,1},{3,2},{2,3},{5,4},{4,5},{7,6},{6,7},{9,8},{8,9},{11,10... | collective-permute-start | bytes 393224 | tf_op jit(solution)/shard_map/ppermute | solution.py:76
  58.2 2.5 %energy_call.1.refs_6_ = f32[256,256]{1,0:T(8,128)S(1)} custom-call(bf16[32,256,256]{2,1,0:T(8,128)(2,1)} %refs_4_.1, f32[2,256,128]{2,1,0:T(8,128)S(1)} %get-tuple-element.34.total, f32[32,256]{1,0:T(8,128)S(1)} %copy-done.3, f32[32,256]{1,0:T(8,128)S(1)} %reshape.268.energy, f32[256,256]{1,0:T(8,128)S(1)} %get-tuple-element.21.my_trial.trial), custom_call_target="tpu_custom_call" | custom-call | flops 1 | bytes 1 | tf_op jit(solution)/shard_map/energy_call/pallas_call | solution.py:538
  60.7 1.9 %collective-permute-done.18.refs_1_ = bf16[256,256]{1,0:T(8,128)(2,1)S(1)} collective-permute-done((bf16[256,256]{1,0:T(8,128)(2,1)S(1)}, bf16[256,256]{1,0:T(8,128)(2,1)S(1)}, u32[]{:S(2)}, u32[]{:S(2)}) %collective-permute-start.18) | collective-permute-done | bytes 131104 | tf_op jit(solution)/shard_map/ppermute | solution.py:76
  62.6 4.7 %second_call.1.refs_0_ = bf16[256,256]{1,0:T(8,128)(2,1)S(1)} custom-call(bf16[512,64]{1,0:T(8,128)(2,1)S(1)} %get-tuple-element.31.weights, bf16[256,256]{1,0:T(8,128)(2,1)S(1)} %get-tuple-element.32.refs_0_, bf16[256,256]{1,0:T(8,128)(2,1)S(1)} %collective-permute-done.18.refs_1_, bf16[12,256,256]{2,1,0:T(8,128)(2,1)S(1)} %unpack_call.1.refs_18_.refs_2_.refs_0_, ...), custom_call_target="tpu_custom_call" | custom-call | flops 1 | bytes 1 | tf_op jit(solution)/shard_map/second_call/pallas_call | solution.py:571
  67.3 1.2 %collective-permute-start.19 = (bf16[4,256,256]{2,1,0:T(8,128)(2,1)S(1)}, bf16[4,256,256]{2,1,0:T(8,128)(2,1)S(1)}, u32[]{:S(2)}, u32[]{:S(2)}) collective-permute-start(bf16[4,256,256]{2,1,0:T(8,128)(2,1)S(1)} %copy-done.9), channel_id=1, source_target_pairs={{1,0},{0,1},{3,2},{2,3},{5,4},{4,5},{7,6},{6,7},{9,8},{8,9},{11,10... | collective-permute-start | bytes 1572872 | tf_op jit(solution)/shard_map/ppermute | solution.py:76
  68.5 1.5 %collective-permute-start.20 = (bf16[256,256]{1,0:T(8,128)(2,1)S(1)}, bf16[256,256]{1,0:T(8,128)(2,1)S(1)}, u32[]{:S(2)}, u32[]{:S(2)}) collective-permute-start(bf16[256,256]{1,0:T(8,128)(2,1)S(1)} %second_call.1.refs_0_), channel_id=1, source_target_pairs={{0,4},{2,6},{4,0},{6,2},{8,12},{10,14},{12,8},{14,10},{16,20},{18,... | collective-permute-start | bytes 393224 | tf_op jit(solution)/shard_map/ppermute | solution.py:81
  70.0 3.0 %collective-permute-start.22 = (bf16[256,256]{1,0:T(8,128)(2,1)S(1)}, bf16[256,256]{1,0:T(8,128)(2,1)S(1)}, u32[]{:S(2)}, u32[]{:S(2)}) collective-permute-start(bf16[256,256]{1,0:T(8,128)(2,1)S(1)} %second_call.1.refs_0_), channel_id=1, source_target_pairs={{8,0},{10,2},{12,4},{14,6},{16,8},{18,10},{20,12},{22,14},{24,16},... | collective-permute-start | bytes 393224 | tf_op jit(solution)/shard_map/ppermute | solution.py:76
  73.5 0.9 collective-permute-start.23
  74.3 6.5 %row_call.1 = bf16[512,256]{1,0:T(8,128)(2,1)S(1)} custom-call(s32[16]{0:T(128)S(1)} %stack.76.order, bf16[64,32]{1,0:T(8,128)(2,1)S(1)} %bitcast.33, bf16[32,128,256]{2,1,0:T(8,128)(2,1)} %get-tuple-element.36.vectors_at, bf16[12,256,256]{2,1,0:T(8,128)(2,1)S(1)} %unpack_call.1.refs_18_.refs_2_.refs_0_, ...), custom_call_target="tpu_custom_call" | custom-call | flops 1 | bytes 1 | tf_op jit(solution)/shard_map/row_call/pallas_call | solution.py:320
  80.9 1.3 %collective-permute-start.30 = (bf16[256,256]{1,0:T(8,128)(2,1)S(1)}, bf16[256,256]{1,0:T(8,128)(2,1)S(1)}, u32[]{:S(2)}, u32[]{:S(2)}) collective-permute-start(bf16[256,256]{1,0:T(8,128)(2,1)S(1)} %collective-permute-done.22.refs_1_), channel_id=1, source_target_pairs={{0,4},{2,6},{4,0},{6,2},{8,12},{10,14},{12,8},{14,10},{16,20},{18,... | collective-permute-start | bytes 393224 | tf_op jit(solution)/shard_map/ppermute | solution.py:81
  82.2 0.7 dynamic-slice_multiply_fusion
  82.9 0.5 collective-permute-done.24.refs_3_
  83.5 0.7 collective-permute-start.31
  84.4 1.6 %collective-permute-done.30.refs_10_ = bf16[256,256]{1,0:T(8,128)(2,1)S(1)} collective-permute-done((bf16[256,256]{1,0:T(8,128)(2,1)S(1)}, bf16[256,256]{1,0:T(8,128)(2,1)S(1)}, u32[]{:S(2)}, u32[]{:S(2)}) %collective-permute-start.30) | collective-permute-done | bytes 131104 | tf_op jit(solution)/shard_map/ppermute | solution.py:81
  85.9 1.2 %collective-permute-start.34 = (bf16[256,256]{1,0:T(8,128)(2,1)S(1)}, bf16[256,256]{1,0:T(8,128)(2,1)S(1)}, u32[]{:S(2)}, u32[]{:S(2)}) collective-permute-start(bf16[256,256]{1,0:T(8,128)(2,1)S(1)} %collective-permute-done.24.refs_3_), channel_id=1, source_target_pairs={{0,4},{2,6},{4,0},{6,2},{8,12},{10,14},{12,8},{14,10},{16,20},{18,... | collective-permute-start | bytes 393224 | tf_op jit(solution)/shard_map/ppermute | solution.py:81
  87.2 1.5 %fusion.1 = bf16[4,256,128]{2,1,0:T(8,128)(2,1)S(1)} fusion(bf16[4,128,256]{2,1,0:T(8,128)(2,1)S(1)} %bitcast.32, bf16[4,256,256]{2,1,0:T(8,128)(2,1)S(1)} %collective-permute-done.19, bf16[4,256,256]{2,1,0:T(8,128)(2,1)S(1)} %copy-done.9, pred[]{:T(512)S(6)} %eq.59, bf16[32,256,128]{2,1,0:T(8,128)(2,1)} %bitcast.34, s32[]{:T(128)S(6)} %select_n.145, ...), kind=kOutput, calls=%fused_computation.2 | convolution fusion | flops 68157440 | bytes 1843206 | tf_op jit(solution)/shard_map/ksv,kns->kvn/dot_general | solution.py:714
  88.7 0.6 collective-permute-start.21
  89.8 0.5 collective-permute-start.32
  90.3 1.9 %collective-permute-done.34.refs_14_ = bf16[256,256]{1,0:T(8,128)(2,1)S(1)} collective-permute-done((bf16[256,256]{1,0:T(8,128)(2,1)S(1)}, bf16[256,256]{1,0:T(8,128)(2,1)S(1)}, u32[]{:S(2)}, u32[]{:S(2)}) %collective-permute-start.34) | collective-permute-done | bytes 131104 | tf_op jit(solution)/shard_map/ppermute | solution.py:81
  92.2 0.5 collective-permute-start.35
  92.7 0.8 collective-permute-done.33.refs_13_
  93.7 3.8 %last_call.1 = f32[8192,128]{1,0:T(8,128)} custom-call(s32[16]{0:T(128)S(1)} %stack.76.order, bf16[8192,128]{1,0:T(8,128)(2,1)} %trial_at.3, bf16[256,256]{1,0:T(8,128)(2,1)S(1)} %second_call.1.refs_0_, bf16[256,256]{1,0:T(8,128)(2,1)S(1)} %collective-permute-done.22.refs_1_, bf16[256,256]{1,0:T(8,128)(2,1)S(1)} %collective-permute-done.23.refs_2_, ...), custom_call_target="tpu_custom_call" | custom-call | flops 1 | bytes 1 | tf_op jit(solution)/shard_map/last_call/pallas_call | solution.py:621
  97.5 0.8 add_convert_fusion
  (75 shorter events, 3.7 us)
Async XLA Ops:
  0.6 9.7 %copy-start = (bf16[1,2048,256]{2,1,0:T(8,128)(2,1)S(1)}, bf16[1,2048,256]{2,1,0:T(8,128)(2,1)}, u32[]{:S(2)}) copy-start(bf16[1,2048,256]{2,1,0:T(8,128)(2,1)} %param.9) | copy-start | bytes 3145732
  0.6 26.4 %collective-permute-start = (bf16[2048,256]{1,0:T(8,128)(2,1)}, bf16[2048,256]{1,0:T(8,128)(2,1)S(1)}, u32[]{:S(2)}, u32[]{:S(2)}) collective-permute-start(bf16[2048,256]{1,0:T(8,128)(2,1)} %bitcast.30), channel_id=1, source_target_pairs={{1,0},{0,1},{3,2},{2,3},{5,4},{4,5},{7,6},{6,7},{9,8},{8,9},{11,10... | collective-permute-start | bytes 3145736 | tf_op jit(solution)/shard_map/ppermute | solution.py:76
  4.4 0.6 copy-start.6
  5.0 5.3 %copy-start.1 = (f32[32,256]{1,0:T(8,128)}, f32[32,256]{1,0:T(8,128)S(1)}, u32[]{:S(2)}) copy-start(f32[32,256]{1,0:T(8,128)S(1)} %constant_dynamic-slice_fusion.1.live.refs_5_) | copy-start | bytes 98308
  19.3 0.7 copy-start.4
  20.0 7.0 %copy-start.8 = (bf16[4,32,4]{1,2,0:T(4,128)(2,1)S(1)}, bf16[4,32,4]{1,2,0:T(4,128)(2,1)}, u32[]{:S(2)}) copy-start(bf16[4,32,4]{1,2,0:T(4,128)(2,1)} %param.14) | copy-start | bytes 3076
  20.0 9.4 %copy-start.7 = (s32[4,32,4]{1,2,0:T(4,128)S(1)}, s32[4,32,4]{1,2,0:T(4,128)}, u32[]{:S(2)}) copy-start(s32[4,32,4]{1,2,0:T(4,128)} %param.13) | copy-start | bytes 6148
  20.8 0.8 copy-start.2
  21.5 5.5 %copy-start.5 = (f32[256,256]{1,0:T(8,128)S(1)}, f32[256,256]{1,0:T(8,128)}, u32[]{:S(2)}) copy-start(f32[256,256]{1,0:T(8,128)} %copy-done.4) | copy-start | bytes 786436
  27.6 4.4 %collective-permute-start.1 = (bf16[272,128]{1,0:T(8,128)(2,1)S(1)}, bf16[272,128]{1,0:T(8,128)(2,1)S(1)}, u32[]{:S(2)}, u32[]{:S(2)}) collective-permute-start(bf16[272,128]{1,0:T(8,128)(2,1)S(1)} %coarse_block.1), channel_id=1, source_target_pairs={{1,0},{0,1},{3,2},{2,3},{5,4},{4,5},{7,6},{6,7},{9,8},{8,9},{11,10... | collective-permute-start | bytes 208904 | tf_op jit(solution)/shard_map/ppermute | solution.py:76
  32.0 7.4 %collective-permute-start.4 = (bf16[288,128]{1,0:T(8,128)(2,1)S(1)}, bf16[288,128]{1,0:T(8,128)(2,1)S(1)}, u32[]{:S(2)}, u32[]{:S(2)}) collective-permute-start(bf16[288,128]{1,0:T(8,128)(2,1)S(1)} %pad_maximum_fusion.refs_0_.refs_2_), channel_id=1, source_target_pairs={{24,0},{26,2},{28,4},{30,6},{0,8},{2,10},{4,12},{6,14},{8,16},{10,... | collective-permute-start | bytes 221192 | tf_op jit(solution)/shard_map/ppermute | solution.py:76
  33.8 5.5 %collective-permute-start.3 = (bf16[288,128]{1,0:T(8,128)(2,1)S(1)}, bf16[288,128]{1,0:T(8,128)(2,1)S(1)}, u32[]{:S(2)}, u32[]{:S(2)}) collective-permute-start(bf16[288,128]{1,0:T(8,128)(2,1)S(1)} %pad_maximum_fusion.refs_0_.refs_2_), channel_id=1, source_target_pairs={{8,0},{10,2},{12,4},{14,6},{16,8},{18,10},{20,12},{22,14},{24,16},... | collective-permute-start | bytes 221192 | tf_op jit(solution)/shard_map/ppermute | solution.py:76
  36.2 9.2 %collective-permute-start.7 = (bf16[288,128]{1,0:T(8,128)(2,1)S(1)}, bf16[288,128]{1,0:T(8,128)(2,1)S(1)}, u32[]{:S(2)}, u32[]{:S(2)}) collective-permute-start(bf16[288,128]{1,0:T(8,128)(2,1)S(1)} %pad_maximum_fusion.refs_0_.refs_2_), channel_id=1, source_target_pairs={{0,2},{2,0},{4,6},{6,4},{8,10},{10,8},{12,14},{14,12},{16,18},{18,... | collective-permute-start | bytes 221192 | tf_op jit(solution)/shard_map/ppermute | solution.py:81
  36.3 6.0 %collective-permute-start.6 = (bf16[288,128]{1,0:T(8,128)(2,1)S(1)}, bf16[288,128]{1,0:T(8,128)(2,1)S(1)}, u32[]{:S(2)}, u32[]{:S(2)}) collective-permute-start(bf16[288,128]{1,0:T(8,128)(2,1)S(1)} %pad_maximum_fusion.refs_0_.refs_2_), channel_id=1, source_target_pairs={{0,4},{2,6},{4,0},{6,2},{8,12},{10,14},{12,8},{14,10},{16,20},{18,... | collective-permute-start | bytes 221192 | tf_op jit(solution)/shard_map/ppermute | solution.py:81
  37.8 5.6 %collective-permute-start.2 = (bf16[256,256]{1,0:T(8,128)(2,1)S(1)}, bf16[256,256]{1,0:T(8,128)(2,1)S(1)}, u32[]{:S(2)}, u32[]{:S(2)}) collective-permute-start(bf16[256,256]{1,0:T(8,128)(2,1)S(1)} %get-tuple-element.27._.refs_2_.refs_0_), channel_id=1, source_target_pairs={{1,0},{0,1},{3,2},{2,3},{5,4},{4,5},{7,6},{6,7},{9,8},{8,9},{11,10... | collective-permute-start | bytes 393224 | tf_op jit(solution)/shard_map/ppermute | solution.py:76
  39.4 6.0 %collective-permute-start.5 = (bf16[288,128]{1,0:T(8,128)(2,1)S(1)}, bf16[288,128]{1,0:T(8,128)(2,1)S(1)}, u32[]{:S(2)}, u32[]{:S(2)}) collective-permute-start(bf16[288,128]{1,0:T(8,128)(2,1)S(1)} %pad_maximum_fusion.refs_0_.refs_2_), channel_id=1, source_target_pairs={{16,0},{18,2},{20,4},{22,6},{24,8},{26,10},{28,12},{30,14},{0,16},... | collective-permute-start | bytes 221192 | tf_op jit(solution)/shard_map/ppermute | solution.py:76
  40.8 6.2 %collective-permute-start.13 = (bf16[288,128]{1,0:T(8,128)(2,1)S(1)}, bf16[288,128]{1,0:T(8,128)(2,1)S(1)}, u32[]{:S(2)}, u32[]{:S(2)}) collective-permute-start(bf16[288,128]{1,0:T(8,128)(2,1)S(1)} %collective-permute-done.4.refs_2_.refs_4_), channel_id=1, source_target_pairs={{0,4},{2,6},{4,0},{6,2},{8,12},{10,14},{12,8},{14,10},{16,20},{18,... | collective-permute-start | bytes 221192 | tf_op jit(solution)/shard_map/ppermute | solution.py:81
  42.3 5.0 %collective-permute-start.9 = (bf16[288,128]{1,0:T(8,128)(2,1)S(1)}, bf16[288,128]{1,0:T(8,128)(2,1)S(1)}, u32[]{:S(2)}, u32[]{:S(2)}) collective-permute-start(bf16[288,128]{1,0:T(8,128)(2,1)S(1)} %collective-permute-done.4.refs_2_.refs_4_), channel_id=1, source_target_pairs={{0,2},{2,0},{4,6},{6,4},{8,10},{10,8},{12,14},{14,12},{16,18},{18,... | collective-permute-start | bytes 221192 | tf_op jit(solution)/shard_map/ppermute | solution.py:81
  43.4 4.4 %collective-permute-start.12 = (bf16[288,128]{1,0:T(8,128)(2,1)S(1)}, bf16[288,128]{1,0:T(8,128)(2,1)S(1)}, u32[]{:S(2)}, u32[]{:S(2)}) collective-permute-start(bf16[288,128]{1,0:T(8,128)(2,1)S(1)} %collective-permute-done.3.refs_1_.refs_3_), channel_id=1, source_target_pairs={{0,4},{2,6},{4,0},{6,2},{8,12},{10,14},{12,8},{14,10},{16,20},{18,... | collective-permute-start | bytes 221192 | tf_op jit(solution)/shard_map/ppermute | solution.py:81
  45.4 1.3 %collective-permute-start.11 = (bf16[288,128]{1,0:T(8,128)(2,1)S(1)}, bf16[288,128]{1,0:T(8,128)(2,1)S(1)}, u32[]{:S(2)}, u32[]{:S(2)}) collective-permute-start(bf16[288,128]{1,0:T(8,128)(2,1)S(1)} %collective-permute-done.6.refs_4_.refs_6_), channel_id=1, source_target_pairs={{0,2},{2,0},{4,6},{6,4},{8,10},{10,8},{12,14},{14,12},{16,18},{18,... | collective-permute-start | bytes 221192 | tf_op jit(solution)/shard_map/ppermute | solution.py:81
  45.4 4.7 %collective-permute-start.16 = (bf16[288,128]{1,0:T(8,128)(2,1)S(1)}, bf16[288,128]{1,0:T(8,128)(2,1)S(1)}, u32[]{:S(2)}, u32[]{:S(2)}) collective-permute-start(bf16[288,128]{1,0:T(8,128)(2,1)S(1)} %collective-permute-done.5.refs_3_.refs_5_), channel_id=1, source_target_pairs={{0,4},{2,6},{4,0},{6,2},{8,12},{10,14},{12,8},{14,10},{16,20},{18,... | collective-permute-start | bytes 221192 | tf_op jit(solution)/shard_map/ppermute | solution.py:81
  46.7 3.4 %collective-permute-start.8 = (bf16[288,128]{1,0:T(8,128)(2,1)S(1)}, bf16[288,128]{1,0:T(8,128)(2,1)S(1)}, u32[]{:S(2)}, u32[]{:S(2)}) collective-permute-start(bf16[288,128]{1,0:T(8,128)(2,1)S(1)} %collective-permute-done.3.refs_1_.refs_3_), channel_id=1, source_target_pairs={{0,2},{2,0},{4,6},{6,4},{8,10},{10,8},{12,14},{14,12},{16,18},{18,... | collective-permute-start | bytes 221192 | tf_op jit(solution)/shard_map/ppermute | solution.py:81
  47.0 3.1 %collective-permute-start.10 = (bf16[288,128]{1,0:T(8,128)(2,1)S(1)}, bf16[288,128]{1,0:T(8,128)(2,1)S(1)}, u32[]{:S(2)}, u32[]{:S(2)}) collective-permute-start(bf16[288,128]{1,0:T(8,128)(2,1)S(1)} %collective-permute-done.5.refs_3_.refs_5_), channel_id=1, source_target_pairs={{0,2},{2,0},{4,6},{6,4},{8,10},{10,8},{12,14},{14,12},{16,18},{18,... | collective-permute-start | bytes 221192 | tf_op jit(solution)/shard_map/ppermute | solution.py:81
  47.3 3.2 %collective-permute-start.15 = (bf16[288,128]{1,0:T(8,128)(2,1)S(1)}, bf16[288,128]{1,0:T(8,128)(2,1)S(1)}, u32[]{:S(2)}, u32[]{:S(2)}) collective-permute-start(bf16[288,128]{1,0:T(8,128)(2,1)S(1)} %collective-permute-done.13.refs_11_.refs_13_), channel_id=1, source_target_pairs={{0,2},{2,0},{4,6},{6,4},{8,10},{10,8},{12,14},{14,12},{16,18},{18,... | collective-permute-start | bytes 221192 | tf_op jit(solution)/shard_map/ppermute | solution.py:81
  47.8 2.8 %collective-permute-start.14 = (bf16[288,128]{1,0:T(8,128)(2,1)S(1)}, bf16[288,128]{1,0:T(8,128)(2,1)S(1)}, u32[]{:S(2)}, u32[]{:S(2)}) collective-permute-start(bf16[288,128]{1,0:T(8,128)(2,1)S(1)} %collective-permute-done.12.refs_10_.refs_12_), channel_id=1, source_target_pairs={{0,2},{2,0},{4,6},{6,4},{8,10},{10,8},{12,14},{14,12},{16,18},{18,... | collective-permute-start | bytes 221192 | tf_op jit(solution)/shard_map/ppermute | solution.py:81
  50.1 1.3 %collective-permute-start.17 = (bf16[288,128]{1,0:T(8,128)(2,1)S(1)}, bf16[288,128]{1,0:T(8,128)(2,1)S(1)}, u32[]{:S(2)}, u32[]{:S(2)}) collective-permute-start(bf16[288,128]{1,0:T(8,128)(2,1)S(1)} %collective-permute-done.16.refs_16_), channel_id=1, source_target_pairs={{0,2},{2,0},{4,6},{6,4},{8,10},{10,8},{12,14},{14,12},{16,18},{18,... | collective-permute-start | bytes 221192 | tf_op jit(solution)/shard_map/ppermute | solution.py:81
  50.5 7.7 %copy-start.3 = (f32[32,256]{1,0:T(8,128)S(1)}, f32[32,256]{1,0:T(8,128)}, u32[]{:S(2)}) copy-start(f32[32,256]{1,0:T(8,128)} %copy-done.1) | copy-start | bytes 98308
  57.0 5.6 %collective-permute-start.18 = (bf16[256,256]{1,0:T(8,128)(2,1)S(1)}, bf16[256,256]{1,0:T(8,128)(2,1)S(1)}, u32[]{:S(2)}, u32[]{:S(2)}) collective-permute-start(bf16[256,256]{1,0:T(8,128)(2,1)S(1)} %get-tuple-element.32.refs_0_), channel_id=1, source_target_pairs={{1,0},{0,1},{3,2},{2,3},{5,4},{4,5},{7,6},{6,7},{9,8},{8,9},{11,10... | collective-permute-start | bytes 393224 | tf_op jit(solution)/shard_map/ppermute | solution.py:76
  60.7 6.6 %copy-start.9 = (bf16[4,256,256]{2,1,0:T(8,128)(2,1)S(1)}, bf16[4,256,256]{2,1,0:T(8,128)(2,1)}, u32[]{:S(2)}) copy-start(bf16[4,256,256]{2,1,0:T(8,128)(2,1)} %get-tuple-element.35) | copy-start | bytes 1572868
  67.3 19.9 %collective-permute-start.19 = (bf16[4,256,256]{2,1,0:T(8,128)(2,1)S(1)}, bf16[4,256,256]{2,1,0:T(8,128)(2,1)S(1)}, u32[]{:S(2)}, u32[]{:S(2)}) collective-permute-start(bf16[4,256,256]{2,1,0:T(8,128)(2,1)S(1)} %copy-done.9), channel_id=1, source_target_pairs={{1,0},{0,1},{3,2},{2,3},{5,4},{4,5},{7,6},{6,7},{9,8},{8,9},{11,10... | collective-permute-start | bytes 1572872 | tf_op jit(solution)/shard_map/ppermute | solution.py:76
  68.5 5.0 %collective-permute-start.20 = (bf16[256,256]{1,0:T(8,128)(2,1)S(1)}, bf16[256,256]{1,0:T(8,128)(2,1)S(1)}, u32[]{:S(2)}, u32[]{:S(2)}) collective-permute-start(bf16[256,256]{1,0:T(8,128)(2,1)S(1)} %second_call.1.refs_0_), channel_id=1, source_target_pairs={{0,4},{2,6},{4,0},{6,2},{8,12},{10,14},{12,8},{14,10},{16,20},{18,... | collective-permute-start | bytes 393224 | tf_op jit(solution)/shard_map/ppermute | solution.py:81
  70.0 10.9 %collective-permute-start.22 = (bf16[256,256]{1,0:T(8,128)(2,1)S(1)}, bf16[256,256]{1,0:T(8,128)(2,1)S(1)}, u32[]{:S(2)}, u32[]{:S(2)}) collective-permute-start(bf16[256,256]{1,0:T(8,128)(2,1)S(1)} %second_call.1.refs_0_), channel_id=1, source_target_pairs={{8,0},{10,2},{12,4},{14,6},{16,8},{18,10},{20,12},{22,14},{24,16},... | collective-permute-start | bytes 393224 | tf_op jit(solution)/shard_map/ppermute | solution.py:76
  73.0 10.4 %collective-permute-start.24 = (bf16[256,256]{1,0:T(8,128)(2,1)S(1)}, bf16[256,256]{1,0:T(8,128)(2,1)S(1)}, u32[]{:S(2)}, u32[]{:S(2)}) collective-permute-start(bf16[256,256]{1,0:T(8,128)(2,1)S(1)} %second_call.1.refs_0_), channel_id=1, source_target_pairs={{16,0},{18,2},{20,4},{22,6},{24,8},{26,10},{28,12},{30,14},{0,16},... | collective-permute-start | bytes 393224 | tf_op jit(solution)/shard_map/ppermute | solution.py:76
  73.1 11.1 %collective-permute-start.25 = (bf16[256,256]{1,0:T(8,128)(2,1)S(1)}, bf16[256,256]{1,0:T(8,128)(2,1)S(1)}, u32[]{:S(2)}, u32[]{:S(2)}) collective-permute-start(bf16[256,256]{1,0:T(8,128)(2,1)S(1)} %second_call.1.refs_0_), channel_id=1, source_target_pairs={{0,2},{2,0},{4,6},{6,4},{8,10},{10,8},{12,14},{14,12},{16,18},{18,... | collective-permute-start | bytes 393224 | tf_op jit(solution)/shard_map/ppermute | solution.py:81
  73.5 10.0 %collective-permute-start.23 = (bf16[256,256]{1,0:T(8,128)(2,1)S(1)}, bf16[256,256]{1,0:T(8,128)(2,1)S(1)}, u32[]{:S(2)}, u32[]{:S(2)}) collective-permute-start(bf16[256,256]{1,0:T(8,128)(2,1)S(1)} %second_call.1.refs_0_), channel_id=1, source_target_pairs={{24,0},{26,2},{28,4},{30,6},{0,8},{2,10},{4,12},{6,14},{8,16},{10,... | collective-permute-start | bytes 393224 | tf_op jit(solution)/shard_map/ppermute | solution.py:76
  80.9 5.0 %collective-permute-start.30 = (bf16[256,256]{1,0:T(8,128)(2,1)S(1)}, bf16[256,256]{1,0:T(8,128)(2,1)S(1)}, u32[]{:S(2)}, u32[]{:S(2)}) collective-permute-start(bf16[256,256]{1,0:T(8,128)(2,1)S(1)} %collective-permute-done.22.refs_1_), channel_id=1, source_target_pairs={{0,4},{2,6},{4,0},{6,2},{8,12},{10,14},{12,8},{14,10},{16,20},{18,... | collective-permute-start | bytes 393224 | tf_op jit(solution)/shard_map/ppermute | solution.py:81
  83.5 5.2 %collective-permute-start.26 = (bf16[256,256]{1,0:T(8,128)(2,1)S(1)}, bf16[256,256]{1,0:T(8,128)(2,1)S(1)}, u32[]{:S(2)}, u32[]{:S(2)}) collective-permute-start(bf16[256,256]{1,0:T(8,128)(2,1)S(1)} %collective-permute-done.22.refs_1_), channel_id=1, source_target_pairs={{0,2},{2,0},{4,6},{6,4},{8,10},{10,8},{12,14},{14,12},{16,18},{18,... | collective-permute-start | bytes 393224 | tf_op jit(solution)/shard_map/ppermute | solution.py:81
  83.5 6.3 %collective-permute-start.31 = (bf16[256,256]{1,0:T(8,128)(2,1)S(1)}, bf16[256,256]{1,0:T(8,128)(2,1)S(1)}, u32[]{:S(2)}, u32[]{:S(2)}) collective-permute-start(bf16[256,256]{1,0:T(8,128)(2,1)S(1)} %collective-permute-done.23.refs_2_), channel_id=1, source_target_pairs={{0,4},{2,6},{4,0},{6,2},{8,12},{10,14},{12,8},{14,10},{16,20},{18,... | collective-permute-start | bytes 393224 | tf_op jit(solution)/shard_map/ppermute | solution.py:81
  84.1 5.6 %collective-permute-start.27 = (bf16[256,256]{1,0:T(8,128)(2,1)S(1)}, bf16[256,256]{1,0:T(8,128)(2,1)S(1)}, u32[]{:S(2)}, u32[]{:S(2)}) collective-permute-start(bf16[256,256]{1,0:T(8,128)(2,1)S(1)} %collective-permute-done.23.refs_2_), channel_id=1, source_target_pairs={{0,2},{2,0},{4,6},{6,4},{8,10},{10,8},{12,14},{14,12},{16,18},{18,... | collective-permute-start | bytes 393224 | tf_op jit(solution)/shard_map/ppermute | solution.py:81
  85.9 6.2 %collective-permute-start.34 = (bf16[256,256]{1,0:T(8,128)(2,1)S(1)}, bf16[256,256]{1,0:T(8,128)(2,1)S(1)}, u32[]{:S(2)}, u32[]{:S(2)}) collective-permute-start(bf16[256,256]{1,0:T(8,128)(2,1)S(1)} %collective-permute-done.24.refs_3_), channel_id=1, source_target_pairs={{0,4},{2,6},{4,0},{6,2},{8,12},{10,14},{12,8},{14,10},{16,20},{18,... | collective-permute-start | bytes 393224 | tf_op jit(solution)/shard_map/ppermute | solution.py:81
  87.2 5.0 %collective-permute-start.28 = (bf16[256,256]{1,0:T(8,128)(2,1)S(1)}, bf16[256,256]{1,0:T(8,128)(2,1)S(1)}, u32[]{:S(2)}, u32[]{:S(2)}) collective-permute-start(bf16[256,256]{1,0:T(8,128)(2,1)S(1)} %collective-permute-done.24.refs_3_), channel_id=1, source_target_pairs={{0,2},{2,0},{4,6},{6,4},{8,10},{10,8},{12,14},{14,12},{16,18},{18,... | collective-permute-start | bytes 393224 | tf_op jit(solution)/shard_map/ppermute | solution.py:81
  88.7 8.8 %collective-permute-start.21 = (bf16[4,256,128]{2,1,0:T(8,128)(2,1)S(1)}, bf16[4,256,128]{2,1,0:T(8,128)(2,1)S(1)}, u32[]{:S(2)}, u32[]{:S(2)}) collective-permute-start(bf16[4,256,128]{2,1,0:T(8,128)(2,1)S(1)} %fusion.1), channel_id=1, source_target_pairs={{1,0},{0,1},{3,2},{2,3},{5,4},{4,5},{7,6},{6,7},{9,8},{8,9},{11,10... | collective-permute-start | bytes 786440 | tf_op jit(solution)/shard_map/ppermute | solution.py:76
  89.8 2.9 %collective-permute-start.29 = (bf16[256,256]{1,0:T(8,128)(2,1)S(1)}, bf16[256,256]{1,0:T(8,128)(2,1)S(1)}, u32[]{:S(2)}, u32[]{:S(2)}) collective-permute-start(bf16[256,256]{1,0:T(8,128)(2,1)S(1)} %collective-permute-done.20.refs_2_.refs_4_), channel_id=1, source_target_pairs={{0,2},{2,0},{4,6},{6,4},{8,10},{10,8},{12,14},{14,12},{16,18},{18,... | collective-permute-start | bytes 393224 | tf_op jit(solution)/shard_map/ppermute | solution.py:81
  89.8 2.9 %collective-permute-start.32 = (bf16[256,256]{1,0:T(8,128)(2,1)S(1)}, bf16[256,256]{1,0:T(8,128)(2,1)S(1)}, u32[]{:S(2)}, u32[]{:S(2)}) collective-permute-start(bf16[256,256]{1,0:T(8,128)(2,1)S(1)} %collective-permute-done.30.refs_10_), channel_id=1, source_target_pairs={{0,2},{2,0},{4,6},{6,4},{8,10},{10,8},{12,14},{14,12},{16,18},{18,... | collective-permute-start | bytes 393224 | tf_op jit(solution)/shard_map/ppermute | solution.py:81
  92.2 1.3 %collective-permute-start.33 = (bf16[256,256]{1,0:T(8,128)(2,1)S(1)}, bf16[256,256]{1,0:T(8,128)(2,1)S(1)}, u32[]{:S(2)}, u32[]{:S(2)}) collective-permute-start(bf16[256,256]{1,0:T(8,128)(2,1)S(1)} %collective-permute-done.31.refs_11_), channel_id=1, source_target_pairs={{0,2},{2,0},{4,6},{6,4},{8,10},{10,8},{12,14},{14,12},{16,18},{18,... | collective-permute-start | bytes 393224 | tf_op jit(solution)/shard_map/ppermute | solution.py:81
  92.2 1.5 %collective-permute-start.35 = (bf16[256,256]{1,0:T(8,128)(2,1)S(1)}, bf16[256,256]{1,0:T(8,128)(2,1)S(1)}, u32[]{:S(2)}, u32[]{:S(2)}) collective-permute-start(bf16[256,256]{1,0:T(8,128)(2,1)S(1)} %collective-permute-done.34.refs_14_), channel_id=1, source_target_pairs={{0,2},{2,0},{4,6},{6,4},{8,10},{10,8},{12,14},{14,12},{16,18},{18,... | collective-permute-start | bytes 393224 | tf_op jit(solution)/shard_map/ppermute | solution.py:81

commit v7 on v6

--- a/solution.py
+++ b/solution.py
@@ -617,7 +617,7 @@
         held = jnp.stack(blocks)[place].reshape(len(blocks), -1, each, width)
         summed = jnp.transpose(held, (1, 3, 0, 2)).reshape(total, columns)
         return 2.0 * summed.astype(F32) - trial.astype(F32)
-    pieces = 8
+    pieces = 16
     return pl.pallas_call(
         functools.partial(last_kernel, each),
         in_specs=[SMEM, HBM] + [VMEM] * len(blocks),

time: 98.7 us -> 99.1 us (level)
  no operation moved by 1% of the time
where the time goes in v7:
time: 99.1 us; the launch traced here: 98.7 us
  Pallas kernels  43.8 us (44%)
  starting transfers between devices  30.6 us (31%)
  waiting for transfers between devices  16.1 us (16%)
  local copies, waits for them, and re-layouts  3.18 us (3%)
  other arithmetic  2.54 us (3%)
  matrix products  1.47 us (1%)
    ppermute x12, starting transfers between devices, from_ahead(): lax.ppermute(value, axis, [((s + step) % count, s) for s in range(count)])  18.9 us
    ppermute x24, starting transfers between devices, flipped(): return lax.ppermute(value, axis, [(s, s ^ bit) for s in range(count)])  11.7 us
    pallas_call x1, Pallas kernels, left_product(): pl.pallas_call(left_kernel, in_specs=[SMEM, HBM, VMEM, ANY], out_specs=[V...  8.9 us
    ppermute x24, waiting for transfers between devices, flipped(): return lax.ppermute(value, axis, [(s, s ^ bit) for s in range(count)])  8.6 us
    ppermute x12, waiting for transfers between devices, from_ahead(): lax.ppermute(value, axis, [((s + step) % count, s) for s in range(count)])  7.51 us
    pallas_call x1, Pallas kernels, row_call(): pl.pallas_call(functools.partial(row_kernel, each, len(kernels)), in_spec...  6.55 us
    pallas_call x1, Pallas kernels, first_call(): pl.pallas_call(functools.partial(first_kernel, each, count, len(blocks)),...  5.64 us
    pallas_call x1, Pallas kernels, fold_call(): pl.pallas_call(functools.partial(fold_kernel, scale, each), in_specs=[SME...  5.43 us
  transfers between devices with their start and end apart: 36, of which 14 were waited for; matrix products, arithmetic and copies ran while one was open for 4% of the time, Pallas kernels for 33%

profile of v7, /device:TPU:0, one launch (start us, length us, event | category | flops | bytes accessed | tf_op | source)
XLA Modules:
  0.0 98.7 jit_solution(13211919251473223286)
XLA Ops:
  0.6 3.0 %collective-permute-start = (bf16[2048,256]{1,0:T(8,128)(2,1)}, bf16[2048,256]{1,0:T(8,128)(2,1)S(1)}, u32[]{:S(2)}, u32[]{:S(2)}) collective-permute-start(bf16[2048,256]{1,0:T(8,128)(2,1)} %bitcast.30), channel_id=1, source_target_pairs={{1,0},{0,1},{3,2},{2,3},{5,4},{4,5},{7,6},{6,7},{9,8},{8,9},{11,10... | collective-permute-start | bytes 3145736 | tf_op jit(solution)/shard_map/ppermute | solution.py:76
  3.7 0.7 compare_convert_fusion
  4.4 0.6 copy-done.6
  5.1 5.1 %start_call.1 = (bf16[32,128,256]{2,1,0:T(8,128)(2,1)}, bf16[256,256]{1,0:T(8,128)(2,1)S(1)}, f32[256,256]{1,0:T(8,128)S(1)}) custom-call(s32[1]{0:T(128)} %bitcast.1.index, bf16[8,128]{1,0:T(8,128)(2,1)S(1)} %fusion.5.pick, bf16[32,256,256]{2,1,0:T(8,128)(2,1)} %refs_4_.1, bf16[8192,128]{1,0:T(8,128)(2,1)} %trial_at.3, ...), custom_call_target="tpu_custom_call" | custom-call | flops 1 | bytes 1 | tf_op jit(solution)/shard_map/start_call/pallas_call | solution.py:387
  10.4 8.9 %left_product.1 = (bf16[1,256,2048]{2,1,0:T(8,128)(2,1)S(1)}, f32[256,256]{1,0:T(8,128)S(1)}) custom-call(s32[2]{0:T(128)S(1)} %pad_add_fusion.planes, bf16[1,2048,4096]{2,1,0:T(8,128)(2,1)} %screened_at.1, bf16[2048,256]{1,0:T(8,128)(2,1)S(1)} %bitcast.31, bf16[256,256]{1,0:T(8,128)(2,1)S(1)} %get-tuple-element.27._.refs_2_.refs_0_), custom_call_target="tpu_custom_call" | custom-call | flops 1 | bytes 1 | tf_op jit(solution)/shard_map/left_product/pallas_call | solution.py:192
  19.3 0.7 copy-done.4
  20.0 0.8 reshape.268.energy
  20.8 0.7 copy-done.2
  21.5 5.4 %fold_call.1 = (bf16[32,256,256]{2,1,0:T(8,128)(2,1)}, f32[256,256]{1,0:T(8,128)S(1)}, bf16[4,256,256]{2,1,0:T(8,128)(2,1)}) custom-call(s32[1]{0:T(128)} %bitcast.place, bf16[32,256,256]{2,1,0:T(8,128)(2,1)} %refs_4_.1, f32[32,256]{1,0:T(8,128)S(1)} %copy-done.2, f32[32,256]{1,0:T(8,128)S(1)} %reshape.268.energy, ...), custom_call_target="tpu_custom_call" | custom-call | flops 1 | bytes 1 | tf_op jit(solution)/shard_map/fold_call/pallas_call | solution.py:435
  27.0 0.5 coarse_block.1
  27.6 1.8 %collective-permute-start.1 = (bf16[272,128]{1,0:T(8,128)(2,1)S(1)}, bf16[272,128]{1,0:T(8,128)(2,1)S(1)}, u32[]{:S(2)}, u32[]{:S(2)}) collective-permute-start(bf16[272,128]{1,0:T(8,128)(2,1)S(1)} %coarse_block.1), channel_id=1, source_target_pairs={{1,0},{0,1},{3,2},{2,3},{5,4},{4,5},{7,6},{6,7},{9,8},{8,9},{11,10... | collective-permute-start | bytes 208904 | tf_op jit(solution)/shard_map/ppermute | solution.py:76
  29.5 2.5 %collective-permute-done.1 = bf16[272,128]{1,0:T(8,128)(2,1)S(1)} collective-permute-done((bf16[272,128]{1,0:T(8,128)(2,1)S(1)}, bf16[272,128]{1,0:T(8,128)(2,1)S(1)}, u32[]{:S(2)}, u32[]{:S(2)}) %collective-permute-start.1) | collective-permute-done | bytes 69664 | tf_op jit(solution)/shard_map/ppermute | solution.py:76
  32.0 1.9 %collective-permute-start.4 = (bf16[288,128]{1,0:T(8,128)(2,1)S(1)}, bf16[288,128]{1,0:T(8,128)(2,1)S(1)}, u32[]{:S(2)}, u32[]{:S(2)}) collective-permute-start(bf16[288,128]{1,0:T(8,128)(2,1)S(1)} %pad_maximum_fusion.refs_0_.refs_2_), channel_id=1, source_target_pairs={{24,0},{26,2},{28,4},{30,6},{0,8},{2,10},{4,12},{6,14},{8,16},{10,... | collective-permute-start | bytes 221192 | tf_op jit(solution)/shard_map/ppermute | solution.py:76
  33.8 2.3 %collective-permute-start.3 = (bf16[288,128]{1,0:T(8,128)(2,1)S(1)}, bf16[288,128]{1,0:T(8,128)(2,1)S(1)}, u32[]{:S(2)}, u32[]{:S(2)}) collective-permute-start(bf16[288,128]{1,0:T(8,128)(2,1)S(1)} %pad_maximum_fusion.refs_0_.refs_2_), channel_id=1, source_target_pairs={{8,0},{10,2},{12,4},{14,6},{16,8},{18,10},{20,12},{22,14},{24,16},... | collective-permute-start | bytes 221192 | tf_op jit(solution)/shard_map/ppermute | solution.py:76
  36.3 1.6 %collective-permute-start.6 = (bf16[288,128]{1,0:T(8,128)(2,1)S(1)}, bf16[288,128]{1,0:T(8,128)(2,1)S(1)}, u32[]{:S(2)}, u32[]{:S(2)}) collective-permute-start(bf16[288,128]{1,0:T(8,128)(2,1)S(1)} %pad_maximum_fusion.refs_0_.refs_2_), channel_id=1, source_target_pairs={{0,4},{2,6},{4,0},{6,2},{8,12},{10,14},{12,8},{14,10},{16,20},{18,... | collective-permute-start | bytes 221192 | tf_op jit(solution)/shard_map/ppermute | solution.py:81
  37.8 1.5 %collective-permute-start.2 = (bf16[256,256]{1,0:T(8,128)(2,1)S(1)}, bf16[256,256]{1,0:T(8,128)(2,1)S(1)}, u32[]{:S(2)}, u32[]{:S(2)}) collective-permute-start(bf16[256,256]{1,0:T(8,128)(2,1)S(1)} %get-tuple-element.27._.refs_2_.refs_0_), channel_id=1, source_target_pairs={{1,0},{0,1},{3,2},{2,3},{5,4},{4,5},{7,6},{6,7},{9,8},{8,9},{11,10... | collective-permute-start | bytes 393224 | tf_op jit(solution)/shard_map/ppermute | solution.py:76
  39.4 1.4 %collective-permute-start.5 = (bf16[288,128]{1,0:T(8,128)(2,1)S(1)}, bf16[288,128]{1,0:T(8,128)(2,1)S(1)}, u32[]{:S(2)}, u32[]{:S(2)}) collective-permute-start(bf16[288,128]{1,0:T(8,128)(2,1)S(1)} %pad_maximum_fusion.refs_0_.refs_2_), channel_id=1, source_target_pairs={{16,0},{18,2},{20,4},{22,6},{24,8},{26,10},{28,12},{30,14},{0,16},... | collective-permute-start | bytes 221192 | tf_op jit(solution)/shard_map/ppermute | solution.py:76
  40.8 1.5 %collective-permute-start.13 = (bf16[288,128]{1,0:T(8,128)(2,1)S(1)}, bf16[288,128]{1,0:T(8,128)(2,1)S(1)}, u32[]{:S(2)}, u32[]{:S(2)}) collective-permute-start(bf16[288,128]{1,0:T(8,128)(2,1)S(1)} %collective-permute-done.4.refs_2_.refs_4_), channel_id=1, source_target_pairs={{0,4},{2,6},{4,0},{6,2},{8,12},{10,14},{12,8},{14,10},{16,20},{18,... | collective-permute-start | bytes 221192 | tf_op jit(solution)/shard_map/ppermute | solution.py:81
  42.3 1.1 %collective-permute-done.2.refs_1_ = bf16[256,256]{1,0:T(8,128)(2,1)S(1)} collective-permute-done((bf16[256,256]{1,0:T(8,128)(2,1)S(1)}, bf16[256,256]{1,0:T(8,128)(2,1)S(1)}, u32[]{:S(2)}, u32[]{:S(2)}) %collective-permute-start.2) | collective-permute-done | bytes 131104 | tf_op jit(solution)/shard_map/ppermute | solution.py:76
  43.4 0.5 collective-permute-start.12
  43.9 1.4 %collective-permute-done.5.refs_3_.refs_5_ = bf16[288,128]{1,0:T(8,128)(2,1)S(1)} collective-permute-done((bf16[288,128]{1,0:T(8,128)(2,1)S(1)}, bf16[288,128]{1,0:T(8,128)(2,1)S(1)}, u32[]{:S(2)}, u32[]{:S(2)}) %collective-permute-start.5) | collective-permute-done | bytes 73760 | tf_op jit(solution)/shard_map/ppermute | solution.py:76
  45.4 1.1 %collective-permute-start.16 = (bf16[288,128]{1,0:T(8,128)(2,1)S(1)}, bf16[288,128]{1,0:T(8,128)(2,1)S(1)}, u32[]{:S(2)}, u32[]{:S(2)}) collective-permute-start(bf16[288,128]{1,0:T(8,128)(2,1)S(1)} %collective-permute-done.5.refs_3_.refs_5_), channel_id=1, source_target_pairs={{0,4},{2,6},{4,0},{6,2},{8,12},{10,14},{12,8},{14,10},{16,20},{18,... | collective-permute-start | bytes 221192 | tf_op jit(solution)/shard_map/ppermute | solution.py:81
  47.8 2.3 %collective-permute-done.16.refs_16_ = bf16[288,128]{1,0:T(8,128)(2,1)S(1)} collective-permute-done((bf16[288,128]{1,0:T(8,128)(2,1)S(1)}, bf16[288,128]{1,0:T(8,128)(2,1)S(1)}, u32[]{:S(2)}, u32[]{:S(2)}) %collective-permute-start.16) | collective-permute-done | bytes 73760 | tf_op jit(solution)/shard_map/ppermute | solution.py:81
  50.5 0.8 collective-permute-done.17.refs_17_
  51.3 5.6 %first_call.1 = (bf16[4,256,256]{2,1,0:T(8,128)(2,1)S(1)}, f32[2,256,128]{2,1,0:T(8,128)S(1)}, bf16[256,256]{1,0:T(8,128)(2,1)S(1)}, bf16[512,64]{1,0:T(8,128)(2,1)S(1)}) custom-call(s32[16]{0:T(128)S(1)} %stack.76.order, s32[256,1]{1,0:T(8,128)S(1)} %add_select_fusion.names, bf16[256,256]{1,0:T(8,128)(2,1)S(1)} %get-tuple-element.27._.refs_2_.refs_0_, ...), custom_call_target="tpu_custom_call" | custom-call | flops 1 | bytes 1 | tf_op jit(solution)/shard_map/first_call/pallas_call | solution.py:501
  57.0 1.2 %collective-permute-start.18 = (bf16[256,256]{1,0:T(8,128)(2,1)S(1)}, bf16[256,256]{1,0:T(8,128)(2,1)S(1)}, u32[]{:S(2)}, u32[]{:S(2)}) collective-permute-start(bf16[256,256]{1,0:T(8,128)(2,1)S(1)} %get-tuple-element.32.refs_0_), channel_id=1, source_target_pairs={{1,0},{0,1},{3,2},{2,3},{5,4},{4,5},{7,6},{6,7},{9,8},{8,9},{11,10... | collective-permute-start | bytes 393224 | tf_op jit(solution)/shard_map/ppermute | solution.py:76
  58.2 2.5 %energy_call.1.refs_6_ = f32[256,256]{1,0:T(8,128)S(1)} custom-call(bf16[32,256,256]{2,1,0:T(8,128)(2,1)} %refs_4_.1, f32[2,256,128]{2,1,0:T(8,128)S(1)} %get-tuple-element.34.total, f32[32,256]{1,0:T(8,128)S(1)} %copy-done.3, f32[32,256]{1,0:T(8,128)S(1)} %reshape.268.energy, f32[256,256]{1,0:T(8,128)S(1)} %get-tuple-element.21.my_trial.trial), custom_call_target="tpu_custom_call" | custom-call | flops 1 | bytes 1 | tf_op jit(solution)/shard_map/energy_call/pallas_call | solution.py:538
  60.7 1.9 %collective-permute-done.18.refs_1_ = bf16[256,256]{1,0:T(8,128)(2,1)S(1)} collective-permute-done((bf16[256,256]{1,0:T(8,128)(2,1)S(1)}, bf16[256,256]{1,0:T(8,128)(2,1)S(1)}, u32[]{:S(2)}, u32[]{:S(2)}) %collective-permute-start.18) | collective-permute-done | bytes 131104 | tf_op jit(solution)/shard_map/ppermute | solution.py:76
  62.6 4.7 %second_call.1.refs_0_ = bf16[256,256]{1,0:T(8,128)(2,1)S(1)} custom-call(bf16[512,64]{1,0:T(8,128)(2,1)S(1)} %get-tuple-element.31.weights, bf16[256,256]{1,0:T(8,128)(2,1)S(1)} %get-tuple-element.32.refs_0_, bf16[256,256]{1,0:T(8,128)(2,1)S(1)} %collective-permute-done.18.refs_1_, bf16[12,256,256]{2,1,0:T(8,128)(2,1)S(1)} %unpack_call.1.refs_18_.refs_2_.refs_0_, ...), custom_call_target="tpu_custom_call" | custom-call | flops 1 | bytes 1 | tf_op jit(solution)/shard_map/second_call/pallas_call | solution.py:571
  67.3 1.2 %collective-permute-start.19 = (bf16[4,256,256]{2,1,0:T(8,128)(2,1)S(1)}, bf16[4,256,256]{2,1,0:T(8,128)(2,1)S(1)}, u32[]{:S(2)}, u32[]{:S(2)}) collective-permute-start(bf16[4,256,256]{2,1,0:T(8,128)(2,1)S(1)} %copy-done.9), channel_id=1, source_target_pairs={{1,0},{0,1},{3,2},{2,3},{5,4},{4,5},{7,6},{6,7},{9,8},{8,9},{11,10... | collective-permute-start | bytes 1572872 | tf_op jit(solution)/shard_map/ppermute | solution.py:76
  68.5 1.5 %collective-permute-start.20 = (bf16[256,256]{1,0:T(8,128)(2,1)S(1)}, bf16[256,256]{1,0:T(8,128)(2,1)S(1)}, u32[]{:S(2)}, u32[]{:S(2)}) collective-permute-start(bf16[256,256]{1,0:T(8,128)(2,1)S(1)} %second_call.1.refs_0_), channel_id=1, source_target_pairs={{0,4},{2,6},{4,0},{6,2},{8,12},{10,14},{12,8},{14,10},{16,20},{18,... | collective-permute-start | bytes 393224 | tf_op jit(solution)/shard_map/ppermute | solution.py:81
  70.0 3.0 %collective-permute-start.22 = (bf16[256,256]{1,0:T(8,128)(2,1)S(1)}, bf16[256,256]{1,0:T(8,128)(2,1)S(1)}, u32[]{:S(2)}, u32[]{:S(2)}) collective-permute-start(bf16[256,256]{1,0:T(8,128)(2,1)S(1)} %second_call.1.refs_0_), channel_id=1, source_target_pairs={{8,0},{10,2},{12,4},{14,6},{16,8},{18,10},{20,12},{22,14},{24,16},... | collective-permute-start | bytes 393224 | tf_op jit(solution)/shard_map/ppermute | solution.py:76
  73.5 0.9 collective-permute-start.23
  74.3 6.5 %row_call.1 = bf16[512,256]{1,0:T(8,128)(2,1)S(1)} custom-call(s32[16]{0:T(128)S(1)} %stack.76.order, bf16[64,32]{1,0:T(8,128)(2,1)S(1)} %bitcast.33, bf16[32,128,256]{2,1,0:T(8,128)(2,1)} %get-tuple-element.36.vectors_at, bf16[12,256,256]{2,1,0:T(8,128)(2,1)S(1)} %unpack_call.1.refs_18_.refs_2_.refs_0_, ...), custom_call_target="tpu_custom_call" | custom-call | flops 1 | bytes 1 | tf_op jit(solution)/shard_map/row_call/pallas_call | solution.py:320
  80.9 1.3 %collective-permute-start.30 = (bf16[256,256]{1,0:T(8,128)(2,1)S(1)}, bf16[256,256]{1,0:T(8,128)(2,1)S(1)}, u32[]{:S(2)}, u32[]{:S(2)}) collective-permute-start(bf16[256,256]{1,0:T(8,128)(2,1)S(1)} %collective-permute-done.22.refs_1_), channel_id=1, source_target_pairs={{0,4},{2,6},{4,0},{6,2},{8,12},{10,14},{12,8},{14,10},{16,20},{18,... | collective-permute-start | bytes 393224 | tf_op jit(solution)/shard_map/ppermute | solution.py:81
  82.2 0.7 dynamic-slice_multiply_fusion
  82.9 0.5 collective-permute-done.24.refs_3_
  83.5 0.7 collective-permute-start.31
  84.4 1.6 %collective-permute-done.30.refs_10_ = bf16[256,256]{1,0:T(8,128)(2,1)S(1)} collective-permute-done((bf16[256,256]{1,0:T(8,128)(2,1)S(1)}, bf16[256,256]{1,0:T(8,128)(2,1)S(1)}, u32[]{:S(2)}, u32[]{:S(2)}) %collective-permute-start.30) | collective-permute-done | bytes 131104 | tf_op jit(solution)/shard_map/ppermute | solution.py:81
  85.9 1.2 %collective-permute-start.34 = (bf16[256,256]{1,0:T(8,128)(2,1)S(1)}, bf16[256,256]{1,0:T(8,128)(2,1)S(1)}, u32[]{:S(2)}, u32[]{:S(2)}) collective-permute-start(bf16[256,256]{1,0:T(8,128)(2,1)S(1)} %collective-permute-done.24.refs_3_), channel_id=1, source_target_pairs={{0,4},{2,6},{4,0},{6,2},{8,12},{10,14},{12,8},{14,10},{16,20},{18,... | collective-permute-start | bytes 393224 | tf_op jit(solution)/shard_map/ppermute | solution.py:81
  87.2 1.5 %fusion.1 = bf16[4,256,128]{2,1,0:T(8,128)(2,1)S(1)} fusion(bf16[4,128,256]{2,1,0:T(8,128)(2,1)S(1)} %bitcast.32, bf16[4,256,256]{2,1,0:T(8,128)(2,1)S(1)} %collective-permute-done.19, bf16[4,256,256]{2,1,0:T(8,128)(2,1)S(1)} %copy-done.9, pred[]{:T(512)S(6)} %eq.59, bf16[32,256,128]{2,1,0:T(8,128)(2,1)} %bitcast.34, s32[]{:T(128)S(6)} %select_n.145, ...), kind=kOutput, calls=%fused_computation.2 | convolution fusion | flops 68157440 | bytes 1843206 | tf_op jit(solution)/shard_map/ksv,kns->kvn/dot_general | solution.py:714
  88.7 0.6 collective-permute-start.21
  89.8 0.5 collective-permute-start.32
  90.3 1.9 %collective-permute-done.34.refs_14_ = bf16[256,256]{1,0:T(8,128)(2,1)S(1)} collective-permute-done((bf16[256,256]{1,0:T(8,128)(2,1)S(1)}, bf16[256,256]{1,0:T(8,128)(2,1)S(1)}, u32[]{:S(2)}, u32[]{:S(2)}) %collective-permute-start.34) | collective-permute-done | bytes 131104 | tf_op jit(solution)/shard_map/ppermute | solution.py:81
  92.2 0.5 collective-permute-start.35
  92.7 0.8 collective-permute-done.33.refs_13_
  93.7 4.1 %last_call.1 = f32[8192,128]{1,0:T(8,128)} custom-call(s32[16]{0:T(128)S(1)} %stack.76.order, bf16[8192,128]{1,0:T(8,128)(2,1)} %trial_at.3, bf16[256,256]{1,0:T(8,128)(2,1)S(1)} %second_call.1.refs_0_, bf16[256,256]{1,0:T(8,128)(2,1)S(1)} %collective-permute-done.22.refs_1_, bf16[256,256]{1,0:T(8,128)(2,1)S(1)} %collective-permute-done.23.refs_2_, ...), custom_call_target="tpu_custom_call" | custom-call | flops 1 | bytes 1 | tf_op jit(solution)/shard_map/last_call/pallas_call | solution.py:621
  97.9 0.8 add_convert_fusion
  (75 shorter events, 3.7 us)
Async XLA Ops:
  0.6 9.7 %copy-start = (bf16[1,2048,256]{2,1,0:T(8,128)(2,1)S(1)}, bf16[1,2048,256]{2,1,0:T(8,128)(2,1)}, u32[]{:S(2)}) copy-start(bf16[1,2048,256]{2,1,0:T(8,128)(2,1)} %param.9) | copy-start | bytes 3145732
  0.6 26.4 %collective-permute-start = (bf16[2048,256]{1,0:T(8,128)(2,1)}, bf16[2048,256]{1,0:T(8,128)(2,1)S(1)}, u32[]{:S(2)}, u32[]{:S(2)}) collective-permute-start(bf16[2048,256]{1,0:T(8,128)(2,1)} %bitcast.30), channel_id=1, source_target_pairs={{1,0},{0,1},{3,2},{2,3},{5,4},{4,5},{7,6},{6,7},{9,8},{8,9},{11,10... | collective-permute-start | bytes 3145736 | tf_op jit(solution)/shard_map/ppermute | solution.py:76
  4.4 0.6 copy-start.6
  5.0 5.3 %copy-start.1 = (f32[32,256]{1,0:T(8,128)}, f32[32,256]{1,0:T(8,128)S(1)}, u32[]{:S(2)}) copy-start(f32[32,256]{1,0:T(8,128)S(1)} %constant_dynamic-slice_fusion.1.live.refs_5_) | copy-start | bytes 98308
  19.3 0.7 copy-start.4
  20.0 7.0 %copy-start.8 = (bf16[4,32,4]{1,2,0:T(4,128)(2,1)S(1)}, bf16[4,32,4]{1,2,0:T(4,128)(2,1)}, u32[]{:S(2)}) copy-start(bf16[4,32,4]{1,2,0:T(4,128)(2,1)} %param.14) | copy-start | bytes 3076
  20.0 9.4 %copy-start.7 = (s32[4,32,4]{1,2,0:T(4,128)S(1)}, s32[4,32,4]{1,2,0:T(4,128)}, u32[]{:S(2)}) copy-start(s32[4,32,4]{1,2,0:T(4,128)} %param.13) | copy-start | bytes 6148
  20.8 0.8 copy-start.2
  21.5 5.5 %copy-start.5 = (f32[256,256]{1,0:T(8,128)S(1)}, f32[256,256]{1,0:T(8,128)}, u32[]{:S(2)}) copy-start(f32[256,256]{1,0:T(8,128)} %copy-done.4) | copy-start | bytes 786436
  27.6 4.4 %collective-permute-start.1 = (bf16[272,128]{1,0:T(8,128)(2,1)S(1)}, bf16[272,128]{1,0:T(8,128)(2,1)S(1)}, u32[]{:S(2)}, u32[]{:S(2)}) collective-permute-start(bf16[272,128]{1,0:T(8,128)(2,1)S(1)} %coarse_block.1), channel_id=1, source_target_pairs={{1,0},{0,1},{3,2},{2,3},{5,4},{4,5},{7,6},{6,7},{9,8},{8,9},{11,10... | collective-permute-start | bytes 208904 | tf_op jit(solution)/shard_map/ppermute | solution.py:76
  32.0 7.4 %collective-permute-start.4 = (bf16[288,128]{1,0:T(8,128)(2,1)S(1)}, bf16[288,128]{1,0:T(8,128)(2,1)S(1)}, u32[]{:S(2)}, u32[]{:S(2)}) collective-permute-start(bf16[288,128]{1,0:T(8,128)(2,1)S(1)} %pad_maximum_fusion.refs_0_.refs_2_), channel_id=1, source_target_pairs={{24,0},{26,2},{28,4},{30,6},{0,8},{2,10},{4,12},{6,14},{8,16},{10,... | collective-permute-start | bytes 221192 | tf_op jit(solution)/shard_map/ppermute | solution.py:76
  33.8 5.5 %collective-permute-start.3 = (bf16[288,128]{1,0:T(8,128)(2,1)S(1)}, bf16[288,128]{1,0:T(8,128)(2,1)S(1)}, u32[]{:S(2)}, u32[]{:S(2)}) collective-permute-start(bf16[288,128]{1,0:T(8,128)(2,1)S(1)} %pad_maximum_fusion.refs_0_.refs_2_), channel_id=1, source_target_pairs={{8,0},{10,2},{12,4},{14,6},{16,8},{18,10},{20,12},{22,14},{24,16},... | collective-permute-start | bytes 221192 | tf_op jit(solution)/shard_map/ppermute | solution.py:76
  36.2 9.2 %collective-permute-start.7 = (bf16[288,128]{1,0:T(8,128)(2,1)S(1)}, bf16[288,128]{1,0:T(8,128)(2,1)S(1)}, u32[]{:S(2)}, u32[]{:S(2)}) collective-permute-start(bf16[288,128]{1,0:T(8,128)(2,1)S(1)} %pad_maximum_fusion.refs_0_.refs_2_), channel_id=1, source_target_pairs={{0,2},{2,0},{4,6},{6,4},{8,10},{10,8},{12,14},{14,12},{16,18},{18,... | collective-permute-start | bytes 221192 | tf_op jit(solution)/shard_map/ppermute | solution.py:81
  36.3 6.0 %collective-permute-start.6 = (bf16[288,128]{1,0:T(8,128)(2,1)S(1)}, bf16[288,128]{1,0:T(8,128)(2,1)S(1)}, u32[]{:S(2)}, u32[]{:S(2)}) collective-permute-start(bf16[288,128]{1,0:T(8,128)(2,1)S(1)} %pad_maximum_fusion.refs_0_.refs_2_), channel_id=1, source_target_pairs={{0,4},{2,6},{4,0},{6,2},{8,12},{10,14},{12,8},{14,10},{16,20},{18,... | collective-permute-start | bytes 221192 | tf_op jit(solution)/shard_map/ppermute | solution.py:81
  37.8 5.6 %collective-permute-start.2 = (bf16[256,256]{1,0:T(8,128)(2,1)S(1)}, bf16[256,256]{1,0:T(8,128)(2,1)S(1)}, u32[]{:S(2)}, u32[]{:S(2)}) collective-permute-start(bf16[256,256]{1,0:T(8,128)(2,1)S(1)} %get-tuple-element.27._.refs_2_.refs_0_), channel_id=1, source_target_pairs={{1,0},{0,1},{3,2},{2,3},{5,4},{4,5},{7,6},{6,7},{9,8},{8,9},{11,10... | collective-permute-start | bytes 393224 | tf_op jit(solution)/shard_map/ppermute | solution.py:76
  39.4 6.0 %collective-permute-start.5 = (bf16[288,128]{1,0:T(8,128)(2,1)S(1)}, bf16[288,128]{1,0:T(8,128)(2,1)S(1)}, u32[]{:S(2)}, u32[]{:S(2)}) collective-permute-start(bf16[288,128]{1,0:T(8,128)(2,1)S(1)} %pad_maximum_fusion.refs_0_.refs_2_), channel_id=1, source_target_pairs={{16,0},{18,2},{20,4},{22,6},{24,8},{26,10},{28,12},{30,14},{0,16},... | collective-permute-start | bytes 221192 | tf_op jit(solution)/shard_map/ppermute | solution.py:76
  40.8 6.2 %collective-permute-start.13 = (bf16[288,128]{1,0:T(8,128)(2,1)S(1)}, bf16[288,128]{1,0:T(8,128)(2,1)S(1)}, u32[]{:S(2)}, u32[]{:S(2)}) collective-permute-start(bf16[288,128]{1,0:T(8,128)(2,1)S(1)} %collective-permute-done.4.refs_2_.refs_4_), channel_id=1, source_target_pairs={{0,4},{2,6},{4,0},{6,2},{8,12},{10,14},{12,8},{14,10},{16,20},{18,... | collective-permute-start | bytes 221192 | tf_op jit(solution)/shard_map/ppermute | solution.py:81
  42.3 5.0 %collective-permute-start.9 = (bf16[288,128]{1,0:T(8,128)(2,1)S(1)}, bf16[288,128]{1,0:T(8,128)(2,1)S(1)}, u32[]{:S(2)}, u32[]{:S(2)}) collective-permute-start(bf16[288,128]{1,0:T(8,128)(2,1)S(1)} %collective-permute-done.4.refs_2_.refs_4_), channel_id=1, source_target_pairs={{0,2},{2,0},{4,6},{6,4},{8,10},{10,8},{12,14},{14,12},{16,18},{18,... | collective-permute-start | bytes 221192 | tf_op jit(solution)/shard_map/ppermute | solution.py:81
  43.4 4.4 %collective-permute-start.12 = (bf16[288,128]{1,0:T(8,128)(2,1)S(1)}, bf16[288,128]{1,0:T(8,128)(2,1)S(1)}, u32[]{:S(2)}, u32[]{:S(2)}) collective-permute-start(bf16[288,128]{1,0:T(8,128)(2,1)S(1)} %collective-permute-done.3.refs_1_.refs_3_), channel_id=1, source_target_pairs={{0,4},{2,6},{4,0},{6,2},{8,12},{10,14},{12,8},{14,10},{16,20},{18,... | collective-permute-start | bytes 221192 | tf_op jit(solution)/shard_map/ppermute | solution.py:81
  45.4 1.3 %collective-permute-start.11 = (bf16[288,128]{1,0:T(8,128)(2,1)S(1)}, bf16[288,128]{1,0:T(8,128)(2,1)S(1)}, u32[]{:S(2)}, u32[]{:S(2)}) collective-permute-start(bf16[288,128]{1,0:T(8,128)(2,1)S(1)} %collective-permute-done.6.refs_4_.refs_6_), channel_id=1, source_target_pairs={{0,2},{2,0},{4,6},{6,4},{8,10},{10,8},{12,14},{14,12},{16,18},{18,... | collective-permute-start | bytes 221192 | tf_op jit(solution)/shard_map/ppermute | solution.py:81
  45.4 4.7 %collective-permute-start.16 = (bf16[288,128]{1,0:T(8,128)(2,1)S(1)}, bf16[288,128]{1,0:T(8,128)(2,1)S(1)}, u32[]{:S(2)}, u32[]{:S(2)}) collective-permute-start(bf16[288,128]{1,0:T(8,128)(2,1)S(1)} %collective-permute-done.5.refs_3_.refs_5_), channel_id=1, source_target_pairs={{0,4},{2,6},{4,0},{6,2},{8,12},{10,14},{12,8},{14,10},{16,20},{18,... | collective-permute-start | bytes 221192 | tf_op jit(solution)/shard_map/ppermute | solution.py:81
  46.7 3.4 %collective-permute-start.8 = (bf16[288,128]{1,0:T(8,128)(2,1)S(1)}, bf16[288,128]{1,0:T(8,128)(2,1)S(1)}, u32[]{:S(2)}, u32[]{:S(2)}) collective-permute-start(bf16[288,128]{1,0:T(8,128)(2,1)S(1)} %collective-permute-done.3.refs_1_.refs_3_), channel_id=1, source_target_pairs={{0,2},{2,0},{4,6},{6,4},{8,10},{10,8},{12,14},{14,12},{16,18},{18,... | collective-permute-start | bytes 221192 | tf_op jit(solution)/shard_map/ppermute | solution.py:81
  47.0 3.1 %collective-permute-start.10 = (bf16[288,128]{1,0:T(8,128)(2,1)S(1)}, bf16[288,128]{1,0:T(8,128)(2,1)S(1)}, u32[]{:S(2)}, u32[]{:S(2)}) collective-permute-start(bf16[288,128]{1,0:T(8,128)(2,1)S(1)} %collective-permute-done.5.refs_3_.refs_5_), channel_id=1, source_target_pairs={{0,2},{2,0},{4,6},{6,4},{8,10},{10,8},{12,14},{14,12},{16,18},{18,... | collective-permute-start | bytes 221192 | tf_op jit(solution)/shard_map/ppermute | solution.py:81
  47.3 3.2 %collective-permute-start.15 = (bf16[288,128]{1,0:T(8,128)(2,1)S(1)}, bf16[288,128]{1,0:T(8,128)(2,1)S(1)}, u32[]{:S(2)}, u32[]{:S(2)}) collective-permute-start(bf16[288,128]{1,0:T(8,128)(2,1)S(1)} %collective-permute-done.13.refs_11_.refs_13_), channel_id=1, source_target_pairs={{0,2},{2,0},{4,6},{6,4},{8,10},{10,8},{12,14},{14,12},{16,18},{18,... | collective-permute-start | bytes 221192 | tf_op jit(solution)/shard_map/ppermute | solution.py:81
  47.8 2.8 %collective-permute-start.14 = (bf16[288,128]{1,0:T(8,128)(2,1)S(1)}, bf16[288,128]{1,0:T(8,128)(2,1)S(1)}, u32[]{:S(2)}, u32[]{:S(2)}) collective-permute-start(bf16[288,128]{1,0:T(8,128)(2,1)S(1)} %collective-permute-done.12.refs_10_.refs_12_), channel_id=1, source_target_pairs={{0,2},{2,0},{4,6},{6,4},{8,10},{10,8},{12,14},{14,12},{16,18},{18,... | collective-permute-start | bytes 221192 | tf_op jit(solution)/shard_map/ppermute | solution.py:81
  50.1 1.3 %collective-permute-start.17 = (bf16[288,128]{1,0:T(8,128)(2,1)S(1)}, bf16[288,128]{1,0:T(8,128)(2,1)S(1)}, u32[]{:S(2)}, u32[]{:S(2)}) collective-permute-start(bf16[288,128]{1,0:T(8,128)(2,1)S(1)} %collective-permute-done.16.refs_16_), channel_id=1, source_target_pairs={{0,2},{2,0},{4,6},{6,4},{8,10},{10,8},{12,14},{14,12},{16,18},{18,... | collective-permute-start | bytes 221192 | tf_op jit(solution)/shard_map/ppermute | solution.py:81
  50.5 7.7 %copy-start.3 = (f32[32,256]{1,0:T(8,128)S(1)}, f32[32,256]{1,0:T(8,128)}, u32[]{:S(2)}) copy-start(f32[32,256]{1,0:T(8,128)} %copy-done.1) | copy-start | bytes 98308
  57.0 5.6 %collective-permute-start.18 = (bf16[256,256]{1,0:T(8,128)(2,1)S(1)}, bf16[256,256]{1,0:T(8,128)(2,1)S(1)}, u32[]{:S(2)}, u32[]{:S(2)}) collective-permute-start(bf16[256,256]{1,0:T(8,128)(2,1)S(1)} %get-tuple-element.32.refs_0_), channel_id=1, source_target_pairs={{1,0},{0,1},{3,2},{2,3},{5,4},{4,5},{7,6},{6,7},{9,8},{8,9},{11,10... | collective-permute-start | bytes 393224 | tf_op jit(solution)/shard_map/ppermute | solution.py:76
  60.7 6.6 %copy-start.9 = (bf16[4,256,256]{2,1,0:T(8,128)(2,1)S(1)}, bf16[4,256,256]{2,1,0:T(8,128)(2,1)}, u32[]{:S(2)}) copy-start(bf16[4,256,256]{2,1,0:T(8,128)(2,1)} %get-tuple-element.35) | copy-start | bytes 1572868
  67.3 19.9 %collective-permute-start.19 = (bf16[4,256,256]{2,1,0:T(8,128)(2,1)S(1)}, bf16[4,256,256]{2,1,0:T(8,128)(2,1)S(1)}, u32[]{:S(2)}, u32[]{:S(2)}) collective-permute-start(bf16[4,256,256]{2,1,0:T(8,128)(2,1)S(1)} %copy-done.9), channel_id=1, source_target_pairs={{1,0},{0,1},{3,2},{2,3},{5,4},{4,5},{7,6},{6,7},{9,8},{8,9},{11,10... | collective-permute-start | bytes 1572872 | tf_op jit(solution)/shard_map/ppermute | solution.py:76
  68.5 5.0 %collective-permute-start.20 = (bf16[256,256]{1,0:T(8,128)(2,1)S(1)}, bf16[256,256]{1,0:T(8,128)(2,1)S(1)}, u32[]{:S(2)}, u32[]{:S(2)}) collective-permute-start(bf16[256,256]{1,0:T(8,128)(2,1)S(1)} %second_call.1.refs_0_), channel_id=1, source_target_pairs={{0,4},{2,6},{4,0},{6,2},{8,12},{10,14},{12,8},{14,10},{16,20},{18,... | collective-permute-start | bytes 393224 | tf_op jit(solution)/shard_map/ppermute | solution.py:81
  70.0 10.9 %collective-permute-start.22 = (bf16[256,256]{1,0:T(8,128)(2,1)S(1)}, bf16[256,256]{1,0:T(8,128)(2,1)S(1)}, u32[]{:S(2)}, u32[]{:S(2)}) collective-permute-start(bf16[256,256]{1,0:T(8,128)(2,1)S(1)} %second_call.1.refs_0_), channel_id=1, source_target_pairs={{8,0},{10,2},{12,4},{14,6},{16,8},{18,10},{20,12},{22,14},{24,16},... | collective-permute-start | bytes 393224 | tf_op jit(solution)/shard_map/ppermute | solution.py:76
  73.0 10.4 %collective-permute-start.24 = (bf16[256,256]{1,0:T(8,128)(2,1)S(1)}, bf16[256,256]{1,0:T(8,128)(2,1)S(1)}, u32[]{:S(2)}, u32[]{:S(2)}) collective-permute-start(bf16[256,256]{1,0:T(8,128)(2,1)S(1)} %second_call.1.refs_0_), channel_id=1, source_target_pairs={{16,0},{18,2},{20,4},{22,6},{24,8},{26,10},{28,12},{30,14},{0,16},... | collective-permute-start | bytes 393224 | tf_op jit(solution)/shard_map/ppermute | solution.py:76
  73.1 11.1 %collective-permute-start.25 = (bf16[256,256]{1,0:T(8,128)(2,1)S(1)}, bf16[256,256]{1,0:T(8,128)(2,1)S(1)}, u32[]{:S(2)}, u32[]{:S(2)}) collective-permute-start(bf16[256,256]{1,0:T(8,128)(2,1)S(1)} %second_call.1.refs_0_), channel_id=1, source_target_pairs={{0,2},{2,0},{4,6},{6,4},{8,10},{10,8},{12,14},{14,12},{16,18},{18,... | collective-permute-start | bytes 393224 | tf_op jit(solution)/shard_map/ppermute | solution.py:81
  73.5 10.0 %collective-permute-start.23 = (bf16[256,256]{1,0:T(8,128)(2,1)S(1)}, bf16[256,256]{1,0:T(8,128)(2,1)S(1)}, u32[]{:S(2)}, u32[]{:S(2)}) collective-permute-start(bf16[256,256]{1,0:T(8,128)(2,1)S(1)} %second_call.1.refs_0_), channel_id=1, source_target_pairs={{24,0},{26,2},{28,4},{30,6},{0,8},{2,10},{4,12},{6,14},{8,16},{10,... | collective-permute-start | bytes 393224 | tf_op jit(solution)/shard_map/ppermute | solution.py:76
  80.9 5.0 %collective-permute-start.30 = (bf16[256,256]{1,0:T(8,128)(2,1)S(1)}, bf16[256,256]{1,0:T(8,128)(2,1)S(1)}, u32[]{:S(2)}, u32[]{:S(2)}) collective-permute-start(bf16[256,256]{1,0:T(8,128)(2,1)S(1)} %collective-permute-done.22.refs_1_), channel_id=1, source_target_pairs={{0,4},{2,6},{4,0},{6,2},{8,12},{10,14},{12,8},{14,10},{16,20},{18,... | collective-permute-start | bytes 393224 | tf_op jit(solution)/shard_map/ppermute | solution.py:81
  83.5 5.2 %collective-permute-start.26 = (bf16[256,256]{1,0:T(8,128)(2,1)S(1)}, bf16[256,256]{1,0:T(8,128)(2,1)S(1)}, u32[]{:S(2)}, u32[]{:S(2)}) collective-permute-start(bf16[256,256]{1,0:T(8,128)(2,1)S(1)} %collective-permute-done.22.refs_1_), channel_id=1, source_target_pairs={{0,2},{2,0},{4,6},{6,4},{8,10},{10,8},{12,14},{14,12},{16,18},{18,... | collective-permute-start | bytes 393224 | tf_op jit(solution)/shard_map/ppermute | solution.py:81
  83.5 6.3 %collective-permute-start.31 = (bf16[256,256]{1,0:T(8,128)(2,1)S(1)}, bf16[256,256]{1,0:T(8,128)(2,1)S(1)}, u32[]{:S(2)}, u32[]{:S(2)}) collective-permute-start(bf16[256,256]{1,0:T(8,128)(2,1)S(1)} %collective-permute-done.23.refs_2_), channel_id=1, source_target_pairs={{0,4},{2,6},{4,0},{6,2},{8,12},{10,14},{12,8},{14,10},{16,20},{18,... | collective-permute-start | bytes 393224 | tf_op jit(solution)/shard_map/ppermute | solution.py:81
  84.1 5.6 %collective-permute-start.27 = (bf16[256,256]{1,0:T(8,128)(2,1)S(1)}, bf16[256,256]{1,0:T(8,128)(2,1)S(1)}, u32[]{:S(2)}, u32[]{:S(2)}) collective-permute-start(bf16[256,256]{1,0:T(8,128)(2,1)S(1)} %collective-permute-done.23.refs_2_), channel_id=1, source_target_pairs={{0,2},{2,0},{4,6},{6,4},{8,10},{10,8},{12,14},{14,12},{16,18},{18,... | collective-permute-start | bytes 393224 | tf_op jit(solution)/shard_map/ppermute | solution.py:81
  85.9 6.2 %collective-permute-start.34 = (bf16[256,256]{1,0:T(8,128)(2,1)S(1)}, bf16[256,256]{1,0:T(8,128)(2,1)S(1)}, u32[]{:S(2)}, u32[]{:S(2)}) collective-permute-start(bf16[256,256]{1,0:T(8,128)(2,1)S(1)} %collective-permute-done.24.refs_3_), channel_id=1, source_target_pairs={{0,4},{2,6},{4,0},{6,2},{8,12},{10,14},{12,8},{14,10},{16,20},{18,... | collective-permute-start | bytes 393224 | tf_op jit(solution)/shard_map/ppermute | solution.py:81
  87.2 5.0 %collective-permute-start.28 = (bf16[256,256]{1,0:T(8,128)(2,1)S(1)}, bf16[256,256]{1,0:T(8,128)(2,1)S(1)}, u32[]{:S(2)}, u32[]{:S(2)}) collective-permute-start(bf16[256,256]{1,0:T(8,128)(2,1)S(1)} %collective-permute-done.24.refs_3_), channel_id=1, source_target_pairs={{0,2},{2,0},{4,6},{6,4},{8,10},{10,8},{12,14},{14,12},{16,18},{18,... | collective-permute-start | bytes 393224 | tf_op jit(solution)/shard_map/ppermute | solution.py:81
  88.7 9.2 %collective-permute-start.21 = (bf16[4,256,128]{2,1,0:T(8,128)(2,1)S(1)}, bf16[4,256,128]{2,1,0:T(8,128)(2,1)S(1)}, u32[]{:S(2)}, u32[]{:S(2)}) collective-permute-start(bf16[4,256,128]{2,1,0:T(8,128)(2,1)S(1)} %fusion.1), channel_id=1, source_target_pairs={{1,0},{0,1},{3,2},{2,3},{5,4},{4,5},{7,6},{6,7},{9,8},{8,9},{11,10... | collective-permute-start | bytes 786440 | tf_op jit(solution)/shard_map/ppermute | solution.py:76
  89.8 2.9 %collective-permute-start.29 = (bf16[256,256]{1,0:T(8,128)(2,1)S(1)}, bf16[256,256]{1,0:T(8,128)(2,1)S(1)}, u32[]{:S(2)}, u32[]{:S(2)}) collective-permute-start(bf16[256,256]{1,0:T(8,128)(2,1)S(1)} %collective-permute-done.20.refs_2_.refs_4_), channel_id=1, source_target_pairs={{0,2},{2,0},{4,6},{6,4},{8,10},{10,8},{12,14},{14,12},{16,18},{18,... | collective-permute-start | bytes 393224 | tf_op jit(solution)/shard_map/ppermute | solution.py:81
  89.8 2.9 %collective-permute-start.32 = (bf16[256,256]{1,0:T(8,128)(2,1)S(1)}, bf16[256,256]{1,0:T(8,128)(2,1)S(1)}, u32[]{:S(2)}, u32[]{:S(2)}) collective-permute-start(bf16[256,256]{1,0:T(8,128)(2,1)S(1)} %collective-permute-done.30.refs_10_), channel_id=1, source_target_pairs={{0,2},{2,0},{4,6},{6,4},{8,10},{10,8},{12,14},{14,12},{16,18},{18,... | collective-permute-start | bytes 393224 | tf_op jit(solution)/shard_map/ppermute | solution.py:81
  92.2 1.3 %collective-permute-start.33 = (bf16[256,256]{1,0:T(8,128)(2,1)S(1)}, bf16[256,256]{1,0:T(8,128)(2,1)S(1)}, u32[]{:S(2)}, u32[]{:S(2)}) collective-permute-start(bf16[256,256]{1,0:T(8,128)(2,1)S(1)} %collective-permute-done.31.refs_11_), channel_id=1, source_target_pairs={{0,2},{2,0},{4,6},{6,4},{8,10},{10,8},{12,14},{14,12},{16,18},{18,... | collective-permute-start | bytes 393224 | tf_op jit(solution)/shard_map/ppermute | solution.py:81
  92.2 1.5 %collective-permute-start.35 = (bf16[256,256]{1,0:T(8,128)(2,1)S(1)}, bf16[256,256]{1,0:T(8,128)(2,1)S(1)}, u32[]{:S(2)}, u32[]{:S(2)}) collective-permute-start(bf16[256,256]{1,0:T(8,128)(2,1)S(1)} %collective-permute-done.34.refs_14_), channel_id=1, source_target_pairs={{0,2},{2,0},{4,6},{6,4},{8,10},{10,8},{12,14},{14,12},{16,18},{18,... | collective-permute-start | bytes 393224 | tf_op jit(solution)/shard_map/ppermute | solution.py:81
